TPU v7x, 256 devices: a whole 4x4x8 slice. The times are simulated.
256 devices in a mesh: prow: 8 (over x, core), pcol: 32 (over z, y).
Axes of the slice: x: 4, y: 4, z: 8, core: 2. Of those that a mesh axis runs over, the one named last changes fastest.
Arguments:
- panel_rhs: float32 [512, 2, 1024], P('prow', None, 'pcol'), may hold values from -6 to 6
- diag_inv: float32 [2, 1024, 1024], P(None, 'pcol'), may hold values from -1 to 2, as said below
- coupling: float32 [1024, 1024], P('pcol'), may hold values from -0.1875 to 0.1875
- trail_factor: float32 [2, 1024, 114688], P(None, 'pcol', 'prow'), may hold values from -0.125 to 0.125
- trail_rhs: float32 [512, 114688], P('pcol', 'prow'), may hold values from -6 to 6
Outputs:
- solved: float32 [512, 2, 1024], P('prow', None, 'pcol')
- trail_reduced: float32 [512, 114688], P('pcol', 'prow')
Inputs may be any that keep to these rules, and one draw needn't show every extreme that they name: Each diag_inv[k] is upper triangular, with diagonal entries between 0.4 and 2.
All inputs are finite; a program needn't handle non-finite values.
Results may differ from a plain program's by a relative error of at most 0.000096.
Values sent between devices are 32-bit elements; how exact they have to be, the bound alone decides.
No kernel may reach another device: no remote copies, remote signals or barrier semaphores. Data moves between devices by JAX's collectives and lax.ppermute only.
A program may use at most 128 MiB of HBM per device.

v0:
```python
import jax
import jax.numpy as jnp
from jax import lax
from jax.sharding import PartitionSpec as P


def product(left, right):
    return jnp.dot(left, right, preferred_element_type=jnp.float32, precision=lax.Precision.HIGHEST)


def solve_panel(rhs_local, inverse_rows):
    return lax.psum_scatter(
        product(rhs_local, inverse_rows), "pcol", scatter_dimension=1, tiled=True
    )


def couple_panels(first, coupling):
    return lax.psum_scatter(product(first, coupling), "pcol", scatter_dimension=1, tiled=True)


def body(panel_rhs, diag_inv, coupling, trail_factor, trail_rhs):
    first = solve_panel(panel_rhs[:, 0, :], diag_inv[0])
    correction = couple_panels(first, coupling)
    latter = solve_panel(panel_rhs[:, 1, :] - correction, diag_inv[1])
    solved = jnp.stack([first, latter], axis=1)
    first_all, latter_all = (
        lax.all_gather(first, "prow", axis=0, tiled=True),
        lax.all_gather(latter, "prow", axis=0, tiled=True),
    )
    stacked = jnp.concatenate([first_all, latter_all], axis=1)
    factor_rows = trail_factor.reshape(2 * trail_factor.shape[1], trail_factor.shape[2])
    update = lax.psum_scatter(
        product(stacked, factor_rows), "pcol", scatter_dimension=0, tiled=True
    )
    return (solved, trail_rhs - update)


def solution(mesh):
    placed = (
        P("prow", None, "pcol"),
        P(None, "pcol", None),
        P("pcol", None),
        P(None, "pcol", "prow"),
        P("pcol", "prow"),
    )
    return jax.shard_map(
        body,
        mesh=mesh,
        in_specs=placed,
        out_specs=(P("prow", None, "pcol"), P("pcol", "prow")),
        check_vma=False,
    )
```

profile of v0, /device:TPU:20, one launch (start us, length us, event | category | flops | bytes accessed | tf_op | source)
XLA Modules:
  0.0 994.3 jit_solution(10475543446265176671)
XLA Ops:
  7.2 0.0 copy-start
  7.2 0.0 reduce-scatter.5.cloned.1.call-start
  7.2 2.7 fusion.6
  10.0 0.0 reduce-scatter.5.cloned.1.call-update
  10.0 0.0 reduce-scatter.7.cloned.1.call-start
  10.0 217.2 %reduce-scatter.5.cloned.1.call-done = f32[64,32]{0,1:T(8,128)} async-done(((f32[64,1024]{0,1:T(8,128)}), f32[64,32]{0,1:T(8,128)}) %reduce-scatter.5.cloned.1.call-update) | async-done | bytes 8208 | tf_op jit(solution)/shard_map/reduce_scatter | solution.py:12
  227.3 0.0 copy-done
  227.3 2.5 fusion.14
  229.8 0.0 reduce-scatter.7.cloned.1.call-update
  229.8 0.0 reduce-scatter.9.cloned.1.call-start
  229.9 213.6 %reduce-scatter.7.cloned.1.call-done = f32[64,32]{0,1:T(8,128)} async-done(((f32[64,1024]{0,1:T(8,128)}), f32[64,32]{0,1:T(8,128)}) %reduce-scatter.7.cloned.1.call-update) | async-done | bytes 8208 | tf_op jit(solution)/shard_map/reduce_scatter | solution.py:18
  443.4 2.7 fusion.4
  446.2 0.0 reduce-scatter.9.cloned.1.call-update
  446.2 0.0 reduce-scatter.11.cloned.1.call-start
  446.2 11.8 %all-gather = f32[8,64,32]{1,2,0:T(8,128)S(1)} all-gather(f32[1,64,32]{1,2,0:T(8,128)} %bitcast.25), channel_id=1, replica_groups=mesh['prow'=8,'pcol'=32] {'prow'}, dimensions={0}, use_global_device_ids=true | all-gather | bytes 73728 | tf_op jit(solution)/shard_map/all_gather | solution.py:27
  458.0 0.1 copy.9
  458.1 0.1 reshape.9
  458.2 201.1 %reduce-scatter.9.cloned.1.call-done = f32[64,32]{0,1:T(8,128)} async-done(((f32[64,1024]{0,1:T(8,128)}), f32[64,32]{0,1:T(8,128)}) %reduce-scatter.9.cloned.1.call-update) | async-done | bytes 8208 | tf_op jit(solution)/shard_map/reduce_scatter | solution.py:12
  659.2 11.7 %all-gather.1 = f32[8,64,32]{1,2,0:T(8,128)S(1)} all-gather(f32[1,64,32]{1,2,0:T(8,128)} %bitcast.27), channel_id=1, replica_groups=mesh['prow'=8,'pcol'=32] {'prow'}, dimensions={0}, use_global_device_ids=true | all-gather | bytes 73728 | tf_op jit(solution)/shard_map/all_gather | solution.py:28
  671.0 0.1 copy.10
  671.0 0.1 reshape.11
  671.1 27.8 %fusion = f32[512,14336]{1,0:T(8,128)} fusion(f32[64,14336]{1,0:T(8,128)} %bitcast.24, f32[512,32]{0,1:T(8,128)S(1)} %reshape.11, f32[512,32]{0,1:T(8,128)S(1)} %reshape.9), kind=kOutput, calls=%fused_computation | convolution fusion | flops 5637177344 | bytes 33161216 | tf_op jit(solution)/shard_map/dot_general | solution.py:8
  699.0 0.0 copy-start.2
  699.0 0.0 copy-start.3
  699.0 0.0 copy-start.1
  699.0 0.0 reduce-scatter.11.cloned.1.call-update
  699.0 0.7 copy-done.2
  699.7 0.0 copy-done.3
  699.7 0.6 pad_maximum_fusion
  700.3 285.2 %reduce-scatter.11.cloned.1.call-done = f32[16,14336]{1,0:T(8,128)} async-done(((f32[512,14336]{1,0:T(8,128)}), f32[16,14336]{1,0:T(8,128)}) %reduce-scatter.11.cloned.1.call-update) | async-done | bytes 917520 | tf_op jit(solution)/shard_map/reduce_scatter | solution.py:32
  985.5 0.0 copy-done.1
  985.5 2.2 sub.7
Async XLA Ops:
  7.2 220.1 %copy-start = (f32[32,1024]{1,0:T(8,128)S(1)}, f32[32,1024]{1,0:T(8,128)}, u32[]{:S(2)}) copy-start(f32[32,1024]{1,0:T(8,128)} %param.7) | copy-start | bytes 393220
  7.2 220.1 %reduce-scatter.5.cloned.1.call-start = ((), (), s32[]{:S(2)}) async-start(), calls=%async_computation.4 | async-start | bytes 540672 | tf_op jit(solution)/shard_map/reduce_scatter | solution.py:12
  10.0 433.4 %reduce-scatter.7.cloned.1.call-start = ((), (), s32[]{:S(2)}) async-start(), calls=%async_computation.5 | async-start | bytes 540672 | tf_op jit(solution)/shard_map/reduce_scatter | solution.py:18
  229.8 429.4 %reduce-scatter.9.cloned.1.call-start = ((), (), s32[]{:S(2)}) async-start(), calls=%async_computation.6 | async-start | bytes 540672 | tf_op jit(solution)/shard_map/reduce_scatter | solution.py:12
  446.2 539.4 %reduce-scatter.11.cloned.1.call-start = ((), (), s32[]{:S(2)}) async-start(), calls=%async_computation.7 | async-start | bytes 30277632 | tf_op jit(solution)/shard_map/reduce_scatter | solution.py:32
  699.0 0.7 copy-start.2
  699.0 0.7 copy-start.3
  699.0 286.6 %copy-start.1 = (f32[16,14336]{1,0:T(8,128)S(1)}, f32[16,14336]{1,0:T(8,128)}, u32[]{:S(2)}) copy-start(f32[16,14336]{1,0:T(8,128)} %param.9) | copy-start | bytes 2752516
Sparse Core Ops, SparseCore 0:
  12.4 214.8 reduce-scatter.4
  232.1 211.2 reduce-scatter.6
  447.8 211.3 reduce-scatter.8
  699.1 286.3 reduce-scatter.10
where the time goes:
time: 996 us; the launch traced here: 994 us
  waiting for transfers between devices  917 us (92%)
  matrix products  35.8 us (4%)
  blocking collectives  23.5 us (2%)
  between operations  13.8 us (1%)
    reduce_scatter x2, waiting for transfers between devices, solve_panel(): lax.psum_scatter(product(rhs_local, inverse_rows), 'pcol', scatter_dimens...  418 us
    reduce_scatter x1, waiting for transfers between devices, body(): lax.psum_scatter(product(stacked, factor_rows), 'pcol', scatter_dimension...  285 us
    reduce_scatter x1, waiting for transfers between devices, couple_panels(): lax.psum_scatter(product(first, coupling), 'pcol', scatter_dimension=1, t...  214 us
    dot_general x4, matrix products, product(): jnp.dot(left, right, preferred_element_type=jnp.float32, precision=lax.Pr...  35.8 us
  transfers between devices with their start and end apart: 4, of which 4 were waited for; matrix products, arithmetic and copies ran while one was open for 0% of the time, Pallas kernels for 0%

commit v1 on v0

v1 whole, which is shorter than its diff:
```python
import jax
import jax.numpy as jnp
from jax import lax
from jax.sharding import Mesh, PartitionSpec as P

X, C, Z, Y = 4, 2, 8, 4
ROWS = ("x", "c")
COLS = ("z", "y")
SPREAD = ("x", "c", "y")
QUAD = 4


def einsum(form, left, right, precision=lax.Precision.HIGHEST):
    return jnp.einsum(form, left, right, preferred_element_type=jnp.float32, precision=precision)


def reduce_over_z(terms):
    return jnp.sum(lax.all_to_all(terms, "z", 0, 0, tiled=True), axis=0)


def gather_rows(piece):
    copies = jnp.broadcast_to(piece[None], (X * C * Y, *piece.shape))
    gathered = lax.all_to_all(copies, SPREAD, 0, 0, tiled=True)
    return gathered.reshape(-1, piece.shape[1])


def gather_y(piece):
    copies = jnp.broadcast_to(piece[None], (Y, *piece.shape))
    return lax.all_to_all(copies, "y", 0, 0, tiled=True).reshape(-1, piece.shape[1])


def shift_y(value, step):
    return lax.ppermute(value, "y", [(y, (y + step) % Y) for y in range(Y)])


def shift_z(value, step):
    return lax.ppermute(value, "z", [(z, (z + step) % Z) for z in range(Z)])


def shift_far(value):
    pairs = [
        (c * Z + z, c * Z + (z + (2 if c else -2)) % Z) for c in range(C) for z in range(Z)
    ]
    return lax.ppermute(value, ("c", "z"), pairs)


def factor_over_y(factor, y):
    rows, width = factor.shape[0], factor.shape[1] // (QUAD * Y)
    blocks = factor.reshape(rows, QUAD, Y, width)
    merged = jnp.zeros((QUAD, Y * rows, width), factor.dtype)
    for step in range(Y):
        block = lax.dynamic_index_in_dim(blocks, (y + step) % Y, 2, keepdims=False)
        block = block.transpose(1, 0, 2)
        if step:
            block = shift_y(block, step)
        merged = lax.dynamic_update_slice_in_dim(merged, block, ((y - step) % Y) * rows, 1)
    return merged


def window(merged, z, core):
    pick = lambda k: lax.dynamic_index_in_dim(merged, k % QUAD, 0, keepdims=False)
    return jnp.concatenate(
        [pick(z), shift_z(pick(z + 1), 1), shift_z(pick(z - 1), -1), shift_far(pick(z + 2))], axis=0
    )


def window_of_solved(rows):
    return jnp.concatenate(
        [rows, shift_z(rows, 1), shift_z(rows, -1), shift_far(rows)], axis=1
    )


def body(panel_rhs, diag_inv, coupling, trail_factor, trail_rhs):
    core, z, y = lax.axis_index("c"), lax.axis_index("z"), lax.axis_index("y")
    prow = lax.axis_index("x") * C + core
    strip, narrow = panel_rhs.shape[0], panel_rhs.shape[2]

    rhs = lax.all_to_all(panel_rhs, "y", 0, 2, tiled=True)
    blocked = lambda m: m.reshape(m.shape[0], Z, -1)
    inv_first = blocked(gather_y(diag_inv[0]))
    couple = blocked(gather_y(coupling))
    inv_second = blocked(gather_y(diag_inv[1]))

    first = reduce_over_z(einsum("rk,kzc->zrc", rhs[:, 0], inv_first))
    second = rhs[:, 1] - reduce_over_z(einsum("rk,kzc->zrc", first, couple))
    latter = reduce_over_z(einsum("rk,kzc->zrc", second, inv_second))

    first_all = gather_rows(first)
    latter_all = gather_rows(latter)
    own = lambda rows: lax.dynamic_slice(rows, (prow * strip, y * narrow), (strip, narrow))
    solved = jnp.stack([own(first_all), own(latter_all)], axis=1)

    factor_first = window(factor_over_y(trail_factor[0], y), z, core)
    factor_latter = window(factor_over_y(trail_factor[1], y), z, core)
    update = einsum("rk,kc->rc", window_of_solved(first_all), factor_first, lax.Precision.HIGH)
    update = update + einsum("rk,kc->rc", window_of_solved(latter_all), factor_latter, lax.Precision.HIGH)

    parts = lax.all_to_all(update.reshape(Z * Y, -1, update.shape[1]), COLS, 0, 0, tiled=True)
    parts = parts.reshape(2, QUAD * Y, *parts.shape[1:])
    total = (parts[0] + parts[1]).transpose(1, 0, 2).reshape(trail_rhs.shape)
    return solved, trail_rhs - total


def solution(mesh):
    devices = Mesh(mesh.devices.reshape(X, C, Z, Y), ("x", "c", "z", "y"))
    placed = (
        P(ROWS, None, COLS),
        P(None, COLS, None),
        P(COLS, None),
        P(None, COLS, ROWS),
        P(COLS, ROWS),
    )
    return jax.shard_map(
        body,
        mesh=devices,
        in_specs=placed,
        out_specs=(P(ROWS, None, COLS), P(COLS, ROWS)),
        check_vma=False,
    )
```

time: 996 us -> 264 us (0.27)
  waiting for transfers between devices: 917 us -> 77.7 us
  starting transfers between devices: 0.16 us -> 82.6 us
  local copies, waits for them, and re-layouts: 1.06 us -> 59 us
  matrix products: 35.8 us -> 10.2 us
  between operations: 13.8 us -> 1.03 us
    reduce_scatter x4 -> x0, waiting for transfers between devices: 917 us -> none  [the longest x2 418 us: solve_panel(): lax.psum_scatter(product(rhs_local, inverse_rows), 'pcol', scatter_dimens...]
    all_to_all x0 -> x8, waiting for transfers between devices: none -> 56.6 us  [the longest x1 34.6 us: body(): lax.all_to_all(update.reshape(Z * Y, -1, update.shape[1]), COLS, 0, 0, ti...]
    all_to_all x0 -> x8, starting transfers between devices: none -> 51.8 us  [the longest x3 15.4 us: gather_y(): lax.all_to_all(copies, 'y', 0, 0, tiled=True).reshape(-1, piece.shape[1])]
    ppermute x0 -> x18, starting transfers between devices: none -> 30.9 us  [the longest x8 14.7 us: shift_z(): return lax.ppermute(value, 'z', [(z, (z + step) % Z) for z in range(Z)])]
    all_to_all x0 -> x2, blocking collectives: none -> 29.6 us  [the longest x1 16 us: reduce_over_z(): return jnp.sum(lax.all_to_all(terms, 'z', 0, 0, tiled=True), axis=0)]
    dot_general x4 -> x5, matrix products: 35.8 us -> 10.2 us  [einsum(): jnp.einsum(form, left, right, preferred_element_type=jnp.float32, precisi...]
    all_gather x2 -> x0, blocking collectives: 23.5 us -> none  [the longest x1 11.8 us: body(): lax.all_gather(first, 'prow', axis=0, tiled=True)]
    ppermute x0 -> x18, waiting for transfers between devices: none -> 21.1 us  [the longest x4 18.3 us: shift_far(): return lax.ppermute(value, ('c', 'z'), pairs)]
  transfers between devices with their start and end apart: 4 -> 26, of which waited for: 4 -> 6; matrix products, arithmetic and copies ran while one was open for 0% -> 24% of each run, Pallas kernels for 0% -> 0%
where the time goes in v1:
time: 264 us; the launch traced here: 263 us
  starting transfers between devices  82.6 us (31%)
  waiting for transfers between devices  77.7 us (29%)
  local copies, waits for them, and re-layouts  59 us (22%)
  blocking collectives  29.6 us (11%)
  matrix products  10.2 us (4%)
    all_to_all x1, waiting for transfers between devices, body(): lax.all_to_all(update.reshape(Z * Y, -1, update.shape[1]), COLS, 0, 0, ti...  34.6 us
    all_to_all x3, waiting for transfers between devices, gather_y(): lax.all_to_all(copies, 'y', 0, 0, tiled=True).reshape(-1, piece.shape[1])  20 us
    ppermute x4, waiting for transfers between devices, shift_far(): return lax.ppermute(value, ('c', 'z'), pairs)  18.3 us
    all_to_all x1, blocking collectives, reduce_over_z(): return jnp.sum(lax.all_to_all(terms, 'z', 0, 0, tiled=True), axis=0)  16 us
    all_to_all x3, starting transfers between devices, gather_y(): lax.all_to_all(copies, 'y', 0, 0, tiled=True).reshape(-1, piece.shape[1])  15.4 us
    ppermute x8, starting transfers between devices, shift_z(): return lax.ppermute(value, 'z', [(z, (z + step) % Z) for z in range(Z)])  14.7 us
    all_to_all x2, starting transfers between devices, reduce_over_z(): return jnp.sum(lax.all_to_all(terms, 'z', 0, 0, tiled=True), axis=0)  14.2 us
    all_to_all x1, blocking collectives, gather_rows(): gathered = lax.all_to_all(copies, SPREAD, 0, 0, tiled=True)  13.6 us
  transfers between devices with their start and end apart: 26, of which 6 were waited for; matrix products, arithmetic and copies ran while one was open for 24% of the time, Pallas kernels for 0%

profile of v1, /device:TPU:20, one launch (start us, length us, event | category | flops | bytes accessed | tf_op | source)
XLA Modules:
  0.0 262.6 jit_solution(1165588485571564765)
XLA Ops:
  2.2 4.8 %all-to-all-start.1 = ((f32[4,1,1024]{2,1,0:T(1,128)}), f32[4,1,1024]{2,1,0:T(1,128)S(1)}, u32[]{:S(2)}, u32[]{:S(2)}) async-start(f32[4,1,1024]{2,1,0:T(1,128)} %reshape.33), calls=%async_computation.1 | async-start | bytes 32768 | tf_op jit(solution)/shard_map/all_to_all | solution.py:78
  10.8 5.8 %all-to-all-start = ((f32[4,32,1024]{2,1,0:T(8,128)}), f32[4,32,1024]{2,1,0:T(8,128)S(1)}, u32[]{:S(2)}, u32[]{:S(2)}) async-start(f32[4,32,1024]{2,1,0:T(8,128)} %broadcast_in_dim.15), calls=%async_computation | async-start | bytes 1048576 | tf_op jit(solution)/shard_map/all_to_all | solution.py:29
  16.7 3.5 %fusion.43 = (f32[1,32,14336]{2,1,0:T(8,128)}, f32[1,32,14336]{2,1,0:T(8,128)S(1)}) fusion(f32[2,32,14336]{2,1,0:T(8,128)} %param.8), kind=kLoop, calls=%fused_computation.87 | loop fusion | bytes 7340032 | tf_op jit(solution)/shard_map/slice | solution.py:93
  20.2 3.6 %reshape_squeeze.6 = f32[32,4,4,896]{3,2,1,0:T(4,128)} reshape(f32[1,32,14336]{2,1,0:T(8,128)} %get-tuple-element.2) | data formatting | bytes 3670016 | tf_op jit(solution)/shard_map/reshape;squeeze | solution.py:49
  23.8 2.5 reshape_squeeze.7
  27.1 4.8 %all-to-all-start.4 = ((f32[4,32,1024]{2,1,0:T(8,128)}), f32[4,32,1024]{2,1,0:T(8,128)S(1)}, u32[]{:S(2)}, u32[]{:S(2)}) async-start(f32[4,32,1024]{2,1,0:T(8,128)} %broadcast_in_dim.17), calls=%async_computation.4 | async-start | bytes 1048576 | tf_op jit(solution)/shard_map/all_to_all | solution.py:29
  31.9 10.4 %constant_dynamic-slice_fusion.4 = (f32[32,4,1,896]{3,2,1,0:T(1,128)}, f32[32,4,1,896]{3,2,1,0:T(1,128)S(1)}, f32[32,4,1,896]{3,2,1,0:T(1,128)S(1)}, f32[32,4,1,...) fusion(f32[32,4,4,896]{3,2,1,0:T(4,128)} %reshape_squeeze.7, ...), kind=kLoop, calls=%fused_computation.68 | loop fusion | bytes 7340048 | tf_op jit(solution)/shard_map/jit(dynamic_index_in_dim)/dynamic_slice | solution.py:52
  50.9 2.6 %collective-permute-start.13 = (f32[4,32,896]{2,0,1:T(4,128)}, f32[4,32,896]{2,0,1:T(4,128)}, u32[]{:S(2)}, u32[]{:S(2)}) collective-permute-start(f32[4,32,896]{2,0,1:T(4,128)} %bitcast.102), channel_id=1, source_target_pairs={{0,2},{1,3},{2,0},{3,1},{4,6},{5,7},{6,4},{7,5},{8,10},{9,11},{10,... | collective-permute-start | bytes 1376264 | tf_op jit(solution)/shard_map/ppermute | solution.py:33
  56.8 4.8 %all-to-all-start.6 = ((f32[4,32,1024]{2,1,0:T(8,128)}), f32[4,32,1024]{2,1,0:T(8,128)S(1)}, u32[]{:S(2)}, u32[]{:S(2)}) async-start(f32[4,32,1024]{2,1,0:T(8,128)} %broadcast_in_dim.37), calls=%async_computation.6 | async-start | bytes 1048576 | tf_op jit(solution)/shard_map/all_to_all | solution.py:29
  68.6 20.0 %all-to-all-done.6 = f32[4,32,1024]{2,1,0:T(8,128)S(1)} async-done(((f32[4,32,1024]{2,1,0:T(8,128)}), f32[4,32,1024]{2,1,0:T(8,128)S(1)}, u32[]{:S(2)}, u32[]{:S(2)}) %all-to-all-start.6) | async-done | bytes 524320 | tf_op jit(solution)/shard_map/all_to_all | solution.py:29
  88.6 8.5 %all-to-all-start.2 = ((f32[8,16,128]{2,1,0:T(8,128)}), f32[8,16,128]{2,1,0:T(8,128)S(1)}, u32[]{:S(2)}, u32[]{:S(2)}) async-start(f32[8,16,128]{2,1,0:T(8,128)} %convolution_bitcast_fusion.2), calls=%async_computation.2 | async-start | bytes 131072 | tf_op jit(solution)/shard_map/all_to_all | solution.py:18
  102.8 6.4 %constant_dynamic-slice_fusion.11 = (f32[1,128,896]{2,0,1:T(1,128)S(1)}, f32[1,128,896]{2,0,1:T(1,128)}, f32[1,128,896]{2,0,1:T(1,128)}, f32[1,128,896]{2,0,1:T(1,128)S(1)}) fusion(f32[4,128,896]{2,0,1:T(4,128)} %constant_dynamic-update-slice_fusion.3, s32[]{:T(128)S(6)} %select_n.149, s32[]{:T(128)S(6)} %select_n.155, s32[]{:T(128)S(6)} %select_n.153, ...), kind=kLoop, calls=%fused_computation.77 | loop fusion | bytes 3670032 | tf_op jit(solution)/shard_map/jit(dynamic_index_in_dim)/dynamic_slice | solution.py:61
  110.1 2.0 collective-permute-start.6
  115.5 5.7 %all-to-all-start.5 = ((f32[8,16,128]{2,1,0:T(8,128)}), f32[8,16,128]{2,1,0:T(8,128)S(1)}, u32[]{:S(2)}, u32[]{:S(2)}) async-start(f32[8,16,128]{2,1,0:T(8,128)} %convolution_bitcast_fusion.1), calls=%async_computation.5 | async-start | bytes 131072 | tf_op jit(solution)/shard_map/all_to_all | solution.py:18
  121.3 2.3 constant_dynamic-slice_fusion.3
  124.4 2.0 collective-permute-start.15
  127.8 3.0 %collective-permute-start.17 = (f32[128,896]{1,0:T(8,128)S(1)}, f32[128,896]{1,0:T(8,128)}, u32[]{:S(2)}, u32[]{:S(2)}) collective-permute-start(f32[128,896]{1,0:T(8,128)S(1)} %bitcast.125), channel_id=1, source_target_pairs={{0,24},{4,28},{8,0},{12,4},{16,8},{20,12},{24,16},{28,20},{32,40},... | collective-permute-start | bytes 1376264 | tf_op jit(solution)/shard_map/ppermute | solution.py:44
  131.2 16.0 %all_to_all.64 = f32[8,16,128]{2,1,0:T(8,128)S(1)} all-to-all(f32[8,16,128]{2,1,0:T(8,128)S(1)} %convolution_bitcast_fusion), channel_id=1, replica_groups=mesh['x'=4,'c'=2,'z'=8,'y'=4] {'z'}, dimensions={0} | all-to-all | bytes 131072 | tf_op jit(solution)/shard_map/all_to_all | solution.py:18
  147.3 13.6 %all_to_all.63 = f32[32,16,128]{2,1,0:T(8,128)} all-to-all(f32[32,16,128]{2,1,0:T(8,128)S(1)} %broadcast_in_dim.38), channel_id=1, replica_groups=mesh['x'=4,'c'=2,'z'=8,'y'=4] {'x','c','y'}, dimensions={0} | all-to-all | bytes 524288 | tf_op jit(solution)/shard_map/all_to_all | solution.py:23
  160.8 2.6 collective-permute-start.10
  167.0 7.7 %all-to-all-start.3 = ((f32[32,16,128]{2,1,0:T(8,128)}), f32[32,16,128]{2,1,0:T(8,128)S(1)}, u32[]{:S(2)}, u32[]{:S(2)}) async-start(f32[32,16,128]{2,1,0:T(8,128)} %broadcast_in_dim.16), calls=%async_computation.3 | async-start | bytes 524288 | tf_op jit(solution)/shard_map/all_to_all | solution.py:23
  176.4 2.3 collective-permute-start.7
  178.7 2.2 collective-permute-start.8
  181.6 2.5 collective-permute-start.1
  184.1 2.5 collective-permute-start.2
  186.7 3.5 %fusion.8 = f32[512,896]{1,0:T(8,128)S(1)} fusion(f32[128,896]{1,0:T(8,128)} %collective-permute-done.17, f32[128,896]{1,0:T(8,128)} %collective-permute-done.16, f32[128,896]{1,0:T(8,128)} %collective-permute-done.15, f32[128,896]{1,0:T(8,128)S(1)} %bitcast.127, f32[512,128]{1,0:T(8,128)} %collective-permute-done.11, ...), kind=kOutput, calls=%fused_computation.8 | convolution fusion | flops 1411448832 | bytes 4718592 | tf_op jit(solution)/shard_map/rk,kc->rc/dot_general | solution.py:14
  190.2 12.6 %collective-permute-done.8 = f32[128,896]{1,0:T(8,128)S(1)} collective-permute-done((f32[128,896]{1,0:T(8,128)}, f32[128,896]{1,0:T(8,128)S(1)}, u32[]{:S(2)}, u32[]{:S(2)}) %collective-permute-start.8) | collective-permute-done | bytes 458784 | tf_op jit(solution)/shard_map/ppermute | solution.py:44
  202.9 2.7 %collective-permute-done.1 = f32[512,128]{1,0:T(8,128)S(1)} collective-permute-done((f32[512,128]{1,0:T(8,128)S(1)}, f32[512,128]{1,0:T(8,128)S(1)}, u32[]{:S(2)}, u32[]{:S(2)}) %collective-permute-start.1) | collective-permute-done | bytes 262176 | tf_op jit(solution)/shard_map/ppermute | solution.py:37
  205.6 5.7 %collective-permute-done.2 = f32[512,128]{1,0:T(8,128)S(1)} collective-permute-done((f32[512,128]{1,0:T(8,128)S(1)}, f32[512,128]{1,0:T(8,128)S(1)}, u32[]{:S(2)}, u32[]{:S(2)}) %collective-permute-start.2) | collective-permute-done | bytes 262176 | tf_op jit(solution)/shard_map/ppermute | solution.py:44
  211.3 4.2 %fusion.16 = f32[512,896]{1,0:T(8,128)} fusion(f32[512,896]{1,0:T(8,128)S(1)} %fusion.8, f32[128,896]{1,0:T(8,128)S(1)} %collective-permute-done.8, f32[128,896]{1,0:T(8,128)S(1)} %collective-permute-done.7, f32[128,896]{1,0:T(8,128)} %collective-permute-done.6, f32[128,896]{1,0:T(8,128)S(1)} %bitcast.118, f32[512,128]{1,0:T(8,128)S(1)} %collective-permute-done.2, ...), kind=kOutput, calls=%fused_computation.16 | convolution fusion | flops 1411907584 | bytes 6553600 | tf_op jit(solution)/shard_map/rk,kc->rc/dot_general | solution.py:14
  215.5 9.6 %all-to-all-start.9 = ((f32[32,16,896]{2,1,0:T(8,128)}), f32[32,16,896]{2,1,0:T(8,128)S(1)}, u32[]{:S(2)}, u32[]{:S(2)}) async-start(f32[32,16,896]{2,1,0:T(8,128)} %bitcast.25), calls=%async_computation.9 | async-start | bytes 3670016 | tf_op jit(solution)/shard_map/all_to_all | solution.py:98
  226.8 34.6 %all-to-all-done.9 = f32[32,16,896]{2,1,0:T(8,128)S(1)} async-done(((f32[32,16,896]{2,1,0:T(8,128)}), f32[32,16,896]{2,1,0:T(8,128)S(1)}, u32[]{:S(2)}, u32[]{:S(2)}) %all-to-all-start.9) | async-done | bytes 1835040 | tf_op jit(solution)/shard_map/all_to_all | solution.py:98
  (97 shorter events, 46.3 us)
Async XLA Ops:
  2.2 7.8 %all-to-all-start.1 = ((f32[4,1,1024]{2,1,0:T(1,128)}), f32[4,1,1024]{2,1,0:T(1,128)S(1)}, u32[]{:S(2)}, u32[]{:S(2)}) async-start(f32[4,1,1024]{2,1,0:T(1,128)} %reshape.33), calls=%async_computation.1 | async-start | bytes 32768 | tf_op jit(solution)/shard_map/all_to_all | solution.py:78
  10.8 15.5 %all-to-all-start = ((f32[4,32,1024]{2,1,0:T(8,128)}), f32[4,32,1024]{2,1,0:T(8,128)S(1)}, u32[]{:S(2)}, u32[]{:S(2)}) async-start(f32[4,32,1024]{2,1,0:T(8,128)} %broadcast_in_dim.15), calls=%async_computation | async-start | bytes 1048576 | tf_op jit(solution)/shard_map/all_to_all | solution.py:29
  23.8 2.5 copy-start.5
  27.1 28.8 %all-to-all-start.4 = ((f32[4,32,1024]{2,1,0:T(8,128)}), f32[4,32,1024]{2,1,0:T(8,128)S(1)}, u32[]{:S(2)}, u32[]{:S(2)}) async-start(f32[4,32,1024]{2,1,0:T(8,128)} %broadcast_in_dim.17), calls=%async_computation.4 | async-start | bytes 1048576 | tf_op jit(solution)/shard_map/all_to_all | solution.py:29
  43.2 54.0 %collective-permute-start.3 = (f32[4,32,896]{2,0,1:T(4,128)}, f32[4,32,896]{2,0,1:T(4,128)}, u32[]{:S(2)}, u32[]{:S(2)}) collective-permute-start(f32[4,32,896]{2,0,1:T(4,128)} %bitcast.110), channel_id=1, source_target_pairs={{0,1},{1,2},{2,3},{3,0},{4,5},{5,6},{6,7},{7,4},{8,9},{9,10},{10,1... | collective-permute-start | bytes 1376264 | tf_op jit(solution)/shard_map/ppermute | solution.py:33
  45.3 53.8 %collective-permute-start.4 = (f32[4,32,896]{2,0,1:T(4,128)}, f32[4,32,896]{2,0,1:T(4,128)}, u32[]{:S(2)}, u32[]{:S(2)}) collective-permute-start(f32[4,32,896]{2,0,1:T(4,128)} %bitcast.109), channel_id=1, source_target_pairs={{0,2},{1,3},{2,0},{3,1},{4,6},{5,7},{6,4},{7,5},{8,10},{9,11},{10,... | collective-permute-start | bytes 1376264 | tf_op jit(solution)/shard_map/ppermute | solution.py:33
  47.0 53.9 %collective-permute-start.5 = (f32[4,32,896]{2,0,1:T(4,128)}, f32[4,32,896]{2,0,1:T(4,128)}, u32[]{:S(2)}, u32[]{:S(2)}) collective-permute-start(f32[4,32,896]{2,0,1:T(4,128)} %bitcast.108), channel_id=1, source_target_pairs={{0,3},{1,0},{2,1},{3,2},{4,7},{5,4},{6,5},{7,6},{8,11},{9,8},{10,9... | collective-permute-start | bytes 1376264 | tf_op jit(solution)/shard_map/ppermute | solution.py:33
  48.6 63.6 %collective-permute-start.12 = (f32[4,32,896]{2,0,1:T(4,128)}, f32[4,32,896]{2,0,1:T(4,128)}, u32[]{:S(2)}, u32[]{:S(2)}) collective-permute-start(f32[4,32,896]{2,0,1:T(4,128)} %bitcast.103), channel_id=1, source_target_pairs={{0,1},{1,2},{2,3},{3,0},{4,5},{5,6},{6,7},{7,4},{8,9},{9,10},{10,1... | collective-permute-start | bytes 1376264 | tf_op jit(solution)/shard_map/ppermute | solution.py:33
  50.9 62.3 %collective-permute-start.13 = (f32[4,32,896]{2,0,1:T(4,128)}, f32[4,32,896]{2,0,1:T(4,128)}, u32[]{:S(2)}, u32[]{:S(2)}) collective-permute-start(f32[4,32,896]{2,0,1:T(4,128)} %bitcast.102), channel_id=1, source_target_pairs={{0,2},{1,3},{2,0},{3,1},{4,6},{5,7},{6,4},{7,5},{8,10},{9,11},{10,... | collective-permute-start | bytes 1376264 | tf_op jit(solution)/shard_map/ppermute | solution.py:33
  56.8 31.8 %all-to-all-start.6 = ((f32[4,32,1024]{2,1,0:T(8,128)}), f32[4,32,1024]{2,1,0:T(8,128)S(1)}, u32[]{:S(2)}, u32[]{:S(2)}) async-start(f32[4,32,1024]{2,1,0:T(8,128)} %broadcast_in_dim.37), calls=%async_computation.6 | async-start | bytes 1048576 | tf_op jit(solution)/shard_map/all_to_all | solution.py:29
  88.6 25.8 %all-to-all-start.2 = ((f32[8,16,128]{2,1,0:T(8,128)}), f32[8,16,128]{2,1,0:T(8,128)S(1)}, u32[]{:S(2)}, u32[]{:S(2)}) async-start(f32[8,16,128]{2,1,0:T(8,128)} %convolution_bitcast_fusion.2), calls=%async_computation.2 | async-start | bytes 131072 | tf_op jit(solution)/shard_map/all_to_all | solution.py:18
  97.2 17.1 %collective-permute-start.14 = (f32[4,32,896]{2,0,1:T(4,128)}, f32[4,32,896]{2,0,1:T(4,128)S(1)}, u32[]{:S(2)}, u32[]{:S(2)}) collective-permute-start(f32[4,32,896]{2,0,1:T(4,128)} %bitcast.124), channel_id=1, source_target_pairs={{0,3},{1,0},{2,1},{3,2},{4,7},{5,4},{6,5},{7,6},{8,11},{9,8},{10,9... | collective-permute-start | bytes 1376264 | tf_op jit(solution)/shard_map/ppermute | solution.py:33
  109.3 5.2 %copy-start = (f32[16,8,8,128]{3,2,1,0:T(8,128)S(1)}, f32[16,8,8,128]{3,2,1,0:T(8,128)}, u32[]{:S(2)}) copy-start(f32[16,8,8,128]{3,2,1,0:T(8,128)} %copy.51) | copy-start | bytes 1572868
  110.1 53.3 %collective-permute-start.6 = (f32[128,896]{1,0:T(8,128)}, f32[128,896]{1,0:T(8,128)}, u32[]{:S(2)}, u32[]{:S(2)}) collective-permute-start(f32[128,896]{1,0:T(8,128)} %bitcast.106), channel_id=1, source_target_pairs={{0,4},{4,8},{8,12},{12,16},{16,20},{20,24},{24,28},{28,0},{1,5},{5... | collective-permute-start | bytes 1376264 | tf_op jit(solution)/shard_map/ppermute | solution.py:37
  115.5 15.3 %all-to-all-start.5 = ((f32[8,16,128]{2,1,0:T(8,128)}), f32[8,16,128]{2,1,0:T(8,128)S(1)}, u32[]{:S(2)}, u32[]{:S(2)}) async-start(f32[8,16,128]{2,1,0:T(8,128)} %convolution_bitcast_fusion.1), calls=%async_computation.5 | async-start | bytes 131072 | tf_op jit(solution)/shard_map/all_to_all | solution.py:18
  124.4 40.6 %collective-permute-start.15 = (f32[128,896]{1,0:T(8,128)}, f32[128,896]{1,0:T(8,128)}, u32[]{:S(2)}, u32[]{:S(2)}) collective-permute-start(f32[128,896]{1,0:T(8,128)} %bitcast.99), channel_id=1, source_target_pairs={{0,4},{4,8},{8,12},{12,16},{16,20},{20,24},{24,28},{28,0},{1,5},{5... | collective-permute-start | bytes 1376264 | tf_op jit(solution)/shard_map/ppermute | solution.py:37
  126.5 48.3 %copy-start.2 = (f32[1,128,896]{2,0,1:T(1,128)S(1)}, f32[1,128,896]{2,0,1:T(1,128)}, u32[]{:S(2)}) copy-start(f32[1,128,896]{2,0,1:T(1,128)} %get-tuple-element.6) | copy-start | bytes 1376260
  126.5 49.9 %collective-permute-start.16 = (f32[128,896]{1,0:T(8,128)S(1)}, f32[128,896]{1,0:T(8,128)}, u32[]{:S(2)}, u32[]{:S(2)}) collective-permute-start(f32[128,896]{1,0:T(8,128)S(1)} %bitcast.126), channel_id=1, source_target_pairs={{0,28},{4,0},{8,4},{12,8},{16,12},{20,16},{24,20},{28,24},{1,29},{... | collective-permute-start | bytes 1376264 | tf_op jit(solution)/shard_map/ppermute | solution.py:37
  127.8 47.8 %copy-start.1 = (f32[1,128,896]{2,0,1:T(1,128)S(1)}, f32[1,128,896]{2,0,1:T(1,128)}, u32[]{:S(2)}) copy-start(f32[1,128,896]{2,0,1:T(1,128)} %get-tuple-element.5) | copy-start | bytes 1376260
  127.8 50.9 %collective-permute-start.17 = (f32[128,896]{1,0:T(8,128)S(1)}, f32[128,896]{1,0:T(8,128)}, u32[]{:S(2)}, u32[]{:S(2)}) collective-permute-start(f32[128,896]{1,0:T(8,128)S(1)} %bitcast.125), channel_id=1, source_target_pairs={{0,24},{4,28},{8,0},{12,4},{16,8},{20,12},{24,16},{28,20},{32,40},... | collective-permute-start | bytes 1376264 | tf_op jit(solution)/shard_map/ppermute | solution.py:44
  160.8 25.8 %copy-start.3 = (f32[1,128,896]{2,0,1:T(1,128)S(1)}, f32[1,128,896]{2,0,1:T(1,128)}, u32[]{:S(2)}) copy-start(f32[1,128,896]{2,0,1:T(1,128)} %get-tuple-element.12) | copy-start | bytes 1376260
  160.8 20.0 %collective-permute-start.10 = (f32[512,128]{1,0:T(8,128)}, f32[512,128]{1,0:T(8,128)}, u32[]{:S(2)}, u32[]{:S(2)}) collective-permute-start(f32[512,128]{1,0:T(8,128)} %bitcast.15), channel_id=1, source_target_pairs={{0,28},{4,0},{8,4},{12,8},{16,12},{20,16},{24,20},{28,24},{1,29},{... | collective-permute-start | bytes 786440 | tf_op jit(solution)/shard_map/ppermute | solution.py:37
  163.4 18.1 %collective-permute-start.11 = (f32[512,128]{1,0:T(8,128)}, f32[512,128]{1,0:T(8,128)}, u32[]{:S(2)}, u32[]{:S(2)}) collective-permute-start(f32[512,128]{1,0:T(8,128)} %bitcast.15), channel_id=1, source_target_pairs={{0,24},{4,28},{8,0},{12,4},{16,8},{20,12},{24,16},{28,20},{32,40},... | collective-permute-start | bytes 786440 | tf_op jit(solution)/shard_map/ppermute | solution.py:44
  165.0 19.1 %collective-permute-start.9 = (f32[512,128]{1,0:T(8,128)}, f32[512,128]{1,0:T(8,128)}, u32[]{:S(2)}, u32[]{:S(2)}) collective-permute-start(f32[512,128]{1,0:T(8,128)} %bitcast.15), channel_id=1, source_target_pairs={{0,4},{4,8},{8,12},{12,16},{16,20},{20,24},{24,28},{28,0},{1,5},{5... | collective-permute-start | bytes 786440 | tf_op jit(solution)/shard_map/ppermute | solution.py:37
  167.0 13.8 %all-to-all-start.3 = ((f32[32,16,128]{2,1,0:T(8,128)}), f32[32,16,128]{2,1,0:T(8,128)S(1)}, u32[]{:S(2)}, u32[]{:S(2)}) async-start(f32[32,16,128]{2,1,0:T(8,128)} %broadcast_in_dim.16), calls=%async_computation.3 | async-start | bytes 524288 | tf_op jit(solution)/shard_map/all_to_all | solution.py:23
  176.4 13.8 %collective-permute-start.7 = (f32[128,896]{1,0:T(8,128)}, f32[128,896]{1,0:T(8,128)S(1)}, u32[]{:S(2)}, u32[]{:S(2)}) collective-permute-start(f32[128,896]{1,0:T(8,128)} %bitcast.105), channel_id=1, source_target_pairs={{0,28},{4,0},{8,4},{12,8},{16,12},{20,16},{24,20},{28,24},{1,29},{... | collective-permute-start | bytes 1376264 | tf_op jit(solution)/shard_map/ppermute | solution.py:37
  178.7 24.2 %collective-permute-start.8 = (f32[128,896]{1,0:T(8,128)}, f32[128,896]{1,0:T(8,128)S(1)}, u32[]{:S(2)}, u32[]{:S(2)}) collective-permute-start(f32[128,896]{1,0:T(8,128)} %bitcast.104), channel_id=1, source_target_pairs={{0,24},{4,28},{8,0},{12,4},{16,8},{20,12},{24,16},{28,20},{32,40},... | collective-permute-start | bytes 1376264 | tf_op jit(solution)/shard_map/ppermute | solution.py:44
  180.9 22.0 %collective-permute-start = (f32[512,128]{1,0:T(8,128)S(1)}, f32[512,128]{1,0:T(8,128)S(1)}, u32[]{:S(2)}, u32[]{:S(2)}) collective-permute-start(f32[512,128]{1,0:T(8,128)S(1)} %bitcast.119), channel_id=1, source_target_pairs={{0,4},{4,8},{8,12},{12,16},{16,20},{20,24},{24,28},{28,0},{1,5},{5... | collective-permute-start | bytes 786440 | tf_op jit(solution)/shard_map/ppermute | solution.py:37
  181.6 24.0 %collective-permute-start.1 = (f32[512,128]{1,0:T(8,128)S(1)}, f32[512,128]{1,0:T(8,128)S(1)}, u32[]{:S(2)}, u32[]{:S(2)}) collective-permute-start(f32[512,128]{1,0:T(8,128)S(1)} %bitcast.120), channel_id=1, source_target_pairs={{0,28},{4,0},{8,4},{12,8},{16,12},{20,16},{24,20},{28,24},{1,29},{... | collective-permute-start | bytes 786440 | tf_op jit(solution)/shard_map/ppermute | solution.py:37
  184.1 27.1 %collective-permute-start.2 = (f32[512,128]{1,0:T(8,128)S(1)}, f32[512,128]{1,0:T(8,128)S(1)}, u32[]{:S(2)}, u32[]{:S(2)}) collective-permute-start(f32[512,128]{1,0:T(8,128)S(1)} %bitcast.121), channel_id=1, source_target_pairs={{0,24},{4,28},{8,0},{12,4},{16,8},{20,12},{24,16},{28,20},{32,40},... | collective-permute-start | bytes 786440 | tf_op jit(solution)/shard_map/ppermute | solution.py:44
  215.5 45.9 %all-to-all-start.9 = ((f32[32,16,896]{2,1,0:T(8,128)}), f32[32,16,896]{2,1,0:T(8,128)S(1)}, u32[]{:S(2)}, u32[]{:S(2)}) async-start(f32[32,16,896]{2,1,0:T(8,128)} %bitcast.25), calls=%async_computation.9 | async-start | bytes 3670016 | tf_op jit(solution)/shard_map/all_to_all | solution.py:98
  226.8 34.8 %copy-start.4 = (f32[16,14336]{1,0:T(8,128)S(1)}, f32[16,14336]{1,0:T(8,128)}, u32[]{:S(2)}) copy-start(f32[16,14336]{1,0:T(8,128)} %param.9) | copy-start | bytes 2752516

commit v2 on v0

v2 whole, which is shorter than its diff:
```python
import functools

import jax
import jax.numpy as jnp
from jax import lax
from jax.experimental import pallas as pl
from jax.experimental.pallas import tpu as pltpu
from jax.sharding import Mesh, PartitionSpec as P

X, C, Z, Y = 4, 2, 8, 4
ROWS = ("x", "c")
COLS = ("z", "y")
SPREAD = ("x", "c", "y")
QUAD = 4
NEAR = (0, -1, 1, 2, -2)
VMEM = pl.BlockSpec(memory_space=pltpu.VMEM)
ANY = pl.BlockSpec(memory_space=pl.ANY)
SMEM = pl.BlockSpec(memory_space=pltpu.SMEM)


def f32(*shape):
    return jax.ShapeDtypeStruct(shape, jnp.float32)


def call(kernel, outs, ins, out_specs, in_specs, scratch=(), flops=0, moved=0, limit=16):
    return pl.pallas_call(
        kernel,
        out_shape=outs,
        in_specs=in_specs,
        out_specs=out_specs,
        scratch_shapes=scratch,
        compiler_params=pltpu.CompilerParams(vmem_limit_bytes=limit << 20),
        cost_estimate=pl.CostEstimate(flops=flops, bytes_accessed=moved, transcendentals=0),
    )(*ins)


def exact_dot(left, right):
    return lax.dot_general(
        left, right, (((1,), (0,)), ((), ())),
        precision=lax.Precision.HIGHEST, preferred_element_type=jnp.float32,
    )


def split(value):
    high = value.astype(jnp.bfloat16)
    return high, (value - high.astype(jnp.float32)).astype(jnp.bfloat16)


def copy_all(copies, sems):
    started = [pltpu.make_async_copy(src, dst, sems.at[i]) for i, (src, dst) in enumerate(copies)]
    for copy in started:
        copy.start()
    for copy in started:
        copy.wait()


def open_kernel(first_rhs, second_rhs, inverse, couple, terms, shared):
    product = exact_dot(first_rhs[...], inverse[0])
    rows = first_rhs.shape[0] // Y
    for z in range(Z):
        for y in range(Y):
            terms[z * Y + y] = product[y * rows:(y + 1) * rows, z * 128:(z + 1) * 128]
    for y in range(Y):
        shared[y, 0:32] = couple[...]
        shared[y, 32:64] = inverse[1]
        shared[y, 64:72] = jnp.zeros((8, shared.shape[2]), jnp.float32)
        shared[y, 64:72, 0:128] = second_rhs[y * rows:y * rows + 8]
        shared[y, 64:72, 128:256] = second_rhs[y * rows + 8:(y + 1) * rows]


def couple_kernel(arrived, shared, first, terms):
    total = jnp.sum(arrived[...], axis=0)
    first[...] = total
    product = exact_dot(total, shared[:, 0:32].reshape(128, -1))
    for z in range(Z):
        terms[z] = product[:, z * 128:(z + 1) * 128]


def latter_kernel(arrived, shared, *refs):
    terms = refs[-1]
    rhs = jnp.concatenate(
        [jnp.sum(shared[:, 64:72, 0:128], axis=0), jnp.sum(shared[:, 64:72, 128:256], axis=0)], axis=0
    )
    second = rhs - jnp.sum(arrived[...], axis=0)
    product = exact_dot(second, shared[:, 32:64].reshape(128, -1))
    part = lambda z: product[:, (z % Z) * 128:(z % Z + 1) * 128]
    for z in range(Z):
        for k, step in enumerate(NEAR):
            terms[z, k] = part(z + step)


def close_kernel(arrived, copies):
    hand_out(jnp.sum(arrived[...], axis=0), copies)


def hand_out(near, copies):
    for place in range(X * C * Y):
        copies[place, 0:3] = near[0:3]
        copies[place, 3] = near[3 + place // Y % C]


def spread_kernel(*refs):
    hand_out(jnp.stack([near[...] for near in refs[:-1]]), refs[-1])


def around(z):
    return (z % QUAD, (z + 1) % QUAD, (z + 3) % QUAD, (z + 2) % QUAD)


def cut_kernel(place, factor, *refs):
    by_class, by_y, sems = refs[:4], refs[4], refs[5]
    z, y = place[1], place[2]
    classes = around(z)
    width = by_y.shape[3]
    copies = []
    for r in range(Y):
        for k in range(QUAD):
            strip = pl.multiple_of((((y + r) % Y) * QUAD + classes[k]) * width, width)
            copies.append((factor.at[0, :, pl.ds(strip, width)], by_class[k].at[r]))
            copies.append((factor.at[1, :, pl.ds(strip, width)], by_y.at[(y + r) % Y, k]))
    copy_all(copies, sems)


def turn_kernel(*refs):
    arrived, sent, sems = refs[:4], refs[4:8], refs[8]
    copy_all([(arrived[k].at[r], sent[r].at[k]) for r in range(Y) for k in range(QUAD)], sems)


def merge_kernel(arrived, *refs):
    sent, sems = refs[:4], refs[4]
    copy_all([(arrived.at[y, k], sent[k].at[y]) for y in range(Y) for k in range(QUAD)], sems)


def multiply(rows, factor, out, acc):
    left = jnp.concatenate([rows[:, k].reshape(-1, 128) for k in range(QUAD)], axis=1)
    left_high, left_low = split(left)
    right_high, right_low = split(factor[...].reshape(left.shape[1], -1))
    dot = functools.partial(jnp.dot, preferred_element_type=jnp.float32)
    step = 128
    for top in range(0, left.shape[0], step):
        at = slice(top, top + step)
        product = dot(left_high[at], right_high) + (dot(left_high[at], right_low) + dot(left_low[at], right_high))
        blocks = slice(top // 16, (top + step) // 16)
        product = product.reshape(step // 16, 16, -1)
        out[blocks] = product if acc is None else product + acc[blocks]


def first_update_kernel(place, rows, *refs):
    arrived, out, factor, sems = refs[:4], refs[4], refs[5], refs[6]
    y = place[2]
    copy_all([(arrived[r], factor.at[:, (y + Y - r) % Y]) for r in range(Y)], sems)
    multiply(rows, factor, out, None)


def latter_update_kernel(rows, acc, *refs):
    arrived, out, factor, sems = refs[:4], refs[4], refs[5], refs[6]
    copy_all([(arrived[k], factor.at[k]) for k in range(QUAD)], sems)
    multiply(rows, factor, out, acc)


def shift_y(value, step):
    return lax.ppermute(value, "y", [(y, (y + step) % Y) for y in range(Y)])


def shift_z(value, step):
    return lax.ppermute(value, "z", [(z, (z + step) % Z) for z in range(Z)])


def shift_far(value):
    pairs = [
        (c * Z + z, c * Z + (z + (2 if c else -2)) % Z) for c in range(C) for z in range(Z)
    ]
    return lax.ppermute(value, ("c", "z"), pairs)


def to_windows(own, up, down, far):
    return own, shift_z(up, 1), shift_z(down, -1), shift_far(far)


def to_ys(own, *others):
    return own, *(shift_y(other, step + 1) for step, other in enumerate(others))


def exchange(value, axes):
    return lax.all_to_all(value, axes, 0, 0, tiled=True)


def body(panel_rhs, diag_inv, coupling, trail_factor, trail_rhs):
    core, z, y = lax.axis_index("c"), lax.axis_index("z"), lax.axis_index("y")
    prow = lax.axis_index("x") * C + core
    place = jnp.stack([core, z, y]).astype(jnp.int32)
    strip, narrow = panel_rhs.shape[0], panel_rhs.shape[2]
    width = trail_rhs.shape[1] // (QUAD * Y)
    block = f32(QUAD, 32, width)
    sems = lambda n: [pltpu.SemaphoreType.DMA((n,))]

    rhs = panel_rhs.transpose(1, 0, 2)
    lanes = lax.broadcasted_iota(jnp.int32, (1, 128), 1) // narrow
    second_rhs = jnp.where(lanes == y, jnp.tile(rhs[1], (1, Y)), 0.0)
    terms, shared = call(
        open_kernel, (f32(Z * Y, 16, 128), f32(Y, 72, 1024)),
        (rhs[0], second_rhs, diag_inv, coupling), (VMEM, VMEM), (VMEM,) * 4,
    )
    arrived = exchange(terms, COLS)
    shared = exchange(shared, "y")

    *by_class, by_y = call(
        cut_kernel, (block,) * 4 + (f32(Y, *block.shape),), (place, trail_factor),
        (ANY,) * 5, (SMEM, VMEM), sems(32), moved=7340032, limit=24,
    )
    by_class = to_windows(*by_class)
    by_y = exchange(by_y, "y")

    first, terms = call(couple_kernel, (f32(16, 128), f32(Z, 16, 128)), (arrived, shared), (VMEM, VMEM), (VMEM,) * 2)
    arrived = exchange(terms, "z")
    terms = call(latter_kernel, f32(Z, len(NEAR), 16, 128), (arrived, shared, *by_class[1:], by_y), VMEM, (VMEM, VMEM) + (ANY,) * 4)
    arrived = exchange(terms, "z")
    copies = call(close_kernel, f32(X * C * Y, QUAD, 16, 128), (arrived,), VMEM, (VMEM,))
    latter_rows = exchange(copies, SPREAD)

    near = (first, *(shift_z(first, -step) for step in NEAR[1:]))
    copies = call(spread_kernel, f32(X * C * Y, QUAD, 16, 128), near, VMEM, (VMEM,) * len(NEAR))
    first_rows = exchange(copies, SPREAD)

    by_r = call(turn_kernel, (block,) * 4, by_class, (ANY,) * 4, (VMEM,) * 4, sems(16), moved=3670016)
    first_factor = to_ys(*by_r)
    by_k = call(merge_kernel, (block,) * 4, (by_y,), (ANY,) * 4, (VMEM,), sems(16), moved=3670016)
    latter_factor = to_windows(*by_k)

    scratch = [pltpu.VMEM((QUAD, Y, 32, width), jnp.float32)] + sems(4)
    update = call(
        first_update_kernel, f32(Z * Y, 16, width), (place, first_rows, *first_factor),
        VMEM, (SMEM, VMEM) + (ANY,) * 4, scratch, flops=1409286144, moved=4718592, limit=40,
    )
    scratch = [pltpu.VMEM((QUAD, QUAD, 32, width), jnp.float32)] + sems(4)
    update = call(
        latter_update_kernel, f32(Z * Y, 16, width), (latter_rows, update, *latter_factor),
        VMEM, (VMEM,) * 2 + (ANY,) * 4, scratch, flops=1409286144, moved=6553600, limit=40,
    )
    parts = exchange(update, COLS)
    parts = parts.reshape(2, QUAD, Y, *parts.shape[1:])
    reduced = trail_rhs - (parts[0] + parts[1]).transpose(2, 1, 0, 3).reshape(trail_rhs.shape)

    own = lambda rows: lax.dynamic_slice(
        rows, (prow * Y, 0, 0, y * narrow), (Y, 1, rows.shape[2], narrow)
    ).reshape(strip, narrow)
    solved = jnp.stack([own(first_rows), own(latter_rows)], axis=1)
    return solved, reduced


def solution(mesh):
    devices = Mesh(mesh.devices.reshape(X, C, Z, Y), ("x", "c", "z", "y"))
    placed = (
        P(ROWS, None, COLS),
        P(None, COLS, None),
        P(COLS, None),
        P(None, COLS, ROWS),
        P(COLS, ROWS),
    )
    return jax.shard_map(
        body,
        mesh=devices,
        in_specs=placed,
        out_specs=(P(ROWS, None, COLS), P(COLS, ROWS)),
        check_vma=False,
    )
```

time: 996 us -> 239 us (0.24)
  waiting for transfers between devices: 917 us -> 92.8 us
  starting transfers between devices: 0.16 us -> 59.7 us
  matrix products: 35.8 us -> 0 us
  local copies, waits for them, and re-layouts: 1.06 us -> 25.8 us
  Pallas kernels: 0 us -> 17.8 us
  blocking collectives: 23.5 us -> 39.1 us
  between operations: 13.8 us -> 0.9 us
    reduce_scatter x4 -> x0, waiting for transfers between devices: 917 us -> none  [the longest x2 418 us: solve_panel(): lax.psum_scatter(product(rhs_local, inverse_rows), 'pcol', scatter_dimens...]
    all_to_all x0 -> x6, waiting for transfers between devices: none -> 55.6 us  [exchange(): return lax.all_to_all(value, axes, 0, 0, tiled=True)]
    all_to_all x0 -> x2, blocking collectives: none -> 39.1 us  [exchange(): return lax.all_to_all(value, axes, 0, 0, tiled=True)]
    all_to_all x0 -> x6, starting transfers between devices: none -> 38.6 us  [exchange(): return lax.all_to_all(value, axes, 0, 0, tiled=True)]
    ppermute x0 -> x13, waiting for transfers between devices: none -> 37.2 us  [the longest x8 18 us: shift_z(): return lax.ppermute(value, 'z', [(z, (z + step) % Z) for z in range(Z)])]
    dot_general x4 -> x0, matrix products: 35.8 us -> none  [product(): jnp.dot(left, right, preferred_element_type=jnp.float32, precision=lax.Pr...]
    all_gather x2 -> x0, blocking collectives: 23.5 us -> none  [the longest x1 11.8 us: body(): lax.all_gather(first, 'prow', axis=0, tiled=True)]
    unnamed x10 -> x50, local copies, waits for them, and re-layouts: 0.9 us -> 23.7 us
  transfers between devices with their start and end apart: 4 -> 19, of which waited for: 4 -> 12; matrix products, arithmetic and copies ran while one was open for 0% -> 1% of each run, Pallas kernels for 0% -> 5%
where the time goes in v2:
time: 239 us; the launch traced here: 237 us
  waiting for transfers between devices  92.8 us (39%)
  starting transfers between devices  59.7 us (25%)
  blocking collectives  39.1 us (16%)
  local copies, waits for them, and re-layouts  25.8 us (11%)
  Pallas kernels  17.8 us (7%)
    all_to_all x6, waiting for transfers between devices, exchange(): return lax.all_to_all(value, axes, 0, 0, tiled=True)  55.6 us
    all_to_all x2, blocking collectives, exchange(): return lax.all_to_all(value, axes, 0, 0, tiled=True)  39.1 us
    all_to_all x6, starting transfers between devices, exchange(): return lax.all_to_all(value, axes, 0, 0, tiled=True)  38.6 us
    unnamed x50, local copies, waits for them, and re-layouts  23.7 us
    ppermute x8, waiting for transfers between devices, shift_z(): return lax.ppermute(value, 'z', [(z, (z + step) % Z) for z in range(Z)])  18 us
    pallas_call x10, Pallas kernels, call(): pl.pallas_call(kernel, out_shape=outs, in_specs=in_specs, out_specs=out_s...  17.8 us
    ppermute x3, waiting for transfers between devices, shift_y(): return lax.ppermute(value, 'y', [(y, (y + step) % Y) for y in range(Y)])  16.3 us
    ppermute x8, starting transfers between devices, shift_z(): return lax.ppermute(value, 'z', [(z, (z + step) % Z) for z in range(Z)])  12.7 us
  transfers between devices with their start and end apart: 19, of which 12 were waited for; matrix products, arithmetic and copies ran while one was open for 1% of the time, Pallas kernels for 5%

profile of v2, /device:TPU:20, one launch (start us, length us, event | category | flops | bytes accessed | tf_op | source)
XLA Modules:
  0.0 237.3 jit_solution(11979961719599334373)
XLA Ops:
  3.9 22.6 %all_to_all.40.arrived = f32[32,16,128]{2,1,0:T(8,128)S(1)} all-to-all(f32[32,16,128]{2,1,0:T(8,128)S(1)} %get-tuple-element.19), channel_id=1, replica_groups=mesh['x'=4,'c'=2,'z'=8,'y'=4] {'z','y'}, dimensions={0} | all-to-all | bytes 524288 | tf_op jit(solution)/shard_map/all_to_all | solution.py:185
  26.5 16.5 %all_to_all.41.shared = f32[4,72,1024]{2,1,0:T(8,128)S(1)} all-to-all(f32[4,72,1024]{2,1,0:T(8,128)S(1)} %get-tuple-element.20), channel_id=1, replica_groups=mesh['x'=4,'c'=2,'z'=8,'y'=4] {'y'}, dimensions={0} | all-to-all | bytes 2359296 | tf_op jit(solution)/shard_map/all_to_all | solution.py:185
  44.0 3.5 %all-to-all-start.3 = ((f32[8,16,128]{2,1,0:T(8,128)}), f32[8,16,128]{2,1,0:T(8,128)S(1)}, u32[]{:S(2)}, u32[]{:S(2)}) async-start(f32[8,16,128]{2,1,0:T(8,128)} %get-tuple-element.22), calls=%async_computation.3 | async-start | bytes 131072 | tf_op jit(solution)/shard_map/all_to_all | solution.py:185
  47.6 2.0 copy-done.1
  49.7 2.1 shard_map.71
  51.8 1.3 copy-done.8
  56.2 6.3 %all-to-all-start.4 = ((f32[4,4,32,896]{3,2,1,0:T(8,128)}), f32[4,4,32,896]{3,2,1,0:T(8,128)S(1)}, u32[]{:S(2)}, u32[]{:S(2)}) async-start(f32[4,4,32,896]{3,2,1,0:T(8,128)} %copy-done.8), calls=%async_computation.4 | async-start | bytes 3670016 | tf_op jit(solution)/shard_map/all_to_all | solution.py:185
  62.5 2.0 collective-permute-start.4
  64.5 1.2 collective-permute-start.5
  65.7 2.9 %collective-permute-start.6 = (f32[4,32,896]{2,1,0:T(8,128)}, f32[4,32,896]{2,1,0:T(8,128)S(1)}, u32[]{:S(2)}, u32[]{:S(2)}) collective-permute-start(f32[4,32,896]{2,1,0:T(8,128)} %copy-done.20), channel_id=1, source_target_pairs={{0,24},{4,28},{8,0},{12,4},{16,8},{20,12},{24,16},{28,20},{32,40},... | collective-permute-start | bytes 1376264 | tf_op jit(solution)/shard_map/ppermute | solution.py:173
  68.6 12.3 %collective-permute-done.4.refs_0_.refs_1_ = f32[4,32,896]{2,1,0:T(8,128)S(1)} collective-permute-done((f32[4,32,896]{2,1,0:T(8,128)}, f32[4,32,896]{2,1,0:T(8,128)S(1)}, u32[]{:S(2)}, u32[]{:S(2)}) %collective-permute-start.4) | collective-permute-done | bytes 458784 | tf_op jit(solution)/shard_map/ppermute | solution.py:166
  81.7 2.9 %collective-permute-done.6.refs_2_.refs_3_ = f32[4,32,896]{2,1,0:T(8,128)S(1)} collective-permute-done((f32[4,32,896]{2,1,0:T(8,128)}, f32[4,32,896]{2,1,0:T(8,128)S(1)}, u32[]{:S(2)}, u32[]{:S(2)}) %collective-permute-start.6) | collective-permute-done | bytes 458784 | tf_op jit(solution)/shard_map/ppermute | solution.py:173
  88.5 6.0 %all-to-all-start.5 = ((f32[8,5,16,128]{3,2,1,0:T(8,128)}), f32[8,5,16,128]{3,2,1,0:T(8,128)S(1)}, u32[]{:S(2)}, u32[]{:S(2)}) async-start(f32[8,5,16,128]{3,2,1,0:T(8,128)} %copy-done.9), calls=%async_computation.5 | async-start | bytes 655360 | tf_op jit(solution)/shard_map/all_to_all | solution.py:185
  94.6 2.0 collective-permute-start
  96.6 1.2 collective-permute-start.1
  97.8 2.9 %collective-permute-start.2 = (f32[16,128]{1,0:T(8,128)S(1)}, f32[16,128]{1,0:T(8,128)S(1)}, u32[]{:S(2)}, u32[]{:S(2)}) collective-permute-start(f32[16,128]{1,0:T(8,128)S(1)} %get-tuple-element.21.refs_0_), channel_id=1, source_target_pairs={{0,24},{4,28},{8,0},{12,4},{16,8},{20,12},{24,16},{28,20},{1,25},{... | collective-permute-start | bytes 24584 | tf_op jit(solution)/shard_map/ppermute | solution.py:166
  100.7 2.9 %collective-permute-done.refs_1_ = f32[16,128]{1,0:T(8,128)S(1)} collective-permute-done((f32[16,128]{1,0:T(8,128)S(1)}, f32[16,128]{1,0:T(8,128)S(1)}, u32[]{:S(2)}, u32[]{:S(2)}) %collective-permute-start) | collective-permute-done | bytes 8224 | tf_op jit(solution)/shard_map/ppermute | solution.py:166
  104.2 2.3 collective-permute-done.3.refs_4_
  107.8 7.4 %all-to-all-start.2 = ((f32[32,4,16,128]{3,2,1,0:T(8,128)}), f32[32,4,16,128]{3,2,1,0:T(8,128)}, u32[]{:S(2)}, u32[]{:S(2)}) async-start(f32[32,4,16,128]{3,2,1,0:T(8,128)} %shard_map.70), calls=%async_computation.2 | async-start | bytes 2097152 | tf_op jit(solution)/shard_map/all_to_all | solution.py:185
  116.4 11.9 %all-to-all-done.2.rows = f32[32,4,16,128]{3,2,1,0:T(8,128)} async-done(((f32[32,4,16,128]{3,2,1,0:T(8,128)}), f32[32,4,16,128]{3,2,1,0:T(8,128)}, u32[]{:S(2)}, u32[]{:S(2)}) %all-to-all-start.2) | async-done | bytes 1048608 | tf_op jit(solution)/shard_map/all_to_all | solution.py:185
  128.2 8.1 %all-to-all-start.6 = ((f32[32,4,16,128]{3,2,1,0:T(8,128)}), f32[32,4,16,128]{3,2,1,0:T(8,128)S(1)}, u32[]{:S(2)}, u32[]{:S(2)}) async-start(f32[32,4,16,128]{3,2,1,0:T(8,128)} %copy-done), calls=%async_computation.6 | async-start | bytes 2097152 | tf_op jit(solution)/shard_map/all_to_all | solution.py:185
  139.4 2.5 %shard_map.74 = (f32[4,32,896]{2,1,0:T(8,128)S(1)}, f32[4,32,896]{2,1,0:T(8,128)S(1)}, f32[4,32,896]{2,1,0:T(8,128)S(1)}, f32[4,32,896]{2,1,0:T(8,128)S(1)}) custom-call(f32[4,32,896]{2,1,0:T(8,128)S(1)} %copy-done.17, f32[4,32,896]{2,1,0:T(8,128)S(1)} %collective-permute-done.4.refs_0_.refs_1_, f32[4,32,896]{2,1,0:T(8,128)S(1)} %copy-done.4, ...), custom_call_target="tpu_custom_call" | custom-call | bytes 3670016 | tf_op jit(solution)/shard_map/pallas_call | solution.py:26
  141.9 1.3 collective-permute-start.7
  145.2 2.5 %shard_map.76 = (f32[4,32,896]{2,1,0:T(8,128)S(1)}, f32[4,32,896]{2,1,0:T(8,128)S(1)}, f32[4,32,896]{2,1,0:T(8,128)S(1)}, f32[4,32,896]{2,1,0:T(8,128)S(1)}) custom-call(f32[4,4,32,896]{3,2,1,0:T(8,128)S(1)} %all-to-all-done.4.refs_3_.arrived), custom_call_target="tpu_custom_call" | custom-call | bytes 3670016 | tf_op jit(solution)/shard_map/pallas_call | solution.py:26
  148.4 2.6 %collective-permute-start.11 = (f32[4,32,896]{2,1,0:T(8,128)S(1)}, f32[4,32,896]{2,1,0:T(8,128)S(1)}, u32[]{:S(2)}, u32[]{:S(2)}) collective-permute-start(f32[4,32,896]{2,1,0:T(8,128)S(1)} %get-tuple-element.34), channel_id=1, source_target_pairs={{0,28},{4,0},{8,4},{12,8},{16,12},{20,16},{24,20},{28,24},{1,29},{... | collective-permute-start | bytes 1376264 | tf_op jit(solution)/shard_map/ppermute | solution.py:166
  151.0 8.4 %collective-permute-done.7.refs_1_ = f32[4,32,896]{2,1,0:T(8,128)S(1)} collective-permute-done((f32[4,32,896]{2,1,0:T(8,128)S(1)}, f32[4,32,896]{2,1,0:T(8,128)S(1)}, u32[]{:S(2)}, u32[]{:S(2)}) %collective-permute-start.7) | collective-permute-done | bytes 458784 | tf_op jit(solution)/shard_map/ppermute | solution.py:162
  159.4 2.1 collective-permute-start.12
  161.5 7.4 %collective-permute-done.8.refs_2_ = f32[4,32,896]{2,1,0:T(8,128)S(1)} collective-permute-done((f32[4,32,896]{2,1,0:T(8,128)S(1)}, f32[4,32,896]{2,1,0:T(8,128)S(1)}, u32[]{:S(2)}, u32[]{:S(2)}) %collective-permute-start.8) | collective-permute-done | bytes 458784 | tf_op jit(solution)/shard_map/ppermute | solution.py:162
  169.4 3.5 %shard_map.75.acc = f32[32,16,896]{2,1,0:T(8,128)S(1)} custom-call(s32[3]{0:T(128)S(1)} %pad_add_fusion.place, f32[32,4,16,128]{3,2,1,0:T(8,128)} %all-to-all-done.2.rows, f32[4,32,896]{2,1,0:T(8,128)S(1)} %get-tuple-element.28.refs_0_, f32[4,32,896]{2,1,0:T(8,128)S(1)} %collective-permute-done.7.refs_1_, f32[4,32,896]{2,1,0:T(8,128)S(1)} %collective-permute-done.8.refs_2_, ...), custom_call_target="tpu_custom_call" | custom-call | flops 1409286144 | bytes 4718592 | tf_op jit(solution)/shard_map/pallas_call | solution.py:26
  178.3 4.2 %shard_map.77 = f32[32,16,896]{2,1,0:T(8,128)} custom-call(f32[32,4,16,128]{3,2,1,0:T(8,128)S(1)} %all-to-all-done.6.rows, f32[32,16,896]{2,1,0:T(8,128)S(1)} %shard_map.75.acc, f32[4,32,896]{2,1,0:T(8,128)S(1)} %get-tuple-element.32.refs_0_, f32[4,32,896]{2,1,0:T(8,128)S(1)} %copy-done.11, f32[4,32,896]{2,1,0:T(8,128)S(1)} %copy-done.13, ...), custom_call_target="tpu_custom_call" | custom-call | flops 1409286144 | bytes 6553600 | tf_op jit(solution)/shard_map/pallas_call | solution.py:26
  182.5 7.3 %all-to-all-start.7 = ((f32[32,16,896]{2,1,0:T(8,128)}), f32[32,16,896]{2,1,0:T(8,128)S(1)}, u32[]{:S(2)}, u32[]{:S(2)}) async-start(f32[32,16,896]{2,1,0:T(8,128)} %shard_map.77), calls=%async_computation.7 | async-start | bytes 3670016 | tf_op jit(solution)/shard_map/all_to_all | solution.py:185
  191.5 43.5 %all-to-all-done.7 = f32[32,16,896]{2,1,0:T(8,128)S(1)} async-done(((f32[32,16,896]{2,1,0:T(8,128)}), f32[32,16,896]{2,1,0:T(8,128)S(1)}, u32[]{:S(2)}, u32[]{:S(2)}) %all-to-all-start.7) | async-done | bytes 1835040 | tf_op jit(solution)/shard_map/all_to_all | solution.py:185
  (82 shorter events, 30.7 us)
Async XLA Ops:
  1.7 1.0 copy-start.18
  44.0 12.2 %all-to-all-start.3 = ((f32[8,16,128]{2,1,0:T(8,128)}), f32[8,16,128]{2,1,0:T(8,128)S(1)}, u32[]{:S(2)}, u32[]{:S(2)}) async-start(f32[8,16,128]{2,1,0:T(8,128)} %get-tuple-element.22), calls=%async_computation.3 | async-start | bytes 131072 | tf_op jit(solution)/shard_map/all_to_all | solution.py:185
  47.6 2.0 copy-start.1
  51.8 1.3 copy-start.8
  56.2 29.2 %all-to-all-start.4 = ((f32[4,4,32,896]{3,2,1,0:T(8,128)}), f32[4,4,32,896]{3,2,1,0:T(8,128)S(1)}, u32[]{:S(2)}, u32[]{:S(2)}) async-start(f32[4,4,32,896]{3,2,1,0:T(8,128)} %copy-done.8), calls=%async_computation.4 | async-start | bytes 3670016 | tf_op jit(solution)/shard_map/all_to_all | solution.py:185
  62.5 18.5 %collective-permute-start.4 = (f32[4,32,896]{2,1,0:T(8,128)}, f32[4,32,896]{2,1,0:T(8,128)S(1)}, u32[]{:S(2)}, u32[]{:S(2)}) collective-permute-start(f32[4,32,896]{2,1,0:T(8,128)} %copy-done.22), channel_id=1, source_target_pairs={{0,4},{4,8},{8,12},{12,16},{16,20},{20,24},{24,28},{28,0},{1,5},{5... | collective-permute-start | bytes 1376264 | tf_op jit(solution)/shard_map/ppermute | solution.py:166
  64.5 16.4 %collective-permute-start.5 = (f32[4,32,896]{2,1,0:T(8,128)}, f32[4,32,896]{2,1,0:T(8,128)S(1)}, u32[]{:S(2)}, u32[]{:S(2)}) collective-permute-start(f32[4,32,896]{2,1,0:T(8,128)} %copy-done.21), channel_id=1, source_target_pairs={{0,28},{4,0},{8,4},{12,8},{16,12},{20,16},{24,20},{28,24},{1,29},{... | collective-permute-start | bytes 1376264 | tf_op jit(solution)/shard_map/ppermute | solution.py:166
  65.7 18.9 %collective-permute-start.6 = (f32[4,32,896]{2,1,0:T(8,128)}, f32[4,32,896]{2,1,0:T(8,128)S(1)}, u32[]{:S(2)}, u32[]{:S(2)}) collective-permute-start(f32[4,32,896]{2,1,0:T(8,128)} %copy-done.20), channel_id=1, source_target_pairs={{0,24},{4,28},{8,0},{12,4},{16,8},{20,12},{24,16},{28,20},{32,40},... | collective-permute-start | bytes 1376264 | tf_op jit(solution)/shard_map/ppermute | solution.py:173
  85.4 1.0 copy-start.3
  86.4 1.0 copy-start.6
  88.5 19.3 %all-to-all-start.5 = ((f32[8,5,16,128]{3,2,1,0:T(8,128)}), f32[8,5,16,128]{3,2,1,0:T(8,128)S(1)}, u32[]{:S(2)}, u32[]{:S(2)}) async-start(f32[8,5,16,128]{3,2,1,0:T(8,128)} %copy-done.9), calls=%async_computation.5 | async-start | bytes 655360 | tf_op jit(solution)/shard_map/all_to_all | solution.py:185
  94.6 9.1 %collective-permute-start = (f32[16,128]{1,0:T(8,128)S(1)}, f32[16,128]{1,0:T(8,128)S(1)}, u32[]{:S(2)}, u32[]{:S(2)}) collective-permute-start(f32[16,128]{1,0:T(8,128)S(1)} %get-tuple-element.21.refs_0_), channel_id=1, source_target_pairs={{0,4},{4,8},{8,12},{12,16},{16,20},{20,24},{24,28},{28,0},{1,5},{5... | collective-permute-start | bytes 24584 | tf_op jit(solution)/shard_map/ppermute | solution.py:166
  96.6 7.4 %collective-permute-start.1 = (f32[16,128]{1,0:T(8,128)S(1)}, f32[16,128]{1,0:T(8,128)S(1)}, u32[]{:S(2)}, u32[]{:S(2)}) collective-permute-start(f32[16,128]{1,0:T(8,128)S(1)} %get-tuple-element.21.refs_0_), channel_id=1, source_target_pairs={{0,28},{4,0},{8,4},{12,8},{16,12},{20,16},{24,20},{28,24},{1,29},{... | collective-permute-start | bytes 24584 | tf_op jit(solution)/shard_map/ppermute | solution.py:166
  97.8 6.4 %collective-permute-start.2 = (f32[16,128]{1,0:T(8,128)S(1)}, f32[16,128]{1,0:T(8,128)S(1)}, u32[]{:S(2)}, u32[]{:S(2)}) collective-permute-start(f32[16,128]{1,0:T(8,128)S(1)} %get-tuple-element.21.refs_0_), channel_id=1, source_target_pairs={{0,24},{4,28},{8,0},{12,4},{16,8},{20,12},{24,16},{28,20},{1,25},{... | collective-permute-start | bytes 24584 | tf_op jit(solution)/shard_map/ppermute | solution.py:166
  100.7 5.8 %collective-permute-start.3 = (f32[16,128]{1,0:T(8,128)S(1)}, f32[16,128]{1,0:T(8,128)S(1)}, u32[]{:S(2)}, u32[]{:S(2)}) collective-permute-start(f32[16,128]{1,0:T(8,128)S(1)} %get-tuple-element.21.refs_0_), channel_id=1, source_target_pairs={{0,8},{4,12},{8,16},{12,20},{16,24},{20,28},{24,0},{28,4},{1,9},{5... | collective-permute-start | bytes 24584 | tf_op jit(solution)/shard_map/ppermute | solution.py:166
  107.8 20.4 %all-to-all-start.2 = ((f32[32,4,16,128]{3,2,1,0:T(8,128)}), f32[32,4,16,128]{3,2,1,0:T(8,128)}, u32[]{:S(2)}, u32[]{:S(2)}) async-start(f32[32,4,16,128]{3,2,1,0:T(8,128)} %shard_map.70), calls=%async_computation.2 | async-start | bytes 2097152 | tf_op jit(solution)/shard_map/all_to_all | solution.py:185
  115.4 1.0 copy-start
  128.2 47.0 %all-to-all-start.6 = ((f32[32,4,16,128]{3,2,1,0:T(8,128)}), f32[32,4,16,128]{3,2,1,0:T(8,128)S(1)}, u32[]{:S(2)}, u32[]{:S(2)}) async-start(f32[32,4,16,128]{3,2,1,0:T(8,128)} %copy-done), calls=%async_computation.6 | async-start | bytes 2097152 | tf_op jit(solution)/shard_map/all_to_all | solution.py:185
  136.3 1.0 copy-start.4
  137.4 1.0 copy-start.7
  138.4 1.0 copy-start.17
  141.9 17.5 %collective-permute-start.7 = (f32[4,32,896]{2,1,0:T(8,128)S(1)}, f32[4,32,896]{2,1,0:T(8,128)S(1)}, u32[]{:S(2)}, u32[]{:S(2)}) collective-permute-start(f32[4,32,896]{2,1,0:T(8,128)S(1)} %get-tuple-element.29), channel_id=1, source_target_pairs={{0,1},{1,2},{2,3},{3,0},{4,5},{5,6},{6,7},{7,4},{8,9},{9,10},{10,1... | collective-permute-start | bytes 1376264 | tf_op jit(solution)/shard_map/ppermute | solution.py:162
  143.2 25.7 %collective-permute-start.8 = (f32[4,32,896]{2,1,0:T(8,128)S(1)}, f32[4,32,896]{2,1,0:T(8,128)S(1)}, u32[]{:S(2)}, u32[]{:S(2)}) collective-permute-start(f32[4,32,896]{2,1,0:T(8,128)S(1)} %get-tuple-element.30), channel_id=1, source_target_pairs={{0,2},{1,3},{2,0},{3,1},{4,6},{5,7},{6,4},{7,5},{8,10},{9,11},{10,... | collective-permute-start | bytes 1376264 | tf_op jit(solution)/shard_map/ppermute | solution.py:162
  144.0 25.4 %collective-permute-start.9 = (f32[4,32,896]{2,1,0:T(8,128)S(1)}, f32[4,32,896]{2,1,0:T(8,128)S(1)}, u32[]{:S(2)}, u32[]{:S(2)}) collective-permute-start(f32[4,32,896]{2,1,0:T(8,128)S(1)} %get-tuple-element.31), channel_id=1, source_target_pairs={{0,3},{1,0},{2,1},{3,2},{4,7},{5,4},{6,5},{7,6},{8,11},{9,8},{10,9... | collective-permute-start | bytes 1376264 | tf_op jit(solution)/shard_map/ppermute | solution.py:162
  147.7 25.2 %collective-permute-start.10 = (f32[4,32,896]{2,1,0:T(8,128)S(1)}, f32[4,32,896]{2,1,0:T(8,128)S(1)}, u32[]{:S(2)}, u32[]{:S(2)}) collective-permute-start(f32[4,32,896]{2,1,0:T(8,128)S(1)} %get-tuple-element.33), channel_id=1, source_target_pairs={{0,4},{4,8},{8,12},{12,16},{16,20},{20,24},{24,28},{28,0},{1,5},{5... | collective-permute-start | bytes 1376264 | tf_op jit(solution)/shard_map/ppermute | solution.py:166
  148.4 25.2 %collective-permute-start.11 = (f32[4,32,896]{2,1,0:T(8,128)S(1)}, f32[4,32,896]{2,1,0:T(8,128)S(1)}, u32[]{:S(2)}, u32[]{:S(2)}) collective-permute-start(f32[4,32,896]{2,1,0:T(8,128)S(1)} %get-tuple-element.34), channel_id=1, source_target_pairs={{0,28},{4,0},{8,4},{12,8},{16,12},{20,16},{24,20},{28,24},{1,29},{... | collective-permute-start | bytes 1376264 | tf_op jit(solution)/shard_map/ppermute | solution.py:166
  159.4 15.1 %collective-permute-start.12 = (f32[4,32,896]{2,1,0:T(8,128)S(1)}, f32[4,32,896]{2,1,0:T(8,128)S(1)}, u32[]{:S(2)}, u32[]{:S(2)}) collective-permute-start(f32[4,32,896]{2,1,0:T(8,128)S(1)} %get-tuple-element.35), channel_id=1, source_target_pairs={{0,24},{4,28},{8,0},{12,4},{16,8},{20,12},{24,16},{28,20},{32,40},... | collective-permute-start | bytes 1376264 | tf_op jit(solution)/shard_map/ppermute | solution.py:173
  175.2 1.0 copy-start.11
  176.3 1.0 copy-start.13
  177.3 1.0 copy-start.15
  182.5 52.4 %all-to-all-start.7 = ((f32[32,16,896]{2,1,0:T(8,128)}), f32[32,16,896]{2,1,0:T(8,128)S(1)}, u32[]{:S(2)}, u32[]{:S(2)}) async-start(f32[32,16,896]{2,1,0:T(8,128)} %shard_map.77), calls=%async_computation.7 | async-start | bytes 3670016 | tf_op jit(solution)/shard_map/all_to_all | solution.py:185
  235.1 1.2 copy-start.23
  (11 other events, 8.6 us)

commit v3 on v2

--- a/solution.py
+++ b/solution.py
@@ -68,7 +68,8 @@
         shared[y, 64:72, 128:256] = second_rhs[y * rows + 8:(y + 1) * rows]
 
 
-def couple_kernel(arrived, shared, first, terms):
+def couple_kernel(arrived, shared, *refs):
+    first, terms = refs[-2:]
     total = jnp.sum(arrived[...], axis=0)
     first[...] = total
     product = exact_dot(total, shared[:, 0:32].reshape(128, -1))
@@ -76,8 +77,7 @@
         terms[z] = product[:, z * 128:(z + 1) * 128]
 
 
-def latter_kernel(arrived, shared, *refs):
-    terms = refs[-1]
+def latter_kernel(arrived, shared, terms):
     rhs = jnp.concatenate(
         [jnp.sum(shared[:, 64:72, 0:128], axis=0), jnp.sum(shared[:, 64:72, 128:256], axis=0)], axis=0
     )
@@ -89,8 +89,8 @@
             terms[z, k] = part(z + step)
 
 
-def close_kernel(arrived, copies):
-    hand_out(jnp.sum(arrived[...], axis=0), copies)
+def close_kernel(arrived, *refs):
+    hand_out(jnp.sum(arrived[...], axis=0), refs[-1])
 
 
 def hand_out(near, copies):
@@ -109,21 +109,20 @@
 
 def cut_kernel(place, factor, *refs):
     by_class, by_y, sems = refs[:4], refs[4], refs[5]
-    z, y = place[1], place[2]
-    classes = around(z)
+    classes = around(place[0])
     width = by_y.shape[3]
     copies = []
-    for r in range(Y):
+    for y in range(Y):
         for k in range(QUAD):
-            strip = pl.multiple_of((((y + r) % Y) * QUAD + classes[k]) * width, width)
-            copies.append((factor.at[0, :, pl.ds(strip, width)], by_class[k].at[r]))
-            copies.append((factor.at[1, :, pl.ds(strip, width)], by_y.at[(y + r) % Y, k]))
+            strip = pl.ds(pl.multiple_of((y * QUAD + classes[k]) * width, width), width)
+            copies.append((factor.at[0, :, strip], by_class[k].at[y]))
+            copies.append((factor.at[1, :, strip], by_y.at[y, k]))
     copy_all(copies, sems)
 
 
 def turn_kernel(*refs):
-    arrived, sent, sems = refs[:4], refs[4:8], refs[8]
-    copy_all([(arrived[k].at[r], sent[r].at[k]) for r in range(Y) for k in range(QUAD)], sems)
+    arrived, sent, sems = refs[:4], refs[4], refs[5]
+    copy_all([(arrived[k].at[y], sent.at[y, k]) for y in range(Y) for k in range(QUAD)], sems)
 
 
 def merge_kernel(arrived, *refs):
@@ -131,35 +130,60 @@
     copy_all([(arrived.at[y, k], sent[k].at[y]) for y in range(Y) for k in range(QUAD)], sems)
 
 
-def multiply(rows, factor, out, acc):
-    left = jnp.concatenate([rows[:, k].reshape(-1, 128) for k in range(QUAD)], axis=1)
-    left_high, left_low = split(left)
-    right_high, right_low = split(factor[...].reshape(left.shape[1], -1))
+def update_kernel(count, *refs):
+    rows, blocks, acc = refs[0], refs[1:1 + count], refs[1 + count:-5]
+    out, left, factor, result, sems = refs[-5:]
+    start = lambda src, dst, i: pltpu.make_async_copy(src, dst, sems.at[i])
+    chunk = 128 // 16
+    steps = left.shape[0] // chunk
+    part = lambda i: slice(i * chunk, (i + 1) * chunk)
+    rows_in = start(rows, left, 0)
+    rows_in.start()
+    if count == 1:
+        factor_in = [start(blocks[0].at[:, k], factor.at[k], 1 + k) for k in range(QUAD)]
+    else:
+        factor_in = [start(blocks[k], factor.at[k], 1 + k) for k in range(QUAD)]
+    for copy in factor_in:
+        copy.start()
+    acc_in = [start(a.at[part(i)], result.at[part(i)], 5 + i) for a in acc for i in range(steps)]
+    for copy in acc_in:
+        copy.start()
+    rows_in.wait()
+    for copy in factor_in:
+        copy.wait()
+    right_high, right_low = split(factor[...].reshape(QUAD * 128, -1))
     dot = functools.partial(jnp.dot, preferred_element_type=jnp.float32)
-    step = 128
-    for top in range(0, left.shape[0], step):
-        at = slice(top, top + step)
-        product = dot(left_high[at], right_high) + (dot(left_high[at], right_low) + dot(left_low[at], right_high))
-        blocks = slice(top // 16, (top + step) // 16)
-        product = product.reshape(step // 16, 16, -1)
-        out[blocks] = product if acc is None else product + acc[blocks]
-
-
-def first_update_kernel(place, rows, *refs):
-    arrived, out, factor, sems = refs[:4], refs[4], refs[5], refs[6]
-    y = place[2]
-    copy_all([(arrived[r], factor.at[:, (y + Y - r) % Y]) for r in range(Y)], sems)
-    multiply(rows, factor, out, None)
-
-
-def latter_update_kernel(rows, acc, *refs):
-    arrived, out, factor, sems = refs[:4], refs[4], refs[5], refs[6]
-    copy_all([(arrived[k], factor.at[k]) for k in range(QUAD)], sems)
-    multiply(rows, factor, out, acc)
-
-
-def shift_y(value, step):
-    return lax.ppermute(value, "y", [(y, (y + step) % Y) for y in range(Y)])
+    sent = []
+    for i in range(steps):
+        piece = left[part(i)]
+        high, low = split(jnp.concatenate([piece[:, k].reshape(128, 128) for k in range(QUAD)], axis=1))
+        product = dot(high, right_high) + (dot(high, right_low) + dot(low, right_high))
+        product = product.reshape(chunk, 16, -1)
+        if acc:
+            acc_in[i].wait()
+            product = product + result[part(i)]
+        result[part(i)] = product
+        sent.append(start(result.at[part(i)], out.at[part(i)], 5 + steps + i))
+        sent[-1].start()
+    for copy in sent:
+        copy.wait()
+
+
+def update_call(rows, blocks, acc=()):
+    width = blocks[0].shape[-1]
+    count = X * C * Y
+    steps = count * 16 // 128
+    return call(
+        functools.partial(update_kernel, len(blocks)), f32(count, 16, width), (rows, *blocks, *acc),
+        ANY, (ANY,) * (1 + len(blocks) + len(acc)),
+        [
+            pltpu.VMEM(rows.shape, jnp.float32),
+            pltpu.VMEM((QUAD, Y, 32, width), jnp.float32),
+            pltpu.VMEM((count, 16, width), jnp.float32),
+            pltpu.SemaphoreType.DMA((5 + 2 * steps,)),
+        ],
+        flops=1409286144, moved=4718592, limit=60,
+    )
 
 
 def shift_z(value, step):
@@ -177,18 +201,13 @@
     return own, shift_z(up, 1), shift_z(down, -1), shift_far(far)
 
 
-def to_ys(own, *others):
-    return own, *(shift_y(other, step + 1) for step, other in enumerate(others))
-
-
 def exchange(value, axes):
     return lax.all_to_all(value, axes, 0, 0, tiled=True)
 
 
 def body(panel_rhs, diag_inv, coupling, trail_factor, trail_rhs):
-    core, z, y = lax.axis_index("c"), lax.axis_index("z"), lax.axis_index("y")
-    prow = lax.axis_index("x") * C + core
-    place = jnp.stack([core, z, y]).astype(jnp.int32)
+    z, y = lax.axis_index("z"), lax.axis_index("y")
+    prow = lax.axis_index("x") * C + lax.axis_index("c")
     strip, narrow = panel_rhs.shape[0], panel_rhs.shape[2]
     width = trail_rhs.shape[1] // (QUAD * Y)
     block = f32(QUAD, 32, width)
@@ -205,38 +224,35 @@
     shared = exchange(shared, "y")
 
     *by_class, by_y = call(
-        cut_kernel, (block,) * 4 + (f32(Y, *block.shape),), (place, trail_factor),
-        (ANY,) * 5, (SMEM, VMEM), sems(32), moved=7340032, limit=24,
+        cut_kernel, (block,) * 4 + (f32(Y, *block.shape),), (z.astype(jnp.int32).reshape(1), trail_factor),
+        (ANY,) * 5, (SMEM, VMEM), sems(32), moved=7340032, limit=60,
     )
     by_class = to_windows(*by_class)
     by_y = exchange(by_y, "y")
 
-    first, terms = call(couple_kernel, (f32(16, 128), f32(Z, 16, 128)), (arrived, shared), (VMEM, VMEM), (VMEM,) * 2)
+    first, terms = call(
+        couple_kernel, (f32(16, 128), f32(Z, 16, 128)), (arrived, shared, *by_class[1:], by_y),
+        (VMEM, VMEM), (VMEM, VMEM) + (ANY,) * 4,
+    )
     arrived = exchange(terms, "z")
-    terms = call(latter_kernel, f32(Z, len(NEAR), 16, 128), (arrived, shared, *by_class[1:], by_y), VMEM, (VMEM, VMEM) + (ANY,) * 4)
-    arrived = exchange(terms, "z")
-    copies = call(close_kernel, f32(X * C * Y, QUAD, 16, 128), (arrived,), VMEM, (VMEM,))
-    latter_rows = exchange(copies, SPREAD)
+    turned = call(turn_kernel, f32(Y, *block.shape), by_class, ANY, (VMEM,) * 4, sems(16), moved=3670016, limit=60)
+    first_factor = exchange(turned, "y")
+    by_k = call(merge_kernel, (block,) * 4, (by_y,), (ANY,) * 4, (VMEM,), sems(16), moved=3670016, limit=60)
+    latter_factor = to_windows(*by_k)
 
     near = (first, *(shift_z(first, -step) for step in NEAR[1:]))
     copies = call(spread_kernel, f32(X * C * Y, QUAD, 16, 128), near, VMEM, (VMEM,) * len(NEAR))
     first_rows = exchange(copies, SPREAD)
 
-    by_r = call(turn_kernel, (block,) * 4, by_class, (ANY,) * 4, (VMEM,) * 4, sems(16), moved=3670016)
-    first_factor = to_ys(*by_r)
-    by_k = call(merge_kernel, (block,) * 4, (by_y,), (ANY,) * 4, (VMEM,), sems(16), moved=3670016)
-    latter_factor = to_windows(*by_k)
-
-    scratch = [pltpu.VMEM((QUAD, Y, 32, width), jnp.float32)] + sems(4)
-    update = call(
-        first_update_kernel, f32(Z * Y, 16, width), (place, first_rows, *first_factor),
-        VMEM, (SMEM, VMEM) + (ANY,) * 4, scratch, flops=1409286144, moved=4718592, limit=40,
-    )
-    scratch = [pltpu.VMEM((QUAD, QUAD, 32, width), jnp.float32)] + sems(4)
-    update = call(
-        latter_update_kernel, f32(Z * Y, 16, width), (latter_rows, update, *latter_factor),
-        VMEM, (VMEM,) * 2 + (ANY,) * 4, scratch, flops=1409286144, moved=6553600, limit=40,
-    )
+    terms = call(latter_kernel, f32(Z, len(NEAR), 16, 128), (arrived, shared), VMEM, (VMEM, VMEM))
+    arrived = exchange(terms, "z")
+    copies = call(
+        close_kernel, f32(X * C * Y, QUAD, 16, 128), (arrived, first_factor, by_k[0]), VMEM, (VMEM, ANY, ANY)
+    )
+    latter_rows = exchange(copies, SPREAD)
+
+    update = update_call(first_rows, (first_factor,))
+    update = update_call(latter_rows, latter_factor, (update,))
     parts = exchange(update, COLS)
     parts = parts.reshape(2, QUAD, Y, *parts.shape[1:])
     reduced = trail_rhs - (parts[0] + parts[1]).transpose(2, 1, 0, 3).reshape(trail_rhs.shape)

time: 239 us -> 246 us (1.029)
  waiting for transfers between devices: 92.8 us -> 116 us
  blocking collectives: 39.1 us -> 22.7 us
  local copies, waits for them, and re-layouts: 25.8 us -> 13.7 us
  Pallas kernels: 17.8 us -> 25.3 us
  starting transfers between devices: 59.7 us -> 64 us
    all_to_all x6 -> x8, waiting for transfers between devices: 55.6 us -> 80 us  [exchange(): return lax.all_to_all(value, axes, 0, 0, tiled=True)]
    all_to_all x2 -> x1, blocking collectives: 39.1 us -> 22.7 us  [exchange(): return lax.all_to_all(value, axes, 0, 0, tiled=True)]
    ppermute x3 -> x0, waiting for transfers between devices: 16.3 us -> none  [shift_y(): return lax.ppermute(value, 'y', [(y, (y + step) % Y) for y in range(Y)])]
    ppermute x8, waiting for transfers between devices: 18 us -> 32.3 us  [shift_z(): return lax.ppermute(value, 'z', [(z, (z + step) % Z) for z in range(Z)])]
    unnamed x50 -> x38, local copies, waits for them, and re-layouts: 23.7 us -> 10.9 us
    all_to_all x6 -> x8, starting transfers between devices: 38.6 us -> 49.3 us  [exchange(): return lax.all_to_all(value, axes, 0, 0, tiled=True)]
    pallas_call x10, Pallas kernels: 17.8 us -> 25.3 us  [call(): pl.pallas_call(kernel, out_shape=outs, in_specs=in_specs, out_specs=out_s...]
    ppermute x3 -> x0, starting transfers between devices: 3.26 us -> none  [shift_y(): return lax.ppermute(value, 'y', [(y, (y + step) % Y) for y in range(Y)])]
  transfers between devices with their start and end apart: 19 -> 18, of which waited for: 12 -> 12; matrix products, arithmetic and copies ran while one was open for 1% -> 1% of each run, Pallas kernels for 5% -> 7%
where the time goes in v3:
time: 246 us; the launch traced here: 244 us
  waiting for transfers between devices  116 us (47%)
  starting transfers between devices  64 us (26%)
  Pallas kernels  25.3 us (10%)
  blocking collectives  22.7 us (9%)
  local copies, waits for them, and re-layouts  13.7 us (6%)
    all_to_all x8, waiting for transfers between devices, exchange(): return lax.all_to_all(value, axes, 0, 0, tiled=True)  80 us
    all_to_all x8, starting transfers between devices, exchange(): return lax.all_to_all(value, axes, 0, 0, tiled=True)  49.3 us
    ppermute x8, waiting for transfers between devices, shift_z(): return lax.ppermute(value, 'z', [(z, (z + step) % Z) for z in range(Z)])  32.3 us
    pallas_call x10, Pallas kernels, call(): pl.pallas_call(kernel, out_shape=outs, in_specs=in_specs, out_specs=out_s...  25.3 us
    all_to_all x1, blocking collectives, exchange(): return lax.all_to_all(value, axes, 0, 0, tiled=True)  22.7 us
    ppermute x8, starting transfers between devices, shift_z(): return lax.ppermute(value, 'z', [(z, (z + step) % Z) for z in range(Z)])  12.8 us
    unnamed x38, local copies, waits for them, and re-layouts  10.9 us
  transfers between devices with their start and end apart: 18, of which 12 were waited for; matrix products, arithmetic and copies ran while one was open for 1% of the time, Pallas kernels for 7%

profile of v3, /device:TPU:20, one launch (start us, length us, event | category | flops | bytes accessed | tf_op | source)
XLA Modules:
  0.0 244.0 jit_solution(18008307081317586109)
XLA Ops:
  3.5 1.3 shard_map.68
  4.9 22.7 %all_to_all.45.arrived = f32[32,16,128]{2,1,0:T(8,128)} all-to-all(f32[32,16,128]{2,1,0:T(8,128)S(1)} %get-tuple-element.15), channel_id=1, replica_groups=mesh['x'=4,'c'=2,'z'=8,'y'=4] {'z','y'}, dimensions={0} | all-to-all | bytes 524288 | tf_op jit(solution)/shard_map/all_to_all | solution.py:205
  27.6 5.2 %all-to-all-start.1 = ((f32[4,72,1024]{2,1,0:T(8,128)}), f32[4,72,1024]{2,1,0:T(8,128)S(1)}, u32[]{:S(2)}, u32[]{:S(2)}) async-start(f32[4,72,1024]{2,1,0:T(8,128)} %get-tuple-element.16), calls=%async_computation.1 | async-start | bytes 2359296 | tf_op jit(solution)/shard_map/all_to_all | solution.py:205
  32.8 4.1 %shard_map.69 = (f32[4,32,896]{2,1,0:T(8,128)}, f32[4,32,896]{2,1,0:T(8,128)}, f32[4,32,896]{2,1,0:T(8,128)}, f32[4,32,896]{2,1,0:T(8,128)}, f32[4,4,32,896]{3,2,1,0:T(8,128)}) custom-call(s32[1]{0:T(128)} %bitcast.4.place, f32[2,32,14336]{2,1,0:T(8,128)} %factor.1), custom_call_target="tpu_custom_call" | custom-call | bytes 7340032 | tf_op jit(solution)/shard_map/pallas_call | solution.py:26
  36.9 7.9 %all-to-all-done.1.shared = f32[4,72,1024]{2,1,0:T(8,128)S(1)} async-done(((f32[4,72,1024]{2,1,0:T(8,128)}), f32[4,72,1024]{2,1,0:T(8,128)S(1)}, u32[]{:S(2)}, u32[]{:S(2)}) %all-to-all-start.1) | async-done | bytes 1179680 | tf_op jit(solution)/shard_map/all_to_all | solution.py:205
  44.8 6.5 %all-to-all-start.2 = ((f32[4,4,32,896]{3,2,1,0:T(8,128)}), f32[4,4,32,896]{3,2,1,0:T(8,128)S(1)}, u32[]{:S(2)}, u32[]{:S(2)}) async-start(f32[4,4,32,896]{3,2,1,0:T(8,128)} %get-tuple-element.20), calls=%async_computation.2 | async-start | bytes 3670016 | tf_op jit(solution)/shard_map/all_to_all | solution.py:205
  51.3 1.1 collective-permute-start
  52.5 2.1 collective-permute-start.1
  55.3 15.8 %collective-permute-done.refs_0_.refs_1_ = f32[4,32,896]{2,1,0:T(8,128)S(1)} collective-permute-done((f32[4,32,896]{2,1,0:T(8,128)}, f32[4,32,896]{2,1,0:T(8,128)S(1)}, u32[]{:S(2)}, u32[]{:S(2)}) %collective-permute-start) | collective-permute-done | bytes 458784 | tf_op jit(solution)/shard_map/ppermute | solution.py:190
  76.4 1.2 shard_map.70
  77.6 4.4 %all-to-all-start.4 = ((f32[8,16,128]{2,1,0:T(8,128)}), f32[8,16,128]{2,1,0:T(8,128)S(1)}, u32[]{:S(2)}, u32[]{:S(2)}) async-start(f32[8,16,128]{2,1,0:T(8,128)} %get-tuple-element.22), calls=%async_computation.4 | async-start | bytes 131072 | tf_op jit(solution)/shard_map/all_to_all | solution.py:205
  82.0 2.8 %shard_map.73 = f32[4,4,32,896]{3,2,1,0:T(8,128)} custom-call(f32[4,32,896]{2,1,0:T(8,128)} %get-tuple-element.23.refs_0_, f32[4,32,896]{2,1,0:T(8,128)} %copy-done.3, f32[4,32,896]{2,1,0:T(8,128)} %copy-done.4, f32[4,32,896]{2,1,0:T(8,128)} %copy-done.6), custom_call_target="tpu_custom_call" | custom-call | bytes 3670016 | tf_op jit(solution)/shard_map/pallas_call | solution.py:26
  84.8 5.5 %all-to-all-done.4.arrived = f32[8,16,128]{2,1,0:T(8,128)S(1)} async-done(((f32[8,16,128]{2,1,0:T(8,128)}), f32[8,16,128]{2,1,0:T(8,128)S(1)}, u32[]{:S(2)}, u32[]{:S(2)}) %all-to-all-start.4) | async-done | bytes 65568 | tf_op jit(solution)/shard_map/all_to_all | solution.py:205
  90.4 4.8 %all-to-all-start.6 = ((f32[4,4,32,896]{3,2,1,0:T(8,128)}), f32[4,4,32,896]{3,2,1,0:T(8,128)S(1)}, u32[]{:S(2)}, u32[]{:S(2)}) async-start(f32[4,4,32,896]{3,2,1,0:T(8,128)} %shard_map.73), calls=%async_computation.6 | async-start | bytes 3670016 | tf_op jit(solution)/shard_map/all_to_all | solution.py:205
  96.3 17.4 %all-to-all-done.6.refs_0_.refs_1_ = f32[4,4,32,896]{3,2,1,0:T(8,128)S(1)} async-done(((f32[4,4,32,896]{3,2,1,0:T(8,128)}), f32[4,4,32,896]{3,2,1,0:T(8,128)S(1)}, u32[]{:S(2)}, u32[]{:S(2)}) %all-to-all-start.6) | async-done | bytes 1835040 | tf_op jit(solution)/shard_map/all_to_all | solution.py:205
  113.6 3.4 %all-to-all-start.5 = ((f32[8,5,16,128]{3,2,1,0:T(8,128)}), f32[8,5,16,128]{3,2,1,0:T(8,128)S(1)}, u32[]{:S(2)}, u32[]{:S(2)}) async-start(f32[8,5,16,128]{3,2,1,0:T(8,128)} %shard_map.72), calls=%async_computation.5 | async-start | bytes 655360 | tf_op jit(solution)/shard_map/all_to_all | solution.py:205
  117.1 1.9 collective-permute-start.3
  119.0 1.4 collective-permute-start.4
  120.4 2.8 %collective-permute-start.5 = (f32[16,128]{1,0:T(8,128)S(1)}, f32[16,128]{1,0:T(8,128)S(1)}, u32[]{:S(2)}, u32[]{:S(2)}) collective-permute-start(f32[16,128]{1,0:T(8,128)S(1)} %get-tuple-element.21.refs_0_), channel_id=1, source_target_pairs={{0,24},{4,28},{8,0},{12,4},{16,8},{20,12},{24,16},{28,20},{1,25},{... | collective-permute-start | bytes 24584 | tf_op jit(solution)/shard_map/ppermute | solution.py:190
  123.3 1.5 collective-permute-done.3.refs_1_
  125.3 3.6 %collective-permute-done.6.refs_4_ = f32[16,128]{1,0:T(8,128)S(1)} collective-permute-done((f32[16,128]{1,0:T(8,128)S(1)}, f32[16,128]{1,0:T(8,128)S(1)}, u32[]{:S(2)}, u32[]{:S(2)}) %collective-permute-start.6) | collective-permute-done | bytes 8224 | tf_op jit(solution)/shard_map/ppermute | solution.py:190
  130.1 8.0 %all-to-all-start.3 = ((f32[32,4,16,128]{3,2,1,0:T(8,128)}), f32[32,4,16,128]{3,2,1,0:T(8,128)}, u32[]{:S(2)}, u32[]{:S(2)}) async-start(f32[32,4,16,128]{3,2,1,0:T(8,128)} %shard_map.71), calls=%async_computation.3 | async-start | bytes 2097152 | tf_op jit(solution)/shard_map/all_to_all | solution.py:205
  138.1 2.8 %shard_map.74 = (f32[4,32,896]{2,1,0:T(8,128)}, f32[4,32,896]{2,1,0:T(8,128)}, f32[4,32,896]{2,1,0:T(8,128)}, f32[4,32,896]{2,1,0:T(8,128)}) custom-call(f32[4,4,32,896]{3,2,1,0:T(8,128)} %copy-done), custom_call_target="tpu_custom_call" | custom-call | bytes 3670016 | tf_op jit(solution)/shard_map/pallas_call | solution.py:26
  143.1 8.0 %all-to-all-done.3.refs_0_ = f32[32,4,16,128]{3,2,1,0:T(8,128)} async-done(((f32[32,4,16,128]{3,2,1,0:T(8,128)}), f32[32,4,16,128]{3,2,1,0:T(8,128)}, u32[]{:S(2)}, u32[]{:S(2)}) %all-to-all-start.3) | async-done | bytes 1048608 | tf_op jit(solution)/shard_map/all_to_all | solution.py:205
  151.1 8.1 %all-to-all-start.7 = ((f32[32,4,16,128]{3,2,1,0:T(8,128)}), f32[32,4,16,128]{3,2,1,0:T(8,128)S(1)}, u32[]{:S(2)}, u32[]{:S(2)}) async-start(f32[32,4,16,128]{3,2,1,0:T(8,128)} %shard_map.75), calls=%async_computation.7 | async-start | bytes 2097152 | tf_op jit(solution)/shard_map/all_to_all | solution.py:205
  160.3 2.3 collective-permute-start.8
  163.7 4.5 %shard_map.76.refs_5_ = f32[32,16,896]{2,1,0:T(8,128)} custom-call(f32[32,4,16,128]{3,2,1,0:T(8,128)} %all-to-all-done.3.refs_0_, f32[4,4,32,896]{3,2,1,0:T(8,128)} %copy-done.1), custom_call_target="tpu_custom_call" | custom-call | flops 1409286144 | bytes 4718592 | tf_op jit(solution)/shard_map/pallas_call | solution.py:26
  168.1 10.9 %collective-permute-done.7.refs_2_ = f32[4,32,896]{2,1,0:T(8,128)S(1)} collective-permute-done((f32[4,32,896]{2,1,0:T(8,128)}, f32[4,32,896]{2,1,0:T(8,128)S(1)}, u32[]{:S(2)}, u32[]{:S(2)}) %collective-permute-start.7) | collective-permute-done | bytes 458784 | tf_op jit(solution)/shard_map/ppermute | solution.py:190
  179.0 3.3 %collective-permute-done.9.refs_4_ = f32[4,32,896]{2,1,0:T(8,128)S(1)} collective-permute-done((f32[4,32,896]{2,1,0:T(8,128)S(1)}, f32[4,32,896]{2,1,0:T(8,128)S(1)}, u32[]{:S(2)}, u32[]{:S(2)}) %collective-permute-start.9) | collective-permute-done | bytes 458784 | tf_op jit(solution)/shard_map/ppermute | solution.py:197
  184.1 5.1 %shard_map.77 = f32[32,16,896]{2,1,0:T(8,128)} custom-call(f32[32,4,16,128]{3,2,1,0:T(8,128)} %copy-done.11, f32[4,32,896]{2,1,0:T(8,128)} %get-tuple-element.24.refs_1_, f32[4,32,896]{2,1,0:T(8,128)} %copy-done.13, f32[4,32,896]{2,1,0:T(8,128)} %copy-done.14, f32[4,32,896]{2,1,0:T(8,128)} %copy-done.15, f32[32,16,896]{2,1,0:T(8,128)} %shard_map.76.refs_5_), custom_call_target="tpu_custom_call" | custom-call | flops 1409286144 | bytes 4718592 | tf_op jit(solution)/shard_map/pallas_call | solution.py:26
  189.2 8.8 %all-to-all-start.8 = ((f32[32,16,896]{2,1,0:T(8,128)}), f32[32,16,896]{2,1,0:T(8,128)S(1)}, u32[]{:S(2)}, u32[]{:S(2)}) async-start(f32[32,16,896]{2,1,0:T(8,128)} %shard_map.77), calls=%async_computation.8 | async-start | bytes 3670016 | tf_op jit(solution)/shard_map/all_to_all | solution.py:205
  200.5 41.3 %all-to-all-done.8 = f32[32,16,896]{2,1,0:T(8,128)S(1)} async-done(((f32[32,16,896]{2,1,0:T(8,128)}), f32[32,16,896]{2,1,0:T(8,128)S(1)}, u32[]{:S(2)}, u32[]{:S(2)}) %all-to-all-start.8) | async-done | bytes 1835040 | tf_op jit(solution)/shard_map/all_to_all | solution.py:205
  (66 shorter events, 22.4 us)
Async XLA Ops:
  1.7 1.0 copy-start.9
  27.6 17.2 %all-to-all-start.1 = ((f32[4,72,1024]{2,1,0:T(8,128)}), f32[4,72,1024]{2,1,0:T(8,128)S(1)}, u32[]{:S(2)}, u32[]{:S(2)}) async-start(f32[4,72,1024]{2,1,0:T(8,128)} %get-tuple-element.16), calls=%async_computation.1 | async-start | bytes 2359296 | tf_op jit(solution)/shard_map/all_to_all | solution.py:205
  44.8 28.6 %all-to-all-start.2 = ((f32[4,4,32,896]{3,2,1,0:T(8,128)}), f32[4,4,32,896]{3,2,1,0:T(8,128)S(1)}, u32[]{:S(2)}, u32[]{:S(2)}) async-start(f32[4,4,32,896]{3,2,1,0:T(8,128)} %get-tuple-element.20), calls=%async_computation.2 | async-start | bytes 3670016 | tf_op jit(solution)/shard_map/all_to_all | solution.py:205
  51.3 19.8 %collective-permute-start = (f32[4,32,896]{2,1,0:T(8,128)}, f32[4,32,896]{2,1,0:T(8,128)S(1)}, u32[]{:S(2)}, u32[]{:S(2)}) collective-permute-start(f32[4,32,896]{2,1,0:T(8,128)} %get-tuple-element.17), channel_id=1, source_target_pairs={{0,4},{4,8},{8,12},{12,16},{16,20},{20,24},{24,28},{28,0},{1,5},{5... | collective-permute-start | bytes 1376264 | tf_op jit(solution)/shard_map/ppermute | solution.py:190
  52.5 18.6 %collective-permute-start.1 = (f32[4,32,896]{2,1,0:T(8,128)}, f32[4,32,896]{2,1,0:T(8,128)S(1)}, u32[]{:S(2)}, u32[]{:S(2)}) collective-permute-start(f32[4,32,896]{2,1,0:T(8,128)} %get-tuple-element.18), channel_id=1, source_target_pairs={{0,28},{4,0},{8,4},{12,8},{16,12},{20,16},{24,20},{28,24},{1,29},{... | collective-permute-start | bytes 1376264 | tf_op jit(solution)/shard_map/ppermute | solution.py:190
  54.6 18.0 %collective-permute-start.2 = (f32[4,32,896]{2,1,0:T(8,128)}, f32[4,32,896]{2,1,0:T(8,128)S(1)}, u32[]{:S(2)}, u32[]{:S(2)}) collective-permute-start(f32[4,32,896]{2,1,0:T(8,128)} %get-tuple-element.19), channel_id=1, source_target_pairs={{0,24},{4,28},{8,0},{12,4},{16,8},{20,12},{24,16},{28,20},{32,40},... | collective-permute-start | bytes 1376264 | tf_op jit(solution)/shard_map/ppermute | solution.py:197
  71.1 6.5 %copy-start.3 = (f32[4,32,896]{2,1,0:T(8,128)}, f32[4,32,896]{2,1,0:T(8,128)S(1)}, u32[]{:S(2)}) copy-start(f32[4,32,896]{2,1,0:T(8,128)S(1)} %collective-permute-done.refs_0_.refs_1_) | copy-start | bytes 1376260
  73.4 1.0 copy-start.5
  74.4 1.0 copy-start.7
  75.4 0.9 copy-start.8
  76.4 1.2 copy-start
  77.6 12.8 %all-to-all-start.4 = ((f32[8,16,128]{2,1,0:T(8,128)}), f32[8,16,128]{2,1,0:T(8,128)S(1)}, u32[]{:S(2)}, u32[]{:S(2)}) async-start(f32[8,16,128]{2,1,0:T(8,128)} %get-tuple-element.22), calls=%async_computation.4 | async-start | bytes 131072 | tf_op jit(solution)/shard_map/all_to_all | solution.py:205
  90.4 23.3 %all-to-all-start.6 = ((f32[4,4,32,896]{3,2,1,0:T(8,128)}), f32[4,4,32,896]{3,2,1,0:T(8,128)S(1)}, u32[]{:S(2)}, u32[]{:S(2)}) async-start(f32[4,4,32,896]{3,2,1,0:T(8,128)} %shard_map.73), calls=%async_computation.6 | async-start | bytes 3670016 | tf_op jit(solution)/shard_map/all_to_all | solution.py:205
  113.6 27.3 %copy-start.1 = (f32[4,4,32,896]{3,2,1,0:T(8,128)}, f32[4,4,32,896]{3,2,1,0:T(8,128)S(1)}, u32[]{:S(2)}) copy-start(f32[4,4,32,896]{3,2,1,0:T(8,128)S(1)} %all-to-all-done.6.refs_0_.refs_1_) | copy-start | bytes 5505028
  113.6 16.4 %all-to-all-start.5 = ((f32[8,5,16,128]{3,2,1,0:T(8,128)}), f32[8,5,16,128]{3,2,1,0:T(8,128)S(1)}, u32[]{:S(2)}, u32[]{:S(2)}) async-start(f32[8,5,16,128]{3,2,1,0:T(8,128)} %shard_map.72), calls=%async_computation.5 | async-start | bytes 655360 | tf_op jit(solution)/shard_map/all_to_all | solution.py:205
  117.1 7.8 %collective-permute-start.3 = (f32[16,128]{1,0:T(8,128)S(1)}, f32[16,128]{1,0:T(8,128)S(1)}, u32[]{:S(2)}, u32[]{:S(2)}) collective-permute-start(f32[16,128]{1,0:T(8,128)S(1)} %get-tuple-element.21.refs_0_), channel_id=1, source_target_pairs={{0,4},{4,8},{8,12},{12,16},{16,20},{20,24},{24,28},{28,0},{1,5},{5... | collective-permute-start | bytes 24584 | tf_op jit(solution)/shard_map/ppermute | solution.py:190
  119.0 5.9 %collective-permute-start.4 = (f32[16,128]{1,0:T(8,128)S(1)}, f32[16,128]{1,0:T(8,128)S(1)}, u32[]{:S(2)}, u32[]{:S(2)}) collective-permute-start(f32[16,128]{1,0:T(8,128)S(1)} %get-tuple-element.21.refs_0_), channel_id=1, source_target_pairs={{0,28},{4,0},{8,4},{12,8},{16,12},{20,16},{24,20},{28,24},{1,29},{... | collective-permute-start | bytes 24584 | tf_op jit(solution)/shard_map/ppermute | solution.py:190
  120.4 4.9 %collective-permute-start.5 = (f32[16,128]{1,0:T(8,128)S(1)}, f32[16,128]{1,0:T(8,128)S(1)}, u32[]{:S(2)}, u32[]{:S(2)}) collective-permute-start(f32[16,128]{1,0:T(8,128)S(1)} %get-tuple-element.21.refs_0_), channel_id=1, source_target_pairs={{0,24},{4,28},{8,0},{12,4},{16,8},{20,12},{24,16},{28,20},{1,25},{... | collective-permute-start | bytes 24584 | tf_op jit(solution)/shard_map/ppermute | solution.py:190
  123.2 5.8 %collective-permute-start.6 = (f32[16,128]{1,0:T(8,128)S(1)}, f32[16,128]{1,0:T(8,128)S(1)}, u32[]{:S(2)}, u32[]{:S(2)}) collective-permute-start(f32[16,128]{1,0:T(8,128)S(1)} %get-tuple-element.21.refs_0_), channel_id=1, source_target_pairs={{0,8},{4,12},{8,16},{12,20},{16,24},{20,28},{24,0},{28,4},{1,9},{5... | collective-permute-start | bytes 24584 | tf_op jit(solution)/shard_map/ppermute | solution.py:190
  130.1 21.0 %all-to-all-start.3 = ((f32[32,4,16,128]{3,2,1,0:T(8,128)}), f32[32,4,16,128]{3,2,1,0:T(8,128)}, u32[]{:S(2)}, u32[]{:S(2)}) async-start(f32[32,4,16,128]{3,2,1,0:T(8,128)} %shard_map.71), calls=%async_computation.3 | async-start | bytes 2097152 | tf_op jit(solution)/shard_map/all_to_all | solution.py:205
  141.0 1.0 copy-start.2
  143.1 17.1 %copy-start.17 = (f32[4,32,896]{2,1,0:T(8,128)S(1)}, f32[4,32,896]{2,1,0:T(8,128)}, u32[]{:S(2)}) copy-start(f32[4,32,896]{2,1,0:T(8,128)} %get-tuple-element.26) | copy-start | bytes 1376260
  143.1 19.4 %copy-start.16 = (f32[4,32,896]{2,1,0:T(8,128)S(1)}, f32[4,32,896]{2,1,0:T(8,128)}, u32[]{:S(2)}) copy-start(f32[4,32,896]{2,1,0:T(8,128)} %get-tuple-element.27) | copy-start | bytes 1376260
  151.1 31.3 %all-to-all-start.7 = ((f32[32,4,16,128]{3,2,1,0:T(8,128)}), f32[32,4,16,128]{3,2,1,0:T(8,128)S(1)}, u32[]{:S(2)}, u32[]{:S(2)}) async-start(f32[32,4,16,128]{3,2,1,0:T(8,128)} %shard_map.75), calls=%async_computation.7 | async-start | bytes 2097152 | tf_op jit(solution)/shard_map/all_to_all | solution.py:205
  159.2 19.8 %collective-permute-start.7 = (f32[4,32,896]{2,1,0:T(8,128)}, f32[4,32,896]{2,1,0:T(8,128)S(1)}, u32[]{:S(2)}, u32[]{:S(2)}) collective-permute-start(f32[4,32,896]{2,1,0:T(8,128)} %get-tuple-element.25), channel_id=1, source_target_pairs={{0,4},{4,8},{8,12},{12,16},{16,20},{20,24},{24,28},{28,0},{1,5},{5... | collective-permute-start | bytes 1376264 | tf_op jit(solution)/shard_map/ppermute | solution.py:190
  160.3 18.7 %collective-permute-start.8 = (f32[4,32,896]{2,1,0:T(8,128)S(1)}, f32[4,32,896]{2,1,0:T(8,128)S(1)}, u32[]{:S(2)}, u32[]{:S(2)}) collective-permute-start(f32[4,32,896]{2,1,0:T(8,128)S(1)} %copy-done.17), channel_id=1, source_target_pairs={{0,28},{4,0},{8,4},{12,8},{16,12},{20,16},{24,20},{28,24},{1,29},{... | collective-permute-start | bytes 1376264 | tf_op jit(solution)/shard_map/ppermute | solution.py:190
  162.5 19.8 %collective-permute-start.9 = (f32[4,32,896]{2,1,0:T(8,128)S(1)}, f32[4,32,896]{2,1,0:T(8,128)S(1)}, u32[]{:S(2)}, u32[]{:S(2)}) collective-permute-start(f32[4,32,896]{2,1,0:T(8,128)S(1)} %copy-done.16), channel_id=1, source_target_pairs={{0,24},{4,28},{8,0},{12,4},{16,8},{20,12},{24,16},{28,20},{32,40},... | collective-permute-start | bytes 1376264 | tf_op jit(solution)/shard_map/ppermute | solution.py:197
  179.0 3.4 %copy-start.13 = (f32[4,32,896]{2,1,0:T(8,128)}, f32[4,32,896]{2,1,0:T(8,128)S(1)}, u32[]{:S(2)}) copy-start(f32[4,32,896]{2,1,0:T(8,128)S(1)} %collective-permute-done.7.refs_2_) | copy-start | bytes 1376260
  179.0 3.4 %copy-start.14 = (f32[4,32,896]{2,1,0:T(8,128)}, f32[4,32,896]{2,1,0:T(8,128)S(1)}, u32[]{:S(2)}) copy-start(f32[4,32,896]{2,1,0:T(8,128)S(1)} %collective-permute-done.8.refs_3_) | copy-start | bytes 1376260
  183.1 1.0 copy-start.11
  189.2 52.5 %all-to-all-start.8 = ((f32[32,16,896]{2,1,0:T(8,128)}), f32[32,16,896]{2,1,0:T(8,128)S(1)}, u32[]{:S(2)}, u32[]{:S(2)}) async-start(f32[32,16,896]{2,1,0:T(8,128)} %shard_map.77), calls=%async_computation.8 | async-start | bytes 3670016 | tf_op jit(solution)/shard_map/all_to_all | solution.py:205
  241.8 1.2 copy-start.12
  (4 other events, 3.3 us)

commit v4 on v2

v4 whole, which is shorter than its diff:
```python
import functools

import jax
import jax.numpy as jnp
from jax import lax
from jax.experimental import pallas as pl
from jax.experimental.pallas import tpu as pltpu
from jax.sharding import Mesh, PartitionSpec as P

X, C, Z, Y = 4, 2, 8, 4
ROWS = ("x", "c")
COLS = ("z", "y")
SPREAD = ("x", "c", "y")
QUAD = 4
NEAR = (0, -1, 1, 2, -2)
VMEM = pl.BlockSpec(memory_space=pltpu.VMEM)
ANY = pl.BlockSpec(memory_space=pl.ANY)
SMEM = pl.BlockSpec(memory_space=pltpu.SMEM)


def f32(*shape):
    return jax.ShapeDtypeStruct(shape, jnp.float32)


def call(kernel, outs, ins, out_specs, in_specs, scratch=(), flops=0, moved=0, limit=16):
    return pl.pallas_call(
        kernel,
        out_shape=outs,
        in_specs=in_specs,
        out_specs=out_specs,
        scratch_shapes=scratch,
        compiler_params=pltpu.CompilerParams(vmem_limit_bytes=limit << 20),
        cost_estimate=pl.CostEstimate(flops=flops, bytes_accessed=moved, transcendentals=0),
    )(*ins)


def exact_dot(left, right):
    return lax.dot_general(
        left, right, (((1,), (0,)), ((), ())),
        precision=lax.Precision.HIGHEST, preferred_element_type=jnp.float32,
    )


def split(value):
    high = value.astype(jnp.bfloat16)
    return high, (value - high.astype(jnp.float32)).astype(jnp.bfloat16)


def copy_all(copies, sems):
    started = [pltpu.make_async_copy(src, dst, sems.at[i]) for i, (src, dst) in enumerate(copies)]
    for copy in started:
        copy.start()
    for copy in started:
        copy.wait()


def open_kernel(rhs, inverse, terms):
    product = exact_dot(rhs[...], inverse[0])
    rows = rhs.shape[0] // Y
    for z in range(Z):
        for y in range(Y):
            terms[z * Y + y] = product[y * rows:(y + 1) * rows, z * 128:(z + 1) * 128]


def share_kernel(place, rhs, inverse, couple, *shared):
    for r in range(Y):
        rows = pl.ds(pl.multiple_of((place[1] + r) % Y * 16, 16), 16)
        piece = rhs[rows]
        shared[r][0:32] = couple[...]
        shared[r][32:64] = inverse[1]
        shared[r][64:72] = jnp.zeros((8, shared[r].shape[1]), jnp.float32)
        shared[r][64:72, 0:128] = piece[0:8]
        shared[r][64:72, 128:256] = piece[8:16]


def in_order(place, shared, rows, matrix):
    for r in range(Y):
        matrix[(place[1] + Y - r) % Y] = shared[r][rows]
    return matrix[...].reshape(Y * 32, -1)


def couple_kernel(place, arrived, *refs):
    shared, (first, terms, matrix) = refs[:Y], refs[-3:]
    total = jnp.sum(arrived[...], axis=0)
    first[...] = total
    product = exact_dot(total, in_order(place, shared, slice(0, 32), matrix))
    for z in range(Z):
        terms[z] = product[:, z * 128:(z + 1) * 128]


def latter_kernel(place, arrived, *refs):
    shared, (terms, matrix) = refs[:Y], refs[-2:]
    rhs = sum(piece[64:72] for piece in shared)
    rhs = jnp.concatenate([rhs[:, 0:128], rhs[:, 128:256]], axis=0)
    second = rhs - jnp.sum(arrived[...], axis=0)
    product = exact_dot(second, in_order(place, shared, slice(32, 64), matrix))
    part = lambda z: product[:, (z % Z) * 128:(z % Z + 1) * 128]
    for z in range(Z):
        for k, step in enumerate(NEAR):
            terms[z, k] = part(z + step)


def close_kernel(arrived, *refs):
    latter = jnp.sum(arrived[...], axis=0)
    first, copies = refs[:-1], refs[-1]
    for place in range(X * C * Y):
        for k in range(QUAD):
            near = k if k < 3 else 3 + place // Y % C
            copies[place, k] = first[near][...]
            copies[place, QUAD + k] = latter[near]


def around(z):
    return (z % QUAD, (z + 1) % QUAD, (z + 3) % QUAD, (z + 2) % QUAD)


def cut_kernel(place, factor, *refs):
    by_class, by_y, sems = refs[:4], refs[4:8], refs[8]
    classes = around(place[0])
    width = by_y[0].shape[2]
    copies = []
    for r in range(Y):
        for k in range(QUAD):
            strip = pl.multiple_of(((place[1] + r) % Y * QUAD + classes[k]) * width, width)
            copies.append((factor.at[0, :, pl.ds(strip, width)], by_class[k].at[r]))
            copies.append((factor.at[1, :, pl.ds(strip, width)], by_y[r].at[k]))
    copy_all(copies, sems)


def turn_kernel(*refs):
    arrived, sent, sems = refs[:4], refs[4:8], refs[8]
    copy_all([(arrived[k].at[r], sent[r].at[k]) for r in range(Y) for k in range(QUAD)], sems)


def merge_kernel(place, *refs):
    arrived, sent, sems = refs[:4], refs[4:8], refs[8]
    copy_all([(arrived[r].at[k], sent[k].at[(place[1] + Y - r) % Y]) for r in range(Y) for k in range(QUAD)], sems)


def update_kernel(place, rows, *refs):
    by_r, by_k = refs[:Y], refs[Y:Y + QUAD]
    out, left, factor, result, sems = refs[-5:]
    start = lambda src, dst, i: pltpu.make_async_copy(src, dst, sems.at[i])
    chunk = 128 // 16
    part = lambda i: slice(i * chunk, (i + 1) * chunk)
    arriving = [start(rows, left, 0)]
    arriving += [start(by_r[r], factor.at[0, :, (place[1] + Y - r) % Y], 1 + r) for r in range(Y)]
    arriving += [start(by_k[k], factor.at[1, k], 1 + Y + k) for k in range(QUAD)]
    for copy in arriving:
        copy.start()
    for copy in arriving:
        copy.wait()
    right_high, right_low = split(factor[...].reshape(2 * QUAD * 128, -1))
    dot = functools.partial(jnp.dot, preferred_element_type=jnp.float32)
    sent = []
    for i in range(left.shape[0] // chunk):
        piece = left[part(i)]
        high, low = split(jnp.concatenate([piece[:, k].reshape(128, 128) for k in range(2 * QUAD)], axis=1))
        product = dot(high, right_high) + (dot(high, right_low) + dot(low, right_high))
        result[part(i)] = product.reshape(chunk, 16, -1)
        sent.append(start(result.at[part(i)], out.at[part(i)], 1 + Y + QUAD + i))
        sent[-1].start()
    for copy in sent:
        copy.wait()


def shift_y(value, step):
    return lax.ppermute(value, "y", [(y, (y + step) % Y) for y in range(Y)])


def shift_z(value, step):
    return lax.ppermute(value, "z", [(z, (z + step) % Z) for z in range(Z)])


def shift_far(value):
    pairs = [
        (c * Z + z, c * Z + (z + (2 if c else -2)) % Z) for c in range(C) for z in range(Z)
    ]
    return lax.ppermute(value, ("c", "z"), pairs)


def to_windows(own, up, down, far):
    return own, shift_z(up, 1), shift_z(down, -1), shift_far(far)


def to_ys(own, *others):
    return own, *(shift_y(other, step + 1) for step, other in enumerate(others))


def exchange(value, axes):
    return lax.all_to_all(value, axes, 0, 0, tiled=True)


def body(panel_rhs, diag_inv, coupling, trail_factor, trail_rhs):
    z, y = lax.axis_index("z"), lax.axis_index("y")
    prow = lax.axis_index("x") * C + lax.axis_index("c")
    place = jnp.stack([z, y]).astype(jnp.int32)
    strip, narrow = panel_rhs.shape[0], panel_rhs.shape[2]
    width = trail_rhs.shape[1] // (QUAD * Y)
    block = f32(QUAD, 32, width)
    sems = lambda n: [pltpu.SemaphoreType.DMA((n,))]
    matrix = [pltpu.VMEM((Y, 32, 1024), jnp.float32)]

    rhs = panel_rhs.transpose(1, 0, 2)
    lanes = lax.broadcasted_iota(jnp.int32, (1, 128), 1) // narrow
    second_rhs = jnp.where(lanes == y, jnp.tile(rhs[1], (1, Y)), 0.0)
    shared = call(
        share_kernel, (f32(72, 1024),) * Y, (place, second_rhs, diag_inv, coupling),
        (VMEM,) * Y, (SMEM,) + (VMEM,) * 3,
    )
    shared = to_ys(*shared)
    terms = call(open_kernel, f32(Z * Y, 16, 128), (rhs[0], diag_inv), VMEM, (VMEM,) * 2)
    arrived = exchange(terms, COLS)

    cut = call(
        cut_kernel, (block,) * 8, (place, trail_factor), (ANY,) * 8, (SMEM, VMEM), sems(32), moved=7340032, limit=60,
    )
    by_class, by_y = to_windows(*cut[:4]), to_ys(*cut[4:])

    first, terms = call(
        couple_kernel, (f32(16, 128), f32(Z, 16, 128)), (place, arrived, *shared, *by_class[1:]),
        (VMEM, VMEM), (SMEM,) + (VMEM,) * 5 + (ANY,) * 3, matrix,
    )
    arrived = exchange(terms, "z")
    by_r = call(turn_kernel, (block,) * 4, by_class, (ANY,) * 4, (VMEM,) * 4, sems(16), moved=3670016, limit=60)
    first_factor = to_ys(*by_r)
    near = (first, *(shift_z(first, -step) for step in NEAR[1:]))

    terms = call(
        latter_kernel, f32(Z, len(NEAR), 16, 128), (place, arrived, *shared, *by_y[1:]),
        VMEM, (SMEM,) + (VMEM,) * 5 + (ANY,) * 3, matrix,
    )
    arrived = exchange(terms, "z")
    by_k = call(merge_kernel, (block,) * 4, (place, *by_y), (ANY,) * 4, (SMEM,) + (VMEM,) * 4, sems(16), moved=3670016, limit=60)
    latter_factor = to_windows(*by_k)
    copies = call(close_kernel, f32(X * C * Y, 2 * QUAD, 16, 128), (arrived, *near), VMEM, (VMEM,) * 6)
    rows = exchange(copies, SPREAD)

    update = call(
        update_kernel, f32(X * C * Y, 16, width), (place, rows, *first_factor, *latter_factor),
        ANY, (SMEM,) + (ANY,) * 9,
        [
            pltpu.VMEM(rows.shape, jnp.float32),
            pltpu.VMEM((2, QUAD, Y, 32, width), jnp.float32),
            pltpu.VMEM((X * C * Y, 16, width), jnp.float32),
        ] + sems(17),
        flops=2818572288, moved=7602176, limit=60,
    )
    parts = exchange(update, COLS)
    parts = parts.reshape(2, QUAD, Y, *parts.shape[1:])
    reduced = trail_rhs - (parts[0] + parts[1]).transpose(2, 1, 0, 3).reshape(trail_rhs.shape)

    own = lambda panel: lax.dynamic_slice(
        rows, (prow * Y, panel * QUAD, 0, y * narrow), (Y, 1, rows.shape[2], narrow)
    ).reshape(strip, narrow)
    solved = jnp.stack([own(0), own(1)], axis=1)
    return solved, reduced


def solution(mesh):
    devices = Mesh(mesh.devices.reshape(X, C, Z, Y), ("x", "c", "z", "y"))
    placed = (
        P(ROWS, None, COLS),
        P(None, COLS, None),
        P(COLS, None),
        P(None, COLS, ROWS),
        P(COLS, ROWS),
    )
    return jax.shard_map(
        body,
        mesh=devices,
        in_specs=placed,
        out_specs=(P(ROWS, None, COLS), P(COLS, ROWS)),
        check_vma=False,
    )
```

time: 239 us -> 208 us (0.87)
  blocking collectives: 39.1 us -> 0 us
  local copies, waits for them, and re-layouts: 25.8 us -> 9.17 us
  waiting for transfers between devices: 92.8 us -> 106 us
  Pallas kernels: 17.8 us -> 25.3 us
  starting transfers between devices: 59.7 us -> 63.4 us
    all_to_all x2 -> x0, blocking collectives: 39.1 us -> none  [exchange(): return lax.all_to_all(value, axes, 0, 0, tiled=True)]
    unnamed x50 -> x48, local copies, waits for them, and re-layouts: 23.7 us -> 7.16 us
    ppermute x3 -> x9, waiting for transfers between devices: 16.3 us -> 29.9 us  [shift_y(): return lax.ppermute(value, 'y', [(y, (y + step) % Y) for y in range(Y)])]
    ppermute x2, waiting for transfers between devices: 2.91 us -> 15 us  [shift_far(): return lax.ppermute(value, ('c', 'z'), pairs)]
    pallas_call x10 -> x9, Pallas kernels: 17.8 us -> 25.3 us  [call(): pl.pallas_call(kernel, out_shape=outs, in_specs=in_specs, out_specs=out_s...]
    ppermute x8, waiting for transfers between devices: 18 us -> 11.1 us  [shift_z(): return lax.ppermute(value, 'z', [(z, (z + step) % Z) for z in range(Z)])]
    ppermute x3 -> x9, starting transfers between devices: 3.26 us -> 9.42 us  [shift_y(): return lax.ppermute(value, 'y', [(y, (y + step) % Y) for y in range(Y)])]
    all_to_all x6 -> x5, waiting for transfers between devices: 55.6 us -> 50 us  [exchange(): return lax.all_to_all(value, axes, 0, 0, tiled=True)]
  transfers between devices with their start and end apart: 19 -> 24, of which waited for: 12 -> 10; matrix products, arithmetic and copies ran while one was open for 1% -> 1% of each run, Pallas kernels for 5% -> 5%
where the time goes in v4:
time: 208 us; the launch traced here: 207 us
  waiting for transfers between devices  106 us (51%)
  starting transfers between devices  63.4 us (30%)
  Pallas kernels  25.3 us (12%)
  local copies, waits for them, and re-layouts  9.17 us (4%)
    all_to_all x5, waiting for transfers between devices, exchange(): return lax.all_to_all(value, axes, 0, 0, tiled=True)  50 us
    all_to_all x5, starting transfers between devices, exchange(): return lax.all_to_all(value, axes, 0, 0, tiled=True)  35.1 us
    ppermute x9, waiting for transfers between devices, shift_y(): return lax.ppermute(value, 'y', [(y, (y + step) % Y) for y in range(Y)])  29.9 us
    pallas_call x9, Pallas kernels, call(): pl.pallas_call(kernel, out_shape=outs, in_specs=in_specs, out_specs=out_s...  25.3 us
    ppermute x2, waiting for transfers between devices, shift_far(): return lax.ppermute(value, ('c', 'z'), pairs)  15 us
    ppermute x8, starting transfers between devices, shift_z(): return lax.ppermute(value, 'z', [(z, (z + step) % Z) for z in range(Z)])  14.4 us
    ppermute x8, waiting for transfers between devices, shift_z(): return lax.ppermute(value, 'z', [(z, (z + step) % Z) for z in range(Z)])  11.1 us
    ppermute x9, starting transfers between devices, shift_y(): return lax.ppermute(value, 'y', [(y, (y + step) % Y) for y in range(Y)])  9.42 us
  transfers between devices with their start and end apart: 24, of which 10 were waited for; matrix products, arithmetic and copies ran while one was open for 1% of the time, Pallas kernels for 5%

profile of v4, /device:TPU:20, one launch (start us, length us, event | category | flops | bytes accessed | tf_op | source)
XLA Modules:
  0.0 206.6 jit_solution(14183517067642859594)
XLA Ops:
  1.2 4.2 %shard_map.70 = (f32[4,32,896]{2,1,0:T(8,128)}, f32[4,32,896]{2,1,0:T(8,128)}, f32[4,32,896]{2,1,0:T(8,128)}, f32[4,32,896]{2,1,0:T(8,128)}, f32[4,32,896]{2,1,0...) custom-call(s32[2]{0:T(128)} %pad_add_fusion.place, f32[2,32,14336]{2,1,0:T(8,128)} %factor.1), custom_call_target="tpu_custom_call" | custom-call | bytes 7340032 | tf_op jit(solution)/shard_map/pallas_call | solution.py:26
  5.5 2.0 collective-permute-start.3
  7.8 1.3 shard_map.69
  9.1 1.3 collective-permute-start
  13.1 11.1 %all-to-all-start = ((f32[32,16,128]{2,1,0:T(8,128)}), f32[32,16,128]{2,1,0:T(8,128)}, u32[]{:S(2)}, u32[]{:S(2)}) async-start(f32[32,16,128]{2,1,0:T(8,128)} %shard_map.68), calls=%async_computation | async-start | bytes 524288 | tf_op jit(solution)/shard_map/all_to_all | solution.py:191
  24.2 2.8 %collective-permute-start.4 = (f32[4,32,896]{2,1,0:T(8,128)}, f32[4,32,896]{2,1,0:T(8,128)S(1)}, u32[]{:S(2)}, u32[]{:S(2)}) collective-permute-start(f32[4,32,896]{2,1,0:T(8,128)} %get-tuple-element.29), channel_id=1, source_target_pairs={{0,28},{4,0},{8,4},{12,8},{16,12},{20,16},{24,20},{28,24},{1,29},{... | collective-permute-start | bytes 1376264 | tf_op jit(solution)/shard_map/ppermute | solution.py:172
  27.0 2.3 %collective-permute-start.5 = (f32[4,32,896]{2,1,0:T(8,128)}, f32[4,32,896]{2,1,0:T(8,128)S(1)}, u32[]{:S(2)}, u32[]{:S(2)}) collective-permute-start(f32[4,32,896]{2,1,0:T(8,128)} %get-tuple-element.30), channel_id=1, source_target_pairs={{0,24},{4,28},{8,0},{12,4},{16,8},{20,12},{24,16},{28,20},{32,40},... | collective-permute-start | bytes 1376264 | tf_op jit(solution)/shard_map/ppermute | solution.py:179
  34.0 6.2 %collective-permute-done.4.refs_5_.refs_2_ = f32[4,32,896]{2,1,0:T(8,128)S(1)} collective-permute-done((f32[4,32,896]{2,1,0:T(8,128)}, f32[4,32,896]{2,1,0:T(8,128)S(1)}, u32[]{:S(2)}, u32[]{:S(2)}) %collective-permute-start.4) | collective-permute-done | bytes 458784 | tf_op jit(solution)/shard_map/ppermute | solution.py:172
  40.2 10.7 %collective-permute-done.5.refs_6_.refs_3_ = f32[4,32,896]{2,1,0:T(8,128)S(1)} collective-permute-done((f32[4,32,896]{2,1,0:T(8,128)}, f32[4,32,896]{2,1,0:T(8,128)S(1)}, u32[]{:S(2)}, u32[]{:S(2)}) %collective-permute-start.5) | collective-permute-done | bytes 458784 | tf_op jit(solution)/shard_map/ppermute | solution.py:179
  53.0 2.0 shard_map.71
  55.0 4.9 %all-to-all-start.1 = ((f32[8,16,128]{2,1,0:T(8,128)}), f32[8,16,128]{2,1,0:T(8,128)S(1)}, u32[]{:S(2)}, u32[]{:S(2)}) async-start(f32[8,16,128]{2,1,0:T(8,128)} %get-tuple-element.31), calls=%async_computation.1 | async-start | bytes 131072 | tf_op jit(solution)/shard_map/all_to_all | solution.py:191
  60.0 8.4 %all-to-all-done.1.arrived = f32[8,16,128]{2,1,0:T(8,128)S(1)} async-done(((f32[8,16,128]{2,1,0:T(8,128)}), f32[8,16,128]{2,1,0:T(8,128)S(1)}, u32[]{:S(2)}, u32[]{:S(2)}) %all-to-all-start.1) | async-done | bytes 65568 | tf_op jit(solution)/shard_map/all_to_all | solution.py:191
  70.3 1.7 shard_map.72
  72.0 3.4 %all-to-all-start.2 = ((f32[8,5,16,128]{3,2,1,0:T(8,128)}), f32[8,5,16,128]{3,2,1,0:T(8,128)S(1)}, u32[]{:S(2)}, u32[]{:S(2)}) async-start(f32[8,5,16,128]{3,2,1,0:T(8,128)} %shard_map.72), calls=%async_computation.2 | async-start | bytes 655360 | tf_op jit(solution)/shard_map/all_to_all | solution.py:191
  75.5 2.8 %collective-permute-start.12 = (f32[16,128]{1,0:T(8,128)S(1)}, f32[16,128]{1,0:T(8,128)S(1)}, u32[]{:S(2)}, u32[]{:S(2)}) collective-permute-start(f32[16,128]{1,0:T(8,128)S(1)} %get-tuple-element.35.refs_0_), channel_id=1, source_target_pairs={{0,8},{4,12},{8,16},{12,20},{16,24},{20,28},{24,0},{28,4},{1,9},{5... | collective-permute-start | bytes 24584 | tf_op jit(solution)/shard_map/ppermute | solution.py:172
  78.3 1.4 collective-permute-start.11
  79.7 1.9 collective-permute-start.10
  81.7 2.8 %collective-permute-done.12.refs_4_ = f32[16,128]{1,0:T(8,128)S(1)} collective-permute-done((f32[16,128]{1,0:T(8,128)S(1)}, f32[16,128]{1,0:T(8,128)S(1)}, u32[]{:S(2)}, u32[]{:S(2)}) %collective-permute-start.12) | collective-permute-done | bytes 8224 | tf_op jit(solution)/shard_map/ppermute | solution.py:172
  84.5 2.2 %collective-permute-done.9.refs_1_ = f32[16,128]{1,0:T(8,128)S(1)} collective-permute-done((f32[16,128]{1,0:T(8,128)S(1)}, f32[16,128]{1,0:T(8,128)S(1)}, u32[]{:S(2)}, u32[]{:S(2)}) %collective-permute-start.9) | collective-permute-done | bytes 8224 | tf_op jit(solution)/shard_map/ppermute | solution.py:172
  86.6 1.6 shard_map.73
  88.2 7.4 %all-to-all-start.3 = ((f32[32,8,16,128]{3,2,1,0:T(8,128)}), f32[32,8,16,128]{3,2,1,0:T(8,128)}, u32[]{:S(2)}, u32[]{:S(2)}) async-start(f32[32,8,16,128]{3,2,1,0:T(8,128)} %shard_map.73), calls=%async_computation.3 | async-start | bytes 4194304 | tf_op jit(solution)/shard_map/all_to_all | solution.py:191
  95.6 2.9 %shard_map.74 = (f32[4,32,896]{2,1,0:T(8,128)}, f32[4,32,896]{2,1,0:T(8,128)}, f32[4,32,896]{2,1,0:T(8,128)}, f32[4,32,896]{2,1,0:T(8,128)}) custom-call(f32[4,32,896]{2,1,0:T(8,128)} %get-tuple-element.36.refs_0_, f32[4,32,896]{2,1,0:T(8,128)} %copy-done, f32[4,32,896]{2,1,0:T(8,128)} %copy-done.2, f32[4,32,896]{2,1,0:T(8,128)} %copy-done.4), custom_call_target="tpu_custom_call" | custom-call | bytes 3670016 | tf_op jit(solution)/shard_map/pallas_call | solution.py:26
  98.5 1.2 collective-permute-start.13
  101.8 2.9 %shard_map.75 = (f32[4,32,896]{2,1,0:T(8,128)}, f32[4,32,896]{2,1,0:T(8,128)}, f32[4,32,896]{2,1,0:T(8,128)}, f32[4,32,896]{2,1,0:T(8,128)}) custom-call(s32[2]{0:T(128)} %pad_add_fusion.place, f32[4,32,896]{2,1,0:T(8,128)} %get-tuple-element.41.refs_0_, f32[4,32,896]{2,1,0:T(8,128)} %copy-done.1, f32[4,32,896]{2,1,0:T(8,128)} %copy-done.3, ...), custom_call_target="tpu_custom_call" | custom-call | bytes 3670016 | tf_op jit(solution)/shard_map/pallas_call | solution.py:26
  105.2 2.8 %collective-permute-start.17 = (f32[4,32,896]{2,1,0:T(8,128)}, f32[4,32,896]{2,1,0:T(8,128)S(1)}, u32[]{:S(2)}, u32[]{:S(2)}) collective-permute-start(f32[4,32,896]{2,1,0:T(8,128)} %get-tuple-element.44), channel_id=1, source_target_pairs={{0,28},{4,0},{8,4},{12,8},{16,12},{20,16},{24,20},{28,24},{1,29},{... | collective-permute-start | bytes 1376264 | tf_op jit(solution)/shard_map/ppermute | solution.py:172
  108.0 22.0 %collective-permute-done.13.refs_1_ = f32[4,32,896]{2,1,0:T(8,128)S(1)} collective-permute-done((f32[4,32,896]{2,1,0:T(8,128)}, f32[4,32,896]{2,1,0:T(8,128)S(1)}, u32[]{:S(2)}, u32[]{:S(2)}) %collective-permute-start.13) | collective-permute-done | bytes 458784 | tf_op jit(solution)/shard_map/ppermute | solution.py:168
  130.0 2.1 %collective-permute-start.18 = (f32[4,32,896]{2,1,0:T(8,128)}, f32[4,32,896]{2,1,0:T(8,128)S(1)}, u32[]{:S(2)}, u32[]{:S(2)}) collective-permute-start(f32[4,32,896]{2,1,0:T(8,128)} %get-tuple-element.45), channel_id=1, source_target_pairs={{0,24},{4,28},{8,0},{12,4},{16,8},{20,12},{24,16},{28,20},{32,40},... | collective-permute-start | bytes 1376264 | tf_op jit(solution)/shard_map/ppermute | solution.py:179
  132.1 7.2 %collective-permute-done.14.refs_2_ = f32[4,32,896]{2,1,0:T(8,128)S(1)} collective-permute-done((f32[4,32,896]{2,1,0:T(8,128)}, f32[4,32,896]{2,1,0:T(8,128)S(1)}, u32[]{:S(2)}, u32[]{:S(2)}) %collective-permute-start.14) | collective-permute-done | bytes 458784 | tf_op jit(solution)/shard_map/ppermute | solution.py:168
  140.0 4.3 %collective-permute-done.18.refs_7_ = f32[4,32,896]{2,1,0:T(8,128)S(1)} collective-permute-done((f32[4,32,896]{2,1,0:T(8,128)}, f32[4,32,896]{2,1,0:T(8,128)S(1)}, u32[]{:S(2)}, u32[]{:S(2)}) %collective-permute-start.18) | collective-permute-done | bytes 458784 | tf_op jit(solution)/shard_map/ppermute | solution.py:179
  145.1 7.7 %shard_map.76 = f32[32,16,896]{2,1,0:T(8,128)} custom-call(s32[2]{0:T(128)} %pad_add_fusion.place, f32[32,8,16,128]{3,2,1,0:T(8,128)} %all-to-all-done.3.rows, f32[4,32,896]{2,1,0:T(8,128)} %get-tuple-element.37.refs_0_, f32[4,32,896]{2,1,0:T(8,128)} %copy-done.17, f32[4,32,896]{2,1,0:T(8,128)} %copy-done.18, f32[4,32,896]{2,1,0:T(8,128)} %copy-done.19, ...), custom_call_target="tpu_custom_call" | custom-call | flops 2818572288 | bytes 7602176 | tf_op jit(solution)/shard_map/pallas_call | solution.py:26
  152.9 8.3 %all-to-all-start.4 = ((f32[32,16,896]{2,1,0:T(8,128)}), f32[32,16,896]{2,1,0:T(8,128)S(1)}, u32[]{:S(2)}, u32[]{:S(2)}) async-start(f32[32,16,896]{2,1,0:T(8,128)} %shard_map.76), calls=%async_computation.4 | async-start | bytes 3670016 | tf_op jit(solution)/shard_map/all_to_all | solution.py:191
  162.7 41.5 %all-to-all-done.4 = f32[32,16,896]{2,1,0:T(8,128)S(1)} async-done(((f32[32,16,896]{2,1,0:T(8,128)}), f32[32,16,896]{2,1,0:T(8,128)S(1)}, u32[]{:S(2)}, u32[]{:S(2)}) %all-to-all-start.4) | async-done | bytes 1835040 | tf_op jit(solution)/shard_map/all_to_all | solution.py:191
  (86 shorter events, 20.1 us)
Async XLA Ops:
  0.6 6.8 %copy-start.16 = (f32[64,2,32]{0,2,1:T(8,128)S(1)}, f32[64,2,32]{0,2,1:T(8,128)}, u32[]{:S(2)}) copy-start(f32[64,2,32]{0,2,1:T(8,128)} %param.5) | copy-start | bytes 49156
  5.5 27.4 %collective-permute-start.3 = (f32[4,32,896]{2,1,0:T(8,128)}, f32[4,32,896]{2,1,0:T(8,128)S(1)}, u32[]{:S(2)}, u32[]{:S(2)}) collective-permute-start(f32[4,32,896]{2,1,0:T(8,128)} %get-tuple-element.28), channel_id=1, source_target_pairs={{0,4},{4,8},{8,12},{12,16},{16,20},{20,24},{24,28},{28,0},{1,5},{5... | collective-permute-start | bytes 1376264 | tf_op jit(solution)/shard_map/ppermute | solution.py:172
  9.1 17.9 %collective-permute-start = (f32[72,1024]{1,0:T(8,128)S(1)}, f32[72,1024]{1,0:T(8,128)S(1)}, u32[]{:S(2)}, u32[]{:S(2)}) collective-permute-start(f32[72,1024]{1,0:T(8,128)S(1)} %get-tuple-element.25), channel_id=1, source_target_pairs={{0,1},{1,2},{2,3},{3,0},{4,5},{5,6},{6,7},{7,4},{8,9},{9,10},{10,1... | collective-permute-start | bytes 884744 | tf_op jit(solution)/shard_map/ppermute | solution.py:168
  10.4 19.0 %collective-permute-start.1 = (f32[72,1024]{1,0:T(8,128)}, f32[72,1024]{1,0:T(8,128)S(1)}, u32[]{:S(2)}, u32[]{:S(2)}) collective-permute-start(f32[72,1024]{1,0:T(8,128)} %get-tuple-element.26), channel_id=1, source_target_pairs={{0,2},{1,3},{2,0},{3,1},{4,6},{5,7},{6,4},{7,5},{8,10},{9,11},{10,... | collective-permute-start | bytes 884744 | tf_op jit(solution)/shard_map/ppermute | solution.py:168
  11.0 20.2 %collective-permute-start.2 = (f32[72,1024]{1,0:T(8,128)S(1)}, f32[72,1024]{1,0:T(8,128)S(1)}, u32[]{:S(2)}, u32[]{:S(2)}) collective-permute-start(f32[72,1024]{1,0:T(8,128)S(1)} %get-tuple-element.27), channel_id=1, source_target_pairs={{0,3},{1,0},{2,1},{3,2},{4,7},{5,4},{6,5},{7,6},{8,11},{9,8},{10,9... | collective-permute-start | bytes 884744 | tf_op jit(solution)/shard_map/ppermute | solution.py:168
  13.1 37.8 %all-to-all-start = ((f32[32,16,128]{2,1,0:T(8,128)}), f32[32,16,128]{2,1,0:T(8,128)}, u32[]{:S(2)}, u32[]{:S(2)}) async-start(f32[32,16,128]{2,1,0:T(8,128)} %shard_map.68), calls=%async_computation | async-start | bytes 524288 | tf_op jit(solution)/shard_map/all_to_all | solution.py:191
  24.2 16.0 %collective-permute-start.4 = (f32[4,32,896]{2,1,0:T(8,128)}, f32[4,32,896]{2,1,0:T(8,128)S(1)}, u32[]{:S(2)}, u32[]{:S(2)}) collective-permute-start(f32[4,32,896]{2,1,0:T(8,128)} %get-tuple-element.29), channel_id=1, source_target_pairs={{0,28},{4,0},{8,4},{12,8},{16,12},{20,16},{24,20},{28,24},{1,29},{... | collective-permute-start | bytes 1376264 | tf_op jit(solution)/shard_map/ppermute | solution.py:172
  27.0 23.9 %collective-permute-start.5 = (f32[4,32,896]{2,1,0:T(8,128)}, f32[4,32,896]{2,1,0:T(8,128)S(1)}, u32[]{:S(2)}, u32[]{:S(2)}) collective-permute-start(f32[4,32,896]{2,1,0:T(8,128)} %get-tuple-element.30), channel_id=1, source_target_pairs={{0,24},{4,28},{8,0},{12,4},{16,8},{20,12},{24,16},{28,20},{32,40},... | collective-permute-start | bytes 1376264 | tf_op jit(solution)/shard_map/ppermute | solution.py:179
  30.1 29.8 %collective-permute-start.6 = (f32[4,32,896]{2,1,0:T(8,128)}, f32[4,32,896]{2,1,0:T(8,128)S(1)}, u32[]{:S(2)}, u32[]{:S(2)}) collective-permute-start(f32[4,32,896]{2,1,0:T(8,128)} %get-tuple-element.32), channel_id=1, source_target_pairs={{0,1},{1,2},{2,3},{3,0},{4,5},{5,6},{6,7},{7,4},{8,9},{9,10},{10,1... | collective-permute-start | bytes 1376264 | tf_op jit(solution)/shard_map/ppermute | solution.py:168
  32.0 28.0 %collective-permute-start.7 = (f32[4,32,896]{2,1,0:T(8,128)}, f32[4,32,896]{2,1,0:T(8,128)S(1)}, u32[]{:S(2)}, u32[]{:S(2)}) collective-permute-start(f32[4,32,896]{2,1,0:T(8,128)} %get-tuple-element.33), channel_id=1, source_target_pairs={{0,2},{1,3},{2,0},{3,1},{4,6},{5,7},{6,4},{7,5},{8,10},{9,11},{10,... | collective-permute-start | bytes 1376264 | tf_op jit(solution)/shard_map/ppermute | solution.py:168
  32.8 39.2 %copy-start = (f32[4,32,896]{2,1,0:T(8,128)}, f32[4,32,896]{2,1,0:T(8,128)S(1)}, u32[]{:S(2)}) copy-start(f32[4,32,896]{2,1,0:T(8,128)S(1)} %collective-permute-done.3.refs_4_.refs_1_) | copy-start | bytes 1376260
  32.8 27.1 %collective-permute-start.8 = (f32[4,32,896]{2,1,0:T(8,128)}, f32[4,32,896]{2,1,0:T(8,128)S(1)}, u32[]{:S(2)}, u32[]{:S(2)}) collective-permute-start(f32[4,32,896]{2,1,0:T(8,128)} %get-tuple-element.34), channel_id=1, source_target_pairs={{0,3},{1,0},{2,1},{3,2},{4,7},{5,4},{6,5},{7,6},{8,11},{9,8},{10,9... | collective-permute-start | bytes 1376264 | tf_op jit(solution)/shard_map/ppermute | solution.py:168
  40.2 31.8 %copy-start.2 = (f32[4,32,896]{2,1,0:T(8,128)}, f32[4,32,896]{2,1,0:T(8,128)S(1)}, u32[]{:S(2)}) copy-start(f32[4,32,896]{2,1,0:T(8,128)S(1)} %collective-permute-done.4.refs_5_.refs_2_) | copy-start | bytes 1376260
  50.9 21.1 %copy-start.4 = (f32[4,32,896]{2,1,0:T(8,128)}, f32[4,32,896]{2,1,0:T(8,128)S(1)}, u32[]{:S(2)}) copy-start(f32[4,32,896]{2,1,0:T(8,128)S(1)} %collective-permute-done.5.refs_6_.refs_3_) | copy-start | bytes 1376260
  55.0 13.4 %all-to-all-start.1 = ((f32[8,16,128]{2,1,0:T(8,128)}), f32[8,16,128]{2,1,0:T(8,128)S(1)}, u32[]{:S(2)}, u32[]{:S(2)}) async-start(f32[8,16,128]{2,1,0:T(8,128)} %get-tuple-element.31), calls=%async_computation.1 | async-start | bytes 131072 | tf_op jit(solution)/shard_map/all_to_all | solution.py:191
  59.9 28.3 %copy-start.1 = (f32[4,32,896]{2,1,0:T(8,128)}, f32[4,32,896]{2,1,0:T(8,128)S(1)}, u32[]{:S(2)}) copy-start(f32[4,32,896]{2,1,0:T(8,128)S(1)} %collective-permute-done.6.refs_4_.refs_1_) | copy-start | bytes 1376260
  59.9 28.3 %copy-start.3 = (f32[4,32,896]{2,1,0:T(8,128)}, f32[4,32,896]{2,1,0:T(8,128)S(1)}, u32[]{:S(2)}) copy-start(f32[4,32,896]{2,1,0:T(8,128)S(1)} %collective-permute-done.7.refs_5_.refs_2_) | copy-start | bytes 1376260
  60.0 28.2 %copy-start.5 = (f32[4,32,896]{2,1,0:T(8,128)}, f32[4,32,896]{2,1,0:T(8,128)S(1)}, u32[]{:S(2)}) copy-start(f32[4,32,896]{2,1,0:T(8,128)S(1)} %collective-permute-done.8.refs_6_.refs_3_) | copy-start | bytes 1376260
  72.0 14.6 %all-to-all-start.2 = ((f32[8,5,16,128]{3,2,1,0:T(8,128)}), f32[8,5,16,128]{3,2,1,0:T(8,128)S(1)}, u32[]{:S(2)}, u32[]{:S(2)}) async-start(f32[8,5,16,128]{3,2,1,0:T(8,128)} %shard_map.72), calls=%async_computation.2 | async-start | bytes 655360 | tf_op jit(solution)/shard_map/all_to_all | solution.py:191
  75.5 9.0 %collective-permute-start.12 = (f32[16,128]{1,0:T(8,128)S(1)}, f32[16,128]{1,0:T(8,128)S(1)}, u32[]{:S(2)}, u32[]{:S(2)}) collective-permute-start(f32[16,128]{1,0:T(8,128)S(1)} %get-tuple-element.35.refs_0_), channel_id=1, source_target_pairs={{0,8},{4,12},{8,16},{12,20},{16,24},{20,28},{24,0},{28,4},{1,9},{5... | collective-permute-start | bytes 24584 | tf_op jit(solution)/shard_map/ppermute | solution.py:172
  78.3 6.2 %collective-permute-start.11 = (f32[16,128]{1,0:T(8,128)S(1)}, f32[16,128]{1,0:T(8,128)S(1)}, u32[]{:S(2)}, u32[]{:S(2)}) collective-permute-start(f32[16,128]{1,0:T(8,128)S(1)} %get-tuple-element.35.refs_0_), channel_id=1, source_target_pairs={{0,24},{4,28},{8,0},{12,4},{16,8},{20,12},{24,16},{28,20},{1,25},{... | collective-permute-start | bytes 24584 | tf_op jit(solution)/shard_map/ppermute | solution.py:172
  79.7 4.8 %collective-permute-start.10 = (f32[16,128]{1,0:T(8,128)S(1)}, f32[16,128]{1,0:T(8,128)S(1)}, u32[]{:S(2)}, u32[]{:S(2)}) collective-permute-start(f32[16,128]{1,0:T(8,128)S(1)} %get-tuple-element.35.refs_0_), channel_id=1, source_target_pairs={{0,28},{4,0},{8,4},{12,8},{16,12},{20,16},{24,20},{28,24},{1,29},{... | collective-permute-start | bytes 24584 | tf_op jit(solution)/shard_map/ppermute | solution.py:172
  81.6 5.1 %collective-permute-start.9 = (f32[16,128]{1,0:T(8,128)S(1)}, f32[16,128]{1,0:T(8,128)S(1)}, u32[]{:S(2)}, u32[]{:S(2)}) collective-permute-start(f32[16,128]{1,0:T(8,128)S(1)} %get-tuple-element.35.refs_0_), channel_id=1, source_target_pairs={{0,4},{4,8},{8,12},{12,16},{16,20},{20,24},{24,28},{28,0},{1,5},{5... | collective-permute-start | bytes 24584 | tf_op jit(solution)/shard_map/ppermute | solution.py:172
  88.2 56.2 %all-to-all-start.3 = ((f32[32,8,16,128]{3,2,1,0:T(8,128)}), f32[32,8,16,128]{3,2,1,0:T(8,128)}, u32[]{:S(2)}, u32[]{:S(2)}) async-start(f32[32,8,16,128]{3,2,1,0:T(8,128)} %shard_map.73), calls=%async_computation.3 | async-start | bytes 4194304 | tf_op jit(solution)/shard_map/all_to_all | solution.py:191
  98.5 31.5 %collective-permute-start.13 = (f32[4,32,896]{2,1,0:T(8,128)}, f32[4,32,896]{2,1,0:T(8,128)S(1)}, u32[]{:S(2)}, u32[]{:S(2)}) collective-permute-start(f32[4,32,896]{2,1,0:T(8,128)} %get-tuple-element.38), channel_id=1, source_target_pairs={{0,1},{1,2},{2,3},{3,0},{4,5},{5,6},{6,7},{7,4},{8,9},{9,10},{10,1... | collective-permute-start | bytes 1376264 | tf_op jit(solution)/shard_map/ppermute | solution.py:168
  99.8 39.6 %collective-permute-start.14 = (f32[4,32,896]{2,1,0:T(8,128)}, f32[4,32,896]{2,1,0:T(8,128)S(1)}, u32[]{:S(2)}, u32[]{:S(2)}) collective-permute-start(f32[4,32,896]{2,1,0:T(8,128)} %get-tuple-element.39), channel_id=1, source_target_pairs={{0,2},{1,3},{2,0},{3,1},{4,6},{5,7},{6,4},{7,5},{8,10},{9,11},{10,... | collective-permute-start | bytes 1376264 | tf_op jit(solution)/shard_map/ppermute | solution.py:168
  100.7 39.4 %collective-permute-start.15 = (f32[4,32,896]{2,1,0:T(8,128)}, f32[4,32,896]{2,1,0:T(8,128)S(1)}, u32[]{:S(2)}, u32[]{:S(2)}) collective-permute-start(f32[4,32,896]{2,1,0:T(8,128)} %get-tuple-element.40), channel_id=1, source_target_pairs={{0,3},{1,0},{2,1},{3,2},{4,7},{5,4},{6,5},{7,6},{8,11},{9,8},{10,9... | collective-permute-start | bytes 1376264 | tf_op jit(solution)/shard_map/ppermute | solution.py:168
  104.7 35.3 %collective-permute-start.16 = (f32[4,32,896]{2,1,0:T(8,128)}, f32[4,32,896]{2,1,0:T(8,128)S(1)}, u32[]{:S(2)}, u32[]{:S(2)}) collective-permute-start(f32[4,32,896]{2,1,0:T(8,128)} %get-tuple-element.43), channel_id=1, source_target_pairs={{0,4},{4,8},{8,12},{12,16},{16,20},{20,24},{24,28},{28,0},{1,5},{5... | collective-permute-start | bytes 1376264 | tf_op jit(solution)/shard_map/ppermute | solution.py:172
  105.2 34.8 %collective-permute-start.17 = (f32[4,32,896]{2,1,0:T(8,128)}, f32[4,32,896]{2,1,0:T(8,128)S(1)}, u32[]{:S(2)}, u32[]{:S(2)}) collective-permute-start(f32[4,32,896]{2,1,0:T(8,128)} %get-tuple-element.44), channel_id=1, source_target_pairs={{0,28},{4,0},{8,4},{12,8},{16,12},{20,16},{24,20},{28,24},{1,29},{... | collective-permute-start | bytes 1376264 | tf_op jit(solution)/shard_map/ppermute | solution.py:172
  130.0 14.3 %copy-start.17 = (f32[4,32,896]{2,1,0:T(8,128)}, f32[4,32,896]{2,1,0:T(8,128)S(1)}, u32[]{:S(2)}) copy-start(f32[4,32,896]{2,1,0:T(8,128)S(1)} %collective-permute-done.13.refs_1_) | copy-start | bytes 1376260
  130.0 14.3 %collective-permute-start.18 = (f32[4,32,896]{2,1,0:T(8,128)}, f32[4,32,896]{2,1,0:T(8,128)S(1)}, u32[]{:S(2)}, u32[]{:S(2)}) collective-permute-start(f32[4,32,896]{2,1,0:T(8,128)} %get-tuple-element.45), channel_id=1, source_target_pairs={{0,24},{4,28},{8,0},{12,4},{16,8},{20,12},{24,16},{28,20},{32,40},... | collective-permute-start | bytes 1376264 | tf_op jit(solution)/shard_map/ppermute | solution.py:179
  152.9 51.4 %all-to-all-start.4 = ((f32[32,16,896]{2,1,0:T(8,128)}), f32[32,16,896]{2,1,0:T(8,128)S(1)}, u32[]{:S(2)}, u32[]{:S(2)}) async-start(f32[32,16,896]{2,1,0:T(8,128)} %shard_map.76), calls=%async_computation.4 | async-start | bytes 3670016 | tf_op jit(solution)/shard_map/all_to_all | solution.py:191
  (15 other events, 45.0 us)

commit v5 on v4

--- a/solution.py
+++ b/solution.py
@@ -102,7 +102,7 @@
 
 def close_kernel(arrived, *refs):
     latter = jnp.sum(arrived[...], axis=0)
-    first, copies = refs[:-1], refs[-1]
+    first, copies = refs[:len(NEAR)], refs[-1]
     for place in range(X * C * Y):
         for k in range(QUAD):
             near = k if k < 3 else 3 + place // Y % C
@@ -218,8 +218,8 @@
     by_class, by_y = to_windows(*cut[:4]), to_ys(*cut[4:])
 
     first, terms = call(
-        couple_kernel, (f32(16, 128), f32(Z, 16, 128)), (place, arrived, *shared, *by_class[1:]),
-        (VMEM, VMEM), (SMEM,) + (VMEM,) * 5 + (ANY,) * 3, matrix,
+        couple_kernel, (f32(16, 128), f32(Z, 16, 128)), (place, arrived, *shared, cut[0], cut[4]),
+        (VMEM, VMEM), (SMEM,) + (VMEM,) * 5 + (ANY,) * 2, matrix, limit=60,
     )
     arrived = exchange(terms, "z")
     by_r = call(turn_kernel, (block,) * 4, by_class, (ANY,) * 4, (VMEM,) * 4, sems(16), moved=3670016, limit=60)
@@ -227,13 +227,13 @@
     near = (first, *(shift_z(first, -step) for step in NEAR[1:]))
 
     terms = call(
-        latter_kernel, f32(Z, len(NEAR), 16, 128), (place, arrived, *shared, *by_y[1:]),
-        VMEM, (SMEM,) + (VMEM,) * 5 + (ANY,) * 3, matrix,
+        latter_kernel, f32(Z, len(NEAR), 16, 128), (place, arrived, *shared, *by_class[1:], *by_y[1:]),
+        VMEM, (SMEM,) + (VMEM,) * 5 + (ANY,) * 6, matrix, limit=60,
     )
     arrived = exchange(terms, "z")
     by_k = call(merge_kernel, (block,) * 4, (place, *by_y), (ANY,) * 4, (SMEM,) + (VMEM,) * 4, sems(16), moved=3670016, limit=60)
     latter_factor = to_windows(*by_k)
-    copies = call(close_kernel, f32(X * C * Y, 2 * QUAD, 16, 128), (arrived, *near), VMEM, (VMEM,) * 6)
+    copies = call(close_kernel, f32(X * C * Y, 2 * QUAD, 16, 128), (arrived, *near, *first_factor[1:], *by_k), VMEM, (VMEM,) * 6 + (ANY,) * 7)
     rows = exchange(copies, SPREAD)
 
     update = call(

time: 208 us -> 195 us (0.938)
  waiting for transfers between devices: 106 us -> 84.1 us
  starting transfers between devices: 63.4 us -> 69.5 us
    ppermute x9, waiting for transfers between devices: 29.9 us -> 5.59 us  [shift_y(): return lax.ppermute(value, 'y', [(y, (y + step) % Y) for y in range(Y)])]
    ppermute x2, waiting for transfers between devices: 15 us -> 18.8 us  [shift_far(): return lax.ppermute(value, ('c', 'z'), pairs)]
    all_to_all x5, starting transfers between devices: 35.1 us -> 37.9 us  [exchange(): return lax.all_to_all(value, axes, 0, 0, tiled=True)]
    all_to_all x5, waiting for transfers between devices: 50 us -> 47.4 us  [exchange(): return lax.all_to_all(value, axes, 0, 0, tiled=True)]
    ppermute x9, starting transfers between devices: 9.42 us -> 11.5 us  [shift_y(): return lax.ppermute(value, 'y', [(y, (y + step) % Y) for y in range(Y)])]
    unnamed x48 -> x62, local copies, waits for them, and re-layouts: 7.16 us -> 9.07 us
  transfers between devices with their start and end apart: 24 -> 24, of which waited for: 10 -> 11; matrix products, arithmetic and copies ran while one was open for 1% -> 1% of each run, Pallas kernels for 5% -> 5%
where the time goes in v5:
time: 195 us; the launch traced here: 193 us
  waiting for transfers between devices  84.1 us (43%)
  starting transfers between devices  69.5 us (36%)
  Pallas kernels  25.5 us (13%)
  local copies, waits for them, and re-layouts  11.1 us (6%)
    all_to_all x5, waiting for transfers between devices, exchange(): return lax.all_to_all(value, axes, 0, 0, tiled=True)  47.4 us
    all_to_all x5, starting transfers between devices, exchange(): return lax.all_to_all(value, axes, 0, 0, tiled=True)  37.9 us
    pallas_call x9, Pallas kernels, call(): pl.pallas_call(kernel, out_shape=outs, in_specs=in_specs, out_specs=out_s...  25.5 us
    ppermute x2, waiting for transfers between devices, shift_far(): return lax.ppermute(value, ('c', 'z'), pairs)  18.8 us
    ppermute x8, starting transfers between devices, shift_z(): return lax.ppermute(value, 'z', [(z, (z + step) % Z) for z in range(Z)])  15.1 us
    ppermute x8, waiting for transfers between devices, shift_z(): return lax.ppermute(value, 'z', [(z, (z + step) % Z) for z in range(Z)])  12.3 us
    ppermute x9, starting transfers between devices, shift_y(): return lax.ppermute(value, 'y', [(y, (y + step) % Y) for y in range(Y)])  11.5 us
    unnamed x62, local copies, waits for them, and re-layouts  9.07 us
  transfers between devices with their start and end apart: 24, of which 11 were waited for; matrix products, arithmetic and copies ran while one was open for 1% of the time, Pallas kernels for 5%

profile of v5, /device:TPU:20, one launch (start us, length us, event | category | flops | bytes accessed | tf_op | source)
XLA Modules:
  0.0 192.9 jit_solution(11451468605687200945)
XLA Ops:
  1.3 4.2 %shard_map.70 = (f32[4,32,896]{2,1,0:T(8,128)}, f32[4,32,896]{2,1,0:T(8,128)}, f32[4,32,896]{2,1,0:T(8,128)}, f32[4,32,896]{2,1,0:T(8,128)}, f32[4,32,896]{2,1,0...) custom-call(s32[2]{0:T(128)} %pad_add_fusion.place, f32[2,32,14336]{2,1,0:T(8,128)} %factor.1), custom_call_target="tpu_custom_call" | custom-call | bytes 7340032 | tf_op jit(solution)/shard_map/pallas_call | solution.py:26
  5.5 2.0 %collective-permute-start.3 = (f32[4,32,896]{2,1,0:T(8,128)}, f32[4,32,896]{2,1,0:T(8,128)S(1)}, u32[]{:S(2)}, u32[]{:S(2)}) collective-permute-start(f32[4,32,896]{2,1,0:T(8,128)} %get-tuple-element.31), channel_id=1, source_target_pairs={{0,4},{4,8},{8,12},{12,16},{16,20},{20,24},{24,28},{28,0},{1,5},{5... | collective-permute-start | bytes 1376264 | tf_op jit(solution)/shard_map/ppermute | solution.py:172
  9.1 1.3 collective-permute-start
  13.1 11.1 %all-to-all-start = ((f32[32,16,128]{2,1,0:T(8,128)}), f32[32,16,128]{2,1,0:T(8,128)}, u32[]{:S(2)}, u32[]{:S(2)}) async-start(f32[32,16,128]{2,1,0:T(8,128)} %shard_map.68), calls=%async_computation | async-start | bytes 524288 | tf_op jit(solution)/shard_map/all_to_all | solution.py:191
  24.2 2.8 %collective-permute-start.4 = (f32[4,32,896]{2,1,0:T(8,128)}, f32[4,32,896]{2,1,0:T(8,128)S(1)}, u32[]{:S(2)}, u32[]{:S(2)}) collective-permute-start(f32[4,32,896]{2,1,0:T(8,128)} %get-tuple-element.32), channel_id=1, source_target_pairs={{0,28},{4,0},{8,4},{12,8},{16,12},{20,16},{24,20},{28,24},{1,29},{... | collective-permute-start | bytes 1376264 | tf_op jit(solution)/shard_map/ppermute | solution.py:172
  27.1 2.3 %collective-permute-start.5 = (f32[4,32,896]{2,1,0:T(8,128)}, f32[4,32,896]{2,1,0:T(8,128)S(1)}, u32[]{:S(2)}, u32[]{:S(2)}) collective-permute-start(f32[4,32,896]{2,1,0:T(8,128)} %get-tuple-element.33), channel_id=1, source_target_pairs={{0,24},{4,28},{8,0},{12,4},{16,8},{20,12},{24,16},{28,20},{32,40},... | collective-permute-start | bytes 1376264 | tf_op jit(solution)/shard_map/ppermute | solution.py:179
  33.3 3.9 %all-to-all-done.arrived = f32[32,16,128]{2,1,0:T(8,128)} async-done(((f32[32,16,128]{2,1,0:T(8,128)}), f32[32,16,128]{2,1,0:T(8,128)}, u32[]{:S(2)}, u32[]{:S(2)}) %all-to-all-start) | async-done | bytes 262176 | tf_op jit(solution)/shard_map/all_to_all | solution.py:191
  37.2 2.4 %shard_map.71 = (f32[16,128]{1,0:T(8,128)}, f32[8,16,128]{2,1,0:T(8,128)}) custom-call(s32[2]{0:T(128)} %pad_add_fusion.place, f32[32,16,128]{2,1,0:T(8,128)} %all-to-all-done.arrived, f32[72,1024]{1,0:T(8,128)} %copy-done, f32[72,1024]{1,0:T(8,128)} %copy-done.21, f32[72,1024]{1,0:T(8,128)} %copy-done.22, f32[72,1024]{1,0:T(8,128)} %copy-done.23, ...), custom_call_target="tpu_custom_call" | custom-call | tf_op jit(solution)/shard_map/pallas_call | solution.py:26
  39.5 3.3 %all-to-all-start.1 = ((f32[8,16,128]{2,1,0:T(8,128)}), f32[8,16,128]{2,1,0:T(8,128)S(1)}, u32[]{:S(2)}, u32[]{:S(2)}) async-start(f32[8,16,128]{2,1,0:T(8,128)} %get-tuple-element.30), calls=%async_computation.1 | async-start | bytes 131072 | tf_op jit(solution)/shard_map/all_to_all | solution.py:191
  42.9 9.0 %collective-permute-done.5.refs_6_.refs_3_ = f32[4,32,896]{2,1,0:T(8,128)S(1)} collective-permute-done((f32[4,32,896]{2,1,0:T(8,128)}, f32[4,32,896]{2,1,0:T(8,128)S(1)}, u32[]{:S(2)}, u32[]{:S(2)}) %collective-permute-start.5) | collective-permute-done | bytes 458784 | tf_op jit(solution)/shard_map/ppermute | solution.py:179
  53.7 2.4 %shard_map.72 = f32[8,5,16,128]{3,2,1,0:T(8,128)} custom-call(s32[2]{0:T(128)} %pad_add_fusion.place, f32[8,16,128]{2,1,0:T(8,128)} %copy-done.25, f32[72,1024]{1,0:T(8,128)} %copy-done, f32[72,1024]{1,0:T(8,128)} %copy-done.21, f32[72,1024]{1,0:T(8,128)} %copy-done.22, f32[72,1024]{1,0:T(8,128)} %copy-done.23, f32[4,32,896]{2,1,0:T(8,128)} %copy-done.15, ...), custom_call_target="tpu_custom_call" | custom-call | tf_op jit(solution)/shard_map/pallas_call | solution.py:26
  56.1 5.5 %all-to-all-start.2 = ((f32[8,5,16,128]{3,2,1,0:T(8,128)}), f32[8,5,16,128]{3,2,1,0:T(8,128)S(1)}, u32[]{:S(2)}, u32[]{:S(2)}) async-start(f32[8,5,16,128]{3,2,1,0:T(8,128)} %shard_map.72), calls=%async_computation.2 | async-start | bytes 655360 | tf_op jit(solution)/shard_map/all_to_all | solution.py:191
  61.6 2.8 %shard_map.73 = (f32[4,32,896]{2,1,0:T(8,128)}, f32[4,32,896]{2,1,0:T(8,128)}, f32[4,32,896]{2,1,0:T(8,128)}, f32[4,32,896]{2,1,0:T(8,128)}) custom-call(f32[4,32,896]{2,1,0:T(8,128)} %get-tuple-element.28.refs_4_.refs_0_, f32[4,32,896]{2,1,0:T(8,128)} %copy-done.15, f32[4,32,896]{2,1,0:T(8,128)} %copy-done.16, f32[4,32,896]{2,1,0:T(8,128)} %copy-done.17), custom_call_target="tpu_custom_call" | custom-call | bytes 3670016 | tf_op jit(solution)/shard_map/pallas_call | solution.py:26
  64.4 3.1 %collective-permute-start.13 = (f32[4,32,896]{2,1,0:T(8,128)}, f32[4,32,896]{2,1,0:T(8,128)S(1)}, u32[]{:S(2)}, u32[]{:S(2)}) collective-permute-start(f32[4,32,896]{2,1,0:T(8,128)} %get-tuple-element.38), channel_id=1, source_target_pairs={{0,1},{1,2},{2,3},{3,0},{4,5},{5,6},{6,7},{7,4},{8,9},{9,10},{10,1... | collective-permute-start | bytes 1376264 | tf_op jit(solution)/shard_map/ppermute | solution.py:168
  67.5 2.3 %collective-permute-start.15 = (f32[4,32,896]{2,1,0:T(8,128)}, f32[4,32,896]{2,1,0:T(8,128)S(1)}, u32[]{:S(2)}, u32[]{:S(2)}) collective-permute-start(f32[4,32,896]{2,1,0:T(8,128)} %get-tuple-element.40), channel_id=1, source_target_pairs={{0,3},{1,0},{2,1},{3,2},{4,7},{5,4},{6,5},{7,6},{8,11},{9,8},{10,9... | collective-permute-start | bytes 1376264 | tf_op jit(solution)/shard_map/ppermute | solution.py:168
  69.8 2.9 %collective-permute-start.12 = (f32[16,128]{1,0:T(8,128)S(1)}, f32[16,128]{1,0:T(8,128)S(1)}, u32[]{:S(2)}, u32[]{:S(2)}) collective-permute-start(f32[16,128]{1,0:T(8,128)S(1)} %copy-done.14), channel_id=1, source_target_pairs={{0,8},{4,12},{8,16},{12,20},{16,24},{20,28},{24,0},{28,4},{1,9},{5... | collective-permute-start | bytes 24584 | tf_op jit(solution)/shard_map/ppermute | solution.py:172
  72.7 1.2 collective-permute-start.11
  74.0 1.6 collective-permute-done.12.refs_4_
  75.6 2.0 %collective-permute-start.10 = (f32[16,128]{1,0:T(8,128)S(1)}, f32[16,128]{1,0:T(8,128)S(1)}, u32[]{:S(2)}, u32[]{:S(2)}) collective-permute-start(f32[16,128]{1,0:T(8,128)S(1)} %copy-done.14), channel_id=1, source_target_pairs={{0,28},{4,0},{8,4},{12,8},{16,12},{20,16},{24,20},{28,24},{1,29},{... | collective-permute-start | bytes 24584 | tf_op jit(solution)/shard_map/ppermute | solution.py:172
  78.8 2.8 %shard_map.74 = (f32[4,32,896]{2,1,0:T(8,128)}, f32[4,32,896]{2,1,0:T(8,128)}, f32[4,32,896]{2,1,0:T(8,128)}, f32[4,32,896]{2,1,0:T(8,128)}) custom-call(s32[2]{0:T(128)} %pad_add_fusion.place, f32[4,32,896]{2,1,0:T(8,128)} %get-tuple-element.29.refs_5_.refs_0_, f32[4,32,896]{2,1,0:T(8,128)} %copy-done.18, f32[4,32,896]{2,1,0:T(8,128)} %copy-done.19, ...), custom_call_target="tpu_custom_call" | custom-call | bytes 3670016 | tf_op jit(solution)/shard_map/pallas_call | solution.py:26
  81.6 1.2 collective-permute-done.9.refs_1_
  82.8 4.8 %collective-permute-done.14.refs_6_.refs_2_ = f32[4,32,896]{2,1,0:T(8,128)S(1)} collective-permute-done((f32[4,32,896]{2,1,0:T(8,128)}, f32[4,32,896]{2,1,0:T(8,128)S(1)}, u32[]{:S(2)}, u32[]{:S(2)}) %collective-permute-start.14) | collective-permute-done | bytes 458784 | tf_op jit(solution)/shard_map/ppermute | solution.py:168
  92.6 1.6 shard_map.75
  94.2 8.9 %all-to-all-start.3 = ((f32[32,8,16,128]{3,2,1,0:T(8,128)}), f32[32,8,16,128]{3,2,1,0:T(8,128)}, u32[]{:S(2)}, u32[]{:S(2)}) async-start(f32[32,8,16,128]{3,2,1,0:T(8,128)} %shard_map.75), calls=%async_computation.3 | async-start | bytes 4194304 | tf_op jit(solution)/shard_map/all_to_all | solution.py:191
  103.1 1.8 collective-permute-start.16
  104.9 1.5 collective-permute-start.17
  106.4 2.6 %collective-permute-start.18 = (f32[4,32,896]{2,1,0:T(8,128)S(1)}, f32[4,32,896]{2,1,0:T(8,128)S(1)}, u32[]{:S(2)}, u32[]{:S(2)}) collective-permute-start(f32[4,32,896]{2,1,0:T(8,128)S(1)} %copy-done.7), channel_id=1, source_target_pairs={{0,24},{4,28},{8,0},{12,4},{16,8},{20,12},{24,16},{28,20},{32,40},... | collective-permute-start | bytes 1376264 | tf_op jit(solution)/shard_map/ppermute | solution.py:179
  109.1 9.1 %collective-permute-done.16.refs_5_ = f32[4,32,896]{2,1,0:T(8,128)S(1)} collective-permute-done((f32[4,32,896]{2,1,0:T(8,128)S(1)}, f32[4,32,896]{2,1,0:T(8,128)S(1)}, u32[]{:S(2)}, u32[]{:S(2)}) %collective-permute-start.16) | collective-permute-done | bytes 458784 | tf_op jit(solution)/shard_map/ppermute | solution.py:172
  118.2 9.8 %collective-permute-done.18.refs_7_ = f32[4,32,896]{2,1,0:T(8,128)S(1)} collective-permute-done((f32[4,32,896]{2,1,0:T(8,128)S(1)}, f32[4,32,896]{2,1,0:T(8,128)S(1)}, u32[]{:S(2)}, u32[]{:S(2)}) %collective-permute-start.18) | collective-permute-done | bytes 458784 | tf_op jit(solution)/shard_map/ppermute | solution.py:179
  128.8 7.7 %shard_map.76 = f32[32,16,896]{2,1,0:T(8,128)} custom-call(s32[2]{0:T(128)} %pad_add_fusion.place, f32[32,8,16,128]{3,2,1,0:T(8,128)} %all-to-all-done.3.rows, f32[4,32,896]{2,1,0:T(8,128)} %get-tuple-element.45.refs_0_, f32[4,32,896]{2,1,0:T(8,128)} %copy-done.2, f32[4,32,896]{2,1,0:T(8,128)} %copy-done.3, f32[4,32,896]{2,1,0:T(8,128)} %copy-done.4, ...), custom_call_target="tpu_custom_call" | custom-call | flops 2818572288 | bytes 7602176 | tf_op jit(solution)/shard_map/pallas_call | solution.py:26
  136.5 9.1 %all-to-all-start.4 = ((f32[32,16,896]{2,1,0:T(8,128)}), f32[32,16,896]{2,1,0:T(8,128)S(1)}, u32[]{:S(2)}, u32[]{:S(2)}) async-start(f32[32,16,896]{2,1,0:T(8,128)} %shard_map.76), calls=%async_computation.4 | async-start | bytes 3670016 | tf_op jit(solution)/shard_map/all_to_all | solution.py:191
  147.2 43.4 %all-to-all-done.4 = f32[32,16,896]{2,1,0:T(8,128)S(1)} async-done(((f32[32,16,896]{2,1,0:T(8,128)}), f32[32,16,896]{2,1,0:T(8,128)S(1)}, u32[]{:S(2)}, u32[]{:S(2)}) %all-to-all-start.4) | async-done | bytes 1835040 | tf_op jit(solution)/shard_map/all_to_all | solution.py:191
  (100 shorter events, 21.5 us)
Async XLA Ops:
  5.5 26.7 %collective-permute-start.3 = (f32[4,32,896]{2,1,0:T(8,128)}, f32[4,32,896]{2,1,0:T(8,128)S(1)}, u32[]{:S(2)}, u32[]{:S(2)}) collective-permute-start(f32[4,32,896]{2,1,0:T(8,128)} %get-tuple-element.31), channel_id=1, source_target_pairs={{0,4},{4,8},{8,12},{12,16},{16,20},{20,24},{24,28},{28,0},{1,5},{5... | collective-permute-start | bytes 1376264 | tf_op jit(solution)/shard_map/ppermute | solution.py:172
  9.1 18.0 %collective-permute-start = (f32[72,1024]{1,0:T(8,128)S(1)}, f32[72,1024]{1,0:T(8,128)S(1)}, u32[]{:S(2)}, u32[]{:S(2)}) collective-permute-start(f32[72,1024]{1,0:T(8,128)S(1)} %get-tuple-element.25), channel_id=1, source_target_pairs={{0,1},{1,2},{2,3},{3,0},{4,5},{5,6},{6,7},{7,4},{8,9},{9,10},{10,1... | collective-permute-start | bytes 884744 | tf_op jit(solution)/shard_map/ppermute | solution.py:168
  10.4 19.0 %collective-permute-start.1 = (f32[72,1024]{1,0:T(8,128)S(1)}, f32[72,1024]{1,0:T(8,128)S(1)}, u32[]{:S(2)}, u32[]{:S(2)}) collective-permute-start(f32[72,1024]{1,0:T(8,128)S(1)} %get-tuple-element.26), channel_id=1, source_target_pairs={{0,2},{1,3},{2,0},{3,1},{4,6},{5,7},{6,4},{7,5},{8,10},{9,11},{10,... | collective-permute-start | bytes 884744 | tf_op jit(solution)/shard_map/ppermute | solution.py:168
  11.0 19.5 %collective-permute-start.2 = (f32[72,1024]{1,0:T(8,128)S(1)}, f32[72,1024]{1,0:T(8,128)S(1)}, u32[]{:S(2)}, u32[]{:S(2)}) collective-permute-start(f32[72,1024]{1,0:T(8,128)S(1)} %get-tuple-element.27), channel_id=1, source_target_pairs={{0,3},{1,0},{2,1},{3,2},{4,7},{5,4},{6,5},{7,6},{8,11},{9,8},{10,9... | collective-permute-start | bytes 884744 | tf_op jit(solution)/shard_map/ppermute | solution.py:168
  13.1 24.0 %all-to-all-start = ((f32[32,16,128]{2,1,0:T(8,128)}), f32[32,16,128]{2,1,0:T(8,128)}, u32[]{:S(2)}, u32[]{:S(2)}) async-start(f32[32,16,128]{2,1,0:T(8,128)} %shard_map.68), calls=%async_computation | async-start | bytes 524288 | tf_op jit(solution)/shard_map/all_to_all | solution.py:191
  24.2 18.7 %collective-permute-start.4 = (f32[4,32,896]{2,1,0:T(8,128)}, f32[4,32,896]{2,1,0:T(8,128)S(1)}, u32[]{:S(2)}, u32[]{:S(2)}) collective-permute-start(f32[4,32,896]{2,1,0:T(8,128)} %get-tuple-element.32), channel_id=1, source_target_pairs={{0,28},{4,0},{8,4},{12,8},{16,12},{20,16},{24,20},{28,24},{1,29},{... | collective-permute-start | bytes 1376264 | tf_op jit(solution)/shard_map/ppermute | solution.py:172
  27.1 10.1 %copy-start.21 = (f32[72,1024]{1,0:T(8,128)}, f32[72,1024]{1,0:T(8,128)S(1)}, u32[]{:S(2)}) copy-start(f32[72,1024]{1,0:T(8,128)S(1)} %collective-permute-done.refs_1_) | copy-start | bytes 884740
  27.1 24.8 %collective-permute-start.5 = (f32[4,32,896]{2,1,0:T(8,128)}, f32[4,32,896]{2,1,0:T(8,128)S(1)}, u32[]{:S(2)}, u32[]{:S(2)}) collective-permute-start(f32[4,32,896]{2,1,0:T(8,128)} %get-tuple-element.33), channel_id=1, source_target_pairs={{0,24},{4,28},{8,0},{12,4},{16,8},{20,12},{24,16},{28,20},{32,40},... | collective-permute-start | bytes 1376264 | tf_op jit(solution)/shard_map/ppermute | solution.py:179
  29.4 22.5 %collective-permute-start.6 = (f32[4,32,896]{2,1,0:T(8,128)}, f32[4,32,896]{2,1,0:T(8,128)S(1)}, u32[]{:S(2)}, u32[]{:S(2)}) collective-permute-start(f32[4,32,896]{2,1,0:T(8,128)} %get-tuple-element.34), channel_id=1, source_target_pairs={{0,1},{1,2},{2,3},{3,0},{4,5},{5,6},{6,7},{7,4},{8,9},{9,10},{10,1... | collective-permute-start | bytes 1376264 | tf_op jit(solution)/shard_map/ppermute | solution.py:168
  31.3 20.6 %collective-permute-start.7 = (f32[4,32,896]{2,1,0:T(8,128)}, f32[4,32,896]{2,1,0:T(8,128)S(1)}, u32[]{:S(2)}, u32[]{:S(2)}) collective-permute-start(f32[4,32,896]{2,1,0:T(8,128)} %get-tuple-element.35), channel_id=1, source_target_pairs={{0,2},{1,3},{2,0},{3,1},{4,6},{5,7},{6,4},{7,5},{8,10},{9,11},{10,... | collective-permute-start | bytes 1376264 | tf_op jit(solution)/shard_map/ppermute | solution.py:168
  32.1 19.9 %copy-start.15 = (f32[4,32,896]{2,1,0:T(8,128)}, f32[4,32,896]{2,1,0:T(8,128)S(1)}, u32[]{:S(2)}) copy-start(f32[4,32,896]{2,1,0:T(8,128)S(1)} %collective-permute-done.3.refs_4_.refs_1_) | copy-start | bytes 1376260
  32.1 19.8 %collective-permute-start.8 = (f32[4,32,896]{2,1,0:T(8,128)}, f32[4,32,896]{2,1,0:T(8,128)S(1)}, u32[]{:S(2)}, u32[]{:S(2)}) collective-permute-start(f32[4,32,896]{2,1,0:T(8,128)} %get-tuple-element.36), channel_id=1, source_target_pairs={{0,3},{1,0},{2,1},{3,2},{4,7},{5,4},{6,5},{7,6},{8,11},{9,8},{10,9... | collective-permute-start | bytes 1376264 | tf_op jit(solution)/shard_map/ppermute | solution.py:168
  39.5 12.5 %all-to-all-start.1 = ((f32[8,16,128]{2,1,0:T(8,128)}), f32[8,16,128]{2,1,0:T(8,128)S(1)}, u32[]{:S(2)}, u32[]{:S(2)}) async-start(f32[8,16,128]{2,1,0:T(8,128)} %get-tuple-element.30), calls=%async_computation.1 | async-start | bytes 131072 | tf_op jit(solution)/shard_map/all_to_all | solution.py:191
  56.1 13.7 %copy-start.14 = (f32[16,128]{1,0:T(8,128)S(1)}, f32[16,128]{1,0:T(8,128)}, u32[]{:S(2)}) copy-start(f32[16,128]{1,0:T(8,128)} %get-tuple-element.37.refs_0_) | copy-start | bytes 24580
  56.1 32.3 %all-to-all-start.2 = ((f32[8,5,16,128]{3,2,1,0:T(8,128)}), f32[8,5,16,128]{3,2,1,0:T(8,128)S(1)}, u32[]{:S(2)}, u32[]{:S(2)}) async-start(f32[8,5,16,128]{3,2,1,0:T(8,128)} %shard_map.72), calls=%async_computation.2 | async-start | bytes 655360 | tf_op jit(solution)/shard_map/all_to_all | solution.py:191
  64.4 18.4 %collective-permute-start.13 = (f32[4,32,896]{2,1,0:T(8,128)}, f32[4,32,896]{2,1,0:T(8,128)S(1)}, u32[]{:S(2)}, u32[]{:S(2)}) collective-permute-start(f32[4,32,896]{2,1,0:T(8,128)} %get-tuple-element.38), channel_id=1, source_target_pairs={{0,1},{1,2},{2,3},{3,0},{4,5},{5,6},{6,7},{7,4},{8,9},{9,10},{10,1... | collective-permute-start | bytes 1376264 | tf_op jit(solution)/shard_map/ppermute | solution.py:168
  67.5 20.1 %collective-permute-start.14 = (f32[4,32,896]{2,1,0:T(8,128)}, f32[4,32,896]{2,1,0:T(8,128)S(1)}, u32[]{:S(2)}, u32[]{:S(2)}) collective-permute-start(f32[4,32,896]{2,1,0:T(8,128)} %get-tuple-element.39), channel_id=1, source_target_pairs={{0,2},{1,3},{2,0},{3,1},{4,6},{5,7},{6,4},{7,5},{8,10},{9,11},{10,... | collective-permute-start | bytes 1376264 | tf_op jit(solution)/shard_map/ppermute | solution.py:168
  67.5 20.8 %collective-permute-start.15 = (f32[4,32,896]{2,1,0:T(8,128)}, f32[4,32,896]{2,1,0:T(8,128)S(1)}, u32[]{:S(2)}, u32[]{:S(2)}) collective-permute-start(f32[4,32,896]{2,1,0:T(8,128)} %get-tuple-element.40), channel_id=1, source_target_pairs={{0,3},{1,0},{2,1},{3,2},{4,7},{5,4},{6,5},{7,6},{8,11},{9,8},{10,9... | collective-permute-start | bytes 1376264 | tf_op jit(solution)/shard_map/ppermute | solution.py:168
  69.8 5.8 %collective-permute-start.12 = (f32[16,128]{1,0:T(8,128)S(1)}, f32[16,128]{1,0:T(8,128)S(1)}, u32[]{:S(2)}, u32[]{:S(2)}) collective-permute-start(f32[16,128]{1,0:T(8,128)S(1)} %copy-done.14), channel_id=1, source_target_pairs={{0,8},{4,12},{8,16},{12,20},{16,24},{20,28},{24,0},{28,4},{1,9},{5... | collective-permute-start | bytes 24584 | tf_op jit(solution)/shard_map/ppermute | solution.py:172
  72.7 5.2 %collective-permute-start.11 = (f32[16,128]{1,0:T(8,128)S(1)}, f32[16,128]{1,0:T(8,128)S(1)}, u32[]{:S(2)}, u32[]{:S(2)}) collective-permute-start(f32[16,128]{1,0:T(8,128)S(1)} %copy-done.14), channel_id=1, source_target_pairs={{0,24},{4,28},{8,0},{12,4},{16,8},{20,12},{24,16},{28,20},{1,25},{... | collective-permute-start | bytes 24584 | tf_op jit(solution)/shard_map/ppermute | solution.py:172
  75.6 6.0 %collective-permute-start.10 = (f32[16,128]{1,0:T(8,128)S(1)}, f32[16,128]{1,0:T(8,128)S(1)}, u32[]{:S(2)}, u32[]{:S(2)}) collective-permute-start(f32[16,128]{1,0:T(8,128)S(1)} %copy-done.14), channel_id=1, source_target_pairs={{0,28},{4,0},{8,4},{12,8},{16,12},{20,16},{24,20},{28,24},{1,29},{... | collective-permute-start | bytes 24584 | tf_op jit(solution)/shard_map/ppermute | solution.py:172
  77.9 4.9 %collective-permute-start.9 = (f32[16,128]{1,0:T(8,128)S(1)}, f32[16,128]{1,0:T(8,128)S(1)}, u32[]{:S(2)}, u32[]{:S(2)}) collective-permute-start(f32[16,128]{1,0:T(8,128)S(1)} %copy-done.14), channel_id=1, source_target_pairs={{0,4},{4,8},{8,12},{12,16},{16,20},{20,24},{24,28},{28,0},{1,5},{5... | collective-permute-start | bytes 24584 | tf_op jit(solution)/shard_map/ppermute | solution.py:172
  82.8 11.4 %copy-start.2 = (f32[4,32,896]{2,1,0:T(8,128)}, f32[4,32,896]{2,1,0:T(8,128)S(1)}, u32[]{:S(2)}) copy-start(f32[4,32,896]{2,1,0:T(8,128)S(1)} %collective-permute-done.13.refs_5_.refs_1_) | copy-start | bytes 1376260
  94.2 10.7 %copy-start.9 = (f32[4,32,896]{2,1,0:T(8,128)S(1)}, f32[4,32,896]{2,1,0:T(8,128)}, u32[]{:S(2)}) copy-start(f32[4,32,896]{2,1,0:T(8,128)} %get-tuple-element.43.refs_10_) | copy-start | bytes 1376260
  94.2 12.2 %copy-start.7 = (f32[4,32,896]{2,1,0:T(8,128)S(1)}, f32[4,32,896]{2,1,0:T(8,128)}, u32[]{:S(2)}) copy-start(f32[4,32,896]{2,1,0:T(8,128)} %get-tuple-element.44.refs_11_) | copy-start | bytes 1376260
  94.2 33.8 %all-to-all-start.3 = ((f32[32,8,16,128]{3,2,1,0:T(8,128)}), f32[32,8,16,128]{3,2,1,0:T(8,128)}, u32[]{:S(2)}, u32[]{:S(2)}) async-start(f32[32,8,16,128]{3,2,1,0:T(8,128)} %shard_map.75), calls=%async_computation.3 | async-start | bytes 4194304 | tf_op jit(solution)/shard_map/all_to_all | solution.py:191
  103.1 15.0 %collective-permute-start.16 = (f32[4,32,896]{2,1,0:T(8,128)S(1)}, f32[4,32,896]{2,1,0:T(8,128)S(1)}, u32[]{:S(2)}, u32[]{:S(2)}) collective-permute-start(f32[4,32,896]{2,1,0:T(8,128)S(1)} %copy-done.11), channel_id=1, source_target_pairs={{0,4},{4,8},{8,12},{12,16},{16,20},{20,24},{24,28},{28,0},{1,5},{5... | collective-permute-start | bytes 1376264 | tf_op jit(solution)/shard_map/ppermute | solution.py:172
  104.9 13.2 %collective-permute-start.17 = (f32[4,32,896]{2,1,0:T(8,128)S(1)}, f32[4,32,896]{2,1,0:T(8,128)S(1)}, u32[]{:S(2)}, u32[]{:S(2)}) collective-permute-start(f32[4,32,896]{2,1,0:T(8,128)S(1)} %copy-done.9), channel_id=1, source_target_pairs={{0,28},{4,0},{8,4},{12,8},{16,12},{20,16},{24,20},{28,24},{1,29},{... | collective-permute-start | bytes 1376264 | tf_op jit(solution)/shard_map/ppermute | solution.py:172
  106.4 21.6 %collective-permute-start.18 = (f32[4,32,896]{2,1,0:T(8,128)S(1)}, f32[4,32,896]{2,1,0:T(8,128)S(1)}, u32[]{:S(2)}, u32[]{:S(2)}) collective-permute-start(f32[4,32,896]{2,1,0:T(8,128)S(1)} %copy-done.7), channel_id=1, source_target_pairs={{0,24},{4,28},{8,0},{12,4},{16,8},{20,12},{24,16},{28,20},{32,40},... | collective-permute-start | bytes 1376264 | tf_op jit(solution)/shard_map/ppermute | solution.py:179
  118.1 9.9 %copy-start.27 = (f32[4,32,896]{2,1,0:T(8,128)}, f32[4,32,896]{2,1,0:T(8,128)S(1)}, u32[]{:S(2)}) copy-start(f32[4,32,896]{2,1,0:T(8,128)S(1)} %collective-permute-done.16.refs_5_) | copy-start | bytes 1376260
  118.2 9.9 %copy-start.28 = (f32[4,32,896]{2,1,0:T(8,128)}, f32[4,32,896]{2,1,0:T(8,128)S(1)}, u32[]{:S(2)}) copy-start(f32[4,32,896]{2,1,0:T(8,128)S(1)} %collective-permute-done.17.refs_6_) | copy-start | bytes 1376260
  136.5 54.1 %all-to-all-start.4 = ((f32[32,16,896]{2,1,0:T(8,128)}), f32[32,16,896]{2,1,0:T(8,128)S(1)}, u32[]{:S(2)}, u32[]{:S(2)}) async-start(f32[32,16,896]{2,1,0:T(8,128)} %shard_map.76), calls=%async_computation.4 | async-start | bytes 3670016 | tf_op jit(solution)/shard_map/all_to_all | solution.py:191
  (22 other events, 76.8 us)

commit v6 on v5

--- a/solution.py
+++ b/solution.py
@@ -80,19 +80,19 @@
 
 
 def couple_kernel(place, arrived, *refs):
-    shared, (first, terms, matrix) = refs[:Y], refs[-3:]
+    shared, (terms, matrix) = refs[:Y], refs[-2:]
     total = jnp.sum(arrived[...], axis=0)
-    first[...] = total
     product = exact_dot(total, in_order(place, shared, slice(0, 32), matrix))
     for z in range(Z):
-        terms[z] = product[:, z * 128:(z + 1) * 128]
+        terms[z, 0] = product[:, z * 128:(z + 1) * 128]
+        terms[z, 1] = total
 
 
 def latter_kernel(place, arrived, *refs):
     shared, (terms, matrix) = refs[:Y], refs[-2:]
     rhs = sum(piece[64:72] for piece in shared)
     rhs = jnp.concatenate([rhs[:, 0:128], rhs[:, 128:256]], axis=0)
-    second = rhs - jnp.sum(arrived[...], axis=0)
+    second = rhs - jnp.sum(arrived[:, 0], axis=0)
     product = exact_dot(second, in_order(place, shared, slice(32, 64), matrix))
     part = lambda z: product[:, (z % Z) * 128:(z % Z + 1) * 128]
     for z in range(Z):
@@ -100,14 +100,14 @@
             terms[z, k] = part(z + step)
 
 
-def close_kernel(arrived, *refs):
+def close_kernel(place, first, arrived, ready, copies):
     latter = jnp.sum(arrived[...], axis=0)
-    first, copies = refs[:len(NEAR)], refs[-1]
-    for place in range(X * C * Y):
+    near = [first[(place[0] + Z + step) % Z, 1] for step in NEAR]
+    for target in range(X * C * Y):
         for k in range(QUAD):
-            near = k if k < 3 else 3 + place // Y % C
-            copies[place, k] = first[near][...]
-            copies[place, QUAD + k] = latter[near]
+            pick = k if k < 3 else 3 + target // Y % C
+            copies[target, k] = near[pick]
+            copies[target, QUAD + k] = latter[pick]
 
 
 def around(z):
@@ -217,23 +217,22 @@
     )
     by_class, by_y = to_windows(*cut[:4]), to_ys(*cut[4:])
 
-    first, terms = call(
-        couple_kernel, (f32(16, 128), f32(Z, 16, 128)), (place, arrived, *shared, cut[0], cut[4]),
-        (VMEM, VMEM), (SMEM,) + (VMEM,) * 5 + (ANY,) * 2, matrix, limit=60,
-    )
-    arrived = exchange(terms, "z")
+    terms = call(
+        couple_kernel, f32(Z, 2, 16, 128), (place, arrived, *shared, cut[0], cut[4]),
+        VMEM, (SMEM,) + (VMEM,) * 5 + (ANY,) * 2, matrix, limit=60,
+    )
+    first = exchange(terms, "z")
     by_r = call(turn_kernel, (block,) * 4, by_class, (ANY,) * 4, (VMEM,) * 4, sems(16), moved=3670016, limit=60)
     first_factor = to_ys(*by_r)
-    near = (first, *(shift_z(first, -step) for step in NEAR[1:]))
 
     terms = call(
-        latter_kernel, f32(Z, len(NEAR), 16, 128), (place, arrived, *shared, *by_class[1:], *by_y[1:]),
+        latter_kernel, f32(Z, len(NEAR), 16, 128), (place, first, *shared, *by_class[1:], *by_y[1:]),
         VMEM, (SMEM,) + (VMEM,) * 5 + (ANY,) * 6, matrix, limit=60,
     )
     arrived = exchange(terms, "z")
     by_k = call(merge_kernel, (block,) * 4, (place, *by_y), (ANY,) * 4, (SMEM,) + (VMEM,) * 4, sems(16), moved=3670016, limit=60)
     latter_factor = to_windows(*by_k)
-    copies = call(close_kernel, f32(X * C * Y, 2 * QUAD, 16, 128), (arrived, *near, *first_factor[1:], *by_k), VMEM, (VMEM,) * 6 + (ANY,) * 7)
+    copies = call(close_kernel, f32(X * C * Y, 2 * QUAD, 16, 128), (place, first, arrived, by_r[0]), VMEM, (SMEM, VMEM, VMEM, ANY))
     rows = exchange(copies, SPREAD)
 
     update = call(

time: 195 us -> 196 us (level)
  waiting for transfers between devices: 84.1 us -> 102 us
  starting transfers between devices: 69.5 us -> 55.2 us
  local copies, waits for them, and re-layouts: 11.1 us -> 9.11 us
    ppermute x9, waiting for transfers between devices: 5.59 us -> 17.7 us  [shift_y(): return lax.ppermute(value, 'y', [(y, (y + step) % Y) for y in range(Y)])]
    all_to_all x5, waiting for transfers between devices: 47.4 us -> 56.8 us  [exchange(): return lax.all_to_all(value, axes, 0, 0, tiled=True)]
    ppermute x8 -> x4, starting transfers between devices: 15.1 us -> 8.14 us  [shift_z(): return lax.ppermute(value, 'z', [(z, (z + step) % Z) for z in range(Z)])]
    ppermute x2, waiting for transfers between devices: 18.8 us -> 12.8 us  [shift_far(): return lax.ppermute(value, ('c', 'z'), pairs)]
    ppermute x9, starting transfers between devices: 11.5 us -> 8.75 us  [shift_y(): return lax.ppermute(value, 'y', [(y, (y + step) % Y) for y in range(Y)])]
    ppermute x2, starting transfers between devices: 4.95 us -> 2.31 us  [shift_far(): return lax.ppermute(value, ('c', 'z'), pairs)]
    ppermute x8 -> x4, waiting for transfers between devices: 12.3 us -> 14.4 us  [shift_z(): return lax.ppermute(value, 'z', [(z, (z + step) % Z) for z in range(Z)])]
    unnamed x62 -> x58, local copies, waits for them, and re-layouts: 9.07 us -> 7.1 us
  transfers between devices with their start and end apart: 24 -> 20, of which waited for: 11 -> 9; matrix products, arithmetic and copies ran while one was open for 1% -> 1% of each run, Pallas kernels for 5% -> 5%
where the time goes in v6:
time: 196 us; the launch traced here: 195 us
  waiting for transfers between devices  102 us (52%)
  starting transfers between devices  55.2 us (28%)
  Pallas kernels  26.2 us (13%)
  local copies, waits for them, and re-layouts  9.11 us (5%)
    all_to_all x5, waiting for transfers between devices, exchange(): return lax.all_to_all(value, axes, 0, 0, tiled=True)  56.8 us
    all_to_all x5, starting transfers between devices, exchange(): return lax.all_to_all(value, axes, 0, 0, tiled=True)  36 us
    pallas_call x9, Pallas kernels, call(): pl.pallas_call(kernel, out_shape=outs, in_specs=in_specs, out_specs=out_s...  26.2 us
    ppermute x9, waiting for transfers between devices, shift_y(): return lax.ppermute(value, 'y', [(y, (y + step) % Y) for y in range(Y)])  17.7 us
    ppermute x4, waiting for transfers between devices, shift_z(): return lax.ppermute(value, 'z', [(z, (z + step) % Z) for z in range(Z)])  14.4 us
    ppermute x2, waiting for transfers between devices, shift_far(): return lax.ppermute(value, ('c', 'z'), pairs)  12.8 us
    ppermute x9, starting transfers between devices, shift_y(): return lax.ppermute(value, 'y', [(y, (y + step) % Y) for y in range(Y)])  8.75 us
    ppermute x4, starting transfers between devices, shift_z(): return lax.ppermute(value, 'z', [(z, (z + step) % Z) for z in range(Z)])  8.14 us
  transfers between devices with their start and end apart: 20, of which 9 were waited for; matrix products, arithmetic and copies ran while one was open for 1% of the time, Pallas kernels for 5%

profile of v6, /device:TPU:20, one launch (start us, length us, event | category | flops | bytes accessed | tf_op | source)
XLA Modules:
  0.0 194.9 jit_solution(2391726171323749819)
XLA Ops:
  1.3 4.2 %shard_map.70 = (f32[4,32,896]{2,1,0:T(8,128)}, f32[4,32,896]{2,1,0:T(8,128)}, f32[4,32,896]{2,1,0:T(8,128)}, f32[4,32,896]{2,1,0:T(8,128)}, f32[4,32,896]{2,1,0...) custom-call(s32[2]{0:T(128)} %pad_add_fusion.place, f32[2,32,14336]{2,1,0:T(8,128)} %factor.1), custom_call_target="tpu_custom_call" | custom-call | bytes 7340032 | tf_op jit(solution)/shard_map/pallas_call | solution.py:26
  5.5 2.0 %collective-permute-start.3 = (f32[4,32,896]{2,1,0:T(8,128)}, f32[4,32,896]{2,1,0:T(8,128)S(1)}, u32[]{:S(2)}, u32[]{:S(2)}) collective-permute-start(f32[4,32,896]{2,1,0:T(8,128)} %get-tuple-element.28), channel_id=1, source_target_pairs={{0,4},{4,8},{8,12},{12,16},{16,20},{20,24},{24,28},{28,0},{1,5},{5... | collective-permute-start | bytes 1376264 | tf_op jit(solution)/shard_map/ppermute | solution.py:172
  9.2 1.3 collective-permute-start
  11.1 1.1 collective-permute-start.2
  12.1 1.1 shard_map.68
  13.2 11.1 %all-to-all-start = ((f32[32,16,128]{2,1,0:T(8,128)}), f32[32,16,128]{2,1,0:T(8,128)}, u32[]{:S(2)}, u32[]{:S(2)}) async-start(f32[32,16,128]{2,1,0:T(8,128)} %shard_map.68), calls=%async_computation | async-start | bytes 524288 | tf_op jit(solution)/shard_map/all_to_all | solution.py:191
  24.3 2.8 %collective-permute-start.4 = (f32[4,32,896]{2,1,0:T(8,128)}, f32[4,32,896]{2,1,0:T(8,128)S(1)}, u32[]{:S(2)}, u32[]{:S(2)}) collective-permute-start(f32[4,32,896]{2,1,0:T(8,128)} %get-tuple-element.29), channel_id=1, source_target_pairs={{0,28},{4,0},{8,4},{12,8},{16,12},{20,16},{24,20},{28,24},{1,29},{... | collective-permute-start | bytes 1376264 | tf_op jit(solution)/shard_map/ppermute | solution.py:172
  27.1 2.3 %collective-permute-start.5 = (f32[4,32,896]{2,1,0:T(8,128)}, f32[4,32,896]{2,1,0:T(8,128)S(1)}, u32[]{:S(2)}, u32[]{:S(2)}) collective-permute-start(f32[4,32,896]{2,1,0:T(8,128)} %get-tuple-element.30), channel_id=1, source_target_pairs={{0,24},{4,28},{8,0},{12,4},{16,8},{20,12},{24,16},{28,20},{32,40},... | collective-permute-start | bytes 1376264 | tf_op jit(solution)/shard_map/ppermute | solution.py:179
  29.4 1.2 collective-permute-start.6
  32.2 1.2 collective-permute-start.8
  33.3 3.9 %all-to-all-done.arrived = f32[32,16,128]{2,1,0:T(8,128)} async-done(((f32[32,16,128]{2,1,0:T(8,128)}), f32[32,16,128]{2,1,0:T(8,128)}, u32[]{:S(2)}, u32[]{:S(2)}) %all-to-all-start) | async-done | bytes 262176 | tf_op jit(solution)/shard_map/all_to_all | solution.py:191
  37.2 2.4 %shard_map.71 = f32[8,2,16,128]{3,2,1,0:T(8,128)} custom-call(s32[2]{0:T(128)} %pad_add_fusion.place, f32[32,16,128]{2,1,0:T(8,128)} %all-to-all-done.arrived, f32[72,1024]{1,0:T(8,128)} %copy-done, f32[72,1024]{1,0:T(8,128)} %copy-done.15, f32[72,1024]{1,0:T(8,128)} %copy-done.16, f32[72,1024]{1,0:T(8,128)} %copy-done.17, ...), custom_call_target="tpu_custom_call" | custom-call | tf_op jit(solution)/shard_map/pallas_call | solution.py:26
  39.6 3.4 %all-to-all-start.1 = ((f32[8,2,16,128]{3,2,1,0:T(8,128)}), f32[8,2,16,128]{3,2,1,0:T(8,128)S(1)}, u32[]{:S(2)}, u32[]{:S(2)}) async-start(f32[8,2,16,128]{3,2,1,0:T(8,128)} %shard_map.71), calls=%async_computation.1 | async-start | bytes 262144 | tf_op jit(solution)/shard_map/all_to_all | solution.py:191
  43.0 9.9 %collective-permute-done.5.refs_6_.refs_3_ = f32[4,32,896]{2,1,0:T(8,128)S(1)} collective-permute-done((f32[4,32,896]{2,1,0:T(8,128)}, f32[4,32,896]{2,1,0:T(8,128)S(1)}, u32[]{:S(2)}, u32[]{:S(2)}) %collective-permute-start.5) | collective-permute-done | bytes 458784 | tf_op jit(solution)/shard_map/ppermute | solution.py:179
  54.8 2.4 %shard_map.72 = f32[8,5,16,128]{3,2,1,0:T(8,128)} custom-call(s32[2]{0:T(128)} %pad_add_fusion.place, f32[8,2,16,128]{3,2,1,0:T(8,128)} %copy-done.1, f32[72,1024]{1,0:T(8,128)} %copy-done, f32[72,1024]{1,0:T(8,128)} %copy-done.15, f32[72,1024]{1,0:T(8,128)} %copy-done.16, f32[72,1024]{1,0:T(8,128)} %copy-done.17, f32[4,32,896]{2,1,0:T(8,128)} %copy-done.9, ...), custom_call_target="tpu_custom_call" | custom-call | tf_op jit(solution)/shard_map/pallas_call | solution.py:26
  57.2 5.2 %all-to-all-start.2 = ((f32[8,5,16,128]{3,2,1,0:T(8,128)}), f32[8,5,16,128]{3,2,1,0:T(8,128)S(1)}, u32[]{:S(2)}, u32[]{:S(2)}) async-start(f32[8,5,16,128]{3,2,1,0:T(8,128)} %shard_map.72), calls=%async_computation.2 | async-start | bytes 655360 | tf_op jit(solution)/shard_map/all_to_all | solution.py:191
  62.4 2.8 %shard_map.73 = (f32[4,32,896]{2,1,0:T(8,128)}, f32[4,32,896]{2,1,0:T(8,128)}, f32[4,32,896]{2,1,0:T(8,128)}, f32[4,32,896]{2,1,0:T(8,128)}) custom-call(f32[4,32,896]{2,1,0:T(8,128)} %get-tuple-element.26.refs_4_.refs_0_, f32[4,32,896]{2,1,0:T(8,128)} %copy-done.9, f32[4,32,896]{2,1,0:T(8,128)} %copy-done.10, f32[4,32,896]{2,1,0:T(8,128)} %copy-done.11), custom_call_target="tpu_custom_call" | custom-call | bytes 3670016 | tf_op jit(solution)/shard_map/pallas_call | solution.py:26
  65.3 9.0 %all-to-all-done.2.arrived = f32[8,5,16,128]{3,2,1,0:T(8,128)S(1)} async-done(((f32[8,5,16,128]{3,2,1,0:T(8,128)}), f32[8,5,16,128]{3,2,1,0:T(8,128)S(1)}, u32[]{:S(2)}, u32[]{:S(2)}) %all-to-all-start.2) | async-done | bytes 327712 | tf_op jit(solution)/shard_map/all_to_all | solution.py:191
  74.3 1.0 copy-done.4
  75.3 2.1 %shard_map.74 = f32[32,8,16,128]{3,2,1,0:T(8,128)} custom-call(s32[2]{0:T(128)S(1)} %copy-done.7, f32[8,2,16,128]{3,2,1,0:T(8,128)S(1)} %copy-done.2, f32[8,5,16,128]{3,2,1,0:T(8,128)S(1)} %all-to-all-done.2.arrived, f32[4,32,896]{2,1,0:T(8,128)S(1)} %copy-done.4), custom_call_target="tpu_custom_call" | custom-call | tf_op jit(solution)/shard_map/pallas_call | solution.py:26
  77.5 9.7 %all-to-all-start.3 = ((f32[32,8,16,128]{3,2,1,0:T(8,128)}), f32[32,8,16,128]{3,2,1,0:T(8,128)S(1)}, u32[]{:S(2)}, u32[]{:S(2)}) async-start(f32[32,8,16,128]{3,2,1,0:T(8,128)} %shard_map.74), calls=%async_computation.3 | async-start | bytes 4194304 | tf_op jit(solution)/shard_map/all_to_all | solution.py:191
  87.2 2.8 %shard_map.75 = (f32[4,32,896]{2,1,0:T(8,128)}, f32[4,32,896]{2,1,0:T(8,128)}, f32[4,32,896]{2,1,0:T(8,128)}, f32[4,32,896]{2,1,0:T(8,128)}) custom-call(s32[2]{0:T(128)} %pad_add_fusion.place, f32[4,32,896]{2,1,0:T(8,128)} %get-tuple-element.27.refs_5_.refs_0_, f32[4,32,896]{2,1,0:T(8,128)} %copy-done.12, f32[4,32,896]{2,1,0:T(8,128)} %copy-done.13, ...), custom_call_target="tpu_custom_call" | custom-call | bytes 3670016 | tf_op jit(solution)/shard_map/pallas_call | solution.py:26
  90.7 2.7 %collective-permute-start.13 = (f32[4,32,896]{2,1,0:T(8,128)}, f32[4,32,896]{2,1,0:T(8,128)S(1)}, u32[]{:S(2)}, u32[]{:S(2)}) collective-permute-start(f32[4,32,896]{2,1,0:T(8,128)} %get-tuple-element.40), channel_id=1, source_target_pairs={{0,28},{4,0},{8,4},{12,8},{16,12},{20,16},{24,20},{28,24},{1,29},{... | collective-permute-start | bytes 1376264 | tf_op jit(solution)/shard_map/ppermute | solution.py:172
  93.3 1.2 collective-permute-start.9
  95.4 14.4 %collective-permute-done.12.refs_5_ = f32[4,32,896]{2,1,0:T(8,128)S(1)} collective-permute-done((f32[4,32,896]{2,1,0:T(8,128)}, f32[4,32,896]{2,1,0:T(8,128)S(1)}, u32[]{:S(2)}, u32[]{:S(2)}) %collective-permute-start.12) | collective-permute-done | bytes 458784 | tf_op jit(solution)/shard_map/ppermute | solution.py:172
  110.4 3.0 %collective-permute-done.14.refs_7_ = f32[4,32,896]{2,1,0:T(8,128)S(1)} collective-permute-done((f32[4,32,896]{2,1,0:T(8,128)}, f32[4,32,896]{2,1,0:T(8,128)S(1)}, u32[]{:S(2)}, u32[]{:S(2)}) %collective-permute-start.14) | collective-permute-done | bytes 458784 | tf_op jit(solution)/shard_map/ppermute | solution.py:179
  113.3 8.3 %collective-permute-done.9.refs_1_ = f32[4,32,896]{2,1,0:T(8,128)S(1)} collective-permute-done((f32[4,32,896]{2,1,0:T(8,128)S(1)}, f32[4,32,896]{2,1,0:T(8,128)S(1)}, u32[]{:S(2)}, u32[]{:S(2)}) %collective-permute-start.9) | collective-permute-done | bytes 458784 | tf_op jit(solution)/shard_map/ppermute | solution.py:168
  121.6 9.4 %collective-permute-done.10.refs_2_ = f32[4,32,896]{2,1,0:T(8,128)S(1)} collective-permute-done((f32[4,32,896]{2,1,0:T(8,128)S(1)}, f32[4,32,896]{2,1,0:T(8,128)S(1)}, u32[]{:S(2)}, u32[]{:S(2)}) %collective-permute-start.10) | collective-permute-done | bytes 458784 | tf_op jit(solution)/shard_map/ppermute | solution.py:168
  131.8 1.3 copy-done.8
  133.1 7.7 %shard_map.76 = f32[32,16,896]{2,1,0:T(8,128)} custom-call(s32[2]{0:T(128)} %pad_add_fusion.place, f32[32,8,16,128]{3,2,1,0:T(8,128)} %copy-done.8, f32[4,32,896]{2,1,0:T(8,128)} %get-tuple-element.34.ready.refs_0_, f32[4,32,896]{2,1,0:T(8,128)} %copy-done.26, f32[4,32,896]{2,1,0:T(8,128)} %copy-done.27, f32[4,32,896]{2,1,0:T(8,128)} %collective-permute-done.11.refs_3_, ...), custom_call_target="tpu_custom_call" | custom-call | flops 2818572288 | bytes 7602176 | tf_op jit(solution)/shard_map/pallas_call | solution.py:26
  140.9 6.6 %all-to-all-start.4 = ((f32[32,16,896]{2,1,0:T(8,128)}), f32[32,16,896]{2,1,0:T(8,128)S(1)}, u32[]{:S(2)}, u32[]{:S(2)}) async-start(f32[32,16,896]{2,1,0:T(8,128)} %shard_map.76), calls=%async_computation.4 | async-start | bytes 3670016 | tf_op jit(solution)/shard_map/all_to_all | solution.py:191
  149.1 43.5 %all-to-all-done.4 = f32[32,16,896]{2,1,0:T(8,128)S(1)} async-done(((f32[32,16,896]{2,1,0:T(8,128)}), f32[32,16,896]{2,1,0:T(8,128)S(1)}, u32[]{:S(2)}, u32[]{:S(2)}) %all-to-all-start.4) | async-done | bytes 1835040 | tf_op jit(solution)/shard_map/all_to_all | solution.py:191
  (88 shorter events, 13.0 us)
Async XLA Ops:
  5.5 26.7 %collective-permute-start.3 = (f32[4,32,896]{2,1,0:T(8,128)}, f32[4,32,896]{2,1,0:T(8,128)S(1)}, u32[]{:S(2)}, u32[]{:S(2)}) collective-permute-start(f32[4,32,896]{2,1,0:T(8,128)} %get-tuple-element.28), channel_id=1, source_target_pairs={{0,4},{4,8},{8,12},{12,16},{16,20},{20,24},{24,28},{28,0},{1,5},{5... | collective-permute-start | bytes 1376264 | tf_op jit(solution)/shard_map/ppermute | solution.py:172
  9.2 18.0 %collective-permute-start = (f32[72,1024]{1,0:T(8,128)S(1)}, f32[72,1024]{1,0:T(8,128)S(1)}, u32[]{:S(2)}, u32[]{:S(2)}) collective-permute-start(f32[72,1024]{1,0:T(8,128)S(1)} %get-tuple-element.23), channel_id=1, source_target_pairs={{0,1},{1,2},{2,3},{3,0},{4,5},{5,6},{6,7},{7,4},{8,9},{9,10},{10,1... | collective-permute-start | bytes 884744 | tf_op jit(solution)/shard_map/ppermute | solution.py:168
  10.4 19.0 %collective-permute-start.1 = (f32[72,1024]{1,0:T(8,128)S(1)}, f32[72,1024]{1,0:T(8,128)S(1)}, u32[]{:S(2)}, u32[]{:S(2)}) collective-permute-start(f32[72,1024]{1,0:T(8,128)S(1)} %get-tuple-element.24), channel_id=1, source_target_pairs={{0,2},{1,3},{2,0},{3,1},{4,6},{5,7},{6,4},{7,5},{8,10},{9,11},{10,... | collective-permute-start | bytes 884744 | tf_op jit(solution)/shard_map/ppermute | solution.py:168
  11.1 19.5 %collective-permute-start.2 = (f32[72,1024]{1,0:T(8,128)S(1)}, f32[72,1024]{1,0:T(8,128)S(1)}, u32[]{:S(2)}, u32[]{:S(2)}) collective-permute-start(f32[72,1024]{1,0:T(8,128)S(1)} %get-tuple-element.25), channel_id=1, source_target_pairs={{0,3},{1,0},{2,1},{3,2},{4,7},{5,4},{6,5},{7,6},{8,11},{9,8},{10,9... | collective-permute-start | bytes 884744 | tf_op jit(solution)/shard_map/ppermute | solution.py:168
  13.2 24.0 %all-to-all-start = ((f32[32,16,128]{2,1,0:T(8,128)}), f32[32,16,128]{2,1,0:T(8,128)}, u32[]{:S(2)}, u32[]{:S(2)}) async-start(f32[32,16,128]{2,1,0:T(8,128)} %shard_map.68), calls=%async_computation | async-start | bytes 524288 | tf_op jit(solution)/shard_map/all_to_all | solution.py:191
  24.3 18.7 %collective-permute-start.4 = (f32[4,32,896]{2,1,0:T(8,128)}, f32[4,32,896]{2,1,0:T(8,128)S(1)}, u32[]{:S(2)}, u32[]{:S(2)}) collective-permute-start(f32[4,32,896]{2,1,0:T(8,128)} %get-tuple-element.29), channel_id=1, source_target_pairs={{0,28},{4,0},{8,4},{12,8},{16,12},{20,16},{24,20},{28,24},{1,29},{... | collective-permute-start | bytes 1376264 | tf_op jit(solution)/shard_map/ppermute | solution.py:172
  27.1 10.1 %copy-start.15 = (f32[72,1024]{1,0:T(8,128)}, f32[72,1024]{1,0:T(8,128)S(1)}, u32[]{:S(2)}) copy-start(f32[72,1024]{1,0:T(8,128)S(1)} %collective-permute-done.refs_1_) | copy-start | bytes 884740
  27.1 25.8 %collective-permute-start.5 = (f32[4,32,896]{2,1,0:T(8,128)}, f32[4,32,896]{2,1,0:T(8,128)S(1)}, u32[]{:S(2)}, u32[]{:S(2)}) collective-permute-start(f32[4,32,896]{2,1,0:T(8,128)} %get-tuple-element.30), channel_id=1, source_target_pairs={{0,24},{4,28},{8,0},{12,4},{16,8},{20,12},{24,16},{28,20},{32,40},... | collective-permute-start | bytes 1376264 | tf_op jit(solution)/shard_map/ppermute | solution.py:179
  29.4 23.5 %collective-permute-start.6 = (f32[4,32,896]{2,1,0:T(8,128)}, f32[4,32,896]{2,1,0:T(8,128)S(1)}, u32[]{:S(2)}, u32[]{:S(2)}) collective-permute-start(f32[4,32,896]{2,1,0:T(8,128)} %get-tuple-element.31), channel_id=1, source_target_pairs={{0,1},{1,2},{2,3},{3,0},{4,5},{5,6},{6,7},{7,4},{8,9},{9,10},{10,1... | collective-permute-start | bytes 1376264 | tf_op jit(solution)/shard_map/ppermute | solution.py:168
  31.3 21.6 %collective-permute-start.7 = (f32[4,32,896]{2,1,0:T(8,128)}, f32[4,32,896]{2,1,0:T(8,128)S(1)}, u32[]{:S(2)}, u32[]{:S(2)}) collective-permute-start(f32[4,32,896]{2,1,0:T(8,128)} %get-tuple-element.32), channel_id=1, source_target_pairs={{0,2},{1,3},{2,0},{3,1},{4,6},{5,7},{6,4},{7,5},{8,10},{9,11},{10,... | collective-permute-start | bytes 1376264 | tf_op jit(solution)/shard_map/ppermute | solution.py:168
  32.2 21.1 %copy-start.9 = (f32[4,32,896]{2,1,0:T(8,128)}, f32[4,32,896]{2,1,0:T(8,128)S(1)}, u32[]{:S(2)}) copy-start(f32[4,32,896]{2,1,0:T(8,128)S(1)} %collective-permute-done.3.refs_4_.refs_1_) | copy-start | bytes 1376260
  32.2 20.8 %collective-permute-start.8 = (f32[4,32,896]{2,1,0:T(8,128)}, f32[4,32,896]{2,1,0:T(8,128)S(1)}, u32[]{:S(2)}, u32[]{:S(2)}) collective-permute-start(f32[4,32,896]{2,1,0:T(8,128)} %get-tuple-element.33), channel_id=1, source_target_pairs={{0,3},{1,0},{2,1},{3,2},{4,7},{5,4},{6,5},{7,6},{8,11},{9,8},{10,9... | collective-permute-start | bytes 1376264 | tf_op jit(solution)/shard_map/ppermute | solution.py:168
  39.6 13.6 %all-to-all-start.1 = ((f32[8,2,16,128]{3,2,1,0:T(8,128)}), f32[8,2,16,128]{3,2,1,0:T(8,128)S(1)}, u32[]{:S(2)}, u32[]{:S(2)}) async-start(f32[8,2,16,128]{3,2,1,0:T(8,128)} %shard_map.71), calls=%async_computation.1 | async-start | bytes 262144 | tf_op jit(solution)/shard_map/all_to_all | solution.py:191
  43.0 10.2 %copy-start.10 = (f32[4,32,896]{2,1,0:T(8,128)}, f32[4,32,896]{2,1,0:T(8,128)S(1)}, u32[]{:S(2)}) copy-start(f32[4,32,896]{2,1,0:T(8,128)S(1)} %collective-permute-done.4.refs_5_.refs_2_) | copy-start | bytes 1376260
  57.2 17.1 %copy-start.2 = (f32[8,2,16,128]{3,2,1,0:T(8,128)S(1)}, f32[8,2,16,128]{3,2,1,0:T(8,128)}, u32[]{:S(2)}) copy-start(f32[8,2,16,128]{3,2,1,0:T(8,128)} %copy-done.1) | copy-start | bytes 393220
  57.2 17.1 %copy-start.7 = (s32[2]{0:T(128)S(1)}, s32[2]{0:T(128)}, u32[]{:S(2)}) copy-start(s32[2]{0:T(128)} %pad_add_fusion.place) | copy-start | bytes 28
  57.2 17.1 %all-to-all-start.2 = ((f32[8,5,16,128]{3,2,1,0:T(8,128)}), f32[8,5,16,128]{3,2,1,0:T(8,128)S(1)}, u32[]{:S(2)}, u32[]{:S(2)}) async-start(f32[8,5,16,128]{3,2,1,0:T(8,128)} %shard_map.72), calls=%async_computation.2 | async-start | bytes 655360 | tf_op jit(solution)/shard_map/all_to_all | solution.py:191
  77.5 15.9 %copy-start.22 = (f32[4,32,896]{2,1,0:T(8,128)S(1)}, f32[4,32,896]{2,1,0:T(8,128)}, u32[]{:S(2)}) copy-start(f32[4,32,896]{2,1,0:T(8,128)} %get-tuple-element.35) | copy-start | bytes 1376260
  77.5 17.1 %copy-start.21 = (f32[4,32,896]{2,1,0:T(8,128)S(1)}, f32[4,32,896]{2,1,0:T(8,128)}, u32[]{:S(2)}) copy-start(f32[4,32,896]{2,1,0:T(8,128)} %get-tuple-element.36) | copy-start | bytes 1376260
  77.5 32.3 %copy-start.20 = (f32[4,32,896]{2,1,0:T(8,128)S(1)}, f32[4,32,896]{2,1,0:T(8,128)}, u32[]{:S(2)}) copy-start(f32[4,32,896]{2,1,0:T(8,128)} %get-tuple-element.37) | copy-start | bytes 1376260
  77.5 54.3 %all-to-all-start.3 = ((f32[32,8,16,128]{3,2,1,0:T(8,128)}), f32[32,8,16,128]{3,2,1,0:T(8,128)S(1)}, u32[]{:S(2)}, u32[]{:S(2)}) async-start(f32[32,8,16,128]{3,2,1,0:T(8,128)} %shard_map.74), calls=%async_computation.3 | async-start | bytes 4194304 | tf_op jit(solution)/shard_map/all_to_all | solution.py:191
  90.0 19.8 %collective-permute-start.12 = (f32[4,32,896]{2,1,0:T(8,128)}, f32[4,32,896]{2,1,0:T(8,128)S(1)}, u32[]{:S(2)}, u32[]{:S(2)}) collective-permute-start(f32[4,32,896]{2,1,0:T(8,128)} %get-tuple-element.39), channel_id=1, source_target_pairs={{0,4},{4,8},{8,12},{12,16},{16,20},{20,24},{24,28},{28,0},{1,5},{5... | collective-permute-start | bytes 1376264 | tf_op jit(solution)/shard_map/ppermute | solution.py:172
  90.7 19.7 %collective-permute-start.13 = (f32[4,32,896]{2,1,0:T(8,128)}, f32[4,32,896]{2,1,0:T(8,128)S(1)}, u32[]{:S(2)}, u32[]{:S(2)}) collective-permute-start(f32[4,32,896]{2,1,0:T(8,128)} %get-tuple-element.40), channel_id=1, source_target_pairs={{0,28},{4,0},{8,4},{12,8},{16,12},{20,16},{24,20},{28,24},{1,29},{... | collective-permute-start | bytes 1376264 | tf_op jit(solution)/shard_map/ppermute | solution.py:172
  93.3 20.0 %collective-permute-start.14 = (f32[4,32,896]{2,1,0:T(8,128)}, f32[4,32,896]{2,1,0:T(8,128)S(1)}, u32[]{:S(2)}, u32[]{:S(2)}) collective-permute-start(f32[4,32,896]{2,1,0:T(8,128)} %get-tuple-element.41), channel_id=1, source_target_pairs={{0,24},{4,28},{8,0},{12,4},{16,8},{20,12},{24,16},{28,20},{32,40},... | collective-permute-start | bytes 1376264 | tf_op jit(solution)/shard_map/ppermute | solution.py:179
  93.3 28.3 %collective-permute-start.9 = (f32[4,32,896]{2,1,0:T(8,128)S(1)}, f32[4,32,896]{2,1,0:T(8,128)S(1)}, u32[]{:S(2)}, u32[]{:S(2)}) collective-permute-start(f32[4,32,896]{2,1,0:T(8,128)S(1)} %copy-done.22), channel_id=1, source_target_pairs={{0,1},{1,2},{2,3},{3,0},{4,5},{5,6},{6,7},{7,4},{8,9},{9,10},{10,1... | collective-permute-start | bytes 1376264 | tf_op jit(solution)/shard_map/ppermute | solution.py:168
  94.5 36.5 %collective-permute-start.10 = (f32[4,32,896]{2,1,0:T(8,128)S(1)}, f32[4,32,896]{2,1,0:T(8,128)S(1)}, u32[]{:S(2)}, u32[]{:S(2)}) collective-permute-start(f32[4,32,896]{2,1,0:T(8,128)S(1)} %copy-done.21), channel_id=1, source_target_pairs={{0,2},{1,3},{2,0},{3,1},{4,6},{5,7},{6,4},{7,5},{8,10},{9,11},{10,... | collective-permute-start | bytes 1376264 | tf_op jit(solution)/shard_map/ppermute | solution.py:168
  109.8 21.2 %copy-start.23 = (f32[4,32,896]{2,1,0:T(8,128)}, f32[4,32,896]{2,1,0:T(8,128)S(1)}, u32[]{:S(2)}) copy-start(f32[4,32,896]{2,1,0:T(8,128)S(1)} %collective-permute-done.12.refs_5_) | copy-start | bytes 1376260
  109.8 22.0 %collective-permute-start.11 = (f32[4,32,896]{2,1,0:T(8,128)S(1)}, f32[4,32,896]{2,1,0:T(8,128)}, u32[]{:S(2)}, u32[]{:S(2)}) collective-permute-start(f32[4,32,896]{2,1,0:T(8,128)S(1)} %copy-done.20), channel_id=1, source_target_pairs={{0,3},{1,0},{2,1},{3,2},{4,7},{5,4},{6,5},{7,6},{8,11},{9,8},{10,9... | collective-permute-start | bytes 1376264 | tf_op jit(solution)/shard_map/ppermute | solution.py:168
  110.4 20.6 %copy-start.24 = (f32[4,32,896]{2,1,0:T(8,128)}, f32[4,32,896]{2,1,0:T(8,128)S(1)}, u32[]{:S(2)}) copy-start(f32[4,32,896]{2,1,0:T(8,128)S(1)} %collective-permute-done.13.refs_6_) | copy-start | bytes 1376260
  113.3 17.7 %copy-start.25 = (f32[4,32,896]{2,1,0:T(8,128)}, f32[4,32,896]{2,1,0:T(8,128)S(1)}, u32[]{:S(2)}) copy-start(f32[4,32,896]{2,1,0:T(8,128)S(1)} %collective-permute-done.14.refs_7_) | copy-start | bytes 1376260
  121.6 9.4 %copy-start.26 = (f32[4,32,896]{2,1,0:T(8,128)}, f32[4,32,896]{2,1,0:T(8,128)S(1)}, u32[]{:S(2)}) copy-start(f32[4,32,896]{2,1,0:T(8,128)S(1)} %collective-permute-done.9.refs_1_) | copy-start | bytes 1376260
  140.9 51.8 %all-to-all-start.4 = ((f32[32,16,896]{2,1,0:T(8,128)}), f32[32,16,896]{2,1,0:T(8,128)S(1)}, u32[]{:S(2)}, u32[]{:S(2)}) async-start(f32[32,16,896]{2,1,0:T(8,128)} %shard_map.76), calls=%async_computation.4 | async-start | bytes 3670016 | tf_op jit(solution)/shard_map/all_to_all | solution.py:191
  (16 other events, 44.6 us)

commit v7 on v6

--- a/solution.py
+++ b/solution.py
@@ -137,28 +137,39 @@
     copy_all([(arrived[r].at[k], sent[k].at[(place[1] + Y - r) % Y]) for r in range(Y) for k in range(QUAD)], sems)
 
 
-def update_kernel(place, rows, *refs):
-    by_r, by_k = refs[:Y], refs[Y:Y + QUAD]
-    out, left, factor, result, sems = refs[-5:]
+def split_first_kernel(place, *refs):
+    arrived, (high, low) = refs[:Y], refs[Y:]
+    for r in range(Y):
+        slot = (place[1] + Y - r) % Y
+        high[:, slot], low[:, slot] = split(arrived[r][...])
+
+
+def split_latter_kernel(*refs):
+    arrived, (high, low) = refs[:QUAD], refs[QUAD:]
+    for k in range(QUAD):
+        high[k], low[k] = split(arrived[k][...])
+
+
+def update_kernel(rows, *refs):
+    parts, (out, left, factor, result, sems) = refs[:4], refs[4:]
     start = lambda src, dst, i: pltpu.make_async_copy(src, dst, sems.at[i])
     chunk = 128 // 16
-    part = lambda i: slice(i * chunk, (i + 1) * chunk)
+    at = lambda i: slice(i * chunk, (i + 1) * chunk)
     arriving = [start(rows, left, 0)]
-    arriving += [start(by_r[r], factor.at[0, :, (place[1] + Y - r) % Y], 1 + r) for r in range(Y)]
-    arriving += [start(by_k[k], factor.at[1, k], 1 + Y + k) for k in range(QUAD)]
+    arriving += [start(parts[i], factor.at[i % 2, i // 2], 1 + i) for i in range(4)]
     for copy in arriving:
         copy.start()
     for copy in arriving:
         copy.wait()
-    right_high, right_low = split(factor[...].reshape(2 * QUAD * 128, -1))
+    right_high, right_low = (factor[i].reshape(2 * QUAD * 128, -1) for i in range(2))
     dot = functools.partial(jnp.dot, preferred_element_type=jnp.float32)
     sent = []
     for i in range(left.shape[0] // chunk):
-        piece = left[part(i)]
+        piece = left[at(i)]
         high, low = split(jnp.concatenate([piece[:, k].reshape(128, 128) for k in range(2 * QUAD)], axis=1))
         product = dot(high, right_high) + (dot(high, right_low) + dot(low, right_high))
-        result[part(i)] = product.reshape(chunk, 16, -1)
-        sent.append(start(result.at[part(i)], out.at[part(i)], 1 + Y + QUAD + i))
+        result[at(i)] = product.reshape(chunk, 16, -1)
+        sent.append(start(result.at[at(i)], out.at[at(i)], 5 + i))
         sent[-1].start()
     for copy in sent:
         copy.wait()
@@ -235,14 +246,20 @@
     copies = call(close_kernel, f32(X * C * Y, 2 * QUAD, 16, 128), (place, first, arrived, by_r[0]), VMEM, (SMEM, VMEM, VMEM, ANY))
     rows = exchange(copies, SPREAD)
 
+    halves = (jax.ShapeDtypeStruct((QUAD, *block.shape), jnp.bfloat16),) * 2
+    first_parts = call(
+        split_first_kernel, halves, (place, *first_factor), (VMEM,) * 2, (SMEM,) + (VMEM,) * 4, moved=100 << 20, limit=60,
+    )
+    latter_parts = call(
+        split_latter_kernel, halves, latter_factor, (VMEM,) * 2, (VMEM,) * 4, moved=50 << 20, limit=60,
+    )
     update = call(
-        update_kernel, f32(X * C * Y, 16, width), (place, rows, *first_factor, *latter_factor),
-        ANY, (SMEM,) + (ANY,) * 9,
+        update_kernel, f32(X * C * Y, 16, width), (rows, *first_parts, *latter_parts), ANY, (ANY,) * 5,
         [
             pltpu.VMEM(rows.shape, jnp.float32),
-            pltpu.VMEM((2, QUAD, Y, 32, width), jnp.float32),
+            pltpu.VMEM((2, 2, QUAD, *block.shape), jnp.bfloat16),
             pltpu.VMEM((X * C * Y, 16, width), jnp.float32),
-        ] + sems(17),
+        ] + sems(9),
         flops=2818572288, moved=7602176, limit=60,
     )
     parts = exchange(update, COLS)

time: 196 us -> 202 us (1.031)
  Pallas kernels: 26.2 us -> 31.5 us
    ppermute x9, waiting for transfers between devices: 17.7 us -> 34.8 us  [shift_y(): return lax.ppermute(value, 'y', [(y, (y + step) % Y) for y in range(Y)])]
    ppermute x4, waiting for transfers between devices: 14.4 us -> 0.01 us  [shift_z(): return lax.ppermute(value, 'z', [(z, (z + step) % Z) for z in range(Z)])]
    pallas_call x9 -> x11, Pallas kernels: 26.2 us -> 31.5 us  [call(): pl.pallas_call(kernel, out_shape=outs, in_specs=in_specs, out_specs=out_s...]
    unnamed x58 -> x52, local copies, waits for them, and re-layouts: 7.1 us -> 7.07 us
  transfers between devices with their start and end apart: 20 -> 20, of which waited for: 9 -> 9; matrix products, arithmetic and copies ran while one was open for 1% -> 1% of each run, Pallas kernels for 5% -> 8%
where the time goes in v7:
time: 202 us; the launch traced here: 200 us
  waiting for transfers between devices  101 us (50%)
  starting transfers between devices  55.6 us (28%)
  Pallas kernels  31.5 us (16%)
  local copies, waits for them, and re-layouts  9.08 us (4%)
    all_to_all x5, waiting for transfers between devices, exchange(): return lax.all_to_all(value, axes, 0, 0, tiled=True)  55.1 us
    all_to_all x5, starting transfers between devices, exchange(): return lax.all_to_all(value, axes, 0, 0, tiled=True)  35.4 us
    ppermute x9, waiting for transfers between devices, shift_y(): return lax.ppermute(value, 'y', [(y, (y + step) % Y) for y in range(Y)])  34.8 us
    pallas_call x11, Pallas kernels, call(): pl.pallas_call(kernel, out_shape=outs, in_specs=in_specs, out_specs=out_s...  31.5 us
    ppermute x2, waiting for transfers between devices, shift_far(): return lax.ppermute(value, ('c', 'z'), pairs)  11.2 us
    ppermute x9, starting transfers between devices, shift_y(): return lax.ppermute(value, 'y', [(y, (y + step) % Y) for y in range(Y)])  9.41 us
    ppermute x4, starting transfers between devices, shift_z(): return lax.ppermute(value, 'z', [(z, (z + step) % Z) for z in range(Z)])  8.14 us
    unnamed x52, local copies, waits for them, and re-layouts  7.07 us
  transfers between devices with their start and end apart: 20, of which 9 were waited for; matrix products, arithmetic and copies ran while one was open for 1% of the time, Pallas kernels for 8%

profile of v7, /device:TPU:20, one launch (start us, length us, event | category | flops | bytes accessed | tf_op | source)
XLA Modules:
  0.0 200.0 jit_solution(8753606588551987609)
XLA Ops:
  1.3 4.2 %shard_map.70 = (f32[4,32,896]{2,1,0:T(8,128)}, f32[4,32,896]{2,1,0:T(8,128)}, f32[4,32,896]{2,1,0:T(8,128)}, f32[4,32,896]{2,1,0:T(8,128)}, f32[4,32,896]{2,1,0...) custom-call(s32[2]{0:T(128)} %pad_add_fusion.place, f32[2,32,14336]{2,1,0:T(8,128)} %factor.1), custom_call_target="tpu_custom_call" | custom-call | bytes 7340032 | tf_op jit(solution)/shard_map/pallas_call | solution.py:26
  5.5 2.0 collective-permute-start.3
  9.2 1.3 collective-permute-start
  12.1 1.1 shard_map.68
  13.2 11.1 %all-to-all-start = ((f32[32,16,128]{2,1,0:T(8,128)}), f32[32,16,128]{2,1,0:T(8,128)}, u32[]{:S(2)}, u32[]{:S(2)}) async-start(f32[32,16,128]{2,1,0:T(8,128)} %shard_map.68), calls=%async_computation | async-start | bytes 524288 | tf_op jit(solution)/shard_map/all_to_all | solution.py:202
  24.3 2.8 %collective-permute-start.4 = (f32[4,32,896]{2,1,0:T(8,128)}, f32[4,32,896]{2,1,0:T(8,128)S(1)}, u32[]{:S(2)}, u32[]{:S(2)}) collective-permute-start(f32[4,32,896]{2,1,0:T(8,128)} %get-tuple-element.33), channel_id=1, source_target_pairs={{0,28},{4,0},{8,4},{12,8},{16,12},{20,16},{24,20},{28,24},{1,29},{... | collective-permute-start | bytes 1376264 | tf_op jit(solution)/shard_map/ppermute | solution.py:183
  27.1 2.3 %collective-permute-start.5 = (f32[4,32,896]{2,1,0:T(8,128)}, f32[4,32,896]{2,1,0:T(8,128)S(1)}, u32[]{:S(2)}, u32[]{:S(2)}) collective-permute-start(f32[4,32,896]{2,1,0:T(8,128)} %get-tuple-element.34), channel_id=1, source_target_pairs={{0,24},{4,28},{8,0},{12,4},{16,8},{20,12},{24,16},{28,20},{32,40},... | collective-permute-start | bytes 1376264 | tf_op jit(solution)/shard_map/ppermute | solution.py:190
  29.4 1.2 collective-permute-start.6
  32.2 1.2 collective-permute-start.8
  33.3 3.9 %all-to-all-done.arrived = f32[32,16,128]{2,1,0:T(8,128)} async-done(((f32[32,16,128]{2,1,0:T(8,128)}), f32[32,16,128]{2,1,0:T(8,128)}, u32[]{:S(2)}, u32[]{:S(2)}) %all-to-all-start) | async-done | bytes 262176 | tf_op jit(solution)/shard_map/all_to_all | solution.py:202
  37.2 2.4 %shard_map.71 = f32[8,2,16,128]{3,2,1,0:T(8,128)} custom-call(s32[2]{0:T(128)} %pad_add_fusion.place, f32[32,16,128]{2,1,0:T(8,128)} %all-to-all-done.arrived, f32[72,1024]{1,0:T(8,128)} %copy-done.1, f32[72,1024]{1,0:T(8,128)} %copy-done.15, f32[72,1024]{1,0:T(8,128)} %copy-done.16, f32[72,1024]{1,0:T(8,128)} %copy-done.17, ...), custom_call_target="tpu_custom_call" | custom-call | tf_op jit(solution)/shard_map/pallas_call | solution.py:26
  39.6 3.4 %all-to-all-start.1 = ((f32[8,2,16,128]{3,2,1,0:T(8,128)}), f32[8,2,16,128]{3,2,1,0:T(8,128)S(1)}, u32[]{:S(2)}, u32[]{:S(2)}) async-start(f32[8,2,16,128]{3,2,1,0:T(8,128)} %shard_map.71), calls=%async_computation.1 | async-start | bytes 262144 | tf_op jit(solution)/shard_map/all_to_all | solution.py:202
  43.0 9.9 %collective-permute-done.5.refs_6_.refs_3_ = f32[4,32,896]{2,1,0:T(8,128)S(1)} collective-permute-done((f32[4,32,896]{2,1,0:T(8,128)}, f32[4,32,896]{2,1,0:T(8,128)S(1)}, u32[]{:S(2)}, u32[]{:S(2)}) %collective-permute-start.5) | collective-permute-done | bytes 458784 | tf_op jit(solution)/shard_map/ppermute | solution.py:190
  54.8 2.4 %shard_map.72 = f32[8,5,16,128]{3,2,1,0:T(8,128)} custom-call(s32[2]{0:T(128)} %pad_add_fusion.place, f32[8,2,16,128]{3,2,1,0:T(8,128)} %copy-done.2, f32[72,1024]{1,0:T(8,128)} %copy-done.1, f32[72,1024]{1,0:T(8,128)} %copy-done.15, f32[72,1024]{1,0:T(8,128)} %copy-done.16, f32[72,1024]{1,0:T(8,128)} %copy-done.17, f32[4,32,896]{2,1,0:T(8,128)} %copy-done.9, ...), custom_call_target="tpu_custom_call" | custom-call | tf_op jit(solution)/shard_map/pallas_call | solution.py:26
  57.2 5.2 %all-to-all-start.2 = ((f32[8,5,16,128]{3,2,1,0:T(8,128)}), f32[8,5,16,128]{3,2,1,0:T(8,128)S(1)}, u32[]{:S(2)}, u32[]{:S(2)}) async-start(f32[8,5,16,128]{3,2,1,0:T(8,128)} %shard_map.72), calls=%async_computation.2 | async-start | bytes 655360 | tf_op jit(solution)/shard_map/all_to_all | solution.py:202
  62.4 2.8 %shard_map.73 = (f32[4,32,896]{2,1,0:T(8,128)}, f32[4,32,896]{2,1,0:T(8,128)}, f32[4,32,896]{2,1,0:T(8,128)}, f32[4,32,896]{2,1,0:T(8,128)}) custom-call(f32[4,32,896]{2,1,0:T(8,128)} %get-tuple-element.30.refs_4_.refs_0_, f32[4,32,896]{2,1,0:T(8,128)} %copy-done.9, f32[4,32,896]{2,1,0:T(8,128)} %copy-done.10, f32[4,32,896]{2,1,0:T(8,128)} %copy-done.11), custom_call_target="tpu_custom_call" | custom-call | bytes 3670016 | tf_op jit(solution)/shard_map/pallas_call | solution.py:26
  65.3 9.0 %all-to-all-done.2.arrived = f32[8,5,16,128]{3,2,1,0:T(8,128)S(1)} async-done(((f32[8,5,16,128]{3,2,1,0:T(8,128)}), f32[8,5,16,128]{3,2,1,0:T(8,128)S(1)}, u32[]{:S(2)}, u32[]{:S(2)}) %all-to-all-start.2) | async-done | bytes 327712 | tf_op jit(solution)/shard_map/all_to_all | solution.py:202
  75.3 2.1 %shard_map.74 = f32[32,8,16,128]{3,2,1,0:T(8,128)} custom-call(s32[2]{0:T(128)S(1)} %copy-done.7, f32[8,2,16,128]{3,2,1,0:T(8,128)S(1)} %copy-done.3, f32[8,5,16,128]{3,2,1,0:T(8,128)S(1)} %all-to-all-done.2.arrived, f32[4,32,896]{2,1,0:T(8,128)S(1)} %copy-done), custom_call_target="tpu_custom_call" | custom-call | tf_op jit(solution)/shard_map/pallas_call | solution.py:26
  77.5 9.7 %all-to-all-start.3 = ((f32[32,8,16,128]{3,2,1,0:T(8,128)}), f32[32,8,16,128]{3,2,1,0:T(8,128)S(1)}, u32[]{:S(2)}, u32[]{:S(2)}) async-start(f32[32,8,16,128]{3,2,1,0:T(8,128)} %shard_map.74), calls=%async_computation.3 | async-start | bytes 4194304 | tf_op jit(solution)/shard_map/all_to_all | solution.py:202
  87.2 1.2 collective-permute-start.9
  88.5 2.8 %shard_map.76 = (f32[4,32,896]{2,1,0:T(8,128)}, f32[4,32,896]{2,1,0:T(8,128)}, f32[4,32,896]{2,1,0:T(8,128)}, f32[4,32,896]{2,1,0:T(8,128)}) custom-call(s32[2]{0:T(128)} %pad_add_fusion.place, f32[4,32,896]{2,1,0:T(8,128)} %get-tuple-element.31.refs_5_.refs_0_, f32[4,32,896]{2,1,0:T(8,128)} %copy-done.12, f32[4,32,896]{2,1,0:T(8,128)} %copy-done.13, ...), custom_call_target="tpu_custom_call" | custom-call | bytes 3670016 | tf_op jit(solution)/shard_map/pallas_call | solution.py:26
  92.8 1.1 collective-permute-start.11
  94.0 2.7 %collective-permute-start.13 = (f32[4,32,896]{2,1,0:T(8,128)}, f32[4,32,896]{2,1,0:T(8,128)S(1)}, u32[]{:S(2)}, u32[]{:S(2)}) collective-permute-start(f32[4,32,896]{2,1,0:T(8,128)} %get-tuple-element.46), channel_id=1, source_target_pairs={{0,28},{4,0},{8,4},{12,8},{16,12},{20,16},{24,20},{28,24},{1,29},{... | collective-permute-start | bytes 1376264 | tf_op jit(solution)/shard_map/ppermute | solution.py:183
  96.6 25.0 %collective-permute-done.9.refs_1_ = f32[4,32,896]{2,1,0:T(8,128)S(1)} collective-permute-done((f32[4,32,896]{2,1,0:T(8,128)S(1)}, f32[4,32,896]{2,1,0:T(8,128)S(1)}, u32[]{:S(2)}, u32[]{:S(2)}) %collective-permute-start.9) | collective-permute-done | bytes 458784 | tf_op jit(solution)/shard_map/ppermute | solution.py:179
  122.0 9.1 %collective-permute-done.10.refs_2_ = f32[4,32,896]{2,1,0:T(8,128)} collective-permute-done((f32[4,32,896]{2,1,0:T(8,128)}, f32[4,32,896]{2,1,0:T(8,128)}, u32[]{:S(2)}, u32[]{:S(2)}) %collective-permute-start.10) | collective-permute-done | bytes 458784 | tf_op jit(solution)/shard_map/ppermute | solution.py:179
  131.7 3.0 %shard_map.75 = (bf16[4,4,32,896]{3,2,1,0:T(8,128)(2,1)}, bf16[4,4,32,896]{3,2,1,0:T(8,128)(2,1)}) custom-call(s32[2]{0:T(128)} %pad_add_fusion.place, f32[4,32,896]{2,1,0:T(8,128)} %get-tuple-element.38.ready.refs_0_, f32[4,32,896]{2,1,0:T(8,128)} %copy-done.22, f32[4,32,896]{2,1,0:T(8,128)} %collective-permute-done.10.refs_2_, ...), custom_call_target="tpu_custom_call" | custom-call | bytes 104857600 | tf_op jit(solution)/shard_map/pallas_call | solution.py:26
  134.8 1.4 collective-permute-done.14.refs_3_
  136.9 3.0 %shard_map.77 = (bf16[4,4,32,896]{3,2,1,0:T(8,128)(2,1)}, bf16[4,4,32,896]{3,2,1,0:T(8,128)(2,1)}) custom-call(f32[4,32,896]{2,1,0:T(8,128)} %get-tuple-element.44.refs_0_, f32[4,32,896]{2,1,0:T(8,128)} %copy-done.19, f32[4,32,896]{2,1,0:T(8,128)} %copy-done.20, f32[4,32,896]{2,1,0:T(8,128)} %copy-done.21), custom_call_target="tpu_custom_call" | custom-call | bytes 52428800 | tf_op jit(solution)/shard_map/pallas_call | solution.py:26
  139.9 1.3 copy-done.8
  141.2 7.0 %shard_map.78 = f32[32,16,896]{2,1,0:T(8,128)} custom-call(f32[32,8,16,128]{3,2,1,0:T(8,128)} %copy-done.8, bf16[4,4,32,896]{3,2,1,0:T(8,128)(2,1)} %get-tuple-element.42.refs_0_, bf16[4,4,32,896]{3,2,1,0:T(8,128)(2,1)} %get-tuple-element.43.refs_1_, bf16[4,4,32,896]{3,2,1,0:T(8,128)(2,1)} %get-tuple-element.48.refs_2_, ...), custom_call_target="tpu_custom_call" | custom-call | flops 2818572288 | bytes 7602176 | tf_op jit(solution)/shard_map/pallas_call | solution.py:26
  148.2 6.0 %all-to-all-start.4 = ((f32[32,16,896]{2,1,0:T(8,128)}), f32[32,16,896]{2,1,0:T(8,128)S(1)}, u32[]{:S(2)}, u32[]{:S(2)}) async-start(f32[32,16,896]{2,1,0:T(8,128)} %shard_map.78), calls=%async_computation.4 | async-start | bytes 3670016 | tf_op jit(solution)/shard_map/all_to_all | solution.py:202
  155.8 41.9 %all-to-all-done.4 = f32[32,16,896]{2,1,0:T(8,128)S(1)} async-done(((f32[32,16,896]{2,1,0:T(8,128)}), f32[32,16,896]{2,1,0:T(8,128)S(1)}, u32[]{:S(2)}, u32[]{:S(2)}) %all-to-all-start.4) | async-done | bytes 1835040 | tf_op jit(solution)/shard_map/all_to_all | solution.py:202
  (84 shorter events, 15.5 us)
Async XLA Ops:
  0.6 6.9 %copy-start.23 = (f32[64,2,32]{0,2,1:T(8,128)S(1)}, f32[64,2,32]{0,2,1:T(8,128)}, u32[]{:S(2)}) copy-start(f32[64,2,32]{0,2,1:T(8,128)} %param.5) | copy-start | bytes 49156
  1.3 6.5 %copy-start.4 = (f32[2,32,1024]{2,1,0:T(8,128)S(1)}, f32[2,32,1024]{2,1,0:T(8,128)}, u32[]{:S(2)}) copy-start(f32[2,32,1024]{2,1,0:T(8,128)} %inverse.3) | copy-start | bytes 786436
  1.3 6.5 %copy-start.5 = (f32[32,1024]{1,0:T(8,128)S(1)}, f32[32,1024]{1,0:T(8,128)}, u32[]{:S(2)}) copy-start(f32[32,1024]{1,0:T(8,128)} %couple.1) | copy-start | bytes 393220
  1.3 6.5 %copy-start.6 = (s32[2]{0:T(128)S(1)}, s32[2]{0:T(128)}, u32[]{:S(2)}) copy-start(s32[2]{0:T(128)} %pad_add_fusion.place) | copy-start | bytes 28
  5.5 26.7 %collective-permute-start.3 = (f32[4,32,896]{2,1,0:T(8,128)}, f32[4,32,896]{2,1,0:T(8,128)S(1)}, u32[]{:S(2)}, u32[]{:S(2)}) collective-permute-start(f32[4,32,896]{2,1,0:T(8,128)} %get-tuple-element.32), channel_id=1, source_target_pairs={{0,4},{4,8},{8,12},{12,16},{16,20},{20,24},{24,28},{28,0},{1,5},{5... | collective-permute-start | bytes 1376264 | tf_op jit(solution)/shard_map/ppermute | solution.py:183
  9.2 17.9 %collective-permute-start = (f32[72,1024]{1,0:T(8,128)S(1)}, f32[72,1024]{1,0:T(8,128)S(1)}, u32[]{:S(2)}, u32[]{:S(2)}) collective-permute-start(f32[72,1024]{1,0:T(8,128)S(1)} %get-tuple-element.27), channel_id=1, source_target_pairs={{0,1},{1,2},{2,3},{3,0},{4,5},{5,6},{6,7},{7,4},{8,9},{9,10},{10,1... | collective-permute-start | bytes 884744 | tf_op jit(solution)/shard_map/ppermute | solution.py:179
  10.5 19.0 %collective-permute-start.1 = (f32[72,1024]{1,0:T(8,128)S(1)}, f32[72,1024]{1,0:T(8,128)S(1)}, u32[]{:S(2)}, u32[]{:S(2)}) collective-permute-start(f32[72,1024]{1,0:T(8,128)S(1)} %get-tuple-element.28), channel_id=1, source_target_pairs={{0,2},{1,3},{2,0},{3,1},{4,6},{5,7},{6,4},{7,5},{8,10},{9,11},{10,... | collective-permute-start | bytes 884744 | tf_op jit(solution)/shard_map/ppermute | solution.py:179
  11.1 19.5 %collective-permute-start.2 = (f32[72,1024]{1,0:T(8,128)S(1)}, f32[72,1024]{1,0:T(8,128)S(1)}, u32[]{:S(2)}, u32[]{:S(2)}) collective-permute-start(f32[72,1024]{1,0:T(8,128)S(1)} %get-tuple-element.29), channel_id=1, source_target_pairs={{0,3},{1,0},{2,1},{3,2},{4,7},{5,4},{6,5},{7,6},{8,11},{9,8},{10,9... | collective-permute-start | bytes 884744 | tf_op jit(solution)/shard_map/ppermute | solution.py:179
  13.2 24.0 %all-to-all-start = ((f32[32,16,128]{2,1,0:T(8,128)}), f32[32,16,128]{2,1,0:T(8,128)}, u32[]{:S(2)}, u32[]{:S(2)}) async-start(f32[32,16,128]{2,1,0:T(8,128)} %shard_map.68), calls=%async_computation | async-start | bytes 524288 | tf_op jit(solution)/shard_map/all_to_all | solution.py:202
  24.3 18.7 %collective-permute-start.4 = (f32[4,32,896]{2,1,0:T(8,128)}, f32[4,32,896]{2,1,0:T(8,128)S(1)}, u32[]{:S(2)}, u32[]{:S(2)}) collective-permute-start(f32[4,32,896]{2,1,0:T(8,128)} %get-tuple-element.33), channel_id=1, source_target_pairs={{0,28},{4,0},{8,4},{12,8},{16,12},{20,16},{24,20},{28,24},{1,29},{... | collective-permute-start | bytes 1376264 | tf_op jit(solution)/shard_map/ppermute | solution.py:183
  27.1 10.1 %copy-start.15 = (f32[72,1024]{1,0:T(8,128)}, f32[72,1024]{1,0:T(8,128)S(1)}, u32[]{:S(2)}) copy-start(f32[72,1024]{1,0:T(8,128)S(1)} %collective-permute-done.refs_1_) | copy-start | bytes 884740
  27.1 25.8 %collective-permute-start.5 = (f32[4,32,896]{2,1,0:T(8,128)}, f32[4,32,896]{2,1,0:T(8,128)S(1)}, u32[]{:S(2)}, u32[]{:S(2)}) collective-permute-start(f32[4,32,896]{2,1,0:T(8,128)} %get-tuple-element.34), channel_id=1, source_target_pairs={{0,24},{4,28},{8,0},{12,4},{16,8},{20,12},{24,16},{28,20},{32,40},... | collective-permute-start | bytes 1376264 | tf_op jit(solution)/shard_map/ppermute | solution.py:190
  29.4 7.8 %copy-start.16 = (f32[72,1024]{1,0:T(8,128)}, f32[72,1024]{1,0:T(8,128)S(1)}, u32[]{:S(2)}) copy-start(f32[72,1024]{1,0:T(8,128)S(1)} %collective-permute-done.1.refs_2_) | copy-start | bytes 884740
  29.4 23.5 %collective-permute-start.6 = (f32[4,32,896]{2,1,0:T(8,128)}, f32[4,32,896]{2,1,0:T(8,128)S(1)}, u32[]{:S(2)}, u32[]{:S(2)}) collective-permute-start(f32[4,32,896]{2,1,0:T(8,128)} %get-tuple-element.35), channel_id=1, source_target_pairs={{0,1},{1,2},{2,3},{3,0},{4,5},{5,6},{6,7},{7,4},{8,9},{9,10},{10,1... | collective-permute-start | bytes 1376264 | tf_op jit(solution)/shard_map/ppermute | solution.py:179
  31.3 21.6 %collective-permute-start.7 = (f32[4,32,896]{2,1,0:T(8,128)}, f32[4,32,896]{2,1,0:T(8,128)S(1)}, u32[]{:S(2)}, u32[]{:S(2)}) collective-permute-start(f32[4,32,896]{2,1,0:T(8,128)} %get-tuple-element.36), channel_id=1, source_target_pairs={{0,2},{1,3},{2,0},{3,1},{4,6},{5,7},{6,4},{7,5},{8,10},{9,11},{10,... | collective-permute-start | bytes 1376264 | tf_op jit(solution)/shard_map/ppermute | solution.py:179
  32.2 21.1 %copy-start.9 = (f32[4,32,896]{2,1,0:T(8,128)}, f32[4,32,896]{2,1,0:T(8,128)S(1)}, u32[]{:S(2)}) copy-start(f32[4,32,896]{2,1,0:T(8,128)S(1)} %collective-permute-done.3.refs_4_.refs_1_) | copy-start | bytes 1376260
  32.2 20.8 %collective-permute-start.8 = (f32[4,32,896]{2,1,0:T(8,128)}, f32[4,32,896]{2,1,0:T(8,128)S(1)}, u32[]{:S(2)}, u32[]{:S(2)}) collective-permute-start(f32[4,32,896]{2,1,0:T(8,128)} %get-tuple-element.37), channel_id=1, source_target_pairs={{0,3},{1,0},{2,1},{3,2},{4,7},{5,4},{6,5},{7,6},{8,11},{9,8},{10,9... | collective-permute-start | bytes 1376264 | tf_op jit(solution)/shard_map/ppermute | solution.py:179
  39.6 13.6 %all-to-all-start.1 = ((f32[8,2,16,128]{3,2,1,0:T(8,128)}), f32[8,2,16,128]{3,2,1,0:T(8,128)S(1)}, u32[]{:S(2)}, u32[]{:S(2)}) async-start(f32[8,2,16,128]{3,2,1,0:T(8,128)} %shard_map.71), calls=%async_computation.1 | async-start | bytes 262144 | tf_op jit(solution)/shard_map/all_to_all | solution.py:202
  43.0 10.2 %copy-start.10 = (f32[4,32,896]{2,1,0:T(8,128)}, f32[4,32,896]{2,1,0:T(8,128)S(1)}, u32[]{:S(2)}) copy-start(f32[4,32,896]{2,1,0:T(8,128)S(1)} %collective-permute-done.4.refs_5_.refs_2_) | copy-start | bytes 1376260
  57.2 17.1 %copy-start.3 = (f32[8,2,16,128]{3,2,1,0:T(8,128)S(1)}, f32[8,2,16,128]{3,2,1,0:T(8,128)}, u32[]{:S(2)}) copy-start(f32[8,2,16,128]{3,2,1,0:T(8,128)} %copy-done.2) | copy-start | bytes 393220
  57.2 17.1 %copy-start.7 = (s32[2]{0:T(128)S(1)}, s32[2]{0:T(128)}, u32[]{:S(2)}) copy-start(s32[2]{0:T(128)} %pad_add_fusion.place) | copy-start | bytes 28
  57.2 17.1 %all-to-all-start.2 = ((f32[8,5,16,128]{3,2,1,0:T(8,128)}), f32[8,5,16,128]{3,2,1,0:T(8,128)S(1)}, u32[]{:S(2)}, u32[]{:S(2)}) async-start(f32[8,5,16,128]{3,2,1,0:T(8,128)} %shard_map.72), calls=%async_computation.2 | async-start | bytes 655360 | tf_op jit(solution)/shard_map/all_to_all | solution.py:202
  77.5 9.8 %copy-start.24 = (f32[4,32,896]{2,1,0:T(8,128)S(1)}, f32[4,32,896]{2,1,0:T(8,128)}, u32[]{:S(2)}) copy-start(f32[4,32,896]{2,1,0:T(8,128)} %get-tuple-element.39) | copy-start | bytes 1376260
  77.5 62.4 %all-to-all-start.3 = ((f32[32,8,16,128]{3,2,1,0:T(8,128)}), f32[32,8,16,128]{3,2,1,0:T(8,128)S(1)}, u32[]{:S(2)}, u32[]{:S(2)}) async-start(f32[32,8,16,128]{3,2,1,0:T(8,128)} %shard_map.74), calls=%async_computation.3 | async-start | bytes 4194304 | tf_op jit(solution)/shard_map/all_to_all | solution.py:202
  87.2 34.4 %collective-permute-start.9 = (f32[4,32,896]{2,1,0:T(8,128)S(1)}, f32[4,32,896]{2,1,0:T(8,128)S(1)}, u32[]{:S(2)}, u32[]{:S(2)}) collective-permute-start(f32[4,32,896]{2,1,0:T(8,128)S(1)} %copy-done.24), channel_id=1, source_target_pairs={{0,1},{1,2},{2,3},{3,0},{4,5},{5,6},{6,7},{7,4},{8,9},{9,10},{10,1... | collective-permute-start | bytes 1376264 | tf_op jit(solution)/shard_map/ppermute | solution.py:179
  91.3 43.4 %collective-permute-start.12 = (f32[4,32,896]{2,1,0:T(8,128)}, f32[4,32,896]{2,1,0:T(8,128)S(1)}, u32[]{:S(2)}, u32[]{:S(2)}) collective-permute-start(f32[4,32,896]{2,1,0:T(8,128)} %get-tuple-element.45), channel_id=1, source_target_pairs={{0,4},{4,8},{8,12},{12,16},{16,20},{20,24},{24,28},{28,0},{1,5},{5... | collective-permute-start | bytes 1376264 | tf_op jit(solution)/shard_map/ppermute | solution.py:183
  92.0 39.1 %collective-permute-start.10 = (f32[4,32,896]{2,1,0:T(8,128)}, f32[4,32,896]{2,1,0:T(8,128)}, u32[]{:S(2)}, u32[]{:S(2)}) collective-permute-start(f32[4,32,896]{2,1,0:T(8,128)} %get-tuple-element.40), channel_id=1, source_target_pairs={{0,2},{1,3},{2,0},{3,1},{4,6},{5,7},{6,4},{7,5},{8,10},{9,11},{10,... | collective-permute-start | bytes 1376264 | tf_op jit(solution)/shard_map/ppermute | solution.py:179
  92.8 38.9 %collective-permute-start.11 = (f32[4,32,896]{2,1,0:T(8,128)}, f32[4,32,896]{2,1,0:T(8,128)}, u32[]{:S(2)}, u32[]{:S(2)}) collective-permute-start(f32[4,32,896]{2,1,0:T(8,128)} %get-tuple-element.41), channel_id=1, source_target_pairs={{0,3},{1,0},{2,1},{3,2},{4,7},{5,4},{6,5},{7,6},{8,11},{9,8},{10,9... | collective-permute-start | bytes 1376264 | tf_op jit(solution)/shard_map/ppermute | solution.py:179
  94.0 40.8 %collective-permute-start.13 = (f32[4,32,896]{2,1,0:T(8,128)}, f32[4,32,896]{2,1,0:T(8,128)S(1)}, u32[]{:S(2)}, u32[]{:S(2)}) collective-permute-start(f32[4,32,896]{2,1,0:T(8,128)} %get-tuple-element.46), channel_id=1, source_target_pairs={{0,28},{4,0},{8,4},{12,8},{16,12},{20,16},{24,20},{28,24},{1,29},{... | collective-permute-start | bytes 1376264 | tf_op jit(solution)/shard_map/ppermute | solution.py:183
  121.6 10.1 %copy-start.22 = (f32[4,32,896]{2,1,0:T(8,128)}, f32[4,32,896]{2,1,0:T(8,128)S(1)}, u32[]{:S(2)}) copy-start(f32[4,32,896]{2,1,0:T(8,128)S(1)} %collective-permute-done.9.refs_1_) | copy-start | bytes 1376260
  121.6 14.5 %collective-permute-start.14 = (f32[4,32,896]{2,1,0:T(8,128)}, f32[4,32,896]{2,1,0:T(8,128)S(1)}, u32[]{:S(2)}, u32[]{:S(2)}) collective-permute-start(f32[4,32,896]{2,1,0:T(8,128)} %get-tuple-element.47), channel_id=1, source_target_pairs={{0,24},{4,28},{8,0},{12,4},{16,8},{20,12},{24,16},{28,20},{32,40},... | collective-permute-start | bytes 1376264 | tf_op jit(solution)/shard_map/ppermute | solution.py:190
  148.2 49.5 %all-to-all-start.4 = ((f32[32,16,896]{2,1,0:T(8,128)}), f32[32,16,896]{2,1,0:T(8,128)S(1)}, u32[]{:S(2)}, u32[]{:S(2)}) async-start(f32[32,16,896]{2,1,0:T(8,128)} %shard_map.78), calls=%async_computation.4 | async-start | bytes 3670016 | tf_op jit(solution)/shard_map/all_to_all | solution.py:202
  (13 other events, 13.2 us)

commit v8 on v6

--- a/solution.py
+++ b/solution.py
@@ -100,7 +100,8 @@
             terms[z, k] = part(z + step)
 
 
-def close_kernel(place, first, arrived, ready, copies):
+def close_kernel(place, first, arrived, *refs):
+    copies = refs[-1]
     latter = jnp.sum(arrived[...], axis=0)
     near = [first[(place[0] + Z + step) % Z, 1] for step in NEAR]
     for target in range(X * C * Y):
@@ -232,7 +233,7 @@
     arrived = exchange(terms, "z")
     by_k = call(merge_kernel, (block,) * 4, (place, *by_y), (ANY,) * 4, (SMEM,) + (VMEM,) * 4, sems(16), moved=3670016, limit=60)
     latter_factor = to_windows(*by_k)
-    copies = call(close_kernel, f32(X * C * Y, 2 * QUAD, 16, 128), (place, first, arrived, by_r[0]), VMEM, (SMEM, VMEM, VMEM, ANY))
+    copies = call(close_kernel, f32(X * C * Y, 2 * QUAD, 16, 128), (place, first, arrived, first_factor[1], first_factor[3]), VMEM, (SMEM, VMEM, VMEM, ANY, ANY))
     rows = exchange(copies, SPREAD)
 
     update = call(

time: 196 us -> 190 us (0.969)
  waiting for transfers between devices: 102 us -> 93.4 us
  starting transfers between devices: 55.2 us -> 60 us
    all_to_all x5, waiting for transfers between devices: 56.8 us -> 48.5 us  [exchange(): return lax.all_to_all(value, axes, 0, 0, tiled=True)]
    ppermute x2, waiting for transfers between devices: 12.8 us -> 19.7 us  [shift_far(): return lax.ppermute(value, ('c', 'z'), pairs)]
    ppermute x4, waiting for transfers between devices: 14.4 us -> 8.77 us  [shift_z(): return lax.ppermute(value, 'z', [(z, (z + step) % Z) for z in range(Z)])]
    ppermute x2, starting transfers between devices: 2.31 us -> 4.95 us  [shift_far(): return lax.ppermute(value, ('c', 'z'), pairs)]
    all_to_all x5, starting transfers between devices: 36 us -> 38.1 us  [exchange(): return lax.all_to_all(value, axes, 0, 0, tiled=True)]
    unnamed x58 -> x50, local copies, waits for them, and re-layouts: 7.1 us -> 5.19 us
where the time goes in v8:
time: 190 us
  waiting for transfers between devices  93.4 us (49%)
  starting transfers between devices  60 us (32%)
  Pallas kernels  26.2 us (14%)
  local copies, waits for them, and re-layouts  7.2 us (4%)
    all_to_all x5, waiting for transfers between devices, exchange(): return lax.all_to_all(value, axes, 0, 0, tiled=True)  48.5 us
    all_to_all x5, starting transfers between devices, exchange(): return lax.all_to_all(value, axes, 0, 0, tiled=True)  38.1 us
    pallas_call x9, Pallas kernels, call(): pl.pallas_call(kernel, out_shape=outs, in_specs=in_specs, out_specs=out_s...  26.2 us
    ppermute x2, waiting for transfers between devices, shift_far(): return lax.ppermute(value, ('c', 'z'), pairs)  19.7 us
    ppermute x9, waiting for transfers between devices, shift_y(): return lax.ppermute(value, 'y', [(y, (y + step) % Y) for y in range(Y)])  16.4 us
    ppermute x9, starting transfers between devices, shift_y(): return lax.ppermute(value, 'y', [(y, (y + step) % Y) for y in range(Y)])  8.79 us
    ppermute x4, waiting for transfers between devices, shift_z(): return lax.ppermute(value, 'z', [(z, (z + step) % Z) for z in range(Z)])  8.77 us
    ppermute x4, starting transfers between devices, shift_z(): return lax.ppermute(value, 'z', [(z, (z + step) % Z) for z in range(Z)])  8.14 us
  transfers between devices with their start and end apart: 20, of which 9 were waited for; matrix products, arithmetic and copies ran while one was open for 1% of the time, Pallas kernels for 5%

profile of v8, /device:TPU:20, one launch (start us, length us, event | category | flops | bytes accessed | tf_op | source)
XLA Modules:
  0.0 189.5 jit_solution(1965982057087760757)
XLA Ops:
  1.3 4.2 %shard_map.70 = (f32[4,32,896]{2,1,0:T(8,128)}, f32[4,32,896]{2,1,0:T(8,128)}, f32[4,32,896]{2,1,0:T(8,128)}, f32[4,32,896]{2,1,0:T(8,128)}, f32[4,32,896]{2,1,0...) custom-call(s32[2]{0:T(128)} %pad_add_fusion.place, f32[2,32,14336]{2,1,0:T(8,128)} %factor.1), custom_call_target="tpu_custom_call" | custom-call | bytes 7340032 | tf_op jit(solution)/shard_map/pallas_call | solution.py:26
  5.5 2.0 %collective-permute-start.3 = (f32[4,32,896]{2,1,0:T(8,128)}, f32[4,32,896]{2,1,0:T(8,128)S(1)}, u32[]{:S(2)}, u32[]{:S(2)}) collective-permute-start(f32[4,32,896]{2,1,0:T(8,128)} %get-tuple-element.28), channel_id=1, source_target_pairs={{0,4},{4,8},{8,12},{12,16},{16,20},{20,24},{24,28},{28,0},{1,5},{5... | collective-permute-start | bytes 1376264 | tf_op jit(solution)/shard_map/ppermute | solution.py:173
  9.2 1.3 collective-permute-start
  11.1 1.1 collective-permute-start.2
  13.2 11.1 %all-to-all-start = ((f32[32,16,128]{2,1,0:T(8,128)}), f32[32,16,128]{2,1,0:T(8,128)}, u32[]{:S(2)}, u32[]{:S(2)}) async-start(f32[32,16,128]{2,1,0:T(8,128)} %shard_map.68), calls=%async_computation | async-start | bytes 524288 | tf_op jit(solution)/shard_map/all_to_all | solution.py:192
  24.3 2.8 %collective-permute-start.4 = (f32[4,32,896]{2,1,0:T(8,128)}, f32[4,32,896]{2,1,0:T(8,128)S(1)}, u32[]{:S(2)}, u32[]{:S(2)}) collective-permute-start(f32[4,32,896]{2,1,0:T(8,128)} %get-tuple-element.29), channel_id=1, source_target_pairs={{0,28},{4,0},{8,4},{12,8},{16,12},{20,16},{24,20},{28,24},{1,29},{... | collective-permute-start | bytes 1376264 | tf_op jit(solution)/shard_map/ppermute | solution.py:173
  27.1 2.3 %collective-permute-start.5 = (f32[4,32,896]{2,1,0:T(8,128)}, f32[4,32,896]{2,1,0:T(8,128)S(1)}, u32[]{:S(2)}, u32[]{:S(2)}) collective-permute-start(f32[4,32,896]{2,1,0:T(8,128)} %get-tuple-element.30), channel_id=1, source_target_pairs={{0,24},{4,28},{8,0},{12,4},{16,8},{20,12},{24,16},{28,20},{32,40},... | collective-permute-start | bytes 1376264 | tf_op jit(solution)/shard_map/ppermute | solution.py:180
  29.4 1.2 collective-permute-start.6
  31.5 1.2 collective-permute-start.8
  32.6 4.6 %all-to-all-done.arrived = f32[32,16,128]{2,1,0:T(8,128)} async-done(((f32[32,16,128]{2,1,0:T(8,128)}), f32[32,16,128]{2,1,0:T(8,128)}, u32[]{:S(2)}, u32[]{:S(2)}) %all-to-all-start) | async-done | bytes 262176 | tf_op jit(solution)/shard_map/all_to_all | solution.py:192
  37.2 2.4 %shard_map.71 = f32[8,2,16,128]{3,2,1,0:T(8,128)} custom-call(s32[2]{0:T(128)} %pad_add_fusion.place, f32[32,16,128]{2,1,0:T(8,128)} %all-to-all-done.arrived, f32[72,1024]{1,0:T(8,128)} %copy-done, f32[72,1024]{1,0:T(8,128)} %copy-done.15, f32[72,1024]{1,0:T(8,128)} %copy-done.16, f32[72,1024]{1,0:T(8,128)} %copy-done.17, ...), custom_call_target="tpu_custom_call" | custom-call | tf_op jit(solution)/shard_map/pallas_call | solution.py:26
  39.6 3.4 %all-to-all-start.1 = ((f32[8,2,16,128]{3,2,1,0:T(8,128)}), f32[8,2,16,128]{3,2,1,0:T(8,128)S(1)}, u32[]{:S(2)}, u32[]{:S(2)}) async-start(f32[8,2,16,128]{3,2,1,0:T(8,128)} %shard_map.71), calls=%async_computation.1 | async-start | bytes 262144 | tf_op jit(solution)/shard_map/all_to_all | solution.py:192
  43.0 9.9 %collective-permute-done.5.refs_6_.refs_3_ = f32[4,32,896]{2,1,0:T(8,128)S(1)} collective-permute-done((f32[4,32,896]{2,1,0:T(8,128)}, f32[4,32,896]{2,1,0:T(8,128)S(1)}, u32[]{:S(2)}, u32[]{:S(2)}) %collective-permute-start.5) | collective-permute-done | bytes 458784 | tf_op jit(solution)/shard_map/ppermute | solution.py:180
  54.6 2.4 %shard_map.72 = f32[8,5,16,128]{3,2,1,0:T(8,128)} custom-call(s32[2]{0:T(128)} %pad_add_fusion.place, f32[8,2,16,128]{3,2,1,0:T(8,128)} %copy-done.1, f32[72,1024]{1,0:T(8,128)} %copy-done, f32[72,1024]{1,0:T(8,128)} %copy-done.15, f32[72,1024]{1,0:T(8,128)} %copy-done.16, f32[72,1024]{1,0:T(8,128)} %copy-done.17, f32[4,32,896]{2,1,0:T(8,128)} %copy-done.10, ...), custom_call_target="tpu_custom_call" | custom-call | tf_op jit(solution)/shard_map/pallas_call | solution.py:26
  57.1 5.2 %all-to-all-start.2 = ((f32[8,5,16,128]{3,2,1,0:T(8,128)}), f32[8,5,16,128]{3,2,1,0:T(8,128)S(1)}, u32[]{:S(2)}, u32[]{:S(2)}) async-start(f32[8,5,16,128]{3,2,1,0:T(8,128)} %shard_map.72), calls=%async_computation.2 | async-start | bytes 655360 | tf_op jit(solution)/shard_map/all_to_all | solution.py:192
  62.3 2.8 %shard_map.73 = (f32[4,32,896]{2,1,0:T(8,128)}, f32[4,32,896]{2,1,0:T(8,128)}, f32[4,32,896]{2,1,0:T(8,128)}, f32[4,32,896]{2,1,0:T(8,128)}) custom-call(f32[4,32,896]{2,1,0:T(8,128)} %get-tuple-element.26.refs_4_.refs_0_, f32[4,32,896]{2,1,0:T(8,128)} %copy-done.10, f32[4,32,896]{2,1,0:T(8,128)} %copy-done.11, f32[4,32,896]{2,1,0:T(8,128)} %copy-done.12), custom_call_target="tpu_custom_call" | custom-call | bytes 3670016 | tf_op jit(solution)/shard_map/pallas_call | solution.py:26
  65.1 1.3 collective-permute-start.9
  67.2 9.0 %collective-permute-done.9.refs_0_.refs_1_ = f32[4,32,896]{2,1,0:T(8,128)S(1)} collective-permute-done((f32[4,32,896]{2,1,0:T(8,128)}, f32[4,32,896]{2,1,0:T(8,128)S(1)}, u32[]{:S(2)}, u32[]{:S(2)}) %collective-permute-start.9) | collective-permute-done | bytes 458784 | tf_op jit(solution)/shard_map/ppermute | solution.py:169
  76.2 2.1 %collective-permute-done.10.refs_1_.refs_3_ = f32[4,32,896]{2,1,0:T(8,128)S(1)} collective-permute-done((f32[4,32,896]{2,1,0:T(8,128)}, f32[4,32,896]{2,1,0:T(8,128)S(1)}, u32[]{:S(2)}, u32[]{:S(2)}) %collective-permute-start.10) | collective-permute-done | bytes 458784 | tf_op jit(solution)/shard_map/ppermute | solution.py:169
  78.3 2.1 %shard_map.74 = f32[32,8,16,128]{3,2,1,0:T(8,128)} custom-call(s32[2]{0:T(128)S(1)} %copy-done.8, f32[8,2,16,128]{3,2,1,0:T(8,128)S(1)} %copy-done.2, f32[8,5,16,128]{3,2,1,0:T(8,128)S(1)} %all-to-all-done.2.arrived, f32[4,32,896]{2,1,0:T(8,128)S(1)} %collective-permute-done.9.refs_0_.refs_1_, f32[4,32,896]{2,1,0:T(8,128)S(1)} %collective-permute-done.10.refs_1_.refs_3_), custom_call_target="tpu_custom_call" | custom-call | tf_op jit(solution)/shard_map/pallas_call | solution.py:26
  80.4 7.6 %all-to-all-start.3 = ((f32[32,8,16,128]{3,2,1,0:T(8,128)}), f32[32,8,16,128]{3,2,1,0:T(8,128)S(1)}, u32[]{:S(2)}, u32[]{:S(2)}) async-start(f32[32,8,16,128]{3,2,1,0:T(8,128)} %shard_map.74), calls=%async_computation.3 | async-start | bytes 4194304 | tf_op jit(solution)/shard_map/all_to_all | solution.py:192
  88.1 2.9 %shard_map.75 = (f32[4,32,896]{2,1,0:T(8,128)}, f32[4,32,896]{2,1,0:T(8,128)}, f32[4,32,896]{2,1,0:T(8,128)}, f32[4,32,896]{2,1,0:T(8,128)}) custom-call(s32[2]{0:T(128)} %pad_add_fusion.place, f32[4,32,896]{2,1,0:T(8,128)} %get-tuple-element.27.refs_5_.refs_0_, f32[4,32,896]{2,1,0:T(8,128)} %copy-done.13, f32[4,32,896]{2,1,0:T(8,128)} %copy-done.14, ...), custom_call_target="tpu_custom_call" | custom-call | bytes 3670016 | tf_op jit(solution)/shard_map/pallas_call | solution.py:26
  90.9 1.8 collective-permute-start.12
  92.7 1.5 collective-permute-start.13
  94.2 2.6 %collective-permute-start.14 = (f32[4,32,896]{2,1,0:T(8,128)}, f32[4,32,896]{2,1,0:T(8,128)S(1)}, u32[]{:S(2)}, u32[]{:S(2)}) collective-permute-start(f32[4,32,896]{2,1,0:T(8,128)} %get-tuple-element.41), channel_id=1, source_target_pairs={{0,24},{4,28},{8,0},{12,4},{16,8},{20,12},{24,16},{28,20},{32,40},... | collective-permute-start | bytes 1376264 | tf_op jit(solution)/shard_map/ppermute | solution.py:180
  97.4 8.8 %collective-permute-done.12.refs_5_ = f32[4,32,896]{2,1,0:T(8,128)S(1)} collective-permute-done((f32[4,32,896]{2,1,0:T(8,128)}, f32[4,32,896]{2,1,0:T(8,128)S(1)}, u32[]{:S(2)}, u32[]{:S(2)}) %collective-permute-start.12) | collective-permute-done | bytes 458784 | tf_op jit(solution)/shard_map/ppermute | solution.py:173
  106.2 9.8 %collective-permute-done.14.refs_7_ = f32[4,32,896]{2,1,0:T(8,128)S(1)} collective-permute-done((f32[4,32,896]{2,1,0:T(8,128)}, f32[4,32,896]{2,1,0:T(8,128)S(1)}, u32[]{:S(2)}, u32[]{:S(2)}) %collective-permute-start.14) | collective-permute-done | bytes 458784 | tf_op jit(solution)/shard_map/ppermute | solution.py:180
  116.8 5.3 %collective-permute-done.11.refs_2_ = f32[4,32,896]{2,1,0:T(8,128)} collective-permute-done((f32[4,32,896]{2,1,0:T(8,128)S(1)}, f32[4,32,896]{2,1,0:T(8,128)}, u32[]{:S(2)}, u32[]{:S(2)}) %collective-permute-start.11) | collective-permute-done | bytes 458784 | tf_op jit(solution)/shard_map/ppermute | solution.py:169
  122.1 1.3 copy-done.9
  123.5 7.7 %shard_map.76 = f32[32,16,896]{2,1,0:T(8,128)} custom-call(s32[2]{0:T(128)} %pad_add_fusion.place, f32[32,8,16,128]{3,2,1,0:T(8,128)} %copy-done.9, f32[4,32,896]{2,1,0:T(8,128)} %get-tuple-element.36.refs_0_, f32[4,32,896]{2,1,0:T(8,128)} %copy-done.4, f32[4,32,896]{2,1,0:T(8,128)} %collective-permute-done.11.refs_2_, f32[4,32,896]{2,1,0:T(8,128)} %copy-done.5, ...), custom_call_target="tpu_custom_call" | custom-call | flops 2818572288 | bytes 7602176 | tf_op jit(solution)/shard_map/pallas_call | solution.py:26
  131.2 10.8 %all-to-all-start.4 = ((f32[32,16,896]{2,1,0:T(8,128)}), f32[32,16,896]{2,1,0:T(8,128)S(1)}, u32[]{:S(2)}, u32[]{:S(2)}) async-start(f32[32,16,896]{2,1,0:T(8,128)} %shard_map.76), calls=%async_computation.4 | async-start | bytes 3670016 | tf_op jit(solution)/shard_map/all_to_all | solution.py:192
  143.7 43.6 %all-to-all-done.4 = f32[32,16,896]{2,1,0:T(8,128)S(1)} async-done(((f32[32,16,896]{2,1,0:T(8,128)}), f32[32,16,896]{2,1,0:T(8,128)S(1)}, u32[]{:S(2)}, u32[]{:S(2)}) %all-to-all-start.4) | async-done | bytes 1835040 | tf_op jit(solution)/shard_map/all_to_all | solution.py:192
  (80 shorter events, 12.6 us)
Async XLA Ops:
  0.6 6.9 %copy-start.19 = (f32[64,2,32]{0,2,1:T(8,128)S(1)}, f32[64,2,32]{0,2,1:T(8,128)}, u32[]{:S(2)}) copy-start(f32[64,2,32]{0,2,1:T(8,128)} %param.5) | copy-start | bytes 49156
  1.3 6.5 %copy-start.7 = (s32[2]{0:T(128)S(1)}, s32[2]{0:T(128)}, u32[]{:S(2)}) copy-start(s32[2]{0:T(128)} %pad_add_fusion.place) | copy-start | bytes 28
  5.5 26.0 %collective-permute-start.3 = (f32[4,32,896]{2,1,0:T(8,128)}, f32[4,32,896]{2,1,0:T(8,128)S(1)}, u32[]{:S(2)}, u32[]{:S(2)}) collective-permute-start(f32[4,32,896]{2,1,0:T(8,128)} %get-tuple-element.28), channel_id=1, source_target_pairs={{0,4},{4,8},{8,12},{12,16},{16,20},{20,24},{24,28},{28,0},{1,5},{5... | collective-permute-start | bytes 1376264 | tf_op jit(solution)/shard_map/ppermute | solution.py:173
  9.2 17.9 %collective-permute-start = (f32[72,1024]{1,0:T(8,128)S(1)}, f32[72,1024]{1,0:T(8,128)S(1)}, u32[]{:S(2)}, u32[]{:S(2)}) collective-permute-start(f32[72,1024]{1,0:T(8,128)S(1)} %get-tuple-element.23), channel_id=1, source_target_pairs={{0,1},{1,2},{2,3},{3,0},{4,5},{5,6},{6,7},{7,4},{8,9},{9,10},{10,1... | collective-permute-start | bytes 884744 | tf_op jit(solution)/shard_map/ppermute | solution.py:169
  10.5 19.0 %collective-permute-start.1 = (f32[72,1024]{1,0:T(8,128)S(1)}, f32[72,1024]{1,0:T(8,128)S(1)}, u32[]{:S(2)}, u32[]{:S(2)}) collective-permute-start(f32[72,1024]{1,0:T(8,128)S(1)} %get-tuple-element.24), channel_id=1, source_target_pairs={{0,2},{1,3},{2,0},{3,1},{4,6},{5,7},{6,4},{7,5},{8,10},{9,11},{10,... | collective-permute-start | bytes 884744 | tf_op jit(solution)/shard_map/ppermute | solution.py:169
  11.1 19.5 %collective-permute-start.2 = (f32[72,1024]{1,0:T(8,128)S(1)}, f32[72,1024]{1,0:T(8,128)S(1)}, u32[]{:S(2)}, u32[]{:S(2)}) collective-permute-start(f32[72,1024]{1,0:T(8,128)S(1)} %get-tuple-element.25), channel_id=1, source_target_pairs={{0,3},{1,0},{2,1},{3,2},{4,7},{5,4},{6,5},{7,6},{8,11},{9,8},{10,9... | collective-permute-start | bytes 884744 | tf_op jit(solution)/shard_map/ppermute | solution.py:169
  13.2 24.0 %all-to-all-start = ((f32[32,16,128]{2,1,0:T(8,128)}), f32[32,16,128]{2,1,0:T(8,128)}, u32[]{:S(2)}, u32[]{:S(2)}) async-start(f32[32,16,128]{2,1,0:T(8,128)} %shard_map.68), calls=%async_computation | async-start | bytes 524288 | tf_op jit(solution)/shard_map/all_to_all | solution.py:192
  24.3 18.7 %collective-permute-start.4 = (f32[4,32,896]{2,1,0:T(8,128)}, f32[4,32,896]{2,1,0:T(8,128)S(1)}, u32[]{:S(2)}, u32[]{:S(2)}) collective-permute-start(f32[4,32,896]{2,1,0:T(8,128)} %get-tuple-element.29), channel_id=1, source_target_pairs={{0,28},{4,0},{8,4},{12,8},{16,12},{20,16},{24,20},{28,24},{1,29},{... | collective-permute-start | bytes 1376264 | tf_op jit(solution)/shard_map/ppermute | solution.py:173
  27.1 10.1 %copy-start.15 = (f32[72,1024]{1,0:T(8,128)}, f32[72,1024]{1,0:T(8,128)S(1)}, u32[]{:S(2)}) copy-start(f32[72,1024]{1,0:T(8,128)S(1)} %collective-permute-done.refs_1_) | copy-start | bytes 884740
  27.1 25.8 %collective-permute-start.5 = (f32[4,32,896]{2,1,0:T(8,128)}, f32[4,32,896]{2,1,0:T(8,128)S(1)}, u32[]{:S(2)}, u32[]{:S(2)}) collective-permute-start(f32[4,32,896]{2,1,0:T(8,128)} %get-tuple-element.30), channel_id=1, source_target_pairs={{0,24},{4,28},{8,0},{12,4},{16,8},{20,12},{24,16},{28,20},{32,40},... | collective-permute-start | bytes 1376264 | tf_op jit(solution)/shard_map/ppermute | solution.py:180
  29.4 7.8 %copy-start.16 = (f32[72,1024]{1,0:T(8,128)}, f32[72,1024]{1,0:T(8,128)S(1)}, u32[]{:S(2)}) copy-start(f32[72,1024]{1,0:T(8,128)S(1)} %collective-permute-done.1.refs_2_) | copy-start | bytes 884740
  29.4 23.5 %collective-permute-start.6 = (f32[4,32,896]{2,1,0:T(8,128)}, f32[4,32,896]{2,1,0:T(8,128)S(1)}, u32[]{:S(2)}, u32[]{:S(2)}) collective-permute-start(f32[4,32,896]{2,1,0:T(8,128)} %get-tuple-element.31), channel_id=1, source_target_pairs={{0,1},{1,2},{2,3},{3,0},{4,5},{5,6},{6,7},{7,4},{8,9},{9,10},{10,1... | collective-permute-start | bytes 1376264 | tf_op jit(solution)/shard_map/ppermute | solution.py:169
  30.6 6.6 %copy-start.17 = (f32[72,1024]{1,0:T(8,128)}, f32[72,1024]{1,0:T(8,128)S(1)}, u32[]{:S(2)}) copy-start(f32[72,1024]{1,0:T(8,128)S(1)} %collective-permute-done.2.refs_3_) | copy-start | bytes 884740
  30.6 22.3 %collective-permute-start.7 = (f32[4,32,896]{2,1,0:T(8,128)}, f32[4,32,896]{2,1,0:T(8,128)S(1)}, u32[]{:S(2)}, u32[]{:S(2)}) collective-permute-start(f32[4,32,896]{2,1,0:T(8,128)} %get-tuple-element.32), channel_id=1, source_target_pairs={{0,2},{1,3},{2,0},{3,1},{4,6},{5,7},{6,4},{7,5},{8,10},{9,11},{10,... | collective-permute-start | bytes 1376264 | tf_op jit(solution)/shard_map/ppermute | solution.py:169
  31.5 21.8 %copy-start.10 = (f32[4,32,896]{2,1,0:T(8,128)}, f32[4,32,896]{2,1,0:T(8,128)S(1)}, u32[]{:S(2)}) copy-start(f32[4,32,896]{2,1,0:T(8,128)S(1)} %collective-permute-done.3.refs_4_.refs_1_) | copy-start | bytes 1376260
  31.5 21.5 %collective-permute-start.8 = (f32[4,32,896]{2,1,0:T(8,128)}, f32[4,32,896]{2,1,0:T(8,128)}, u32[]{:S(2)}, u32[]{:S(2)}) collective-permute-start(f32[4,32,896]{2,1,0:T(8,128)} %get-tuple-element.33), channel_id=1, source_target_pairs={{0,3},{1,0},{2,1},{3,2},{4,7},{5,4},{6,5},{7,6},{8,11},{9,8},{10,9... | collective-permute-start | bytes 1376264 | tf_op jit(solution)/shard_map/ppermute | solution.py:169
  39.6 13.6 %all-to-all-start.1 = ((f32[8,2,16,128]{3,2,1,0:T(8,128)}), f32[8,2,16,128]{3,2,1,0:T(8,128)S(1)}, u32[]{:S(2)}, u32[]{:S(2)}) async-start(f32[8,2,16,128]{3,2,1,0:T(8,128)} %shard_map.71), calls=%async_computation.1 | async-start | bytes 262144 | tf_op jit(solution)/shard_map/all_to_all | solution.py:192
  43.0 10.2 %copy-start.11 = (f32[4,32,896]{2,1,0:T(8,128)}, f32[4,32,896]{2,1,0:T(8,128)S(1)}, u32[]{:S(2)}) copy-start(f32[4,32,896]{2,1,0:T(8,128)S(1)} %collective-permute-done.4.refs_5_.refs_2_) | copy-start | bytes 1376260
  57.1 21.2 %copy-start.2 = (f32[8,2,16,128]{3,2,1,0:T(8,128)S(1)}, f32[8,2,16,128]{3,2,1,0:T(8,128)}, u32[]{:S(2)}) copy-start(f32[8,2,16,128]{3,2,1,0:T(8,128)} %copy-done.1) | copy-start | bytes 393220
  57.1 21.2 %copy-start.8 = (s32[2]{0:T(128)S(1)}, s32[2]{0:T(128)}, u32[]{:S(2)}) copy-start(s32[2]{0:T(128)} %pad_add_fusion.place) | copy-start | bytes 28
  57.1 21.2 %all-to-all-start.2 = ((f32[8,5,16,128]{3,2,1,0:T(8,128)}), f32[8,5,16,128]{3,2,1,0:T(8,128)S(1)}, u32[]{:S(2)}, u32[]{:S(2)}) async-start(f32[8,5,16,128]{3,2,1,0:T(8,128)} %shard_map.72), calls=%async_computation.2 | async-start | bytes 655360 | tf_op jit(solution)/shard_map/all_to_all | solution.py:192
  65.1 11.1 %collective-permute-start.9 = (f32[4,32,896]{2,1,0:T(8,128)}, f32[4,32,896]{2,1,0:T(8,128)S(1)}, u32[]{:S(2)}, u32[]{:S(2)}) collective-permute-start(f32[4,32,896]{2,1,0:T(8,128)} %get-tuple-element.34), channel_id=1, source_target_pairs={{0,1},{1,2},{2,3},{3,0},{4,5},{5,6},{6,7},{7,4},{8,9},{9,10},{10,1... | collective-permute-start | bytes 1376264 | tf_op jit(solution)/shard_map/ppermute | solution.py:169
  66.4 11.9 %collective-permute-start.10 = (f32[4,32,896]{2,1,0:T(8,128)}, f32[4,32,896]{2,1,0:T(8,128)S(1)}, u32[]{:S(2)}, u32[]{:S(2)}) collective-permute-start(f32[4,32,896]{2,1,0:T(8,128)} %get-tuple-element.35), channel_id=1, source_target_pairs={{0,3},{1,0},{2,1},{3,2},{4,7},{5,4},{6,5},{7,6},{8,11},{9,8},{10,9... | collective-permute-start | bytes 1376264 | tf_op jit(solution)/shard_map/ppermute | solution.py:169
  80.4 16.5 %copy-start.20 = (f32[4,32,896]{2,1,0:T(8,128)S(1)}, f32[4,32,896]{2,1,0:T(8,128)}, u32[]{:S(2)}) copy-start(f32[4,32,896]{2,1,0:T(8,128)} %get-tuple-element.37) | copy-start | bytes 1376260
  80.4 41.7 %all-to-all-start.3 = ((f32[32,8,16,128]{3,2,1,0:T(8,128)}), f32[32,8,16,128]{3,2,1,0:T(8,128)S(1)}, u32[]{:S(2)}, u32[]{:S(2)}) async-start(f32[32,8,16,128]{3,2,1,0:T(8,128)} %shard_map.74), calls=%async_computation.3 | async-start | bytes 4194304 | tf_op jit(solution)/shard_map/all_to_all | solution.py:192
  90.9 15.3 %collective-permute-start.12 = (f32[4,32,896]{2,1,0:T(8,128)}, f32[4,32,896]{2,1,0:T(8,128)S(1)}, u32[]{:S(2)}, u32[]{:S(2)}) collective-permute-start(f32[4,32,896]{2,1,0:T(8,128)} %get-tuple-element.39), channel_id=1, source_target_pairs={{0,4},{4,8},{8,12},{12,16},{16,20},{20,24},{24,28},{28,0},{1,5},{5... | collective-permute-start | bytes 1376264 | tf_op jit(solution)/shard_map/ppermute | solution.py:173
  92.7 13.4 %collective-permute-start.13 = (f32[4,32,896]{2,1,0:T(8,128)}, f32[4,32,896]{2,1,0:T(8,128)S(1)}, u32[]{:S(2)}, u32[]{:S(2)}) collective-permute-start(f32[4,32,896]{2,1,0:T(8,128)} %get-tuple-element.40), channel_id=1, source_target_pairs={{0,28},{4,0},{8,4},{12,8},{16,12},{20,16},{24,20},{28,24},{1,29},{... | collective-permute-start | bytes 1376264 | tf_op jit(solution)/shard_map/ppermute | solution.py:173
  94.2 21.8 %collective-permute-start.14 = (f32[4,32,896]{2,1,0:T(8,128)}, f32[4,32,896]{2,1,0:T(8,128)S(1)}, u32[]{:S(2)}, u32[]{:S(2)}) collective-permute-start(f32[4,32,896]{2,1,0:T(8,128)} %get-tuple-element.41), channel_id=1, source_target_pairs={{0,24},{4,28},{8,0},{12,4},{16,8},{20,12},{24,16},{28,20},{32,40},... | collective-permute-start | bytes 1376264 | tf_op jit(solution)/shard_map/ppermute | solution.py:180
  96.9 25.2 %collective-permute-start.11 = (f32[4,32,896]{2,1,0:T(8,128)S(1)}, f32[4,32,896]{2,1,0:T(8,128)}, u32[]{:S(2)}, u32[]{:S(2)}) collective-permute-start(f32[4,32,896]{2,1,0:T(8,128)S(1)} %copy-done.20), channel_id=1, source_target_pairs={{0,2},{1,3},{2,0},{3,1},{4,6},{5,7},{6,4},{7,5},{8,10},{9,11},{10,... | collective-permute-start | bytes 1376264 | tf_op jit(solution)/shard_map/ppermute | solution.py:169
  106.2 15.9 %copy-start.21 = (f32[4,32,896]{2,1,0:T(8,128)}, f32[4,32,896]{2,1,0:T(8,128)S(1)}, u32[]{:S(2)}) copy-start(f32[4,32,896]{2,1,0:T(8,128)S(1)} %collective-permute-done.12.refs_5_) | copy-start | bytes 1376260
  106.2 15.9 %copy-start.22 = (f32[4,32,896]{2,1,0:T(8,128)}, f32[4,32,896]{2,1,0:T(8,128)S(1)}, u32[]{:S(2)}) copy-start(f32[4,32,896]{2,1,0:T(8,128)S(1)} %collective-permute-done.13.refs_6_) | copy-start | bytes 1376260
  131.2 56.0 %all-to-all-start.4 = ((f32[32,16,896]{2,1,0:T(8,128)}), f32[32,16,896]{2,1,0:T(8,128)S(1)}, u32[]{:S(2)}, u32[]{:S(2)}) async-start(f32[32,16,896]{2,1,0:T(8,128)} %shard_map.76), calls=%async_computation.4 | async-start | bytes 3670016 | tf_op jit(solution)/shard_map/all_to_all | solution.py:192
  (12 other events, 26.9 us)

commit v9 on v8

--- a/solution.py
+++ b/solution.py
@@ -62,7 +62,7 @@
             terms[z * Y + y] = product[y * rows:(y + 1) * rows, z * 128:(z + 1) * 128]
 
 
-def share_kernel(place, rhs, inverse, couple, *shared):
+def share_kernel(place, rhs, inverse, couple, ready, *shared):
     for r in range(Y):
         rows = pl.ds(pl.multiple_of((place[1] + r) % Y * 16, 16), 16)
         piece = rhs[rows]
@@ -115,14 +115,14 @@
     return (z % QUAD, (z + 1) % QUAD, (z + 3) % QUAD, (z + 2) % QUAD)
 
 
-def cut_kernel(place, factor, *refs):
+def cut_kernel(place, factor, ready, *refs):
     by_class, by_y, sems = refs[:4], refs[4:8], refs[8]
     classes = around(place[0])
     width = by_y[0].shape[2]
     copies = []
     for r in range(Y):
         for k in range(QUAD):
-            strip = pl.multiple_of(((place[1] + r) % Y * QUAD + classes[k]) * width, width)
+            strip = pl.multiple_of((classes[k] * Y + (place[1] + r) % Y) * width, width)
             copies.append((factor.at[0, :, pl.ds(strip, width)], by_class[k].at[r]))
             copies.append((factor.at[1, :, pl.ds(strip, width)], by_y[r].at[k]))
     copy_all(copies, sems)
@@ -142,8 +142,6 @@
     by_r, by_k = refs[:Y], refs[Y:Y + QUAD]
     out, left, factor, result, sems = refs[-5:]
     start = lambda src, dst, i: pltpu.make_async_copy(src, dst, sems.at[i])
-    chunk = 128 // 16
-    part = lambda i: slice(i * chunk, (i + 1) * chunk)
     arriving = [start(rows, left, 0)]
     arriving += [start(by_r[r], factor.at[0, :, (place[1] + Y - r) % Y], 1 + r) for r in range(Y)]
     arriving += [start(by_k[k], factor.at[1, k], 1 + Y + k) for k in range(QUAD)]
@@ -151,15 +149,16 @@
         copy.start()
     for copy in arriving:
         copy.wait()
-    right_high, right_low = split(factor[...].reshape(2 * QUAD * 128, -1))
+    high, low = split(jnp.concatenate([left[:, k].reshape(-1, 128) for k in range(2 * QUAD)], axis=1))
     dot = functools.partial(jnp.dot, preferred_element_type=jnp.float32)
+    width = factor.shape[-1]
     sent = []
-    for i in range(left.shape[0] // chunk):
-        piece = left[part(i)]
-        high, low = split(jnp.concatenate([piece[:, k].reshape(128, 128) for k in range(2 * QUAD)], axis=1))
+    for i, begin in enumerate(range(0, width, 256)):
+        at = slice(begin, min(begin + 256, width))
+        right_high, right_low = split(factor[..., at].reshape(2 * QUAD * 128, -1))
         product = dot(high, right_high) + (dot(high, right_low) + dot(low, right_high))
-        result[part(i)] = product.reshape(chunk, 16, -1)
-        sent.append(start(result.at[part(i)], out.at[part(i)], 1 + Y + QUAD + i))
+        result[..., at] = product.reshape(left.shape[0], 16, -1)
+        sent.append(start(result.at[..., at], out.at[..., at], 1 + Y + QUAD + i))
         sent[-1].start()
     for copy in sent:
         copy.wait()
@@ -205,16 +204,16 @@
     rhs = panel_rhs.transpose(1, 0, 2)
     lanes = lax.broadcasted_iota(jnp.int32, (1, 128), 1) // narrow
     second_rhs = jnp.where(lanes == y, jnp.tile(rhs[1], (1, Y)), 0.0)
-    shared = call(
-        share_kernel, (f32(72, 1024),) * Y, (place, second_rhs, diag_inv, coupling),
-        (VMEM,) * Y, (SMEM,) + (VMEM,) * 3,
-    )
-    shared = to_ys(*shared)
     terms = call(open_kernel, f32(Z * Y, 16, 128), (rhs[0], diag_inv), VMEM, (VMEM,) * 2)
     arrived = exchange(terms, COLS)
+    shared = call(
+        share_kernel, (f32(72, 1024),) * Y, (place, second_rhs, diag_inv, coupling, terms),
+        (VMEM,) * Y, (SMEM,) + (VMEM,) * 3 + (ANY,),
+    )
+    shared = to_ys(*shared)
 
     cut = call(
-        cut_kernel, (block,) * 8, (place, trail_factor), (ANY,) * 8, (SMEM, VMEM), sems(32), moved=7340032, limit=60,
+        cut_kernel, (block,) * 8, (place, trail_factor, terms), (ANY,) * 8, (SMEM, VMEM, ANY), sems(32), moved=7340032, limit=60,
     )
     by_class, by_y = to_windows(*cut[:4]), to_ys(*cut[4:])
 
@@ -247,8 +246,8 @@
         flops=2818572288, moved=7602176, limit=60,
     )
     parts = exchange(update, COLS)
-    parts = parts.reshape(2, QUAD, Y, *parts.shape[1:])
-    reduced = trail_rhs - (parts[0] + parts[1]).transpose(2, 1, 0, 3).reshape(trail_rhs.shape)
+    parts = parts.reshape(2, QUAD * Y, *parts.shape[1:])
+    reduced = trail_rhs - (parts[0] + parts[1]).transpose(1, 0, 2).reshape(trail_rhs.shape)
 
     own = lambda panel: lax.dynamic_slice(
         rows, (prow * Y, panel * QUAD, 0, y * narrow), (Y, 1, rows.shape[2], narrow)

time: 190 us -> 195 us (1.026)
  local copies, waits for them, and re-layouts: 7.2 us -> 10.3 us
  starting transfers between devices: 60 us -> 62.5 us
    unnamed x50 -> x56, local copies, waits for them, and re-layouts: 5.19 us -> 9.26 us
  transfers between devices with their start and end apart: 20 -> 20, of which waited for: 9 -> 9; matrix products, arithmetic and copies ran while one was open for 1% -> 1% of each run, Pallas kernels for 5% -> 4%
where the time goes in v9:
time: 195 us; the launch traced here: 194 us
  waiting for transfers between devices  92.8 us (48%)
  starting transfers between devices  62.5 us (32%)
  Pallas kernels  25.6 us (13%)
  local copies, waits for them, and re-layouts  10.3 us (5%)
    all_to_all x5, waiting for transfers between devices, exchange(): return lax.all_to_all(value, axes, 0, 0, tiled=True)  47.7 us
    all_to_all x5, starting transfers between devices, exchange(): return lax.all_to_all(value, axes, 0, 0, tiled=True)  39.6 us
    pallas_call x9, Pallas kernels, call(): pl.pallas_call(kernel, out_shape=outs, in_specs=in_specs, out_specs=out_s...  25.6 us
    ppermute x2, waiting for transfers between devices, shift_far(): return lax.ppermute(value, ('c', 'z'), pairs)  19.1 us
    ppermute x9, waiting for transfers between devices, shift_y(): return lax.ppermute(value, 'y', [(y, (y + step) % Y) for y in range(Y)])  17.3 us
    ppermute x9, starting transfers between devices, shift_y(): return lax.ppermute(value, 'y', [(y, (y + step) % Y) for y in range(Y)])  9.78 us
    unnamed x56, local copies, waits for them, and re-layouts  9.26 us
    ppermute x4, waiting for transfers between devices, shift_z(): return lax.ppermute(value, 'z', [(z, (z + step) % Z) for z in range(Z)])  8.74 us
  transfers between devices with their start and end apart: 20, of which 9 were waited for; matrix products, arithmetic and copies ran while one was open for 1% of the time, Pallas kernels for 4%

profile of v9, /device:TPU:20, one launch (start us, length us, event | category | flops | bytes accessed | tf_op | source)
XLA Modules:
  0.0 193.9 jit_solution(3322174579222618066)
XLA Ops:
  4.1 4.2 %shard_map.70 = (f32[4,32,896]{2,1,0:T(8,128)}, f32[4,32,896]{2,1,0:T(8,128)}, f32[4,32,896]{2,1,0:T(8,128)}, f32[4,32,896]{2,1,0:T(8,128)}, f32[4,32,896]{2,1,0...) custom-call(s32[2]{0:T(128)} %pad_add_fusion.place, f32[2,32,14336]{2,1,0:T(8,128)} %factor.1, ...), custom_call_target="tpu_custom_call" | custom-call | bytes 7340032 | tf_op jit(solution)/shard_map/pallas_call | solution.py:26
  8.3 2.0 %collective-permute-start.3 = (f32[4,32,896]{2,1,0:T(8,128)}, f32[4,32,896]{2,1,0:T(8,128)S(1)}, u32[]{:S(2)}, u32[]{:S(2)}) collective-permute-start(f32[4,32,896]{2,1,0:T(8,128)} %get-tuple-element.28), channel_id=1, source_target_pairs={{0,4},{4,8},{8,12},{12,16},{16,20},{20,24},{24,28},{28,0},{1,5},{5... | collective-permute-start | bytes 1376264 | tf_op jit(solution)/shard_map/ppermute | solution.py:172
  12.8 1.3 collective-permute-start
  14.7 1.0 collective-permute-start.2
  15.8 11.1 %all-to-all-start = ((f32[32,16,128]{2,1,0:T(8,128)}), f32[32,16,128]{2,1,0:T(8,128)}, u32[]{:S(2)}, u32[]{:S(2)}) async-start(f32[32,16,128]{2,1,0:T(8,128)} %copy-done), calls=%async_computation | async-start | bytes 524288 | tf_op jit(solution)/shard_map/all_to_all | solution.py:191
  26.9 2.8 %collective-permute-start.4 = (f32[4,32,896]{2,1,0:T(8,128)}, f32[4,32,896]{2,1,0:T(8,128)S(1)}, u32[]{:S(2)}, u32[]{:S(2)}) collective-permute-start(f32[4,32,896]{2,1,0:T(8,128)} %get-tuple-element.29), channel_id=1, source_target_pairs={{0,28},{4,0},{8,4},{12,8},{16,12},{20,16},{24,20},{28,24},{1,29},{... | collective-permute-start | bytes 1376264 | tf_op jit(solution)/shard_map/ppermute | solution.py:172
  29.7 2.3 %collective-permute-start.5 = (f32[4,32,896]{2,1,0:T(8,128)}, f32[4,32,896]{2,1,0:T(8,128)S(1)}, u32[]{:S(2)}, u32[]{:S(2)}) collective-permute-start(f32[4,32,896]{2,1,0:T(8,128)} %get-tuple-element.30), channel_id=1, source_target_pairs={{0,24},{4,28},{8,0},{12,4},{16,8},{20,12},{24,16},{28,20},{32,40},... | collective-permute-start | bytes 1376264 | tf_op jit(solution)/shard_map/ppermute | solution.py:179
  32.0 1.2 collective-permute-start.6
  34.8 1.2 collective-permute-start.8
  35.9 3.9 %all-to-all-done.arrived = f32[32,16,128]{2,1,0:T(8,128)} async-done(((f32[32,16,128]{2,1,0:T(8,128)}), f32[32,16,128]{2,1,0:T(8,128)}, u32[]{:S(2)}, u32[]{:S(2)}) %all-to-all-start) | async-done | bytes 262176 | tf_op jit(solution)/shard_map/all_to_all | solution.py:191
  39.8 2.4 %shard_map.71 = f32[8,2,16,128]{3,2,1,0:T(8,128)} custom-call(s32[2]{0:T(128)} %pad_add_fusion.place, f32[32,16,128]{2,1,0:T(8,128)} %all-to-all-done.arrived, f32[72,1024]{1,0:T(8,128)} %copy-done.2, f32[72,1024]{1,0:T(8,128)} %copy-done.19, f32[72,1024]{1,0:T(8,128)} %copy-done.20, f32[72,1024]{1,0:T(8,128)} %copy-done.21, ...), custom_call_target="tpu_custom_call" | custom-call | tf_op jit(solution)/shard_map/pallas_call | solution.py:26
  42.2 4.0 %all-to-all-start.1 = ((f32[8,2,16,128]{3,2,1,0:T(8,128)}), f32[8,2,16,128]{3,2,1,0:T(8,128)S(1)}, u32[]{:S(2)}, u32[]{:S(2)}) async-start(f32[8,2,16,128]{3,2,1,0:T(8,128)} %shard_map.71), calls=%async_computation.1 | async-start | bytes 262144 | tf_op jit(solution)/shard_map/all_to_all | solution.py:191
  46.3 9.2 %collective-permute-done.5.refs_6_.refs_3_ = f32[4,32,896]{2,1,0:T(8,128)S(1)} collective-permute-done((f32[4,32,896]{2,1,0:T(8,128)}, f32[4,32,896]{2,1,0:T(8,128)S(1)}, u32[]{:S(2)}, u32[]{:S(2)}) %collective-permute-start.5) | collective-permute-done | bytes 458784 | tf_op jit(solution)/shard_map/ppermute | solution.py:179
  57.4 2.4 %shard_map.72 = f32[8,5,16,128]{3,2,1,0:T(8,128)} custom-call(s32[2]{0:T(128)} %pad_add_fusion.place, f32[8,2,16,128]{3,2,1,0:T(8,128)} %copy-done.3, f32[72,1024]{1,0:T(8,128)} %copy-done.2, f32[72,1024]{1,0:T(8,128)} %copy-done.19, f32[72,1024]{1,0:T(8,128)} %copy-done.20, f32[72,1024]{1,0:T(8,128)} %copy-done.21, f32[4,32,896]{2,1,0:T(8,128)} %copy-done.13, ...), custom_call_target="tpu_custom_call" | custom-call | tf_op jit(solution)/shard_map/pallas_call | solution.py:26
  59.8 6.0 %all-to-all-start.2 = ((f32[8,5,16,128]{3,2,1,0:T(8,128)}), f32[8,5,16,128]{3,2,1,0:T(8,128)S(1)}, u32[]{:S(2)}, u32[]{:S(2)}) async-start(f32[8,5,16,128]{3,2,1,0:T(8,128)} %shard_map.72), calls=%async_computation.2 | async-start | bytes 655360 | tf_op jit(solution)/shard_map/all_to_all | solution.py:191
  65.8 2.9 %shard_map.73 = (f32[4,32,896]{2,1,0:T(8,128)}, f32[4,32,896]{2,1,0:T(8,128)}, f32[4,32,896]{2,1,0:T(8,128)}, f32[4,32,896]{2,1,0:T(8,128)}) custom-call(f32[4,32,896]{2,1,0:T(8,128)} %get-tuple-element.26.refs_4_.refs_0_, f32[4,32,896]{2,1,0:T(8,128)} %copy-done.13, f32[4,32,896]{2,1,0:T(8,128)} %copy-done.14, f32[4,32,896]{2,1,0:T(8,128)} %copy-done.15), custom_call_target="tpu_custom_call" | custom-call | bytes 3670016 | tf_op jit(solution)/shard_map/pallas_call | solution.py:26
  68.7 3.1 %collective-permute-start.9 = (f32[4,32,896]{2,1,0:T(8,128)}, f32[4,32,896]{2,1,0:T(8,128)S(1)}, u32[]{:S(2)}, u32[]{:S(2)}) collective-permute-start(f32[4,32,896]{2,1,0:T(8,128)} %get-tuple-element.34), channel_id=1, source_target_pairs={{0,1},{1,2},{2,3},{3,0},{4,5},{5,6},{6,7},{7,4},{8,9},{9,10},{10,1... | collective-permute-start | bytes 1376264 | tf_op jit(solution)/shard_map/ppermute | solution.py:168
  71.8 9.8 %collective-permute-done.9.refs_0_.refs_1_ = f32[4,32,896]{2,1,0:T(8,128)S(1)} collective-permute-done((f32[4,32,896]{2,1,0:T(8,128)}, f32[4,32,896]{2,1,0:T(8,128)S(1)}, u32[]{:S(2)}, u32[]{:S(2)}) %collective-permute-start.9) | collective-permute-done | bytes 458784 | tf_op jit(solution)/shard_map/ppermute | solution.py:168
  81.6 2.1 %collective-permute-done.10.refs_1_.refs_3_ = f32[4,32,896]{2,1,0:T(8,128)S(1)} collective-permute-done((f32[4,32,896]{2,1,0:T(8,128)}, f32[4,32,896]{2,1,0:T(8,128)S(1)}, u32[]{:S(2)}, u32[]{:S(2)}) %collective-permute-start.10) | collective-permute-done | bytes 458784 | tf_op jit(solution)/shard_map/ppermute | solution.py:168
  83.7 2.1 %shard_map.74 = f32[32,8,16,128]{3,2,1,0:T(8,128)} custom-call(s32[2]{0:T(128)S(1)} %copy-done.11, f32[8,2,16,128]{3,2,1,0:T(8,128)S(1)} %copy-done.4, f32[8,5,16,128]{3,2,1,0:T(8,128)S(1)} %all-to-all-done.2.arrived, f32[4,32,896]{2,1,0:T(8,128)S(1)} %collective-permute-done.9.refs_0_.refs_1_, f32[4,32,896]{2,1,0:T(8,128)S(1)} %collective-permute-done.10.refs_1_.refs_3_), custom_call_target="tpu_custom_call" | custom-call | tf_op jit(solution)/shard_map/pallas_call | solution.py:26
  85.8 7.6 %all-to-all-start.3 = ((f32[32,8,16,128]{3,2,1,0:T(8,128)}), f32[32,8,16,128]{3,2,1,0:T(8,128)S(1)}, u32[]{:S(2)}, u32[]{:S(2)}) async-start(f32[32,8,16,128]{3,2,1,0:T(8,128)} %shard_map.74), calls=%async_computation.3 | async-start | bytes 4194304 | tf_op jit(solution)/shard_map/all_to_all | solution.py:191
  93.5 2.8 %shard_map.75 = (f32[4,32,896]{2,1,0:T(8,128)}, f32[4,32,896]{2,1,0:T(8,128)}, f32[4,32,896]{2,1,0:T(8,128)}, f32[4,32,896]{2,1,0:T(8,128)}) custom-call(s32[2]{0:T(128)} %pad_add_fusion.place, f32[4,32,896]{2,1,0:T(8,128)} %get-tuple-element.27.refs_5_.refs_0_, f32[4,32,896]{2,1,0:T(8,128)} %copy-done.16, f32[4,32,896]{2,1,0:T(8,128)} %copy-done.17, ...), custom_call_target="tpu_custom_call" | custom-call | bytes 3670016 | tf_op jit(solution)/shard_map/pallas_call | solution.py:26
  96.3 1.8 collective-permute-start.12
  98.1 1.5 collective-permute-start.13
  99.6 2.6 %collective-permute-start.14 = (f32[4,32,896]{2,1,0:T(8,128)}, f32[4,32,896]{2,1,0:T(8,128)S(1)}, u32[]{:S(2)}, u32[]{:S(2)}) collective-permute-start(f32[4,32,896]{2,1,0:T(8,128)} %get-tuple-element.41), channel_id=1, source_target_pairs={{0,24},{4,28},{8,0},{12,4},{16,8},{20,12},{24,16},{28,20},{32,40},... | collective-permute-start | bytes 1376264 | tf_op jit(solution)/shard_map/ppermute | solution.py:179
  102.8 8.7 %collective-permute-done.12.refs_5_ = f32[4,32,896]{2,1,0:T(8,128)S(1)} collective-permute-done((f32[4,32,896]{2,1,0:T(8,128)}, f32[4,32,896]{2,1,0:T(8,128)S(1)}, u32[]{:S(2)}, u32[]{:S(2)}) %collective-permute-start.12) | collective-permute-done | bytes 458784 | tf_op jit(solution)/shard_map/ppermute | solution.py:172
  111.6 9.8 %collective-permute-done.14.refs_7_ = f32[4,32,896]{2,1,0:T(8,128)S(1)} collective-permute-done((f32[4,32,896]{2,1,0:T(8,128)}, f32[4,32,896]{2,1,0:T(8,128)S(1)}, u32[]{:S(2)}, u32[]{:S(2)}) %collective-permute-start.14) | collective-permute-done | bytes 458784 | tf_op jit(solution)/shard_map/ppermute | solution.py:179
  122.2 5.4 %collective-permute-done.11.refs_2_ = f32[4,32,896]{2,1,0:T(8,128)} collective-permute-done((f32[4,32,896]{2,1,0:T(8,128)S(1)}, f32[4,32,896]{2,1,0:T(8,128)}, u32[]{:S(2)}, u32[]{:S(2)}) %collective-permute-start.11) | collective-permute-done | bytes 458784 | tf_op jit(solution)/shard_map/ppermute | solution.py:168
  127.6 1.3 copy-done.12
  128.9 7.8 %shard_map.76 = f32[32,16,896]{2,1,0:T(8,128)} custom-call(s32[2]{0:T(128)} %pad_add_fusion.place, f32[32,8,16,128]{3,2,1,0:T(8,128)} %copy-done.12, f32[4,32,896]{2,1,0:T(8,128)} %get-tuple-element.36.refs_0_, f32[4,32,896]{2,1,0:T(8,128)} %copy-done.7, f32[4,32,896]{2,1,0:T(8,128)} %collective-permute-done.11.refs_2_, f32[4,32,896]{2,1,0:T(8,128)} %copy-done.8, ...), custom_call_target="tpu_custom_call" | custom-call | flops 2818572288 | bytes 7602176 | tf_op jit(solution)/shard_map/pallas_call | solution.py:26
  136.7 10.8 %all-to-all-start.4 = ((f32[32,16,896]{2,1,0:T(8,128)}), f32[32,16,896]{2,1,0:T(8,128)S(1)}, u32[]{:S(2)}, u32[]{:S(2)}) async-start(f32[32,16,896]{2,1,0:T(8,128)} %shard_map.76), calls=%async_computation.4 | async-start | bytes 3670016 | tf_op jit(solution)/shard_map/all_to_all | solution.py:191
  149.1 43.6 %all-to-all-done.4 = f32[32,16,896]{2,1,0:T(8,128)S(1)} async-done(((f32[32,16,896]{2,1,0:T(8,128)}), f32[32,16,896]{2,1,0:T(8,128)S(1)}, u32[]{:S(2)}, u32[]{:S(2)}) %all-to-all-start.4) | async-done | bytes 1835040 | tf_op jit(solution)/shard_map/all_to_all | solution.py:191
  (85 shorter events, 14.1 us)
Async XLA Ops:
  4.1 6.4 %copy-start.9 = (f32[32,1024]{1,0:T(8,128)S(1)}, f32[32,1024]{1,0:T(8,128)}, u32[]{:S(2)}) copy-start(f32[32,1024]{1,0:T(8,128)} %couple.1) | copy-start | bytes 393220
  4.1 6.4 %copy-start.10 = (s32[2]{0:T(128)S(1)}, s32[2]{0:T(128)}, u32[]{:S(2)}) copy-start(s32[2]{0:T(128)} %pad_add_fusion.place) | copy-start | bytes 28
  8.3 26.5 %collective-permute-start.3 = (f32[4,32,896]{2,1,0:T(8,128)}, f32[4,32,896]{2,1,0:T(8,128)S(1)}, u32[]{:S(2)}, u32[]{:S(2)}) collective-permute-start(f32[4,32,896]{2,1,0:T(8,128)} %get-tuple-element.28), channel_id=1, source_target_pairs={{0,4},{4,8},{8,12},{12,16},{16,20},{20,24},{24,28},{28,0},{1,5},{5... | collective-permute-start | bytes 1376264 | tf_op jit(solution)/shard_map/ppermute | solution.py:172
  12.8 16.9 %collective-permute-start = (f32[72,1024]{1,0:T(8,128)S(1)}, f32[72,1024]{1,0:T(8,128)S(1)}, u32[]{:S(2)}, u32[]{:S(2)}) collective-permute-start(f32[72,1024]{1,0:T(8,128)S(1)} %get-tuple-element.23), channel_id=1, source_target_pairs={{0,1},{1,2},{2,3},{3,0},{4,5},{5,6},{6,7},{7,4},{8,9},{9,10},{10,1... | collective-permute-start | bytes 884744 | tf_op jit(solution)/shard_map/ppermute | solution.py:168
  14.1 17.9 %collective-permute-start.1 = (f32[72,1024]{1,0:T(8,128)S(1)}, f32[72,1024]{1,0:T(8,128)S(1)}, u32[]{:S(2)}, u32[]{:S(2)}) collective-permute-start(f32[72,1024]{1,0:T(8,128)S(1)} %get-tuple-element.24), channel_id=1, source_target_pairs={{0,2},{1,3},{2,0},{3,1},{4,6},{5,7},{6,4},{7,5},{8,10},{9,11},{10,... | collective-permute-start | bytes 884744 | tf_op jit(solution)/shard_map/ppermute | solution.py:168
  14.7 18.5 %collective-permute-start.2 = (f32[72,1024]{1,0:T(8,128)S(1)}, f32[72,1024]{1,0:T(8,128)S(1)}, u32[]{:S(2)}, u32[]{:S(2)}) collective-permute-start(f32[72,1024]{1,0:T(8,128)S(1)} %get-tuple-element.25), channel_id=1, source_target_pairs={{0,3},{1,0},{2,1},{3,2},{4,7},{5,4},{6,5},{7,6},{8,11},{9,8},{10,9... | collective-permute-start | bytes 884744 | tf_op jit(solution)/shard_map/ppermute | solution.py:168
  15.8 24.0 %all-to-all-start = ((f32[32,16,128]{2,1,0:T(8,128)}), f32[32,16,128]{2,1,0:T(8,128)}, u32[]{:S(2)}, u32[]{:S(2)}) async-start(f32[32,16,128]{2,1,0:T(8,128)} %copy-done), calls=%async_computation | async-start | bytes 524288 | tf_op jit(solution)/shard_map/all_to_all | solution.py:191
  26.9 19.4 %collective-permute-start.4 = (f32[4,32,896]{2,1,0:T(8,128)}, f32[4,32,896]{2,1,0:T(8,128)S(1)}, u32[]{:S(2)}, u32[]{:S(2)}) collective-permute-start(f32[4,32,896]{2,1,0:T(8,128)} %get-tuple-element.29), channel_id=1, source_target_pairs={{0,28},{4,0},{8,4},{12,8},{16,12},{20,16},{24,20},{28,24},{1,29},{... | collective-permute-start | bytes 1376264 | tf_op jit(solution)/shard_map/ppermute | solution.py:172
  29.7 10.1 %copy-start.19 = (f32[72,1024]{1,0:T(8,128)}, f32[72,1024]{1,0:T(8,128)S(1)}, u32[]{:S(2)}) copy-start(f32[72,1024]{1,0:T(8,128)S(1)} %collective-permute-done.refs_1_) | copy-start | bytes 884740
  29.7 25.8 %collective-permute-start.5 = (f32[4,32,896]{2,1,0:T(8,128)}, f32[4,32,896]{2,1,0:T(8,128)S(1)}, u32[]{:S(2)}, u32[]{:S(2)}) collective-permute-start(f32[4,32,896]{2,1,0:T(8,128)} %get-tuple-element.30), channel_id=1, source_target_pairs={{0,24},{4,28},{8,0},{12,4},{16,8},{20,12},{24,16},{28,20},{32,40},... | collective-permute-start | bytes 1376264 | tf_op jit(solution)/shard_map/ppermute | solution.py:179
  32.0 7.8 %copy-start.20 = (f32[72,1024]{1,0:T(8,128)}, f32[72,1024]{1,0:T(8,128)S(1)}, u32[]{:S(2)}) copy-start(f32[72,1024]{1,0:T(8,128)S(1)} %collective-permute-done.1.refs_2_) | copy-start | bytes 884740
  32.0 23.5 %collective-permute-start.6 = (f32[4,32,896]{2,1,0:T(8,128)}, f32[4,32,896]{2,1,0:T(8,128)S(1)}, u32[]{:S(2)}, u32[]{:S(2)}) collective-permute-start(f32[4,32,896]{2,1,0:T(8,128)} %get-tuple-element.31), channel_id=1, source_target_pairs={{0,1},{1,2},{2,3},{3,0},{4,5},{5,6},{6,7},{7,4},{8,9},{9,10},{10,1... | collective-permute-start | bytes 1376264 | tf_op jit(solution)/shard_map/ppermute | solution.py:168
  33.9 21.6 %collective-permute-start.7 = (f32[4,32,896]{2,1,0:T(8,128)}, f32[4,32,896]{2,1,0:T(8,128)S(1)}, u32[]{:S(2)}, u32[]{:S(2)}) collective-permute-start(f32[4,32,896]{2,1,0:T(8,128)} %get-tuple-element.32), channel_id=1, source_target_pairs={{0,2},{1,3},{2,0},{3,1},{4,6},{5,7},{6,4},{7,5},{8,10},{9,11},{10,... | collective-permute-start | bytes 1376264 | tf_op jit(solution)/shard_map/ppermute | solution.py:168
  34.8 21.1 %copy-start.13 = (f32[4,32,896]{2,1,0:T(8,128)}, f32[4,32,896]{2,1,0:T(8,128)S(1)}, u32[]{:S(2)}) copy-start(f32[4,32,896]{2,1,0:T(8,128)S(1)} %collective-permute-done.3.refs_4_.refs_1_) | copy-start | bytes 1376260
  34.8 20.7 %collective-permute-start.8 = (f32[4,32,896]{2,1,0:T(8,128)}, f32[4,32,896]{2,1,0:T(8,128)S(1)}, u32[]{:S(2)}, u32[]{:S(2)}) collective-permute-start(f32[4,32,896]{2,1,0:T(8,128)} %get-tuple-element.33), channel_id=1, source_target_pairs={{0,3},{1,0},{2,1},{3,2},{4,7},{5,4},{6,5},{7,6},{8,11},{9,8},{10,9... | collective-permute-start | bytes 1376264 | tf_op jit(solution)/shard_map/ppermute | solution.py:168
  42.2 13.6 %all-to-all-start.1 = ((f32[8,2,16,128]{3,2,1,0:T(8,128)}), f32[8,2,16,128]{3,2,1,0:T(8,128)S(1)}, u32[]{:S(2)}, u32[]{:S(2)}) async-start(f32[8,2,16,128]{3,2,1,0:T(8,128)} %shard_map.71), calls=%async_computation.1 | async-start | bytes 262144 | tf_op jit(solution)/shard_map/all_to_all | solution.py:191
  46.2 9.6 %copy-start.14 = (f32[4,32,896]{2,1,0:T(8,128)}, f32[4,32,896]{2,1,0:T(8,128)S(1)}, u32[]{:S(2)}) copy-start(f32[4,32,896]{2,1,0:T(8,128)S(1)} %collective-permute-done.4.refs_5_.refs_2_) | copy-start | bytes 1376260
  59.8 23.9 %copy-start.4 = (f32[8,2,16,128]{3,2,1,0:T(8,128)S(1)}, f32[8,2,16,128]{3,2,1,0:T(8,128)}, u32[]{:S(2)}) copy-start(f32[8,2,16,128]{3,2,1,0:T(8,128)} %copy-done.3) | copy-start | bytes 393220
  59.8 23.9 %copy-start.11 = (s32[2]{0:T(128)S(1)}, s32[2]{0:T(128)}, u32[]{:S(2)}) copy-start(s32[2]{0:T(128)} %pad_add_fusion.place) | copy-start | bytes 28
  59.8 23.9 %all-to-all-start.2 = ((f32[8,5,16,128]{3,2,1,0:T(8,128)}), f32[8,5,16,128]{3,2,1,0:T(8,128)S(1)}, u32[]{:S(2)}, u32[]{:S(2)}) async-start(f32[8,5,16,128]{3,2,1,0:T(8,128)} %shard_map.72), calls=%async_computation.2 | async-start | bytes 655360 | tf_op jit(solution)/shard_map/all_to_all | solution.py:191
  68.7 12.9 %collective-permute-start.9 = (f32[4,32,896]{2,1,0:T(8,128)}, f32[4,32,896]{2,1,0:T(8,128)S(1)}, u32[]{:S(2)}, u32[]{:S(2)}) collective-permute-start(f32[4,32,896]{2,1,0:T(8,128)} %get-tuple-element.34), channel_id=1, source_target_pairs={{0,1},{1,2},{2,3},{3,0},{4,5},{5,6},{6,7},{7,4},{8,9},{9,10},{10,1... | collective-permute-start | bytes 1376264 | tf_op jit(solution)/shard_map/ppermute | solution.py:168
  71.8 11.9 %collective-permute-start.10 = (f32[4,32,896]{2,1,0:T(8,128)}, f32[4,32,896]{2,1,0:T(8,128)S(1)}, u32[]{:S(2)}, u32[]{:S(2)}) collective-permute-start(f32[4,32,896]{2,1,0:T(8,128)} %get-tuple-element.35), channel_id=1, source_target_pairs={{0,3},{1,0},{2,1},{3,2},{4,7},{5,4},{6,5},{7,6},{8,11},{9,8},{10,9... | collective-permute-start | bytes 1376264 | tf_op jit(solution)/shard_map/ppermute | solution.py:168
  85.8 16.4 %copy-start.23 = (f32[4,32,896]{2,1,0:T(8,128)S(1)}, f32[4,32,896]{2,1,0:T(8,128)}, u32[]{:S(2)}) copy-start(f32[4,32,896]{2,1,0:T(8,128)} %get-tuple-element.37) | copy-start | bytes 1376260
  85.8 41.7 %all-to-all-start.3 = ((f32[32,8,16,128]{3,2,1,0:T(8,128)}), f32[32,8,16,128]{3,2,1,0:T(8,128)S(1)}, u32[]{:S(2)}, u32[]{:S(2)}) async-start(f32[32,8,16,128]{3,2,1,0:T(8,128)} %shard_map.74), calls=%async_computation.3 | async-start | bytes 4194304 | tf_op jit(solution)/shard_map/all_to_all | solution.py:191
  96.3 15.3 %collective-permute-start.12 = (f32[4,32,896]{2,1,0:T(8,128)}, f32[4,32,896]{2,1,0:T(8,128)S(1)}, u32[]{:S(2)}, u32[]{:S(2)}) collective-permute-start(f32[4,32,896]{2,1,0:T(8,128)} %get-tuple-element.39), channel_id=1, source_target_pairs={{0,4},{4,8},{8,12},{12,16},{16,20},{20,24},{24,28},{28,0},{1,5},{5... | collective-permute-start | bytes 1376264 | tf_op jit(solution)/shard_map/ppermute | solution.py:172
  98.1 13.4 %collective-permute-start.13 = (f32[4,32,896]{2,1,0:T(8,128)}, f32[4,32,896]{2,1,0:T(8,128)S(1)}, u32[]{:S(2)}, u32[]{:S(2)}) collective-permute-start(f32[4,32,896]{2,1,0:T(8,128)} %get-tuple-element.40), channel_id=1, source_target_pairs={{0,28},{4,0},{8,4},{12,8},{16,12},{20,16},{24,20},{28,24},{1,29},{... | collective-permute-start | bytes 1376264 | tf_op jit(solution)/shard_map/ppermute | solution.py:172
  99.6 21.8 %collective-permute-start.14 = (f32[4,32,896]{2,1,0:T(8,128)}, f32[4,32,896]{2,1,0:T(8,128)S(1)}, u32[]{:S(2)}, u32[]{:S(2)}) collective-permute-start(f32[4,32,896]{2,1,0:T(8,128)} %get-tuple-element.41), channel_id=1, source_target_pairs={{0,24},{4,28},{8,0},{12,4},{16,8},{20,12},{24,16},{28,20},{32,40},... | collective-permute-start | bytes 1376264 | tf_op jit(solution)/shard_map/ppermute | solution.py:179
  102.3 25.3 %collective-permute-start.11 = (f32[4,32,896]{2,1,0:T(8,128)S(1)}, f32[4,32,896]{2,1,0:T(8,128)}, u32[]{:S(2)}, u32[]{:S(2)}) collective-permute-start(f32[4,32,896]{2,1,0:T(8,128)S(1)} %copy-done.23), channel_id=1, source_target_pairs={{0,2},{1,3},{2,0},{3,1},{4,6},{5,7},{6,4},{7,5},{8,10},{9,11},{10,... | collective-permute-start | bytes 1376264 | tf_op jit(solution)/shard_map/ppermute | solution.py:168
  111.6 16.0 %copy-start.24 = (f32[4,32,896]{2,1,0:T(8,128)}, f32[4,32,896]{2,1,0:T(8,128)S(1)}, u32[]{:S(2)}) copy-start(f32[4,32,896]{2,1,0:T(8,128)S(1)} %collective-permute-done.12.refs_5_) | copy-start | bytes 1376260
  111.6 16.0 %copy-start.25 = (f32[4,32,896]{2,1,0:T(8,128)}, f32[4,32,896]{2,1,0:T(8,128)S(1)}, u32[]{:S(2)}) copy-start(f32[4,32,896]{2,1,0:T(8,128)S(1)} %collective-permute-done.13.refs_6_) | copy-start | bytes 1376260
  136.7 56.0 %all-to-all-start.4 = ((f32[32,16,896]{2,1,0:T(8,128)}), f32[32,16,896]{2,1,0:T(8,128)S(1)}, u32[]{:S(2)}, u32[]{:S(2)}) async-start(f32[32,16,896]{2,1,0:T(8,128)} %shard_map.76), calls=%async_computation.4 | async-start | bytes 3670016 | tf_op jit(solution)/shard_map/all_to_all | solution.py:191
  149.1 43.7 %copy-start.22 = (f32[16,14336]{1,0:T(8,128)S(1)}, f32[16,14336]{1,0:T(8,128)}, u32[]{:S(2)}) copy-start(f32[16,14336]{1,0:T(8,128)} %param.9) | copy-start | bytes 2752516
  (15 other events, 23.6 us)

commit v10 on v9

--- a/solution.py
+++ b/solution.py
@@ -62,7 +62,7 @@
             terms[z * Y + y] = product[y * rows:(y + 1) * rows, z * 128:(z + 1) * 128]
 
 
-def share_kernel(place, rhs, inverse, couple, ready, *shared):
+def share_kernel(place, rhs, inverse, couple, *shared):
     for r in range(Y):
         rows = pl.ds(pl.multiple_of((place[1] + r) % Y * 16, 16), 16)
         piece = rhs[rows]
@@ -140,25 +140,22 @@
 
 def update_kernel(place, rows, *refs):
     by_r, by_k = refs[:Y], refs[Y:Y + QUAD]
-    out, left, factor, result, sems = refs[-5:]
-    start = lambda src, dst, i: pltpu.make_async_copy(src, dst, sems.at[i])
-    arriving = [start(rows, left, 0)]
-    arriving += [start(by_r[r], factor.at[0, :, (place[1] + Y - r) % Y], 1 + r) for r in range(Y)]
-    arriving += [start(by_k[k], factor.at[1, k], 1 + Y + k) for k in range(QUAD)]
-    for copy in arriving:
-        copy.start()
-    for copy in arriving:
-        copy.wait()
-    high, low = split(jnp.concatenate([left[:, k].reshape(-1, 128) for k in range(2 * QUAD)], axis=1))
+    out, high, low, result, sems = refs[Y + QUAD:]
+    for r in range(Y):
+        slot = (place[1] + Y - r) % Y
+        high[0, :, slot], low[0, :, slot] = split(by_r[r][...])
+    for k in range(QUAD):
+        high[1, k], low[1, k] = split(by_k[k][...])
+    left_high, left_low = split(jnp.concatenate([rows[:, k].reshape(-1, 128) for k in range(2 * QUAD)], axis=1))
     dot = functools.partial(jnp.dot, preferred_element_type=jnp.float32)
-    width = factor.shape[-1]
+    width = result.shape[2]
     sent = []
     for i, begin in enumerate(range(0, width, 256)):
         at = slice(begin, min(begin + 256, width))
-        right_high, right_low = split(factor[..., at].reshape(2 * QUAD * 128, -1))
-        product = dot(high, right_high) + (dot(high, right_low) + dot(low, right_high))
-        result[..., at] = product.reshape(left.shape[0], 16, -1)
-        sent.append(start(result.at[..., at], out.at[..., at], 1 + Y + QUAD + i))
+        right_high, right_low = (part[..., at].reshape(2 * QUAD * 128, -1) for part in (high, low))
+        product = dot(left_high, right_high) + (dot(left_high, right_low) + dot(left_low, right_high))
+        result[..., at] = product.reshape(result.shape[0], 16, -1)
+        sent.append(pltpu.make_async_copy(result.at[..., at], out.at[..., at], sems.at[i]))
         sent[-1].start()
     for copy in sent:
         copy.wait()
@@ -207,13 +204,13 @@
     terms = call(open_kernel, f32(Z * Y, 16, 128), (rhs[0], diag_inv), VMEM, (VMEM,) * 2)
     arrived = exchange(terms, COLS)
     shared = call(
-        share_kernel, (f32(72, 1024),) * Y, (place, second_rhs, diag_inv, coupling, terms),
-        (VMEM,) * Y, (SMEM,) + (VMEM,) * 3 + (ANY,),
+        share_kernel, (f32(72, 1024),) * Y, (place, second_rhs, diag_inv, coupling),
+        (VMEM,) * Y, (SMEM,) + (VMEM,) * 3,
     )
     shared = to_ys(*shared)
 
     cut = call(
-        cut_kernel, (block,) * 8, (place, trail_factor, terms), (ANY,) * 8, (SMEM, VMEM, ANY), sems(32), moved=7340032, limit=60,
+        cut_kernel, (block,) * 8, (place, trail_factor, shared[1]), (ANY,) * 8, (SMEM, VMEM, ANY), sems(32), moved=7340032, limit=60,
     )
     by_class, by_y = to_windows(*cut[:4]), to_ys(*cut[4:])
 
@@ -235,15 +232,11 @@
     copies = call(close_kernel, f32(X * C * Y, 2 * QUAD, 16, 128), (place, first, arrived, first_factor[1], first_factor[3]), VMEM, (SMEM, VMEM, VMEM, ANY, ANY))
     rows = exchange(copies, SPREAD)
 
+    part = pltpu.VMEM((2, QUAD, *block.shape), jnp.bfloat16)
     update = call(
         update_kernel, f32(X * C * Y, 16, width), (place, rows, *first_factor, *latter_factor),
-        ANY, (SMEM,) + (ANY,) * 9,
-        [
-            pltpu.VMEM(rows.shape, jnp.float32),
-            pltpu.VMEM((2, QUAD, Y, 32, width), jnp.float32),
-            pltpu.VMEM((X * C * Y, 16, width), jnp.float32),
-        ] + sems(17),
-        flops=2818572288, moved=7602176, limit=60,
+        ANY, (SMEM,) + (VMEM,) * 9, [part, part, pltpu.VMEM((X * C * Y, 16, width), jnp.float32)] + sems(4),
+        flops=2818572288, moved=7602176, limit=24,
     )
     parts = exchange(update, COLS)
     parts = parts.reshape(2, QUAD * Y, *parts.shape[1:])

time: 195 us -> 209 us (1.072)
  blocking collectives: 0 us -> 13.1 us
  local copies, waits for them, and re-layouts: 10.3 us -> 17.2 us
  starting transfers between devices: 62.5 us -> 57.7 us
  waiting for transfers between devices: 92.8 us -> 89.4 us
    all_to_all x0 -> x1, blocking collectives: none -> 13.1 us  [exchange(): return lax.all_to_all(value, axes, 0, 0, tiled=True)]
    ppermute x2, waiting for transfers between devices: 19.1 us -> 8.3 us  [shift_far(): return lax.ppermute(value, ('c', 'z'), pairs)]
    unnamed x56 -> x60, local copies, waits for them, and re-layouts: 9.26 us -> 16.9 us
    ppermute x9, waiting for transfers between devices: 17.3 us -> 23.9 us  [shift_y(): return lax.ppermute(value, 'y', [(y, (y + step) % Y) for y in range(Y)])]
    all_to_all x5 -> x4, starting transfers between devices: 39.6 us -> 34.7 us  [exchange(): return lax.all_to_all(value, axes, 0, 0, tiled=True)]
    all_to_all x5 -> x4, waiting for transfers between devices: 47.7 us -> 48.5 us  [exchange(): return lax.all_to_all(value, axes, 0, 0, tiled=True)]
  transfers between devices with their start and end apart: 20 -> 19, of which waited for: 9 -> 8; matrix products, arithmetic and copies ran while one was open for 1% -> 0% of each run, Pallas kernels for 4% -> 4%
where the time goes in v10:
time: 209 us; the launch traced here: 208 us
  waiting for transfers between devices  89.4 us (43%)
  starting transfers between devices  57.7 us (28%)
  Pallas kernels  26.8 us (13%)
  local copies, waits for them, and re-layouts  17.2 us (8%)
  blocking collectives  13.1 us (6%)
  other arithmetic  2.68 us (1%)
    all_to_all x4, waiting for transfers between devices, exchange(): return lax.all_to_all(value, axes, 0, 0, tiled=True)  48.5 us
    all_to_all x4, starting transfers between devices, exchange(): return lax.all_to_all(value, axes, 0, 0, tiled=True)  34.7 us
    pallas_call x9, Pallas kernels, call(): pl.pallas_call(kernel, out_shape=outs, in_specs=in_specs, out_specs=out_s...  26.8 us
    ppermute x9, waiting for transfers between devices, shift_y(): return lax.ppermute(value, 'y', [(y, (y + step) % Y) for y in range(Y)])  23.9 us
    unnamed x60, local copies, waits for them, and re-layouts  16.9 us
    all_to_all x1, blocking collectives, exchange(): return lax.all_to_all(value, axes, 0, 0, tiled=True)  13.1 us
    ppermute x9, starting transfers between devices, shift_y(): return lax.ppermute(value, 'y', [(y, (y + step) % Y) for y in range(Y)])  9.89 us
    ppermute x4, waiting for transfers between devices, shift_z(): return lax.ppermute(value, 'z', [(z, (z + step) % Z) for z in range(Z)])  8.73 us
  transfers between devices with their start and end apart: 19, of which 8 were waited for; matrix products, arithmetic and copies ran while one was open for 0% of the time, Pallas kernels for 4%

profile of v10, /device:TPU:20, one launch (start us, length us, event | category | flops | bytes accessed | tf_op | source)
XLA Modules:
  0.0 207.7 jit_solution(2211563132302461678)
XLA Ops:
  5.0 1.3 collective-permute-start
  6.3 7.5 %collective-permute-done.ready.refs_1_ = f32[72,1024]{1,0:T(8,128)S(1)} collective-permute-done((f32[72,1024]{1,0:T(8,128)S(1)}, f32[72,1024]{1,0:T(8,128)S(1)}, u32[]{:S(2)}, u32[]{:S(2)}) %collective-permute-start) | collective-permute-done | bytes 294944 | tf_op jit(solution)/shard_map/ppermute | solution.py:165
  14.4 4.2 %shard_map.70 = (f32[4,32,896]{2,1,0:T(8,128)}, f32[4,32,896]{2,1,0:T(8,128)}, f32[4,32,896]{2,1,0:T(8,128)}, f32[4,32,896]{2,1,0:T(8,128)}, f32[4,32,896]{2,1,0...) custom-call(s32[2]{0:T(128)} %copy-done.6, f32[2,32,14336]{2,1,0:T(8,128)} %factor.1, ...), custom_call_target="tpu_custom_call" | custom-call | bytes 7340032 | tf_op jit(solution)/shard_map/pallas_call | solution.py:26
  18.6 2.0 collective-permute-start.3
  20.6 1.6 collective-permute-start.1
  24.4 10.7 %all-to-all-start = ((f32[32,16,128]{2,1,0:T(8,128)}), f32[32,16,128]{2,1,0:T(8,128)}, u32[]{:S(2)}, u32[]{:S(2)}) async-start(f32[32,16,128]{2,1,0:T(8,128)} %shard_map.68), calls=%async_computation | async-start | bytes 524288 | tf_op jit(solution)/shard_map/all_to_all | solution.py:188
  35.1 2.8 %collective-permute-start.4 = (f32[4,32,896]{2,1,0:T(8,128)}, f32[4,32,896]{2,1,0:T(8,128)S(1)}, u32[]{:S(2)}, u32[]{:S(2)}) collective-permute-start(f32[4,32,896]{2,1,0:T(8,128)} %get-tuple-element.29), channel_id=1, source_target_pairs={{0,28},{4,0},{8,4},{12,8},{16,12},{20,16},{24,20},{28,24},{1,29},{... | collective-permute-start | bytes 1376264 | tf_op jit(solution)/shard_map/ppermute | solution.py:169
  38.0 2.3 %collective-permute-start.5 = (f32[4,32,896]{2,1,0:T(8,128)}, f32[4,32,896]{2,1,0:T(8,128)S(1)}, u32[]{:S(2)}, u32[]{:S(2)}) collective-permute-start(f32[4,32,896]{2,1,0:T(8,128)} %get-tuple-element.30), channel_id=1, source_target_pairs={{0,24},{4,28},{8,0},{12,4},{16,8},{20,12},{24,16},{28,20},{32,40},... | collective-permute-start | bytes 1376264 | tf_op jit(solution)/shard_map/ppermute | solution.py:176
  40.3 1.2 collective-permute-start.6
  44.2 4.1 %all-to-all-done.arrived = f32[32,16,128]{2,1,0:T(8,128)} async-done(((f32[32,16,128]{2,1,0:T(8,128)}), f32[32,16,128]{2,1,0:T(8,128)}, u32[]{:S(2)}, u32[]{:S(2)}) %all-to-all-start) | async-done | bytes 262176 | tf_op jit(solution)/shard_map/all_to_all | solution.py:188
  48.3 2.4 %shard_map.71 = f32[8,2,16,128]{3,2,1,0:T(8,128)} custom-call(s32[2]{0:T(128)} %copy-done.6, f32[32,16,128]{2,1,0:T(8,128)} %all-to-all-done.arrived, f32[72,1024]{1,0:T(8,128)} %copy-done.1, f32[72,1024]{1,0:T(8,128)} %copy-done.19, f32[72,1024]{1,0:T(8,128)} %copy-done.26, f32[72,1024]{1,0:T(8,128)} %copy-done.27, ...), custom_call_target="tpu_custom_call" | custom-call | tf_op jit(solution)/shard_map/pallas_call | solution.py:26
  50.6 13.1 %all_to_all.25.arrived.first = f32[8,2,16,128]{3,2,1,0:T(8,128)} all-to-all(f32[8,2,16,128]{3,2,1,0:T(8,128)} %shard_map.71), channel_id=1, replica_groups=mesh['x'=4,'c'=2,'z'=8,'y'=4] {'z'}, dimensions={0} | all-to-all | bytes 262144 | tf_op jit(solution)/shard_map/all_to_all | solution.py:188
  65.7 2.4 %shard_map.72 = f32[8,5,16,128]{3,2,1,0:T(8,128)} custom-call(s32[2]{0:T(128)} %copy-done.6, f32[8,2,16,128]{3,2,1,0:T(8,128)} %all_to_all.25.arrived.first, f32[72,1024]{1,0:T(8,128)} %copy-done.1, f32[72,1024]{1,0:T(8,128)} %copy-done.19, f32[72,1024]{1,0:T(8,128)} %copy-done.26, f32[72,1024]{1,0:T(8,128)} %copy-done.27, f32[4,32,896]{2,1,0:T(8,128)} %copy-done.20, ...), custom_call_target="tpu_custom_call" | custom-call | tf_op jit(solution)/shard_map/pallas_call | solution.py:26
  68.2 5.5 %all-to-all-start.2 = ((f32[8,5,16,128]{3,2,1,0:T(8,128)}), f32[8,5,16,128]{3,2,1,0:T(8,128)S(1)}, u32[]{:S(2)}, u32[]{:S(2)}) async-start(f32[8,5,16,128]{3,2,1,0:T(8,128)} %shard_map.72), calls=%async_computation.2 | async-start | bytes 655360 | tf_op jit(solution)/shard_map/all_to_all | solution.py:188
  73.6 2.8 %shard_map.73 = (f32[4,32,896]{2,1,0:T(8,128)}, f32[4,32,896]{2,1,0:T(8,128)}, f32[4,32,896]{2,1,0:T(8,128)}, f32[4,32,896]{2,1,0:T(8,128)}) custom-call(f32[4,32,896]{2,1,0:T(8,128)} %get-tuple-element.26.refs_4_.refs_0_, f32[4,32,896]{2,1,0:T(8,128)} %copy-done.20, f32[4,32,896]{2,1,0:T(8,128)} %copy-done.21, f32[4,32,896]{2,1,0:T(8,128)} %copy-done.22), custom_call_target="tpu_custom_call" | custom-call | bytes 3670016 | tf_op jit(solution)/shard_map/pallas_call | solution.py:26
  76.5 1.3 collective-permute-start.9
  78.6 9.1 %collective-permute-done.9.refs_0_.refs_1_ = f32[4,32,896]{2,1,0:T(8,128)S(1)} collective-permute-done((f32[4,32,896]{2,1,0:T(8,128)}, f32[4,32,896]{2,1,0:T(8,128)S(1)}, u32[]{:S(2)}, u32[]{:S(2)}) %collective-permute-start.9) | collective-permute-done | bytes 458784 | tf_op jit(solution)/shard_map/ppermute | solution.py:165
  87.6 2.1 %collective-permute-done.10.refs_1_.refs_3_ = f32[4,32,896]{2,1,0:T(8,128)S(1)} collective-permute-done((f32[4,32,896]{2,1,0:T(8,128)}, f32[4,32,896]{2,1,0:T(8,128)S(1)}, u32[]{:S(2)}, u32[]{:S(2)}) %collective-permute-start.10) | collective-permute-done | bytes 458784 | tf_op jit(solution)/shard_map/ppermute | solution.py:165
  89.7 2.1 %shard_map.74 = f32[32,8,16,128]{3,2,1,0:T(8,128)} custom-call(s32[2]{0:T(128)S(1)} %copy-done.7, f32[8,2,16,128]{3,2,1,0:T(8,128)S(1)} %copy-done.2, f32[8,5,16,128]{3,2,1,0:T(8,128)S(1)} %all-to-all-done.2.arrived, f32[4,32,896]{2,1,0:T(8,128)S(1)} %collective-permute-done.9.refs_0_.refs_1_, f32[4,32,896]{2,1,0:T(8,128)S(1)} %collective-permute-done.10.refs_1_.refs_3_), custom_call_target="tpu_custom_call" | custom-call | tf_op jit(solution)/shard_map/pallas_call | solution.py:26
  91.8 7.6 %all-to-all-start.3 = ((f32[32,8,16,128]{3,2,1,0:T(8,128)}), f32[32,8,16,128]{3,2,1,0:T(8,128)S(1)}, u32[]{:S(2)}, u32[]{:S(2)}) async-start(f32[32,8,16,128]{3,2,1,0:T(8,128)} %shard_map.74), calls=%async_computation.3 | async-start | bytes 4194304 | tf_op jit(solution)/shard_map/all_to_all | solution.py:188
  99.5 2.8 %shard_map.75 = (f32[4,32,896]{2,1,0:T(8,128)}, f32[4,32,896]{2,1,0:T(8,128)}, f32[4,32,896]{2,1,0:T(8,128)}, f32[4,32,896]{2,1,0:T(8,128)}) custom-call(s32[2]{0:T(128)} %copy-done.6, f32[4,32,896]{2,1,0:T(8,128)} %get-tuple-element.27.refs_5_.refs_0_, f32[4,32,896]{2,1,0:T(8,128)} %copy-done.23, f32[4,32,896]{2,1,0:T(8,128)} %copy-done.24, ...), custom_call_target="tpu_custom_call" | custom-call | bytes 3670016 | tf_op jit(solution)/shard_map/pallas_call | solution.py:26
  102.3 1.8 collective-permute-start.12
  104.1 1.5 collective-permute-start.13
  105.6 2.6 %collective-permute-start.14 = (f32[4,32,896]{2,1,0:T(8,128)}, f32[4,32,896]{2,1,0:T(8,128)S(1)}, u32[]{:S(2)}, u32[]{:S(2)}) collective-permute-start(f32[4,32,896]{2,1,0:T(8,128)} %get-tuple-element.41), channel_id=1, source_target_pairs={{0,24},{4,28},{8,0},{12,4},{16,8},{20,12},{24,16},{28,20},{32,40},... | collective-permute-start | bytes 1376264 | tf_op jit(solution)/shard_map/ppermute | solution.py:176
  108.8 8.7 %collective-permute-done.12.refs_5_ = f32[4,32,896]{2,1,0:T(8,128)S(1)} collective-permute-done((f32[4,32,896]{2,1,0:T(8,128)}, f32[4,32,896]{2,1,0:T(8,128)S(1)}, u32[]{:S(2)}, u32[]{:S(2)}) %collective-permute-start.12) | collective-permute-done | bytes 458784 | tf_op jit(solution)/shard_map/ppermute | solution.py:169
  119.1 8.3 %collective-permute-done.14.refs_7_ = f32[4,32,896]{2,1,0:T(8,128)S(1)} collective-permute-done((f32[4,32,896]{2,1,0:T(8,128)}, f32[4,32,896]{2,1,0:T(8,128)S(1)}, u32[]{:S(2)}, u32[]{:S(2)}) %collective-permute-start.14) | collective-permute-done | bytes 458784 | tf_op jit(solution)/shard_map/ppermute | solution.py:176
  128.1 5.3 %collective-permute-done.11.refs_2_ = f32[4,32,896]{2,1,0:T(8,128)S(1)} collective-permute-done((f32[4,32,896]{2,1,0:T(8,128)}, f32[4,32,896]{2,1,0:T(8,128)S(1)}, u32[]{:S(2)}, u32[]{:S(2)}) %collective-permute-start.11) | collective-permute-done | bytes 458784 | tf_op jit(solution)/shard_map/ppermute | solution.py:165
  139.3 8.4 %shard_map.76 = f32[32,16,896]{2,1,0:T(8,128)S(1)} custom-call(s32[2]{0:T(128)S(1)} %copy-done.8, f32[32,8,16,128]{3,2,1,0:T(8,128)S(1)} %all-to-all-done.3.rows, f32[4,32,896]{2,1,0:T(8,128)S(1)} %copy-done.9, f32[4,32,896]{2,1,0:T(8,128)S(1)} %collective-permute-done.9.refs_0_.refs_1_, f32[4,32,896]{2,1,0:T(8,128)S(1)} %copy-done.18, ...), custom_call_target="tpu_custom_call" | custom-call | flops 2818572288 | bytes 7602176 | tf_op jit(solution)/shard_map/pallas_call | solution.py:26
  147.7 1.2 copy-done
  149.0 10.9 %all-to-all-start.4 = ((f32[32,16,896]{2,1,0:T(8,128)}), f32[32,16,896]{2,1,0:T(8,128)}, u32[]{:S(2)}, u32[]{:S(2)}) async-start(f32[32,16,896]{2,1,0:T(8,128)} %copy-done), calls=%async_computation.4 | async-start | bytes 3670016 | tf_op jit(solution)/shard_map/all_to_all | solution.py:188
  160.7 44.4 %all-to-all-done.4 = f32[32,16,896]{2,1,0:T(8,128)} async-done(((f32[32,16,896]{2,1,0:T(8,128)}), f32[32,16,896]{2,1,0:T(8,128)}, u32[]{:S(2)}, u32[]{:S(2)}) %all-to-all-start.4) | async-done | bytes 1835040 | tf_op jit(solution)/shard_map/all_to_all | solution.py:188
  205.1 1.5 fusion
  (88 shorter events, 23.4 us)
Async XLA Ops:
  1.7 12.0 %copy-start.6 = (s32[2]{0:T(128)}, s32[2]{0:T(128)S(1)}, u32[]{:S(2)}) copy-start(s32[2]{0:T(128)S(1)} %pad_add_fusion.place) | copy-start | bytes 28
  3.6 19.7 %copy-start.4 = (f32[2,32,1024]{2,1,0:T(8,128)S(1)}, f32[2,32,1024]{2,1,0:T(8,128)}, u32[]{:S(2)}) copy-start(f32[2,32,1024]{2,1,0:T(8,128)} %inverse.3) | copy-start | bytes 786436
  5.0 8.7 %collective-permute-start = (f32[72,1024]{1,0:T(8,128)S(1)}, f32[72,1024]{1,0:T(8,128)S(1)}, u32[]{:S(2)}, u32[]{:S(2)}) collective-permute-start(f32[72,1024]{1,0:T(8,128)S(1)} %get-tuple-element.23), channel_id=1, source_target_pairs={{0,1},{1,2},{2,3},{3,0},{4,5},{5,6},{6,7},{7,4},{8,9},{9,10},{10,1... | collective-permute-start | bytes 884744 | tf_op jit(solution)/shard_map/ppermute | solution.py:165
  18.6 24.4 %collective-permute-start.3 = (f32[4,32,896]{2,1,0:T(8,128)}, f32[4,32,896]{2,1,0:T(8,128)S(1)}, u32[]{:S(2)}, u32[]{:S(2)}) collective-permute-start(f32[4,32,896]{2,1,0:T(8,128)} %get-tuple-element.28), channel_id=1, source_target_pairs={{0,4},{4,8},{8,12},{12,16},{16,20},{20,24},{24,28},{28,0},{1,5},{5... | collective-permute-start | bytes 1376264 | tf_op jit(solution)/shard_map/ppermute | solution.py:169
  20.6 19.7 %collective-permute-start.1 = (f32[72,1024]{1,0:T(8,128)S(1)}, f32[72,1024]{1,0:T(8,128)S(1)}, u32[]{:S(2)}, u32[]{:S(2)}) collective-permute-start(f32[72,1024]{1,0:T(8,128)S(1)} %get-tuple-element.24), channel_id=1, source_target_pairs={{0,2},{1,3},{2,0},{3,1},{4,6},{5,7},{6,4},{7,5},{8,10},{9,11},{10,... | collective-permute-start | bytes 884744 | tf_op jit(solution)/shard_map/ppermute | solution.py:165
  22.2 19.3 %collective-permute-start.2 = (f32[72,1024]{1,0:T(8,128)S(1)}, f32[72,1024]{1,0:T(8,128)S(1)}, u32[]{:S(2)}, u32[]{:S(2)}) collective-permute-start(f32[72,1024]{1,0:T(8,128)S(1)} %get-tuple-element.25), channel_id=1, source_target_pairs={{0,3},{1,0},{2,1},{3,2},{4,7},{5,4},{6,5},{7,6},{8,11},{9,8},{10,9... | collective-permute-start | bytes 884744 | tf_op jit(solution)/shard_map/ppermute | solution.py:165
  24.4 23.9 %all-to-all-start = ((f32[32,16,128]{2,1,0:T(8,128)}), f32[32,16,128]{2,1,0:T(8,128)}, u32[]{:S(2)}, u32[]{:S(2)}) async-start(f32[32,16,128]{2,1,0:T(8,128)} %shard_map.68), calls=%async_computation | async-start | bytes 524288 | tf_op jit(solution)/shard_map/all_to_all | solution.py:188
  35.1 28.6 %collective-permute-start.4 = (f32[4,32,896]{2,1,0:T(8,128)}, f32[4,32,896]{2,1,0:T(8,128)S(1)}, u32[]{:S(2)}, u32[]{:S(2)}) collective-permute-start(f32[4,32,896]{2,1,0:T(8,128)} %get-tuple-element.29), channel_id=1, source_target_pairs={{0,28},{4,0},{8,4},{12,8},{16,12},{20,16},{24,20},{28,24},{1,29},{... | collective-permute-start | bytes 1376264 | tf_op jit(solution)/shard_map/ppermute | solution.py:169
  38.0 25.7 %collective-permute-start.5 = (f32[4,32,896]{2,1,0:T(8,128)}, f32[4,32,896]{2,1,0:T(8,128)S(1)}, u32[]{:S(2)}, u32[]{:S(2)}) collective-permute-start(f32[4,32,896]{2,1,0:T(8,128)} %get-tuple-element.30), channel_id=1, source_target_pairs={{0,24},{4,28},{8,0},{12,4},{16,8},{20,12},{24,16},{28,20},{32,40},... | collective-permute-start | bytes 1376264 | tf_op jit(solution)/shard_map/ppermute | solution.py:176
  40.3 8.0 %copy-start.26 = (f32[72,1024]{1,0:T(8,128)}, f32[72,1024]{1,0:T(8,128)S(1)}, u32[]{:S(2)}) copy-start(f32[72,1024]{1,0:T(8,128)S(1)} %collective-permute-done.1.refs_2_) | copy-start | bytes 884740
  40.3 23.4 %collective-permute-start.6 = (f32[4,32,896]{2,1,0:T(8,128)}, f32[4,32,896]{2,1,0:T(8,128)S(1)}, u32[]{:S(2)}, u32[]{:S(2)}) collective-permute-start(f32[4,32,896]{2,1,0:T(8,128)} %get-tuple-element.31), channel_id=1, source_target_pairs={{0,1},{1,2},{2,3},{3,0},{4,5},{5,6},{6,7},{7,4},{8,9},{9,10},{10,1... | collective-permute-start | bytes 1376264 | tf_op jit(solution)/shard_map/ppermute | solution.py:165
  42.2 21.6 %collective-permute-start.7 = (f32[4,32,896]{2,1,0:T(8,128)}, f32[4,32,896]{2,1,0:T(8,128)S(1)}, u32[]{:S(2)}, u32[]{:S(2)}) collective-permute-start(f32[4,32,896]{2,1,0:T(8,128)} %get-tuple-element.32), channel_id=1, source_target_pairs={{0,2},{1,3},{2,0},{3,1},{4,6},{5,7},{6,4},{7,5},{8,10},{9,11},{10,... | collective-permute-start | bytes 1376264 | tf_op jit(solution)/shard_map/ppermute | solution.py:165
  43.0 20.7 %copy-start.20 = (f32[4,32,896]{2,1,0:T(8,128)}, f32[4,32,896]{2,1,0:T(8,128)S(1)}, u32[]{:S(2)}) copy-start(f32[4,32,896]{2,1,0:T(8,128)S(1)} %collective-permute-done.3.refs_4_.refs_1_) | copy-start | bytes 1376260
  43.0 20.7 %collective-permute-start.8 = (f32[4,32,896]{2,1,0:T(8,128)}, f32[4,32,896]{2,1,0:T(8,128)S(1)}, u32[]{:S(2)}, u32[]{:S(2)}) collective-permute-start(f32[4,32,896]{2,1,0:T(8,128)} %get-tuple-element.33), channel_id=1, source_target_pairs={{0,3},{1,0},{2,1},{3,2},{4,7},{5,4},{6,5},{7,6},{8,11},{9,8},{10,9... | collective-permute-start | bytes 1376264 | tf_op jit(solution)/shard_map/ppermute | solution.py:165
  63.7 1.1 copy-start.23
  63.8 1.2 copy-start.24
  68.2 21.6 %copy-start.2 = (f32[8,2,16,128]{3,2,1,0:T(8,128)S(1)}, f32[8,2,16,128]{3,2,1,0:T(8,128)}, u32[]{:S(2)}) copy-start(f32[8,2,16,128]{3,2,1,0:T(8,128)} %all_to_all.25.arrived.first) | copy-start | bytes 393220
  68.2 21.6 %copy-start.7 = (s32[2]{0:T(128)S(1)}, s32[2]{0:T(128)}, u32[]{:S(2)}) copy-start(s32[2]{0:T(128)} %copy-done.6) | copy-start | bytes 28
  68.2 21.6 %all-to-all-start.2 = ((f32[8,5,16,128]{3,2,1,0:T(8,128)}), f32[8,5,16,128]{3,2,1,0:T(8,128)S(1)}, u32[]{:S(2)}, u32[]{:S(2)}) async-start(f32[8,5,16,128]{3,2,1,0:T(8,128)} %shard_map.72), calls=%async_computation.2 | async-start | bytes 655360 | tf_op jit(solution)/shard_map/all_to_all | solution.py:188
  76.5 11.2 %collective-permute-start.9 = (f32[4,32,896]{2,1,0:T(8,128)}, f32[4,32,896]{2,1,0:T(8,128)S(1)}, u32[]{:S(2)}, u32[]{:S(2)}) collective-permute-start(f32[4,32,896]{2,1,0:T(8,128)} %get-tuple-element.34), channel_id=1, source_target_pairs={{0,1},{1,2},{2,3},{3,0},{4,5},{5,6},{6,7},{7,4},{8,9},{9,10},{10,1... | collective-permute-start | bytes 1376264 | tf_op jit(solution)/shard_map/ppermute | solution.py:165
  77.7 12.0 %collective-permute-start.10 = (f32[4,32,896]{2,1,0:T(8,128)}, f32[4,32,896]{2,1,0:T(8,128)S(1)}, u32[]{:S(2)}, u32[]{:S(2)}) collective-permute-start(f32[4,32,896]{2,1,0:T(8,128)} %get-tuple-element.35), channel_id=1, source_target_pairs={{0,3},{1,0},{2,1},{3,2},{4,7},{5,4},{6,5},{7,6},{8,11},{9,8},{10,9... | collective-permute-start | bytes 1376264 | tf_op jit(solution)/shard_map/ppermute | solution.py:165
  91.8 42.4 %copy-start.8 = (s32[2]{0:T(128)S(1)}, s32[2]{0:T(128)}, u32[]{:S(2)}) copy-start(s32[2]{0:T(128)} %copy-done.6) | copy-start | bytes 28
  91.8 42.4 %copy-start.9 = (f32[4,32,896]{2,1,0:T(8,128)S(1)}, f32[4,32,896]{2,1,0:T(8,128)}, u32[]{:S(2)}) copy-start(f32[4,32,896]{2,1,0:T(8,128)} %get-tuple-element.36.refs_0_) | copy-start | bytes 1376260
  91.8 42.4 %all-to-all-start.3 = ((f32[32,8,16,128]{3,2,1,0:T(8,128)}), f32[32,8,16,128]{3,2,1,0:T(8,128)S(1)}, u32[]{:S(2)}, u32[]{:S(2)}) async-start(f32[32,8,16,128]{3,2,1,0:T(8,128)} %shard_map.74), calls=%async_computation.3 | async-start | bytes 4194304 | tf_op jit(solution)/shard_map/all_to_all | solution.py:188
  102.3 15.3 %collective-permute-start.12 = (f32[4,32,896]{2,1,0:T(8,128)}, f32[4,32,896]{2,1,0:T(8,128)S(1)}, u32[]{:S(2)}, u32[]{:S(2)}) collective-permute-start(f32[4,32,896]{2,1,0:T(8,128)} %get-tuple-element.39), channel_id=1, source_target_pairs={{0,4},{4,8},{8,12},{12,16},{16,20},{20,24},{24,28},{28,0},{1,5},{5... | collective-permute-start | bytes 1376264 | tf_op jit(solution)/shard_map/ppermute | solution.py:169
  104.1 14.2 %collective-permute-start.13 = (f32[4,32,896]{2,1,0:T(8,128)}, f32[4,32,896]{2,1,0:T(8,128)S(1)}, u32[]{:S(2)}, u32[]{:S(2)}) collective-permute-start(f32[4,32,896]{2,1,0:T(8,128)} %get-tuple-element.40), channel_id=1, source_target_pairs={{0,28},{4,0},{8,4},{12,8},{16,12},{20,16},{24,20},{28,24},{1,29},{... | collective-permute-start | bytes 1376264 | tf_op jit(solution)/shard_map/ppermute | solution.py:169
  105.6 21.8 %collective-permute-start.14 = (f32[4,32,896]{2,1,0:T(8,128)}, f32[4,32,896]{2,1,0:T(8,128)S(1)}, u32[]{:S(2)}, u32[]{:S(2)}) collective-permute-start(f32[4,32,896]{2,1,0:T(8,128)} %get-tuple-element.41), channel_id=1, source_target_pairs={{0,24},{4,28},{8,0},{12,4},{16,8},{20,12},{24,16},{28,20},{32,40},... | collective-permute-start | bytes 1376264 | tf_op jit(solution)/shard_map/ppermute | solution.py:176
  108.2 25.2 %collective-permute-start.11 = (f32[4,32,896]{2,1,0:T(8,128)}, f32[4,32,896]{2,1,0:T(8,128)S(1)}, u32[]{:S(2)}, u32[]{:S(2)}) collective-permute-start(f32[4,32,896]{2,1,0:T(8,128)} %get-tuple-element.37), channel_id=1, source_target_pairs={{0,2},{1,3},{2,0},{3,1},{4,6},{5,7},{6,4},{7,5},{8,10},{9,11},{10,... | collective-permute-start | bytes 1376264 | tf_op jit(solution)/shard_map/ppermute | solution.py:165
  134.2 1.0 copy-start.10
  147.7 1.2 copy-start
  149.0 56.1 %all-to-all-start.4 = ((f32[32,16,896]{2,1,0:T(8,128)}), f32[32,16,896]{2,1,0:T(8,128)}, u32[]{:S(2)}, u32[]{:S(2)}) async-start(f32[32,16,896]{2,1,0:T(8,128)} %copy-done), calls=%async_computation.4 | async-start | bytes 3670016 | tf_op jit(solution)/shard_map/all_to_all | solution.py:188
  160.7 46.0 %copy-start.28 = (f32[16,14336]{1,0:T(8,128)S(1)}, f32[16,14336]{1,0:T(8,128)}, u32[]{:S(2)}) copy-start(f32[16,14336]{1,0:T(8,128)} %param.9) | copy-start | bytes 2752516
  (16 other events, 13.7 us)

commit v11 on v10

--- a/solution.py
+++ b/solution.py
@@ -115,7 +115,7 @@
     return (z % QUAD, (z + 1) % QUAD, (z + 3) % QUAD, (z + 2) % QUAD)
 
 
-def cut_kernel(place, factor, ready, *refs):
+def cut_kernel(place, factor, *refs):
     by_class, by_y, sems = refs[:4], refs[4:8], refs[8]
     classes = around(place[0])
     width = by_y[0].shape[2]
@@ -140,13 +140,20 @@
 
 def update_kernel(place, rows, *refs):
     by_r, by_k = refs[:Y], refs[Y:Y + QUAD]
-    out, high, low, result, sems = refs[Y + QUAD:]
-    for r in range(Y):
-        slot = (place[1] + Y - r) % Y
-        high[0, :, slot], low[0, :, slot] = split(by_r[r][...])
+    out, factor, high, low, result, sems = refs[Y + QUAD:]
+    start = lambda src, dst, i: pltpu.make_async_copy(src, dst, sems.at[i])
+    slots = [(place[1] + Y - r) % Y for r in range(Y)]
+    arriving = [start(by_r[r], factor.at[0, r], r) for r in range(Y)]
+    arriving += [start(by_k[k], factor.at[1, k], Y + k) for k in range(QUAD)]
+    for copy in arriving:
+        copy.start()
+    left_high, left_low = split(jnp.concatenate([rows[:, k].reshape(-1, 128) for k in range(2 * QUAD)], axis=1))
+    for r in range(Y):
+        arriving[r].wait()
+        high[0, :, slots[r]], low[0, :, slots[r]] = split(factor[0, r])
     for k in range(QUAD):
-        high[1, k], low[1, k] = split(by_k[k][...])
-    left_high, left_low = split(jnp.concatenate([rows[:, k].reshape(-1, 128) for k in range(2 * QUAD)], axis=1))
+        arriving[Y + k].wait()
+        high[1, k], low[1, k] = split(factor[1, k])
     dot = functools.partial(jnp.dot, preferred_element_type=jnp.float32)
     width = result.shape[2]
     sent = []
@@ -155,7 +162,7 @@
         right_high, right_low = (part[..., at].reshape(2 * QUAD * 128, -1) for part in (high, low))
         product = dot(left_high, right_high) + (dot(left_high, right_low) + dot(left_low, right_high))
         result[..., at] = product.reshape(result.shape[0], 16, -1)
-        sent.append(pltpu.make_async_copy(result.at[..., at], out.at[..., at], sems.at[i]))
+        sent.append(start(result.at[..., at], out.at[..., at], Y + QUAD + i))
         sent[-1].start()
     for copy in sent:
         copy.wait()
@@ -210,7 +217,7 @@
     shared = to_ys(*shared)
 
     cut = call(
-        cut_kernel, (block,) * 8, (place, trail_factor, shared[1]), (ANY,) * 8, (SMEM, VMEM, ANY), sems(32), moved=7340032, limit=60,
+        cut_kernel, (block,) * 8, (place, trail_factor), (ANY,) * 8, (SMEM, VMEM), sems(32), moved=7340032, limit=60,
     )
     by_class, by_y = to_windows(*cut[:4]), to_ys(*cut[4:])
 
@@ -232,11 +239,12 @@
     copies = call(close_kernel, f32(X * C * Y, 2 * QUAD, 16, 128), (place, first, arrived, first_factor[1], first_factor[3]), VMEM, (SMEM, VMEM, VMEM, ANY, ANY))
     rows = exchange(copies, SPREAD)
 
-    part = pltpu.VMEM((2, QUAD, *block.shape), jnp.bfloat16)
+    factor = lambda dtype: pltpu.VMEM((2, QUAD, *block.shape), dtype)
     update = call(
         update_kernel, f32(X * C * Y, 16, width), (place, rows, *first_factor, *latter_factor),
-        ANY, (SMEM,) + (VMEM,) * 9, [part, part, pltpu.VMEM((X * C * Y, 16, width), jnp.float32)] + sems(4),
-        flops=2818572288, moved=7602176, limit=24,
+        ANY, (SMEM, VMEM) + (ANY,) * 8,
+        [factor(jnp.float32), factor(jnp.bfloat16), factor(jnp.bfloat16), pltpu.VMEM((X * C * Y, 16, width), jnp.float32)] + sems(12),
+        flops=2818572288, moved=7602176, limit=56,
     )
     parts = exchange(update, COLS)
     parts = parts.reshape(2, QUAD * Y, *parts.shape[1:])

time: 209 us -> 189 us (0.904)
  blocking collectives: 13.1 us -> 0 us
  local copies, waits for them, and re-layouts: 17.2 us -> 6.11 us
  waiting for transfers between devices: 89.4 us -> 93.4 us
  starting transfers between devices: 57.7 us -> 60 us
    all_to_all x1 -> x0, blocking collectives: 13.1 us -> none  [exchange(): return lax.all_to_all(value, axes, 0, 0, tiled=True)]
    unnamed x60 -> x50, local copies, waits for them, and re-layouts: 16.9 us -> 5.04 us
    ppermute x2, waiting for transfers between devices: 8.3 us -> 19.7 us  [shift_far(): return lax.ppermute(value, ('c', 'z'), pairs)]
    ppermute x9, waiting for transfers between devices: 23.9 us -> 16.4 us  [shift_y(): return lax.ppermute(value, 'y', [(y, (y + step) % Y) for y in range(Y)])]
    all_to_all x4 -> x5, starting transfers between devices: 34.7 us -> 38.1 us  [exchange(): return lax.all_to_all(value, axes, 0, 0, tiled=True)]
    all_to_all x4 -> x5, waiting for transfers between devices: 48.5 us -> 48.5 us  [exchange(): return lax.all_to_all(value, axes, 0, 0, tiled=True)]
  transfers between devices with their start and end apart: 19 -> 20, of which waited for: 8 -> 9; matrix products, arithmetic and copies ran while one was open for 0% -> 1% of each run, Pallas kernels for 4% -> 5%
where the time goes in v11:
time: 189 us
  waiting for transfers between devices  93.4 us (49%)
  starting transfers between devices  60 us (32%)
  Pallas kernels  26.6 us (14%)
  local copies, waits for them, and re-layouts  6.11 us (3%)
    all_to_all x5, waiting for transfers between devices, exchange(): return lax.all_to_all(value, axes, 0, 0, tiled=True)  48.5 us
    all_to_all x5, starting transfers between devices, exchange(): return lax.all_to_all(value, axes, 0, 0, tiled=True)  38.1 us
    pallas_call x9, Pallas kernels, call(): pl.pallas_call(kernel, out_shape=outs, in_specs=in_specs, out_specs=out_s...  26.6 us
    ppermute x2, waiting for transfers between devices, shift_far(): return lax.ppermute(value, ('c', 'z'), pairs)  19.7 us
    ppermute x9, waiting for transfers between devices, shift_y(): return lax.ppermute(value, 'y', [(y, (y + step) % Y) for y in range(Y)])  16.4 us
    ppermute x9, starting transfers between devices, shift_y(): return lax.ppermute(value, 'y', [(y, (y + step) % Y) for y in range(Y)])  8.79 us
    ppermute x4, waiting for transfers between devices, shift_z(): return lax.ppermute(value, 'z', [(z, (z + step) % Z) for z in range(Z)])  8.77 us
    ppermute x4, starting transfers between devices, shift_z(): return lax.ppermute(value, 'z', [(z, (z + step) % Z) for z in range(Z)])  8.14 us
  transfers between devices with their start and end apart: 20, of which 9 were waited for; matrix products, arithmetic and copies ran while one was open for 1% of the time, Pallas kernels for 5%

profile of v11, /device:TPU:20, one launch (start us, length us, event | category | flops | bytes accessed | tf_op | source)
XLA Modules:
  0.0 188.7 jit_solution(12916450207793115060)
XLA Ops:
  1.3 4.2 %shard_map.70 = (f32[4,32,896]{2,1,0:T(8,128)}, f32[4,32,896]{2,1,0:T(8,128)}, f32[4,32,896]{2,1,0:T(8,128)}, f32[4,32,896]{2,1,0:T(8,128)}, f32[4,32,896]{2,1,0...) custom-call(s32[2]{0:T(128)} %pad_add_fusion.place, f32[2,32,14336]{2,1,0:T(8,128)} %factor.1), custom_call_target="tpu_custom_call" | custom-call | bytes 7340032 | tf_op jit(solution)/shard_map/pallas_call | solution.py:26
  5.5 2.0 %collective-permute-start.3 = (f32[4,32,896]{2,1,0:T(8,128)}, f32[4,32,896]{2,1,0:T(8,128)S(1)}, u32[]{:S(2)}, u32[]{:S(2)}) collective-permute-start(f32[4,32,896]{2,1,0:T(8,128)} %get-tuple-element.28), channel_id=1, source_target_pairs={{0,4},{4,8},{8,12},{12,16},{16,20},{20,24},{24,28},{28,0},{1,5},{5... | collective-permute-start | bytes 1376264 | tf_op jit(solution)/shard_map/ppermute | solution.py:176
  9.2 1.3 collective-permute-start
  11.1 1.1 collective-permute-start.2
  13.2 11.1 %all-to-all-start = ((f32[32,16,128]{2,1,0:T(8,128)}), f32[32,16,128]{2,1,0:T(8,128)}, u32[]{:S(2)}, u32[]{:S(2)}) async-start(f32[32,16,128]{2,1,0:T(8,128)} %shard_map.68), calls=%async_computation | async-start | bytes 524288 | tf_op jit(solution)/shard_map/all_to_all | solution.py:195
  24.3 2.8 %collective-permute-start.4 = (f32[4,32,896]{2,1,0:T(8,128)}, f32[4,32,896]{2,1,0:T(8,128)S(1)}, u32[]{:S(2)}, u32[]{:S(2)}) collective-permute-start(f32[4,32,896]{2,1,0:T(8,128)} %get-tuple-element.29), channel_id=1, source_target_pairs={{0,28},{4,0},{8,4},{12,8},{16,12},{20,16},{24,20},{28,24},{1,29},{... | collective-permute-start | bytes 1376264 | tf_op jit(solution)/shard_map/ppermute | solution.py:176
  27.1 2.3 %collective-permute-start.5 = (f32[4,32,896]{2,1,0:T(8,128)}, f32[4,32,896]{2,1,0:T(8,128)S(1)}, u32[]{:S(2)}, u32[]{:S(2)}) collective-permute-start(f32[4,32,896]{2,1,0:T(8,128)} %get-tuple-element.30), channel_id=1, source_target_pairs={{0,24},{4,28},{8,0},{12,4},{16,8},{20,12},{24,16},{28,20},{32,40},... | collective-permute-start | bytes 1376264 | tf_op jit(solution)/shard_map/ppermute | solution.py:183
  29.4 1.2 collective-permute-start.6
  31.5 1.2 collective-permute-start.8
  32.6 4.6 %all-to-all-done.arrived = f32[32,16,128]{2,1,0:T(8,128)} async-done(((f32[32,16,128]{2,1,0:T(8,128)}), f32[32,16,128]{2,1,0:T(8,128)}, u32[]{:S(2)}, u32[]{:S(2)}) %all-to-all-start) | async-done | bytes 262176 | tf_op jit(solution)/shard_map/all_to_all | solution.py:195
  37.2 2.4 %shard_map.71 = f32[8,2,16,128]{3,2,1,0:T(8,128)} custom-call(s32[2]{0:T(128)} %pad_add_fusion.place, f32[32,16,128]{2,1,0:T(8,128)} %all-to-all-done.arrived, f32[72,1024]{1,0:T(8,128)} %copy-done, f32[72,1024]{1,0:T(8,128)} %copy-done.15, f32[72,1024]{1,0:T(8,128)} %copy-done.16, f32[72,1024]{1,0:T(8,128)} %copy-done.17, ...), custom_call_target="tpu_custom_call" | custom-call | tf_op jit(solution)/shard_map/pallas_call | solution.py:26
  39.6 3.4 %all-to-all-start.1 = ((f32[8,2,16,128]{3,2,1,0:T(8,128)}), f32[8,2,16,128]{3,2,1,0:T(8,128)S(1)}, u32[]{:S(2)}, u32[]{:S(2)}) async-start(f32[8,2,16,128]{3,2,1,0:T(8,128)} %shard_map.71), calls=%async_computation.1 | async-start | bytes 262144 | tf_op jit(solution)/shard_map/all_to_all | solution.py:195
  43.0 9.9 %collective-permute-done.5.refs_6_.refs_3_ = f32[4,32,896]{2,1,0:T(8,128)S(1)} collective-permute-done((f32[4,32,896]{2,1,0:T(8,128)}, f32[4,32,896]{2,1,0:T(8,128)S(1)}, u32[]{:S(2)}, u32[]{:S(2)}) %collective-permute-start.5) | collective-permute-done | bytes 458784 | tf_op jit(solution)/shard_map/ppermute | solution.py:183
  54.6 2.4 %shard_map.72 = f32[8,5,16,128]{3,2,1,0:T(8,128)} custom-call(s32[2]{0:T(128)} %pad_add_fusion.place, f32[8,2,16,128]{3,2,1,0:T(8,128)} %copy-done.1, f32[72,1024]{1,0:T(8,128)} %copy-done, f32[72,1024]{1,0:T(8,128)} %copy-done.15, f32[72,1024]{1,0:T(8,128)} %copy-done.16, f32[72,1024]{1,0:T(8,128)} %copy-done.17, f32[4,32,896]{2,1,0:T(8,128)} %copy-done.10, ...), custom_call_target="tpu_custom_call" | custom-call | tf_op jit(solution)/shard_map/pallas_call | solution.py:26
  57.1 5.2 %all-to-all-start.2 = ((f32[8,5,16,128]{3,2,1,0:T(8,128)}), f32[8,5,16,128]{3,2,1,0:T(8,128)S(1)}, u32[]{:S(2)}, u32[]{:S(2)}) async-start(f32[8,5,16,128]{3,2,1,0:T(8,128)} %shard_map.72), calls=%async_computation.2 | async-start | bytes 655360 | tf_op jit(solution)/shard_map/all_to_all | solution.py:195
  62.3 2.8 %shard_map.73 = (f32[4,32,896]{2,1,0:T(8,128)}, f32[4,32,896]{2,1,0:T(8,128)}, f32[4,32,896]{2,1,0:T(8,128)}, f32[4,32,896]{2,1,0:T(8,128)}) custom-call(f32[4,32,896]{2,1,0:T(8,128)} %get-tuple-element.26.refs_4_.refs_0_, f32[4,32,896]{2,1,0:T(8,128)} %copy-done.10, f32[4,32,896]{2,1,0:T(8,128)} %copy-done.11, f32[4,32,896]{2,1,0:T(8,128)} %copy-done.12), custom_call_target="tpu_custom_call" | custom-call | bytes 3670016 | tf_op jit(solution)/shard_map/pallas_call | solution.py:26
  65.1 1.3 collective-permute-start.9
  67.2 9.0 %collective-permute-done.9.refs_0_.refs_1_ = f32[4,32,896]{2,1,0:T(8,128)S(1)} collective-permute-done((f32[4,32,896]{2,1,0:T(8,128)}, f32[4,32,896]{2,1,0:T(8,128)S(1)}, u32[]{:S(2)}, u32[]{:S(2)}) %collective-permute-start.9) | collective-permute-done | bytes 458784 | tf_op jit(solution)/shard_map/ppermute | solution.py:172
  76.2 2.1 %collective-permute-done.10.refs_1_.refs_3_ = f32[4,32,896]{2,1,0:T(8,128)S(1)} collective-permute-done((f32[4,32,896]{2,1,0:T(8,128)}, f32[4,32,896]{2,1,0:T(8,128)S(1)}, u32[]{:S(2)}, u32[]{:S(2)}) %collective-permute-start.10) | collective-permute-done | bytes 458784 | tf_op jit(solution)/shard_map/ppermute | solution.py:172
  78.3 2.1 %shard_map.74 = f32[32,8,16,128]{3,2,1,0:T(8,128)} custom-call(s32[2]{0:T(128)S(1)} %copy-done.8, f32[8,2,16,128]{3,2,1,0:T(8,128)S(1)} %copy-done.2, f32[8,5,16,128]{3,2,1,0:T(8,128)S(1)} %all-to-all-done.2.arrived, f32[4,32,896]{2,1,0:T(8,128)S(1)} %collective-permute-done.9.refs_0_.refs_1_, f32[4,32,896]{2,1,0:T(8,128)S(1)} %collective-permute-done.10.refs_1_.refs_3_), custom_call_target="tpu_custom_call" | custom-call | tf_op jit(solution)/shard_map/pallas_call | solution.py:26
  80.4 7.6 %all-to-all-start.3 = ((f32[32,8,16,128]{3,2,1,0:T(8,128)}), f32[32,8,16,128]{3,2,1,0:T(8,128)S(1)}, u32[]{:S(2)}, u32[]{:S(2)}) async-start(f32[32,8,16,128]{3,2,1,0:T(8,128)} %shard_map.74), calls=%async_computation.3 | async-start | bytes 4194304 | tf_op jit(solution)/shard_map/all_to_all | solution.py:195
  88.1 2.9 %shard_map.75 = (f32[4,32,896]{2,1,0:T(8,128)}, f32[4,32,896]{2,1,0:T(8,128)}, f32[4,32,896]{2,1,0:T(8,128)}, f32[4,32,896]{2,1,0:T(8,128)}) custom-call(s32[2]{0:T(128)} %pad_add_fusion.place, f32[4,32,896]{2,1,0:T(8,128)} %get-tuple-element.27.refs_5_.refs_0_, f32[4,32,896]{2,1,0:T(8,128)} %copy-done.13, f32[4,32,896]{2,1,0:T(8,128)} %copy-done.14, ...), custom_call_target="tpu_custom_call" | custom-call | bytes 3670016 | tf_op jit(solution)/shard_map/pallas_call | solution.py:26
  90.9 1.8 collective-permute-start.12
  92.7 1.5 collective-permute-start.13
  94.2 2.6 %collective-permute-start.14 = (f32[4,32,896]{2,1,0:T(8,128)}, f32[4,32,896]{2,1,0:T(8,128)S(1)}, u32[]{:S(2)}, u32[]{:S(2)}) collective-permute-start(f32[4,32,896]{2,1,0:T(8,128)} %get-tuple-element.41), channel_id=1, source_target_pairs={{0,24},{4,28},{8,0},{12,4},{16,8},{20,12},{24,16},{28,20},{32,40},... | collective-permute-start | bytes 1376264 | tf_op jit(solution)/shard_map/ppermute | solution.py:183
  97.4 8.8 %collective-permute-done.12.refs_5_ = f32[4,32,896]{2,1,0:T(8,128)S(1)} collective-permute-done((f32[4,32,896]{2,1,0:T(8,128)}, f32[4,32,896]{2,1,0:T(8,128)S(1)}, u32[]{:S(2)}, u32[]{:S(2)}) %collective-permute-start.12) | collective-permute-done | bytes 458784 | tf_op jit(solution)/shard_map/ppermute | solution.py:176
  106.2 9.8 %collective-permute-done.14.refs_7_ = f32[4,32,896]{2,1,0:T(8,128)S(1)} collective-permute-done((f32[4,32,896]{2,1,0:T(8,128)}, f32[4,32,896]{2,1,0:T(8,128)S(1)}, u32[]{:S(2)}, u32[]{:S(2)}) %collective-permute-start.14) | collective-permute-done | bytes 458784 | tf_op jit(solution)/shard_map/ppermute | solution.py:183
  116.8 5.3 %collective-permute-done.11.refs_2_ = f32[4,32,896]{2,1,0:T(8,128)} collective-permute-done((f32[4,32,896]{2,1,0:T(8,128)S(1)}, f32[4,32,896]{2,1,0:T(8,128)}, u32[]{:S(2)}, u32[]{:S(2)}) %collective-permute-start.11) | collective-permute-done | bytes 458784 | tf_op jit(solution)/shard_map/ppermute | solution.py:172
  122.1 1.3 copy-done.9
  123.5 8.1 %shard_map.76 = f32[32,16,896]{2,1,0:T(8,128)} custom-call(s32[2]{0:T(128)} %pad_add_fusion.place, f32[32,8,16,128]{3,2,1,0:T(8,128)} %copy-done.9, f32[4,32,896]{2,1,0:T(8,128)} %get-tuple-element.36.refs_0_, f32[4,32,896]{2,1,0:T(8,128)} %copy-done.4, f32[4,32,896]{2,1,0:T(8,128)} %collective-permute-done.11.refs_2_, f32[4,32,896]{2,1,0:T(8,128)} %copy-done.5, ...), custom_call_target="tpu_custom_call" | custom-call | flops 2818572288 | bytes 7602176 | tf_op jit(solution)/shard_map/pallas_call | solution.py:26
  131.5 10.8 %all-to-all-start.4 = ((f32[32,16,896]{2,1,0:T(8,128)}), f32[32,16,896]{2,1,0:T(8,128)S(1)}, u32[]{:S(2)}, u32[]{:S(2)}) async-start(f32[32,16,896]{2,1,0:T(8,128)} %shard_map.76), calls=%async_computation.4 | async-start | bytes 3670016 | tf_op jit(solution)/shard_map/all_to_all | solution.py:195
  144.0 43.6 %all-to-all-done.4 = f32[32,16,896]{2,1,0:T(8,128)S(1)} async-done(((f32[32,16,896]{2,1,0:T(8,128)}), f32[32,16,896]{2,1,0:T(8,128)S(1)}, u32[]{:S(2)}, u32[]{:S(2)}) %all-to-all-start.4) | async-done | bytes 1835040 | tf_op jit(solution)/shard_map/all_to_all | solution.py:195
  (79 shorter events, 11.5 us)
Async XLA Ops:
  0.6 6.9 %copy-start.19 = (f32[64,2,32]{0,2,1:T(8,128)S(1)}, f32[64,2,32]{0,2,1:T(8,128)}, u32[]{:S(2)}) copy-start(f32[64,2,32]{0,2,1:T(8,128)} %param.5) | copy-start | bytes 49156
  5.5 26.0 %collective-permute-start.3 = (f32[4,32,896]{2,1,0:T(8,128)}, f32[4,32,896]{2,1,0:T(8,128)S(1)}, u32[]{:S(2)}, u32[]{:S(2)}) collective-permute-start(f32[4,32,896]{2,1,0:T(8,128)} %get-tuple-element.28), channel_id=1, source_target_pairs={{0,4},{4,8},{8,12},{12,16},{16,20},{20,24},{24,28},{28,0},{1,5},{5... | collective-permute-start | bytes 1376264 | tf_op jit(solution)/shard_map/ppermute | solution.py:176
  9.2 17.9 %collective-permute-start = (f32[72,1024]{1,0:T(8,128)S(1)}, f32[72,1024]{1,0:T(8,128)S(1)}, u32[]{:S(2)}, u32[]{:S(2)}) collective-permute-start(f32[72,1024]{1,0:T(8,128)S(1)} %get-tuple-element.23), channel_id=1, source_target_pairs={{0,1},{1,2},{2,3},{3,0},{4,5},{5,6},{6,7},{7,4},{8,9},{9,10},{10,1... | collective-permute-start | bytes 884744 | tf_op jit(solution)/shard_map/ppermute | solution.py:172
  10.5 19.0 %collective-permute-start.1 = (f32[72,1024]{1,0:T(8,128)S(1)}, f32[72,1024]{1,0:T(8,128)S(1)}, u32[]{:S(2)}, u32[]{:S(2)}) collective-permute-start(f32[72,1024]{1,0:T(8,128)S(1)} %get-tuple-element.24), channel_id=1, source_target_pairs={{0,2},{1,3},{2,0},{3,1},{4,6},{5,7},{6,4},{7,5},{8,10},{9,11},{10,... | collective-permute-start | bytes 884744 | tf_op jit(solution)/shard_map/ppermute | solution.py:172
  11.1 19.5 %collective-permute-start.2 = (f32[72,1024]{1,0:T(8,128)S(1)}, f32[72,1024]{1,0:T(8,128)S(1)}, u32[]{:S(2)}, u32[]{:S(2)}) collective-permute-start(f32[72,1024]{1,0:T(8,128)S(1)} %get-tuple-element.25), channel_id=1, source_target_pairs={{0,3},{1,0},{2,1},{3,2},{4,7},{5,4},{6,5},{7,6},{8,11},{9,8},{10,9... | collective-permute-start | bytes 884744 | tf_op jit(solution)/shard_map/ppermute | solution.py:172
  13.2 24.0 %all-to-all-start = ((f32[32,16,128]{2,1,0:T(8,128)}), f32[32,16,128]{2,1,0:T(8,128)}, u32[]{:S(2)}, u32[]{:S(2)}) async-start(f32[32,16,128]{2,1,0:T(8,128)} %shard_map.68), calls=%async_computation | async-start | bytes 524288 | tf_op jit(solution)/shard_map/all_to_all | solution.py:195
  24.3 18.7 %collective-permute-start.4 = (f32[4,32,896]{2,1,0:T(8,128)}, f32[4,32,896]{2,1,0:T(8,128)S(1)}, u32[]{:S(2)}, u32[]{:S(2)}) collective-permute-start(f32[4,32,896]{2,1,0:T(8,128)} %get-tuple-element.29), channel_id=1, source_target_pairs={{0,28},{4,0},{8,4},{12,8},{16,12},{20,16},{24,20},{28,24},{1,29},{... | collective-permute-start | bytes 1376264 | tf_op jit(solution)/shard_map/ppermute | solution.py:176
  27.1 10.1 %copy-start.15 = (f32[72,1024]{1,0:T(8,128)}, f32[72,1024]{1,0:T(8,128)S(1)}, u32[]{:S(2)}) copy-start(f32[72,1024]{1,0:T(8,128)S(1)} %collective-permute-done.refs_1_) | copy-start | bytes 884740
  27.1 25.8 %collective-permute-start.5 = (f32[4,32,896]{2,1,0:T(8,128)}, f32[4,32,896]{2,1,0:T(8,128)S(1)}, u32[]{:S(2)}, u32[]{:S(2)}) collective-permute-start(f32[4,32,896]{2,1,0:T(8,128)} %get-tuple-element.30), channel_id=1, source_target_pairs={{0,24},{4,28},{8,0},{12,4},{16,8},{20,12},{24,16},{28,20},{32,40},... | collective-permute-start | bytes 1376264 | tf_op jit(solution)/shard_map/ppermute | solution.py:183
  29.4 7.8 %copy-start.16 = (f32[72,1024]{1,0:T(8,128)}, f32[72,1024]{1,0:T(8,128)S(1)}, u32[]{:S(2)}) copy-start(f32[72,1024]{1,0:T(8,128)S(1)} %collective-permute-done.1.refs_2_) | copy-start | bytes 884740
  29.4 23.5 %collective-permute-start.6 = (f32[4,32,896]{2,1,0:T(8,128)}, f32[4,32,896]{2,1,0:T(8,128)S(1)}, u32[]{:S(2)}, u32[]{:S(2)}) collective-permute-start(f32[4,32,896]{2,1,0:T(8,128)} %get-tuple-element.31), channel_id=1, source_target_pairs={{0,1},{1,2},{2,3},{3,0},{4,5},{5,6},{6,7},{7,4},{8,9},{9,10},{10,1... | collective-permute-start | bytes 1376264 | tf_op jit(solution)/shard_map/ppermute | solution.py:172
  30.6 6.6 %copy-start.17 = (f32[72,1024]{1,0:T(8,128)}, f32[72,1024]{1,0:T(8,128)S(1)}, u32[]{:S(2)}) copy-start(f32[72,1024]{1,0:T(8,128)S(1)} %collective-permute-done.2.refs_3_) | copy-start | bytes 884740
  30.6 22.3 %collective-permute-start.7 = (f32[4,32,896]{2,1,0:T(8,128)}, f32[4,32,896]{2,1,0:T(8,128)S(1)}, u32[]{:S(2)}, u32[]{:S(2)}) collective-permute-start(f32[4,32,896]{2,1,0:T(8,128)} %get-tuple-element.32), channel_id=1, source_target_pairs={{0,2},{1,3},{2,0},{3,1},{4,6},{5,7},{6,4},{7,5},{8,10},{9,11},{10,... | collective-permute-start | bytes 1376264 | tf_op jit(solution)/shard_map/ppermute | solution.py:172
  31.5 21.8 %copy-start.10 = (f32[4,32,896]{2,1,0:T(8,128)}, f32[4,32,896]{2,1,0:T(8,128)S(1)}, u32[]{:S(2)}) copy-start(f32[4,32,896]{2,1,0:T(8,128)S(1)} %collective-permute-done.3.refs_4_.refs_1_) | copy-start | bytes 1376260
  31.5 21.5 %collective-permute-start.8 = (f32[4,32,896]{2,1,0:T(8,128)}, f32[4,32,896]{2,1,0:T(8,128)}, u32[]{:S(2)}, u32[]{:S(2)}) collective-permute-start(f32[4,32,896]{2,1,0:T(8,128)} %get-tuple-element.33), channel_id=1, source_target_pairs={{0,3},{1,0},{2,1},{3,2},{4,7},{5,4},{6,5},{7,6},{8,11},{9,8},{10,9... | collective-permute-start | bytes 1376264 | tf_op jit(solution)/shard_map/ppermute | solution.py:172
  39.6 13.6 %all-to-all-start.1 = ((f32[8,2,16,128]{3,2,1,0:T(8,128)}), f32[8,2,16,128]{3,2,1,0:T(8,128)S(1)}, u32[]{:S(2)}, u32[]{:S(2)}) async-start(f32[8,2,16,128]{3,2,1,0:T(8,128)} %shard_map.71), calls=%async_computation.1 | async-start | bytes 262144 | tf_op jit(solution)/shard_map/all_to_all | solution.py:195
  43.0 10.2 %copy-start.11 = (f32[4,32,896]{2,1,0:T(8,128)}, f32[4,32,896]{2,1,0:T(8,128)S(1)}, u32[]{:S(2)}) copy-start(f32[4,32,896]{2,1,0:T(8,128)S(1)} %collective-permute-done.4.refs_5_.refs_2_) | copy-start | bytes 1376260
  57.1 21.2 %copy-start.2 = (f32[8,2,16,128]{3,2,1,0:T(8,128)S(1)}, f32[8,2,16,128]{3,2,1,0:T(8,128)}, u32[]{:S(2)}) copy-start(f32[8,2,16,128]{3,2,1,0:T(8,128)} %copy-done.1) | copy-start | bytes 393220
  57.1 21.2 %copy-start.8 = (s32[2]{0:T(128)S(1)}, s32[2]{0:T(128)}, u32[]{:S(2)}) copy-start(s32[2]{0:T(128)} %pad_add_fusion.place) | copy-start | bytes 28
  57.1 21.2 %all-to-all-start.2 = ((f32[8,5,16,128]{3,2,1,0:T(8,128)}), f32[8,5,16,128]{3,2,1,0:T(8,128)S(1)}, u32[]{:S(2)}, u32[]{:S(2)}) async-start(f32[8,5,16,128]{3,2,1,0:T(8,128)} %shard_map.72), calls=%async_computation.2 | async-start | bytes 655360 | tf_op jit(solution)/shard_map/all_to_all | solution.py:195
  65.1 11.1 %collective-permute-start.9 = (f32[4,32,896]{2,1,0:T(8,128)}, f32[4,32,896]{2,1,0:T(8,128)S(1)}, u32[]{:S(2)}, u32[]{:S(2)}) collective-permute-start(f32[4,32,896]{2,1,0:T(8,128)} %get-tuple-element.34), channel_id=1, source_target_pairs={{0,1},{1,2},{2,3},{3,0},{4,5},{5,6},{6,7},{7,4},{8,9},{9,10},{10,1... | collective-permute-start | bytes 1376264 | tf_op jit(solution)/shard_map/ppermute | solution.py:172
  66.4 11.9 %collective-permute-start.10 = (f32[4,32,896]{2,1,0:T(8,128)}, f32[4,32,896]{2,1,0:T(8,128)S(1)}, u32[]{:S(2)}, u32[]{:S(2)}) collective-permute-start(f32[4,32,896]{2,1,0:T(8,128)} %get-tuple-element.35), channel_id=1, source_target_pairs={{0,3},{1,0},{2,1},{3,2},{4,7},{5,4},{6,5},{7,6},{8,11},{9,8},{10,9... | collective-permute-start | bytes 1376264 | tf_op jit(solution)/shard_map/ppermute | solution.py:172
  80.4 16.5 %copy-start.20 = (f32[4,32,896]{2,1,0:T(8,128)S(1)}, f32[4,32,896]{2,1,0:T(8,128)}, u32[]{:S(2)}) copy-start(f32[4,32,896]{2,1,0:T(8,128)} %get-tuple-element.37) | copy-start | bytes 1376260
  80.4 41.7 %all-to-all-start.3 = ((f32[32,8,16,128]{3,2,1,0:T(8,128)}), f32[32,8,16,128]{3,2,1,0:T(8,128)S(1)}, u32[]{:S(2)}, u32[]{:S(2)}) async-start(f32[32,8,16,128]{3,2,1,0:T(8,128)} %shard_map.74), calls=%async_computation.3 | async-start | bytes 4194304 | tf_op jit(solution)/shard_map/all_to_all | solution.py:195
  90.9 15.3 %collective-permute-start.12 = (f32[4,32,896]{2,1,0:T(8,128)}, f32[4,32,896]{2,1,0:T(8,128)S(1)}, u32[]{:S(2)}, u32[]{:S(2)}) collective-permute-start(f32[4,32,896]{2,1,0:T(8,128)} %get-tuple-element.39), channel_id=1, source_target_pairs={{0,4},{4,8},{8,12},{12,16},{16,20},{20,24},{24,28},{28,0},{1,5},{5... | collective-permute-start | bytes 1376264 | tf_op jit(solution)/shard_map/ppermute | solution.py:176
  92.7 13.4 %collective-permute-start.13 = (f32[4,32,896]{2,1,0:T(8,128)}, f32[4,32,896]{2,1,0:T(8,128)S(1)}, u32[]{:S(2)}, u32[]{:S(2)}) collective-permute-start(f32[4,32,896]{2,1,0:T(8,128)} %get-tuple-element.40), channel_id=1, source_target_pairs={{0,28},{4,0},{8,4},{12,8},{16,12},{20,16},{24,20},{28,24},{1,29},{... | collective-permute-start | bytes 1376264 | tf_op jit(solution)/shard_map/ppermute | solution.py:176
  94.2 21.8 %collective-permute-start.14 = (f32[4,32,896]{2,1,0:T(8,128)}, f32[4,32,896]{2,1,0:T(8,128)S(1)}, u32[]{:S(2)}, u32[]{:S(2)}) collective-permute-start(f32[4,32,896]{2,1,0:T(8,128)} %get-tuple-element.41), channel_id=1, source_target_pairs={{0,24},{4,28},{8,0},{12,4},{16,8},{20,12},{24,16},{28,20},{32,40},... | collective-permute-start | bytes 1376264 | tf_op jit(solution)/shard_map/ppermute | solution.py:183
  96.9 25.2 %collective-permute-start.11 = (f32[4,32,896]{2,1,0:T(8,128)S(1)}, f32[4,32,896]{2,1,0:T(8,128)}, u32[]{:S(2)}, u32[]{:S(2)}) collective-permute-start(f32[4,32,896]{2,1,0:T(8,128)S(1)} %copy-done.20), channel_id=1, source_target_pairs={{0,2},{1,3},{2,0},{3,1},{4,6},{5,7},{6,4},{7,5},{8,10},{9,11},{10,... | collective-permute-start | bytes 1376264 | tf_op jit(solution)/shard_map/ppermute | solution.py:172
  106.2 15.9 %copy-start.21 = (f32[4,32,896]{2,1,0:T(8,128)}, f32[4,32,896]{2,1,0:T(8,128)S(1)}, u32[]{:S(2)}) copy-start(f32[4,32,896]{2,1,0:T(8,128)S(1)} %collective-permute-done.12.refs_5_) | copy-start | bytes 1376260
  106.2 15.9 %copy-start.22 = (f32[4,32,896]{2,1,0:T(8,128)}, f32[4,32,896]{2,1,0:T(8,128)S(1)}, u32[]{:S(2)}) copy-start(f32[4,32,896]{2,1,0:T(8,128)S(1)} %collective-permute-done.13.refs_6_) | copy-start | bytes 1376260
  131.5 56.0 %all-to-all-start.4 = ((f32[32,16,896]{2,1,0:T(8,128)}), f32[32,16,896]{2,1,0:T(8,128)S(1)}, u32[]{:S(2)}, u32[]{:S(2)}) async-start(f32[32,16,896]{2,1,0:T(8,128)} %shard_map.76), calls=%async_computation.4 | async-start | bytes 3670016 | tf_op jit(solution)/shard_map/all_to_all | solution.py:195
  144.0 43.7 %copy-start.18 = (f32[16,14336]{1,0:T(8,128)S(1)}, f32[16,14336]{1,0:T(8,128)}, u32[]{:S(2)}) copy-start(f32[16,14336]{1,0:T(8,128)} %param.9) | copy-start | bytes 2752516
  (12 other events, 32.2 us)

commit v12 on v11

--- a/solution.py
+++ b/solution.py
@@ -13,6 +13,7 @@
 SPREAD = ("x", "c", "y")
 QUAD = 4
 NEAR = (0, -1, 1, 2, -2)
+SIDES = (0, 1, 3)
 VMEM = pl.BlockSpec(memory_space=pltpu.VMEM)
 ANY = pl.BlockSpec(memory_space=pl.ANY)
 SMEM = pl.BlockSpec(memory_space=pltpu.SMEM)
@@ -123,37 +124,41 @@
     for r in range(Y):
         for k in range(QUAD):
             strip = pl.multiple_of((classes[k] * Y + (place[1] + r) % Y) * width, width)
-            copies.append((factor.at[0, :, pl.ds(strip, width)], by_class[k].at[r]))
+            target = by_class[k].at[SIDES.index(r)] if r in SIDES else by_y[r].at[QUAD + k]
+            copies.append((factor.at[0, :, pl.ds(strip, width)], target))
             copies.append((factor.at[1, :, pl.ds(strip, width)], by_y[r].at[k]))
     copy_all(copies, sems)
 
 
 def turn_kernel(*refs):
-    arrived, sent, sems = refs[:4], refs[4:8], refs[8]
-    copy_all([(arrived[k].at[r], sent[r].at[k]) for r in range(Y) for k in range(QUAD)], sems)
+    arrived, sent, sems = refs[:4], refs[4:7], refs[7]
+    copy_all([(arrived[k].at[i], sent[i].at[k]) for i in range(len(SIDES)) for k in range(QUAD)], sems)
 
 
 def merge_kernel(place, *refs):
     arrived, sent, sems = refs[:4], refs[4:8], refs[8]
-    copy_all([(arrived[r].at[k], sent[k].at[(place[1] + Y - r) % Y]) for r in range(Y) for k in range(QUAD)], sems)
+    copies = [(arrived[r].at[k], sent[k].at[(place[1] + Y - r) % Y]) for r in range(Y) for k in range(QUAD)]
+    copies += [(arrived[2].at[QUAD + k], sent[k].at[Y]) for k in range(QUAD)]
+    copy_all(copies, sems)
 
 
 def update_kernel(place, rows, *refs):
-    by_r, by_k = refs[:Y], refs[Y:Y + QUAD]
-    out, factor, high, low, result, sems = refs[Y + QUAD:]
+    by_r, by_k = refs[:3], refs[3:3 + QUAD]
+    out, sides, classes, high, low, result, sems = refs[3 + QUAD:]
     start = lambda src, dst, i: pltpu.make_async_copy(src, dst, sems.at[i])
-    slots = [(place[1] + Y - r) % Y for r in range(Y)]
-    arriving = [start(by_r[r], factor.at[0, r], r) for r in range(Y)]
-    arriving += [start(by_k[k], factor.at[1, k], Y + k) for k in range(QUAD)]
+    slot = lambda r: (place[1] + Y - r) % Y
+    arriving = [start(by_r[i], sides.at[i], i) for i in range(3)]
+    arriving += [start(by_k[k], classes.at[k], 3 + k) for k in range(QUAD)]
     for copy in arriving:
         copy.start()
     left_high, left_low = split(jnp.concatenate([rows[:, k].reshape(-1, 128) for k in range(2 * QUAD)], axis=1))
-    for r in range(Y):
-        arriving[r].wait()
-        high[0, :, slots[r]], low[0, :, slots[r]] = split(factor[0, r])
+    for i, r in enumerate(SIDES):
+        arriving[i].wait()
+        high[0, :, slot(r)], low[0, :, slot(r)] = split(sides[i])
     for k in range(QUAD):
-        arriving[Y + k].wait()
-        high[1, k], low[1, k] = split(factor[1, k])
+        arriving[3 + k].wait()
+        high[1, k], low[1, k] = split(classes[k, 0:Y])
+        high[0, k, slot(2)], low[0, k, slot(2)] = split(classes[k, Y])
     dot = functools.partial(jnp.dot, preferred_element_type=jnp.float32)
     width = result.shape[2]
     sent = []
@@ -162,7 +167,7 @@
         right_high, right_low = (part[..., at].reshape(2 * QUAD * 128, -1) for part in (high, low))
         product = dot(left_high, right_high) + (dot(left_high, right_low) + dot(left_low, right_high))
         result[..., at] = product.reshape(result.shape[0], 16, -1)
-        sent.append(start(result.at[..., at], out.at[..., at], Y + QUAD + i))
+        sent.append(start(result.at[..., at], out.at[..., at], 3 + QUAD + i))
         sent[-1].start()
     for copy in sent:
         copy.wait()
@@ -187,8 +192,8 @@
     return own, shift_z(up, 1), shift_z(down, -1), shift_far(far)
 
 
-def to_ys(own, *others):
-    return own, *(shift_y(other, step + 1) for step, other in enumerate(others))
+def to_ys(own, *others, steps=(1, 2, 3)):
+    return own, *(shift_y(other, step) for step, other in zip(steps, others))
 
 
 def exchange(value, axes):
@@ -216,8 +221,10 @@
     )
     shared = to_ys(*shared)
 
+    blocks = lambda count: f32(count, 32, width)
     cut = call(
-        cut_kernel, (block,) * 8, (place, trail_factor), (ANY,) * 8, (SMEM, VMEM), sems(32), moved=7340032, limit=60,
+        cut_kernel, (blocks(3),) * 4 + tuple(blocks(8 if r == 2 else 4) for r in range(Y)), (place, trail_factor),
+        (ANY,) * 8, (SMEM, VMEM), sems(32), moved=7340032, limit=60,
     )
     by_class, by_y = to_windows(*cut[:4]), to_ys(*cut[4:])
 
@@ -226,24 +233,30 @@
         VMEM, (SMEM,) + (VMEM,) * 5 + (ANY,) * 2, matrix, limit=60,
     )
     first = exchange(terms, "z")
-    by_r = call(turn_kernel, (block,) * 4, by_class, (ANY,) * 4, (VMEM,) * 4, sems(16), moved=3670016, limit=60)
-    first_factor = to_ys(*by_r)
+    by_r = call(turn_kernel, (block,) * 3, by_class, (ANY,) * 3, (VMEM,) * 4, sems(12), moved=3670016, limit=60)
+    first_factor = to_ys(*by_r, steps=SIDES[1:])
 
     terms = call(
         latter_kernel, f32(Z, len(NEAR), 16, 128), (place, first, *shared, *by_class[1:], *by_y[1:]),
         VMEM, (SMEM,) + (VMEM,) * 5 + (ANY,) * 6, matrix, limit=60,
     )
     arrived = exchange(terms, "z")
-    by_k = call(merge_kernel, (block,) * 4, (place, *by_y), (ANY,) * 4, (SMEM,) + (VMEM,) * 4, sems(16), moved=3670016, limit=60)
+    by_k = call(merge_kernel, (blocks(Y + 1),) * 4, (place, *by_y), (ANY,) * 4, (SMEM,) + (VMEM,) * 4, sems(20), moved=3670016, limit=60)
     latter_factor = to_windows(*by_k)
-    copies = call(close_kernel, f32(X * C * Y, 2 * QUAD, 16, 128), (place, first, arrived, first_factor[1], first_factor[3]), VMEM, (SMEM, VMEM, VMEM, ANY, ANY))
+    copies = call(close_kernel, f32(X * C * Y, 2 * QUAD, 16, 128), (place, first, arrived, *first_factor[1:], by_k[0]), VMEM, (SMEM, VMEM, VMEM) + (ANY,) * 3)
     rows = exchange(copies, SPREAD)
 
-    factor = lambda dtype: pltpu.VMEM((2, QUAD, *block.shape), dtype)
+    part = pltpu.VMEM((2, QUAD, *block.shape), jnp.bfloat16)
     update = call(
         update_kernel, f32(X * C * Y, 16, width), (place, rows, *first_factor, *latter_factor),
-        ANY, (SMEM, VMEM) + (ANY,) * 8,
-        [factor(jnp.float32), factor(jnp.bfloat16), factor(jnp.bfloat16), pltpu.VMEM((X * C * Y, 16, width), jnp.float32)] + sems(12),
+        ANY, (SMEM, VMEM) + (ANY,) * 7,
+        [
+            pltpu.VMEM((3, *block.shape), jnp.float32),
+            pltpu.VMEM((QUAD, Y + 1, 32, width), jnp.float32),
+            part,
+            part,
+            pltpu.VMEM((X * C * Y, 16, width), jnp.float32),
+        ] + sems(11),
         flops=2818572288, moved=7602176, limit=56,
     )
     parts = exchange(update, COLS)

time: 189 us -> 198 us (1.048)
  waiting for transfers between devices: 93.4 us -> 100 us
  local copies, waits for them, and re-layouts: 6.11 us -> 8.12 us
    ppermute x9 -> x8, waiting for transfers between devices: 16.4 us -> 24.9 us  [shift_y(): return lax.ppermute(value, 'y', [(y, (y + step) % Y) for y in range(Y)])]
    ppermute x4, waiting for transfers between devices: 8.77 us -> 13.8 us  [shift_z(): return lax.ppermute(value, 'z', [(z, (z + step) % Z) for z in range(Z)])]
    all_to_all x5, waiting for transfers between devices: 48.5 us -> 44.3 us  [exchange(): return lax.all_to_all(value, axes, 0, 0, tiled=True)]
    ppermute x4, starting transfers between devices: 8.14 us -> 11 us  [shift_z(): return lax.ppermute(value, 'z', [(z, (z + step) % Z) for z in range(Z)])]
    ppermute x2, waiting for transfers between devices: 19.7 us -> 17.5 us  [shift_far(): return lax.ppermute(value, ('c', 'z'), pairs)]
    unnamed x50 -> x52, local copies, waits for them, and re-layouts: 5.04 us -> 7.05 us
    ppermute x9 -> x8, starting transfers between devices: 8.79 us -> 6.97 us  [shift_y(): return lax.ppermute(value, 'y', [(y, (y + step) % Y) for y in range(Y)])]
  transfers between devices with their start and end apart: 20 -> 19, of which waited for: 9 -> 11; matrix products, arithmetic and copies ran while one was open for 1% -> 1% of each run, Pallas kernels for 5% -> 5%
where the time goes in v12:
time: 198 us; the launch traced here: 197 us
  waiting for transfers between devices  100 us (51%)
  starting transfers between devices  59.3 us (30%)
  Pallas kernels  26.6 us (13%)
  local copies, waits for them, and re-layouts  8.12 us (4%)
    all_to_all x5, waiting for transfers between devices, exchange(): return lax.all_to_all(value, axes, 0, 0, tiled=True)  44.3 us
    all_to_all x5, starting transfers between devices, exchange(): return lax.all_to_all(value, axes, 0, 0, tiled=True)  37 us
    pallas_call x9, Pallas kernels, call(): pl.pallas_call(kernel, out_shape=outs, in_specs=in_specs, out_specs=out_s...  26.6 us
    ppermute x8, waiting for transfers between devices, shift_y(): return lax.ppermute(value, 'y', [(y, (y + step) % Y) for y in range(Y)])  24.9 us
    ppermute x2, waiting for transfers between devices, shift_far(): return lax.ppermute(value, ('c', 'z'), pairs)  17.5 us
    ppermute x4, waiting for transfers between devices, shift_z(): return lax.ppermute(value, 'z', [(z, (z + step) % Z) for z in range(Z)])  13.8 us
    ppermute x4, starting transfers between devices, shift_z(): return lax.ppermute(value, 'z', [(z, (z + step) % Z) for z in range(Z)])  11 us
    unnamed x52, local copies, waits for them, and re-layouts  7.05 us
  transfers between devices with their start and end apart: 19, of which 11 were waited for; matrix products, arithmetic and copies ran while one was open for 1% of the time, Pallas kernels for 5%

profile of v12, /device:TPU:20, one launch (start us, length us, event | category | flops | bytes accessed | tf_op | source)
XLA Modules:
  0.0 197.0 jit_solution(17876658571618757616)
XLA Ops:
  1.2 4.2 %shard_map.70 = (f32[3,32,896]{2,1,0:T(8,128)}, f32[3,32,896]{2,1,0:T(8,128)}, f32[3,32,896]{2,1,0:T(8,128)}, f32[3,32,896]{2,1,0:T(8,128)}, f32[4,32,896]{2,1,0...) custom-call(s32[2]{0:T(128)} %pad_add_fusion.place, f32[2,32,14336]{2,1,0:T(8,128)} %factor.1), custom_call_target="tpu_custom_call" | custom-call | bytes 7340032 | tf_op jit(solution)/shard_map/pallas_call | solution.py:27
  7.5 2.2 %collective-permute-start = (f32[72,1024]{1,0:T(8,128)S(1)}, f32[72,1024]{1,0:T(8,128)S(1)}, u32[]{:S(2)}, u32[]{:S(2)}) collective-permute-start(f32[72,1024]{1,0:T(8,128)S(1)} %get-tuple-element.22), channel_id=1, source_target_pairs={{0,1},{1,2},{2,3},{3,0},{4,5},{5,6},{6,7},{7,4},{8,9},{9,10},{10,1... | collective-permute-start | bytes 884744 | tf_op jit(solution)/shard_map/ppermute | solution.py:177
  9.7 1.7 collective-permute-start.1
  12.4 11.6 %all-to-all-start = ((f32[32,16,128]{2,1,0:T(8,128)}), f32[32,16,128]{2,1,0:T(8,128)S(1)}, u32[]{:S(2)}, u32[]{:S(2)}) async-start(f32[32,16,128]{2,1,0:T(8,128)} %shard_map.68), calls=%async_computation | async-start | bytes 524288 | tf_op jit(solution)/shard_map/all_to_all | solution.py:200
  24.0 1.5 collective-permute-start.3
  26.1 13.2 %collective-permute-done.refs_1_ = f32[72,1024]{1,0:T(8,128)S(1)} collective-permute-done((f32[72,1024]{1,0:T(8,128)S(1)}, f32[72,1024]{1,0:T(8,128)S(1)}, u32[]{:S(2)}, u32[]{:S(2)}) %collective-permute-start) | collective-permute-done | bytes 294944 | tf_op jit(solution)/shard_map/ppermute | solution.py:177
  39.3 6.3 %collective-permute-done.1.refs_2_ = f32[72,1024]{1,0:T(8,128)S(1)} collective-permute-done((f32[72,1024]{1,0:T(8,128)S(1)}, f32[72,1024]{1,0:T(8,128)S(1)}, u32[]{:S(2)}, u32[]{:S(2)}) %collective-permute-start.1) | collective-permute-done | bytes 294944 | tf_op jit(solution)/shard_map/ppermute | solution.py:177
  46.4 5.9 %collective-permute-start.4 = (f32[3,32,896]{2,1,0:T(8,128)}, f32[3,32,896]{2,1,0:T(8,128)S(1)}, u32[]{:S(2)}, u32[]{:S(2)}) collective-permute-start(f32[3,32,896]{2,1,0:T(8,128)} %get-tuple-element.28), channel_id=1, source_target_pairs={{0,28},{4,0},{8,4},{12,8},{16,12},{20,16},{24,20},{28,24},{1,29},{... | collective-permute-start | bytes 1032200 | tf_op jit(solution)/shard_map/ppermute | solution.py:181
  52.3 1.6 collective-permute-start.5
  54.6 2.4 %shard_map.71 = f32[8,2,16,128]{3,2,1,0:T(8,128)} custom-call(s32[2]{0:T(128)} %pad_add_fusion.place, f32[32,16,128]{2,1,0:T(8,128)} %copy-done.20, f32[72,1024]{1,0:T(8,128)} %copy-done, f32[72,1024]{1,0:T(8,128)} %copy-done.17, f32[72,1024]{1,0:T(8,128)} %copy-done.18, f32[72,1024]{1,0:T(8,128)} %copy-done.19, ...), custom_call_target="tpu_custom_call" | custom-call | tf_op jit(solution)/shard_map/pallas_call | solution.py:27
  56.9 3.4 %all-to-all-start.1 = ((f32[8,2,16,128]{3,2,1,0:T(8,128)}), f32[8,2,16,128]{3,2,1,0:T(8,128)S(1)}, u32[]{:S(2)}, u32[]{:S(2)}) async-start(f32[8,2,16,128]{3,2,1,0:T(8,128)} %shard_map.71), calls=%async_computation.1 | async-start | bytes 262144 | tf_op jit(solution)/shard_map/all_to_all | solution.py:200
  60.3 2.5 %collective-permute-done.4.refs_5_.refs_2_ = f32[3,32,896]{2,1,0:T(8,128)S(1)} collective-permute-done((f32[3,32,896]{2,1,0:T(8,128)}, f32[3,32,896]{2,1,0:T(8,128)S(1)}, u32[]{:S(2)}, u32[]{:S(2)}) %collective-permute-start.4) | collective-permute-done | bytes 344096 | tf_op jit(solution)/shard_map/ppermute | solution.py:181
  62.8 4.6 %collective-permute-done.5.refs_6_.refs_3_ = f32[3,32,896]{2,1,0:T(8,128)S(1)} collective-permute-done((f32[3,32,896]{2,1,0:T(8,128)}, f32[3,32,896]{2,1,0:T(8,128)S(1)}, u32[]{:S(2)}, u32[]{:S(2)}) %collective-permute-start.5) | collective-permute-done | bytes 344096 | tf_op jit(solution)/shard_map/ppermute | solution.py:188
  67.5 1.8 all-to-all-done.1.arrived.first
  70.9 2.4 %shard_map.72 = f32[8,5,16,128]{3,2,1,0:T(8,128)} custom-call(s32[2]{0:T(128)} %pad_add_fusion.place, f32[8,2,16,128]{3,2,1,0:T(8,128)} %copy-done.1, f32[72,1024]{1,0:T(8,128)} %copy-done, f32[72,1024]{1,0:T(8,128)} %copy-done.17, f32[72,1024]{1,0:T(8,128)} %copy-done.18, f32[72,1024]{1,0:T(8,128)} %copy-done.19, f32[3,32,896]{2,1,0:T(8,128)} %copy-done.14, ...), custom_call_target="tpu_custom_call" | custom-call | tf_op jit(solution)/shard_map/pallas_call | solution.py:27
  73.3 5.6 %all-to-all-start.2 = ((f32[8,5,16,128]{3,2,1,0:T(8,128)}), f32[8,5,16,128]{3,2,1,0:T(8,128)S(1)}, u32[]{:S(2)}, u32[]{:S(2)}) async-start(f32[8,5,16,128]{3,2,1,0:T(8,128)} %shard_map.72), calls=%async_computation.2 | async-start | bytes 655360 | tf_op jit(solution)/shard_map/all_to_all | solution.py:200
  78.9 2.5 %shard_map.73 = (f32[4,32,896]{2,1,0:T(8,128)}, f32[4,32,896]{2,1,0:T(8,128)}, f32[4,32,896]{2,1,0:T(8,128)}) custom-call(f32[3,32,896]{2,1,0:T(8,128)} %get-tuple-element.25.refs_4_.refs_0_, f32[3,32,896]{2,1,0:T(8,128)} %copy-done.14, f32[3,32,896]{2,1,0:T(8,128)} %copy-done.15, f32[3,32,896]{2,1,0:T(8,128)} %copy-done.16), custom_call_target="tpu_custom_call" | custom-call | bytes 3670016 | tf_op jit(solution)/shard_map/pallas_call | solution.py:27
  81.4 1.9 collective-permute-start.9
  83.5 3.2 %shard_map.74 = (f32[5,32,896]{2,1,0:T(8,128)}, f32[5,32,896]{2,1,0:T(8,128)}, f32[5,32,896]{2,1,0:T(8,128)}, f32[5,32,896]{2,1,0:T(8,128)}) custom-call(s32[2]{0:T(128)} %pad_add_fusion.place, f32[4,32,896]{2,1,0:T(8,128)} %get-tuple-element.26.refs_5_.refs_0_, f32[4,32,896]{2,1,0:T(8,128)} %copy-done.12, f32[8,32,896]{2,1,0:T(8,128)} %copy-done.10, ...), custom_call_target="tpu_custom_call" | custom-call | bytes 3670016 | tf_op jit(solution)/shard_map/pallas_call | solution.py:27
  86.7 3.5 %collective-permute-done.9.refs_0_.refs_1_ = f32[4,32,896]{2,1,0:T(8,128)S(1)} collective-permute-done((f32[4,32,896]{2,1,0:T(8,128)}, f32[4,32,896]{2,1,0:T(8,128)S(1)}, u32[]{:S(2)}, u32[]{:S(2)}) %collective-permute-start.9) | collective-permute-done | bytes 458784 | tf_op jit(solution)/shard_map/ppermute | solution.py:177
  90.2 1.9 collective-permute-done.10.refs_1_.refs_2_
  93.3 2.1 %shard_map.75 = f32[32,8,16,128]{3,2,1,0:T(8,128)} custom-call(s32[2]{0:T(128)S(1)} %copy-done.9, f32[8,2,16,128]{3,2,1,0:T(8,128)S(1)} %copy-done.2, f32[8,5,16,128]{3,2,1,0:T(8,128)S(1)} %all-to-all-done.2.arrived, f32[4,32,896]{2,1,0:T(8,128)S(1)} %collective-permute-done.9.refs_0_.refs_1_, f32[4,32,896]{2,1,0:T(8,128)S(1)} %collective-permute-done.10.refs_1_.refs_2_, ...), custom_call_target="tpu_custom_call" | custom-call | tf_op jit(solution)/shard_map/pallas_call | solution.py:27
  95.4 7.4 %all-to-all-start.3 = ((f32[32,8,16,128]{3,2,1,0:T(8,128)}), f32[32,8,16,128]{3,2,1,0:T(8,128)S(1)}, u32[]{:S(2)}, u32[]{:S(2)}) async-start(f32[32,8,16,128]{3,2,1,0:T(8,128)} %shard_map.75), calls=%async_computation.3 | async-start | bytes 4194304 | tf_op jit(solution)/shard_map/all_to_all | solution.py:200
  102.8 2.1 %collective-permute-start.11 = (f32[5,32,896]{2,1,0:T(8,128)}, f32[5,32,896]{2,1,0:T(8,128)S(1)}, u32[]{:S(2)}, u32[]{:S(2)}) collective-permute-start(f32[5,32,896]{2,1,0:T(8,128)} %get-tuple-element.37), channel_id=1, source_target_pairs={{0,4},{4,8},{8,12},{12,16},{16,20},{20,24},{24,28},{28,0},{1,5},{5... | collective-permute-start | bytes 1720328 | tf_op jit(solution)/shard_map/ppermute | solution.py:181
  104.9 1.5 collective-permute-start.12
  106.4 2.7 %collective-permute-start.13 = (f32[5,32,896]{2,1,0:T(8,128)}, f32[5,32,896]{2,1,0:T(8,128)}, u32[]{:S(2)}, u32[]{:S(2)}) collective-permute-start(f32[5,32,896]{2,1,0:T(8,128)} %get-tuple-element.39), channel_id=1, source_target_pairs={{0,24},{4,28},{8,0},{12,4},{16,8},{20,12},{24,16},{28,20},{32,40},... | collective-permute-start | bytes 1720328 | tf_op jit(solution)/shard_map/ppermute | solution.py:188
  109.0 11.1 %collective-permute-done.11.refs_4_ = f32[5,32,896]{2,1,0:T(8,128)S(1)} collective-permute-done((f32[5,32,896]{2,1,0:T(8,128)}, f32[5,32,896]{2,1,0:T(8,128)S(1)}, u32[]{:S(2)}, u32[]{:S(2)}) %collective-permute-start.11) | collective-permute-done | bytes 573472 | tf_op jit(solution)/shard_map/ppermute | solution.py:181
  120.3 12.9 %collective-permute-done.13.refs_6_ = f32[5,32,896]{2,1,0:T(8,128)} collective-permute-done((f32[5,32,896]{2,1,0:T(8,128)}, f32[5,32,896]{2,1,0:T(8,128)}, u32[]{:S(2)}, u32[]{:S(2)}) %collective-permute-start.13) | collective-permute-done | bytes 573472 | tf_op jit(solution)/shard_map/ppermute | solution.py:188
  133.2 1.3 copy-done.11
  134.5 8.1 %shard_map.76 = f32[32,16,896]{2,1,0:T(8,128)} custom-call(s32[2]{0:T(128)} %pad_add_fusion.place, f32[32,8,16,128]{3,2,1,0:T(8,128)} %copy-done.11, f32[4,32,896]{2,1,0:T(8,128)} %get-tuple-element.36.refs_0_, f32[4,32,896]{2,1,0:T(8,128)} %copy-done.5, f32[4,32,896]{2,1,0:T(8,128)} %copy-done.6, f32[5,32,896]{2,1,0:T(8,128)} %get-tuple-element.35.refs_2_.refs_3_, ...), custom_call_target="tpu_custom_call" | custom-call | flops 2818572288 | bytes 7602176 | tf_op jit(solution)/shard_map/pallas_call | solution.py:27
  142.6 9.2 %all-to-all-start.4 = ((f32[32,16,896]{2,1,0:T(8,128)}), f32[32,16,896]{2,1,0:T(8,128)S(1)}, u32[]{:S(2)}, u32[]{:S(2)}) async-start(f32[32,16,896]{2,1,0:T(8,128)} %shard_map.76), calls=%async_computation.4 | async-start | bytes 3670016 | tf_op jit(solution)/shard_map/all_to_all | solution.py:200
  153.4 42.4 %all-to-all-done.4 = f32[32,16,896]{2,1,0:T(8,128)S(1)} async-done(((f32[32,16,896]{2,1,0:T(8,128)}), f32[32,16,896]{2,1,0:T(8,128)S(1)}, u32[]{:S(2)}, u32[]{:S(2)}) %all-to-all-start.4) | async-done | bytes 1835040 | tf_op jit(solution)/shard_map/all_to_all | solution.py:200
  (79 shorter events, 11.5 us)
Async XLA Ops:
  0.6 5.2 %copy-start.22 = (f32[64,2,32]{0,2,1:T(8,128)S(1)}, f32[64,2,32]{0,2,1:T(8,128)}, u32[]{:S(2)}) copy-start(f32[64,2,32]{0,2,1:T(8,128)} %param.5) | copy-start | bytes 49156
  1.2 4.9 %copy-start.7 = (f32[32,1024]{1,0:T(8,128)S(1)}, f32[32,1024]{1,0:T(8,128)}, u32[]{:S(2)}) copy-start(f32[32,1024]{1,0:T(8,128)} %couple.1) | copy-start | bytes 393220
  1.2 4.9 %copy-start.8 = (s32[2]{0:T(128)S(1)}, s32[2]{0:T(128)}, u32[]{:S(2)}) copy-start(s32[2]{0:T(128)} %pad_add_fusion.place) | copy-start | bytes 28
  5.4 63.9 %collective-permute-start.7 = (f32[8,32,896]{2,1,0:T(8,128)}, f32[8,32,896]{2,1,0:T(8,128)S(1)}, u32[]{:S(2)}, u32[]{:S(2)}) collective-permute-start(f32[8,32,896]{2,1,0:T(8,128)} %get-tuple-element.31), channel_id=1, source_target_pairs={{0,2},{1,3},{2,0},{3,1},{4,6},{5,7},{6,4},{7,5},{8,10},{9,11},{10,... | collective-permute-start | bytes 2752520 | tf_op jit(solution)/shard_map/ppermute | solution.py:177
  7.5 31.8 %collective-permute-start = (f32[72,1024]{1,0:T(8,128)S(1)}, f32[72,1024]{1,0:T(8,128)S(1)}, u32[]{:S(2)}, u32[]{:S(2)}) collective-permute-start(f32[72,1024]{1,0:T(8,128)S(1)} %get-tuple-element.22), channel_id=1, source_target_pairs={{0,1},{1,2},{2,3},{3,0},{4,5},{5,6},{6,7},{7,4},{8,9},{9,10},{10,1... | collective-permute-start | bytes 884744 | tf_op jit(solution)/shard_map/ppermute | solution.py:177
  9.7 35.9 %collective-permute-start.1 = (f32[72,1024]{1,0:T(8,128)S(1)}, f32[72,1024]{1,0:T(8,128)S(1)}, u32[]{:S(2)}, u32[]{:S(2)}) collective-permute-start(f32[72,1024]{1,0:T(8,128)S(1)} %get-tuple-element.23), channel_id=1, source_target_pairs={{0,2},{1,3},{2,0},{3,1},{4,6},{5,7},{6,4},{7,5},{8,10},{9,11},{10,... | collective-permute-start | bytes 884744 | tf_op jit(solution)/shard_map/ppermute | solution.py:177
  12.4 41.4 %all-to-all-start = ((f32[32,16,128]{2,1,0:T(8,128)}), f32[32,16,128]{2,1,0:T(8,128)S(1)}, u32[]{:S(2)}, u32[]{:S(2)}) async-start(f32[32,16,128]{2,1,0:T(8,128)} %shard_map.68), calls=%async_computation | async-start | bytes 524288 | tf_op jit(solution)/shard_map/all_to_all | solution.py:200
  24.0 28.2 %collective-permute-start.3 = (f32[3,32,896]{2,1,0:T(8,128)}, f32[3,32,896]{2,1,0:T(8,128)S(1)}, u32[]{:S(2)}, u32[]{:S(2)}) collective-permute-start(f32[3,32,896]{2,1,0:T(8,128)} %get-tuple-element.27), channel_id=1, source_target_pairs={{0,4},{4,8},{8,12},{12,16},{16,20},{20,24},{24,28},{28,0},{1,5},{5... | collective-permute-start | bytes 1032200 | tf_op jit(solution)/shard_map/ppermute | solution.py:181
  25.6 20.1 %collective-permute-start.2 = (f32[72,1024]{1,0:T(8,128)S(1)}, f32[72,1024]{1,0:T(8,128)S(1)}, u32[]{:S(2)}, u32[]{:S(2)}) collective-permute-start(f32[72,1024]{1,0:T(8,128)S(1)} %get-tuple-element.24), channel_id=1, source_target_pairs={{0,3},{1,0},{2,1},{3,2},{4,7},{5,4},{6,5},{7,6},{8,11},{9,8},{10,9... | collective-permute-start | bytes 884744 | tf_op jit(solution)/shard_map/ppermute | solution.py:177
  39.3 14.5 %copy-start.17 = (f32[72,1024]{1,0:T(8,128)}, f32[72,1024]{1,0:T(8,128)S(1)}, u32[]{:S(2)}) copy-start(f32[72,1024]{1,0:T(8,128)S(1)} %collective-permute-done.refs_1_) | copy-start | bytes 884740
  39.3 28.1 %collective-permute-start.6 = (f32[4,32,896]{2,1,0:T(8,128)}, f32[4,32,896]{2,1,0:T(8,128)S(1)}, u32[]{:S(2)}, u32[]{:S(2)}) collective-permute-start(f32[4,32,896]{2,1,0:T(8,128)} %get-tuple-element.30), channel_id=1, source_target_pairs={{0,1},{1,2},{2,3},{3,0},{4,5},{5,6},{6,7},{7,4},{8,9},{9,10},{10,1... | collective-permute-start | bytes 1376264 | tf_op jit(solution)/shard_map/ppermute | solution.py:177
  45.6 21.8 %collective-permute-start.8 = (f32[4,32,896]{2,1,0:T(8,128)}, f32[4,32,896]{2,1,0:T(8,128)S(1)}, u32[]{:S(2)}, u32[]{:S(2)}) collective-permute-start(f32[4,32,896]{2,1,0:T(8,128)} %get-tuple-element.32), channel_id=1, source_target_pairs={{0,3},{1,0},{2,1},{3,2},{4,7},{5,4},{6,5},{7,6},{8,11},{9,8},{10,9... | collective-permute-start | bytes 1376264 | tf_op jit(solution)/shard_map/ppermute | solution.py:177
  46.4 5.9 %copy-start.19 = (f32[72,1024]{1,0:T(8,128)}, f32[72,1024]{1,0:T(8,128)S(1)}, u32[]{:S(2)}) copy-start(f32[72,1024]{1,0:T(8,128)S(1)} %collective-permute-done.2.refs_3_) | copy-start | bytes 884740
  46.4 16.5 %collective-permute-start.4 = (f32[3,32,896]{2,1,0:T(8,128)}, f32[3,32,896]{2,1,0:T(8,128)S(1)}, u32[]{:S(2)}, u32[]{:S(2)}) collective-permute-start(f32[3,32,896]{2,1,0:T(8,128)} %get-tuple-element.28), channel_id=1, source_target_pairs={{0,28},{4,0},{8,4},{12,8},{16,12},{20,16},{24,20},{28,24},{1,29},{... | collective-permute-start | bytes 1032200 | tf_op jit(solution)/shard_map/ppermute | solution.py:181
  52.3 17.0 %copy-start.14 = (f32[3,32,896]{2,1,0:T(8,128)}, f32[3,32,896]{2,1,0:T(8,128)S(1)}, u32[]{:S(2)}) copy-start(f32[3,32,896]{2,1,0:T(8,128)S(1)} %collective-permute-done.3.refs_4_.refs_1_) | copy-start | bytes 1032196
  52.3 15.2 %collective-permute-start.5 = (f32[3,32,896]{2,1,0:T(8,128)}, f32[3,32,896]{2,1,0:T(8,128)S(1)}, u32[]{:S(2)}, u32[]{:S(2)}) collective-permute-start(f32[3,32,896]{2,1,0:T(8,128)} %get-tuple-element.29), channel_id=1, source_target_pairs={{0,24},{4,28},{8,0},{12,4},{16,8},{20,12},{24,16},{28,20},{32,40},... | collective-permute-start | bytes 1032200 | tf_op jit(solution)/shard_map/ppermute | solution.py:188
  56.9 12.4 %all-to-all-start.1 = ((f32[8,2,16,128]{3,2,1,0:T(8,128)}), f32[8,2,16,128]{3,2,1,0:T(8,128)S(1)}, u32[]{:S(2)}, u32[]{:S(2)}) async-start(f32[8,2,16,128]{3,2,1,0:T(8,128)} %shard_map.71), calls=%async_computation.1 | async-start | bytes 262144 | tf_op jit(solution)/shard_map/all_to_all | solution.py:200
  62.8 6.5 %copy-start.15 = (f32[3,32,896]{2,1,0:T(8,128)}, f32[3,32,896]{2,1,0:T(8,128)S(1)}, u32[]{:S(2)}) copy-start(f32[3,32,896]{2,1,0:T(8,128)S(1)} %collective-permute-done.4.refs_5_.refs_2_) | copy-start | bytes 1032196
  73.3 18.7 %copy-start.2 = (f32[8,2,16,128]{3,2,1,0:T(8,128)S(1)}, f32[8,2,16,128]{3,2,1,0:T(8,128)}, u32[]{:S(2)}) copy-start(f32[8,2,16,128]{3,2,1,0:T(8,128)} %copy-done.1) | copy-start | bytes 393220
  73.3 18.7 %copy-start.9 = (s32[2]{0:T(128)S(1)}, s32[2]{0:T(128)}, u32[]{:S(2)}) copy-start(s32[2]{0:T(128)} %pad_add_fusion.place) | copy-start | bytes 28
  73.3 18.7 %all-to-all-start.2 = ((f32[8,5,16,128]{3,2,1,0:T(8,128)}), f32[8,5,16,128]{3,2,1,0:T(8,128)S(1)}, u32[]{:S(2)}, u32[]{:S(2)}) async-start(f32[8,5,16,128]{3,2,1,0:T(8,128)} %shard_map.72), calls=%async_computation.2 | async-start | bytes 655360 | tf_op jit(solution)/shard_map/all_to_all | solution.py:200
  81.4 8.8 %collective-permute-start.9 = (f32[4,32,896]{2,1,0:T(8,128)}, f32[4,32,896]{2,1,0:T(8,128)S(1)}, u32[]{:S(2)}, u32[]{:S(2)}) collective-permute-start(f32[4,32,896]{2,1,0:T(8,128)} %get-tuple-element.33), channel_id=1, source_target_pairs={{0,1},{1,2},{2,3},{3,0},{4,5},{5,6},{6,7},{7,4},{8,9},{9,10},{10,1... | collective-permute-start | bytes 1376264 | tf_op jit(solution)/shard_map/ppermute | solution.py:177
  83.3 8.7 %collective-permute-start.10 = (f32[4,32,896]{2,1,0:T(8,128)}, f32[4,32,896]{2,1,0:T(8,128)S(1)}, u32[]{:S(2)}, u32[]{:S(2)}) collective-permute-start(f32[4,32,896]{2,1,0:T(8,128)} %get-tuple-element.34), channel_id=1, source_target_pairs={{0,3},{1,0},{2,1},{3,2},{4,7},{5,4},{6,5},{7,6},{8,11},{9,8},{10,9... | collective-permute-start | bytes 1376264 | tf_op jit(solution)/shard_map/ppermute | solution.py:177
  90.2 5.2 %copy-start.5 = (f32[4,32,896]{2,1,0:T(8,128)}, f32[4,32,896]{2,1,0:T(8,128)S(1)}, u32[]{:S(2)}) copy-start(f32[4,32,896]{2,1,0:T(8,128)S(1)} %collective-permute-done.9.refs_0_.refs_1_) | copy-start | bytes 1376260
  95.4 37.8 %all-to-all-start.3 = ((f32[32,8,16,128]{3,2,1,0:T(8,128)}), f32[32,8,16,128]{3,2,1,0:T(8,128)S(1)}, u32[]{:S(2)}, u32[]{:S(2)}) async-start(f32[32,8,16,128]{3,2,1,0:T(8,128)} %shard_map.75), calls=%async_computation.3 | async-start | bytes 4194304 | tf_op jit(solution)/shard_map/all_to_all | solution.py:200
  102.8 17.4 %collective-permute-start.11 = (f32[5,32,896]{2,1,0:T(8,128)}, f32[5,32,896]{2,1,0:T(8,128)S(1)}, u32[]{:S(2)}, u32[]{:S(2)}) collective-permute-start(f32[5,32,896]{2,1,0:T(8,128)} %get-tuple-element.37), channel_id=1, source_target_pairs={{0,4},{4,8},{8,12},{12,16},{16,20},{20,24},{24,28},{28,0},{1,5},{5... | collective-permute-start | bytes 1720328 | tf_op jit(solution)/shard_map/ppermute | solution.py:181
  104.9 15.4 %collective-permute-start.12 = (f32[5,32,896]{2,1,0:T(8,128)}, f32[5,32,896]{2,1,0:T(8,128)S(1)}, u32[]{:S(2)}, u32[]{:S(2)}) collective-permute-start(f32[5,32,896]{2,1,0:T(8,128)} %get-tuple-element.38), channel_id=1, source_target_pairs={{0,28},{4,0},{8,4},{12,8},{16,12},{20,16},{24,20},{28,24},{1,29},{... | collective-permute-start | bytes 1720328 | tf_op jit(solution)/shard_map/ppermute | solution.py:181
  106.4 26.8 %collective-permute-start.13 = (f32[5,32,896]{2,1,0:T(8,128)}, f32[5,32,896]{2,1,0:T(8,128)}, u32[]{:S(2)}, u32[]{:S(2)}) collective-permute-start(f32[5,32,896]{2,1,0:T(8,128)} %get-tuple-element.39), channel_id=1, source_target_pairs={{0,24},{4,28},{8,0},{12,4},{16,8},{20,12},{24,16},{28,20},{32,40},... | collective-permute-start | bytes 1720328 | tf_op jit(solution)/shard_map/ppermute | solution.py:188
  120.1 13.0 %copy-start.23 = (f32[5,32,896]{2,1,0:T(8,128)}, f32[5,32,896]{2,1,0:T(8,128)S(1)}, u32[]{:S(2)}) copy-start(f32[5,32,896]{2,1,0:T(8,128)S(1)} %collective-permute-done.11.refs_4_) | copy-start | bytes 1720324
  120.3 12.9 %copy-start.24 = (f32[5,32,896]{2,1,0:T(8,128)}, f32[5,32,896]{2,1,0:T(8,128)S(1)}, u32[]{:S(2)}) copy-start(f32[5,32,896]{2,1,0:T(8,128)S(1)} %collective-permute-done.12.refs_5_) | copy-start | bytes 1720324
  142.6 53.2 %all-to-all-start.4 = ((f32[32,16,896]{2,1,0:T(8,128)}), f32[32,16,896]{2,1,0:T(8,128)S(1)}, u32[]{:S(2)}, u32[]{:S(2)}) async-start(f32[32,16,896]{2,1,0:T(8,128)} %shard_map.76), calls=%async_computation.4 | async-start | bytes 3670016 | tf_op jit(solution)/shard_map/all_to_all | solution.py:200
  153.4 42.6 %copy-start.21 = (f32[16,14336]{1,0:T(8,128)S(1)}, f32[16,14336]{1,0:T(8,128)}, u32[]{:S(2)}) copy-start(f32[16,14336]{1,0:T(8,128)} %param.9) | copy-start | bytes 2752516
  (12 other events, 20.3 us)

commit v13 on v11

--- a/solution.py
+++ b/solution.py
@@ -236,7 +236,7 @@
     arrived = exchange(terms, "z")
     by_k = call(merge_kernel, (block,) * 4, (place, *by_y), (ANY,) * 4, (SMEM,) + (VMEM,) * 4, sems(16), moved=3670016, limit=60)
     latter_factor = to_windows(*by_k)
-    copies = call(close_kernel, f32(X * C * Y, 2 * QUAD, 16, 128), (place, first, arrived, first_factor[1], first_factor[3]), VMEM, (SMEM, VMEM, VMEM, ANY, ANY))
+    copies = call(close_kernel, f32(X * C * Y, 2 * QUAD, 16, 128), (place, first, arrived, first_factor[2], first_factor[3], by_k[0]), VMEM, (SMEM, VMEM, VMEM) + (ANY,) * 3)
     rows = exchange(copies, SPREAD)
 
     factor = lambda dtype: pltpu.VMEM((2, QUAD, *block.shape), dtype)

time: 189 us -> 201 us (1.063)
  waiting for transfers between devices: 93.4 us -> 99.3 us
  starting transfers between devices: 60 us -> 62.8 us
  local copies, waits for them, and re-layouts: 6.11 us -> 8.14 us
    ppermute x9, waiting for transfers between devices: 16.4 us -> 24.7 us  [shift_y(): return lax.ppermute(value, 'y', [(y, (y + step) % Y) for y in range(Y)])]
    ppermute x9, starting transfers between devices: 8.79 us -> 11.2 us  [shift_y(): return lax.ppermute(value, 'y', [(y, (y + step) % Y) for y in range(Y)])]
    unnamed x50 -> x54, local copies, waits for them, and re-layouts: 5.04 us -> 7.07 us
where the time goes in v13:
time: 201 us; the launch traced here: 200 us
  waiting for transfers between devices  99.3 us (49%)
  starting transfers between devices  62.8 us (31%)
  Pallas kernels  26.5 us (13%)
  local copies, waits for them, and re-layouts  8.14 us (4%)
    all_to_all x5, waiting for transfers between devices, exchange(): return lax.all_to_all(value, axes, 0, 0, tiled=True)  46.7 us
    all_to_all x5, starting transfers between devices, exchange(): return lax.all_to_all(value, axes, 0, 0, tiled=True)  38.5 us
    pallas_call x9, Pallas kernels, call(): pl.pallas_call(kernel, out_shape=outs, in_specs=in_specs, out_specs=out_s...  26.5 us
    ppermute x9, waiting for transfers between devices, shift_y(): return lax.ppermute(value, 'y', [(y, (y + step) % Y) for y in range(Y)])  24.7 us
    ppermute x2, waiting for transfers between devices, shift_far(): return lax.ppermute(value, ('c', 'z'), pairs)  19.7 us
    ppermute x9, starting transfers between devices, shift_y(): return lax.ppermute(value, 'y', [(y, (y + step) % Y) for y in range(Y)])  11.2 us
    ppermute x4, starting transfers between devices, shift_z(): return lax.ppermute(value, 'z', [(z, (z + step) % Z) for z in range(Z)])  8.14 us
    ppermute x4, waiting for transfers between devices, shift_z(): return lax.ppermute(value, 'z', [(z, (z + step) % Z) for z in range(Z)])  8.13 us
  transfers between devices with their start and end apart: 20, of which 9 were waited for; matrix products, arithmetic and copies ran while one was open for 1% of the time, Pallas kernels for 5%

profile of v13, /device:TPU:20, one launch (start us, length us, event | category | flops | bytes accessed | tf_op | source)
XLA Modules:
  0.0 199.5 jit_solution(8111902757791445059)
XLA Ops:
  1.3 4.2 %shard_map.70 = (f32[4,32,896]{2,1,0:T(8,128)}, f32[4,32,896]{2,1,0:T(8,128)}, f32[4,32,896]{2,1,0:T(8,128)}, f32[4,32,896]{2,1,0:T(8,128)}, f32[4,32,896]{2,1,0...) custom-call(s32[2]{0:T(128)} %pad_add_fusion.place, f32[2,32,14336]{2,1,0:T(8,128)} %factor.1), custom_call_target="tpu_custom_call" | custom-call | bytes 7340032 | tf_op jit(solution)/shard_map/pallas_call | solution.py:26
  5.5 2.0 collective-permute-start.3
  9.2 1.3 collective-permute-start
  13.2 11.1 %all-to-all-start = ((f32[32,16,128]{2,1,0:T(8,128)}), f32[32,16,128]{2,1,0:T(8,128)}, u32[]{:S(2)}, u32[]{:S(2)}) async-start(f32[32,16,128]{2,1,0:T(8,128)} %shard_map.68), calls=%async_computation | async-start | bytes 524288 | tf_op jit(solution)/shard_map/all_to_all | solution.py:195
  24.3 2.8 %collective-permute-start.4 = (f32[4,32,896]{2,1,0:T(8,128)}, f32[4,32,896]{2,1,0:T(8,128)S(1)}, u32[]{:S(2)}, u32[]{:S(2)}) collective-permute-start(f32[4,32,896]{2,1,0:T(8,128)} %get-tuple-element.29), channel_id=1, source_target_pairs={{0,28},{4,0},{8,4},{12,8},{16,12},{20,16},{24,20},{28,24},{1,29},{... | collective-permute-start | bytes 1376264 | tf_op jit(solution)/shard_map/ppermute | solution.py:176
  27.1 2.3 %collective-permute-start.5 = (f32[4,32,896]{2,1,0:T(8,128)}, f32[4,32,896]{2,1,0:T(8,128)S(1)}, u32[]{:S(2)}, u32[]{:S(2)}) collective-permute-start(f32[4,32,896]{2,1,0:T(8,128)} %get-tuple-element.30), channel_id=1, source_target_pairs={{0,24},{4,28},{8,0},{12,4},{16,8},{20,12},{24,16},{28,20},{32,40},... | collective-permute-start | bytes 1376264 | tf_op jit(solution)/shard_map/ppermute | solution.py:183
  29.4 1.2 collective-permute-start.6
  33.4 3.9 %all-to-all-done.arrived = f32[32,16,128]{2,1,0:T(8,128)} async-done(((f32[32,16,128]{2,1,0:T(8,128)}), f32[32,16,128]{2,1,0:T(8,128)}, u32[]{:S(2)}, u32[]{:S(2)}) %all-to-all-start) | async-done | bytes 262176 | tf_op jit(solution)/shard_map/all_to_all | solution.py:195
  37.2 2.4 %shard_map.71 = f32[8,2,16,128]{3,2,1,0:T(8,128)} custom-call(s32[2]{0:T(128)} %pad_add_fusion.place, f32[32,16,128]{2,1,0:T(8,128)} %all-to-all-done.arrived, f32[72,1024]{1,0:T(8,128)} %copy-done, f32[72,1024]{1,0:T(8,128)} %copy-done.17, f32[72,1024]{1,0:T(8,128)} %copy-done.18, f32[72,1024]{1,0:T(8,128)} %copy-done.19, ...), custom_call_target="tpu_custom_call" | custom-call | tf_op jit(solution)/shard_map/pallas_call | solution.py:26
  39.6 3.4 %all-to-all-start.1 = ((f32[8,2,16,128]{3,2,1,0:T(8,128)}), f32[8,2,16,128]{3,2,1,0:T(8,128)S(1)}, u32[]{:S(2)}, u32[]{:S(2)}) async-start(f32[8,2,16,128]{3,2,1,0:T(8,128)} %shard_map.71), calls=%async_computation.1 | async-start | bytes 262144 | tf_op jit(solution)/shard_map/all_to_all | solution.py:195
  43.0 9.9 %collective-permute-done.5.refs_6_.refs_3_ = f32[4,32,896]{2,1,0:T(8,128)S(1)} collective-permute-done((f32[4,32,896]{2,1,0:T(8,128)}, f32[4,32,896]{2,1,0:T(8,128)S(1)}, u32[]{:S(2)}, u32[]{:S(2)}) %collective-permute-start.5) | collective-permute-done | bytes 458784 | tf_op jit(solution)/shard_map/ppermute | solution.py:183
  54.8 2.4 %shard_map.72 = f32[8,5,16,128]{3,2,1,0:T(8,128)} custom-call(s32[2]{0:T(128)} %pad_add_fusion.place, f32[8,2,16,128]{3,2,1,0:T(8,128)} %copy-done.1, f32[72,1024]{1,0:T(8,128)} %copy-done, f32[72,1024]{1,0:T(8,128)} %copy-done.17, f32[72,1024]{1,0:T(8,128)} %copy-done.18, f32[72,1024]{1,0:T(8,128)} %copy-done.19, f32[4,32,896]{2,1,0:T(8,128)} %copy-done.11, ...), custom_call_target="tpu_custom_call" | custom-call | tf_op jit(solution)/shard_map/pallas_call | solution.py:26
  57.2 5.2 %all-to-all-start.2 = ((f32[8,5,16,128]{3,2,1,0:T(8,128)}), f32[8,5,16,128]{3,2,1,0:T(8,128)S(1)}, u32[]{:S(2)}, u32[]{:S(2)}) async-start(f32[8,5,16,128]{3,2,1,0:T(8,128)} %shard_map.72), calls=%async_computation.2 | async-start | bytes 655360 | tf_op jit(solution)/shard_map/all_to_all | solution.py:195
  62.4 2.8 %shard_map.73 = (f32[4,32,896]{2,1,0:T(8,128)}, f32[4,32,896]{2,1,0:T(8,128)}, f32[4,32,896]{2,1,0:T(8,128)}, f32[4,32,896]{2,1,0:T(8,128)}) custom-call(f32[4,32,896]{2,1,0:T(8,128)} %get-tuple-element.26.refs_4_.refs_0_, f32[4,32,896]{2,1,0:T(8,128)} %copy-done.11, f32[4,32,896]{2,1,0:T(8,128)} %copy-done.12, f32[4,32,896]{2,1,0:T(8,128)} %copy-done.13), custom_call_target="tpu_custom_call" | custom-call | bytes 3670016 | tf_op jit(solution)/shard_map/pallas_call | solution.py:26
  65.2 2.1 %collective-permute-start.9 = (f32[4,32,896]{2,1,0:T(8,128)}, f32[4,32,896]{2,1,0:T(8,128)S(1)}, u32[]{:S(2)}, u32[]{:S(2)}) collective-permute-start(f32[4,32,896]{2,1,0:T(8,128)} %get-tuple-element.34), channel_id=1, source_target_pairs={{0,2},{1,3},{2,0},{3,1},{4,6},{5,7},{6,4},{7,5},{8,10},{9,11},{10,... | collective-permute-start | bytes 1376264 | tf_op jit(solution)/shard_map/ppermute | solution.py:172
  67.3 1.8 collective-permute-start.10
  69.1 2.8 %shard_map.74 = (f32[4,32,896]{2,1,0:T(8,128)}, f32[4,32,896]{2,1,0:T(8,128)}, f32[4,32,896]{2,1,0:T(8,128)}, f32[4,32,896]{2,1,0:T(8,128)}) custom-call(s32[2]{0:T(128)} %pad_add_fusion.place, f32[4,32,896]{2,1,0:T(8,128)} %get-tuple-element.27.refs_5_.refs_0_, f32[4,32,896]{2,1,0:T(8,128)} %copy-done.14, f32[4,32,896]{2,1,0:T(8,128)} %copy-done.15, ...), custom_call_target="tpu_custom_call" | custom-call | bytes 3670016 | tf_op jit(solution)/shard_map/pallas_call | solution.py:26
  71.9 5.7 %collective-permute-done.9.refs_0_.refs_2_ = f32[4,32,896]{2,1,0:T(8,128)S(1)} collective-permute-done((f32[4,32,896]{2,1,0:T(8,128)}, f32[4,32,896]{2,1,0:T(8,128)S(1)}, u32[]{:S(2)}, u32[]{:S(2)}) %collective-permute-start.9) | collective-permute-done | bytes 458784 | tf_op jit(solution)/shard_map/ppermute | solution.py:172
  77.6 10.8 %collective-permute-done.10.refs_1_.refs_3_ = f32[4,32,896]{2,1,0:T(8,128)S(1)} collective-permute-done((f32[4,32,896]{2,1,0:T(8,128)}, f32[4,32,896]{2,1,0:T(8,128)S(1)}, u32[]{:S(2)}, u32[]{:S(2)}) %collective-permute-start.10) | collective-permute-done | bytes 458784 | tf_op jit(solution)/shard_map/ppermute | solution.py:172
  88.5 1.2 copy-done.6
  89.6 2.1 %shard_map.75 = f32[32,8,16,128]{3,2,1,0:T(8,128)} custom-call(s32[2]{0:T(128)S(1)} %copy-done.9, f32[8,2,16,128]{3,2,1,0:T(8,128)S(1)} %copy-done.2, f32[8,5,16,128]{3,2,1,0:T(8,128)S(1)} %all-to-all-done.2.arrived, f32[4,32,896]{2,1,0:T(8,128)S(1)} %collective-permute-done.9.refs_0_.refs_2_, f32[4,32,896]{2,1,0:T(8,128)S(1)} %collective-permute-done.10.refs_1_.refs_3_, ...), custom_call_target="tpu_custom_call" | custom-call | tf_op jit(solution)/shard_map/pallas_call | solution.py:26
  91.8 8.8 %all-to-all-start.3 = ((f32[32,8,16,128]{3,2,1,0:T(8,128)}), f32[32,8,16,128]{3,2,1,0:T(8,128)S(1)}, u32[]{:S(2)}, u32[]{:S(2)}) async-start(f32[32,8,16,128]{3,2,1,0:T(8,128)} %shard_map.75), calls=%async_computation.3 | async-start | bytes 4194304 | tf_op jit(solution)/shard_map/all_to_all | solution.py:195
  100.6 1.8 collective-permute-start.12
  102.4 1.5 collective-permute-start.13
  103.9 2.6 %collective-permute-start.14 = (f32[4,32,896]{2,1,0:T(8,128)}, f32[4,32,896]{2,1,0:T(8,128)S(1)}, u32[]{:S(2)}, u32[]{:S(2)}) collective-permute-start(f32[4,32,896]{2,1,0:T(8,128)} %get-tuple-element.41), channel_id=1, source_target_pairs={{0,24},{4,28},{8,0},{12,4},{16,8},{20,12},{24,16},{28,20},{32,40},... | collective-permute-start | bytes 1376264 | tf_op jit(solution)/shard_map/ppermute | solution.py:183
  107.7 8.1 %collective-permute-done.12.refs_5_ = f32[4,32,896]{2,1,0:T(8,128)S(1)} collective-permute-done((f32[4,32,896]{2,1,0:T(8,128)}, f32[4,32,896]{2,1,0:T(8,128)S(1)}, u32[]{:S(2)}, u32[]{:S(2)}) %collective-permute-start.12) | collective-permute-done | bytes 458784 | tf_op jit(solution)/shard_map/ppermute | solution.py:176
  115.8 9.8 %collective-permute-done.14.refs_7_ = f32[4,32,896]{2,1,0:T(8,128)S(1)} collective-permute-done((f32[4,32,896]{2,1,0:T(8,128)}, f32[4,32,896]{2,1,0:T(8,128)S(1)}, u32[]{:S(2)}, u32[]{:S(2)}) %collective-permute-start.14) | collective-permute-done | bytes 458784 | tf_op jit(solution)/shard_map/ppermute | solution.py:183
  126.4 8.2 %collective-permute-done.11.refs_1_ = f32[4,32,896]{2,1,0:T(8,128)} collective-permute-done((f32[4,32,896]{2,1,0:T(8,128)S(1)}, f32[4,32,896]{2,1,0:T(8,128)}, u32[]{:S(2)}, u32[]{:S(2)}) %collective-permute-start.11) | collective-permute-done | bytes 458784 | tf_op jit(solution)/shard_map/ppermute | solution.py:172
  134.6 1.3 copy-done.10
  136.0 8.1 %shard_map.76 = f32[32,16,896]{2,1,0:T(8,128)} custom-call(s32[2]{0:T(128)} %pad_add_fusion.place, f32[32,8,16,128]{3,2,1,0:T(8,128)} %copy-done.10, f32[4,32,896]{2,1,0:T(8,128)} %get-tuple-element.37.refs_0_, f32[4,32,896]{2,1,0:T(8,128)} %collective-permute-done.11.refs_1_, f32[4,32,896]{2,1,0:T(8,128)} %copy-done.4, f32[4,32,896]{2,1,0:T(8,128)} %copy-done.5, ...), custom_call_target="tpu_custom_call" | custom-call | flops 2818572288 | bytes 7602176 | tf_op jit(solution)/shard_map/pallas_call | solution.py:26
  144.1 10.1 %all-to-all-start.4 = ((f32[32,16,896]{2,1,0:T(8,128)}), f32[32,16,896]{2,1,0:T(8,128)S(1)}, u32[]{:S(2)}, u32[]{:S(2)}) async-start(f32[32,16,896]{2,1,0:T(8,128)} %shard_map.76), calls=%async_computation.4 | async-start | bytes 3670016 | tf_op jit(solution)/shard_map/all_to_all | solution.py:195
  155.8 42.6 %all-to-all-done.4 = f32[32,16,896]{2,1,0:T(8,128)S(1)} async-done(((f32[32,16,896]{2,1,0:T(8,128)}), f32[32,16,896]{2,1,0:T(8,128)S(1)}, u32[]{:S(2)}, u32[]{:S(2)}) %all-to-all-start.4) | async-done | bytes 1835040 | tf_op jit(solution)/shard_map/all_to_all | solution.py:195
  (83 shorter events, 14.3 us)
Async XLA Ops:
  0.6 6.9 %copy-start.21 = (f32[64,2,32]{0,2,1:T(8,128)S(1)}, f32[64,2,32]{0,2,1:T(8,128)}, u32[]{:S(2)}) copy-start(f32[64,2,32]{0,2,1:T(8,128)} %param.5) | copy-start | bytes 49156
  5.5 26.7 %collective-permute-start.3 = (f32[4,32,896]{2,1,0:T(8,128)}, f32[4,32,896]{2,1,0:T(8,128)S(1)}, u32[]{:S(2)}, u32[]{:S(2)}) collective-permute-start(f32[4,32,896]{2,1,0:T(8,128)} %get-tuple-element.28), channel_id=1, source_target_pairs={{0,4},{4,8},{8,12},{12,16},{16,20},{20,24},{24,28},{28,0},{1,5},{5... | collective-permute-start | bytes 1376264 | tf_op jit(solution)/shard_map/ppermute | solution.py:176
  9.2 18.0 %collective-permute-start = (f32[72,1024]{1,0:T(8,128)S(1)}, f32[72,1024]{1,0:T(8,128)S(1)}, u32[]{:S(2)}, u32[]{:S(2)}) collective-permute-start(f32[72,1024]{1,0:T(8,128)S(1)} %get-tuple-element.23), channel_id=1, source_target_pairs={{0,1},{1,2},{2,3},{3,0},{4,5},{5,6},{6,7},{7,4},{8,9},{9,10},{10,1... | collective-permute-start | bytes 884744 | tf_op jit(solution)/shard_map/ppermute | solution.py:172
  10.5 19.0 %collective-permute-start.1 = (f32[72,1024]{1,0:T(8,128)S(1)}, f32[72,1024]{1,0:T(8,128)S(1)}, u32[]{:S(2)}, u32[]{:S(2)}) collective-permute-start(f32[72,1024]{1,0:T(8,128)S(1)} %get-tuple-element.24), channel_id=1, source_target_pairs={{0,2},{1,3},{2,0},{3,1},{4,6},{5,7},{6,4},{7,5},{8,10},{9,11},{10,... | collective-permute-start | bytes 884744 | tf_op jit(solution)/shard_map/ppermute | solution.py:172
  11.1 19.5 %collective-permute-start.2 = (f32[72,1024]{1,0:T(8,128)S(1)}, f32[72,1024]{1,0:T(8,128)S(1)}, u32[]{:S(2)}, u32[]{:S(2)}) collective-permute-start(f32[72,1024]{1,0:T(8,128)S(1)} %get-tuple-element.25), channel_id=1, source_target_pairs={{0,3},{1,0},{2,1},{3,2},{4,7},{5,4},{6,5},{7,6},{8,11},{9,8},{10,9... | collective-permute-start | bytes 884744 | tf_op jit(solution)/shard_map/ppermute | solution.py:172
  13.2 24.0 %all-to-all-start = ((f32[32,16,128]{2,1,0:T(8,128)}), f32[32,16,128]{2,1,0:T(8,128)}, u32[]{:S(2)}, u32[]{:S(2)}) async-start(f32[32,16,128]{2,1,0:T(8,128)} %shard_map.68), calls=%async_computation | async-start | bytes 524288 | tf_op jit(solution)/shard_map/all_to_all | solution.py:195
  24.3 18.7 %collective-permute-start.4 = (f32[4,32,896]{2,1,0:T(8,128)}, f32[4,32,896]{2,1,0:T(8,128)S(1)}, u32[]{:S(2)}, u32[]{:S(2)}) collective-permute-start(f32[4,32,896]{2,1,0:T(8,128)} %get-tuple-element.29), channel_id=1, source_target_pairs={{0,28},{4,0},{8,4},{12,8},{16,12},{20,16},{24,20},{28,24},{1,29},{... | collective-permute-start | bytes 1376264 | tf_op jit(solution)/shard_map/ppermute | solution.py:176
  27.1 10.1 %copy-start.17 = (f32[72,1024]{1,0:T(8,128)}, f32[72,1024]{1,0:T(8,128)S(1)}, u32[]{:S(2)}) copy-start(f32[72,1024]{1,0:T(8,128)S(1)} %collective-permute-done.refs_1_) | copy-start | bytes 884740
  27.1 25.8 %collective-permute-start.5 = (f32[4,32,896]{2,1,0:T(8,128)}, f32[4,32,896]{2,1,0:T(8,128)S(1)}, u32[]{:S(2)}, u32[]{:S(2)}) collective-permute-start(f32[4,32,896]{2,1,0:T(8,128)} %get-tuple-element.30), channel_id=1, source_target_pairs={{0,24},{4,28},{8,0},{12,4},{16,8},{20,12},{24,16},{28,20},{32,40},... | collective-permute-start | bytes 1376264 | tf_op jit(solution)/shard_map/ppermute | solution.py:183
  29.4 7.8 %copy-start.18 = (f32[72,1024]{1,0:T(8,128)}, f32[72,1024]{1,0:T(8,128)S(1)}, u32[]{:S(2)}) copy-start(f32[72,1024]{1,0:T(8,128)S(1)} %collective-permute-done.1.refs_2_) | copy-start | bytes 884740
  29.4 23.5 %collective-permute-start.6 = (f32[4,32,896]{2,1,0:T(8,128)}, f32[4,32,896]{2,1,0:T(8,128)S(1)}, u32[]{:S(2)}, u32[]{:S(2)}) collective-permute-start(f32[4,32,896]{2,1,0:T(8,128)} %get-tuple-element.31), channel_id=1, source_target_pairs={{0,1},{1,2},{2,3},{3,0},{4,5},{5,6},{6,7},{7,4},{8,9},{9,10},{10,1... | collective-permute-start | bytes 1376264 | tf_op jit(solution)/shard_map/ppermute | solution.py:172
  31.4 21.6 %collective-permute-start.7 = (f32[4,32,896]{2,1,0:T(8,128)}, f32[4,32,896]{2,1,0:T(8,128)S(1)}, u32[]{:S(2)}, u32[]{:S(2)}) collective-permute-start(f32[4,32,896]{2,1,0:T(8,128)} %get-tuple-element.32), channel_id=1, source_target_pairs={{0,2},{1,3},{2,0},{3,1},{4,6},{5,7},{6,4},{7,5},{8,10},{9,11},{10,... | collective-permute-start | bytes 1376264 | tf_op jit(solution)/shard_map/ppermute | solution.py:172
  32.2 21.0 %copy-start.11 = (f32[4,32,896]{2,1,0:T(8,128)}, f32[4,32,896]{2,1,0:T(8,128)S(1)}, u32[]{:S(2)}) copy-start(f32[4,32,896]{2,1,0:T(8,128)S(1)} %collective-permute-done.3.refs_4_.refs_1_) | copy-start | bytes 1376260
  32.2 20.7 %collective-permute-start.8 = (f32[4,32,896]{2,1,0:T(8,128)}, f32[4,32,896]{2,1,0:T(8,128)S(1)}, u32[]{:S(2)}, u32[]{:S(2)}) collective-permute-start(f32[4,32,896]{2,1,0:T(8,128)} %get-tuple-element.33), channel_id=1, source_target_pairs={{0,3},{1,0},{2,1},{3,2},{4,7},{5,4},{6,5},{7,6},{8,11},{9,8},{10,9... | collective-permute-start | bytes 1376264 | tf_op jit(solution)/shard_map/ppermute | solution.py:172
  39.6 13.6 %all-to-all-start.1 = ((f32[8,2,16,128]{3,2,1,0:T(8,128)}), f32[8,2,16,128]{3,2,1,0:T(8,128)S(1)}, u32[]{:S(2)}, u32[]{:S(2)}) async-start(f32[8,2,16,128]{3,2,1,0:T(8,128)} %shard_map.71), calls=%async_computation.1 | async-start | bytes 262144 | tf_op jit(solution)/shard_map/all_to_all | solution.py:195
  43.0 10.2 %copy-start.12 = (f32[4,32,896]{2,1,0:T(8,128)}, f32[4,32,896]{2,1,0:T(8,128)S(1)}, u32[]{:S(2)}) copy-start(f32[4,32,896]{2,1,0:T(8,128)S(1)} %collective-permute-done.4.refs_5_.refs_2_) | copy-start | bytes 1376260
  57.2 31.2 %copy-start.2 = (f32[8,2,16,128]{3,2,1,0:T(8,128)S(1)}, f32[8,2,16,128]{3,2,1,0:T(8,128)}, u32[]{:S(2)}) copy-start(f32[8,2,16,128]{3,2,1,0:T(8,128)} %copy-done.1) | copy-start | bytes 393220
  57.2 31.2 %copy-start.9 = (s32[2]{0:T(128)S(1)}, s32[2]{0:T(128)}, u32[]{:S(2)}) copy-start(s32[2]{0:T(128)} %pad_add_fusion.place) | copy-start | bytes 28
  57.2 31.2 %all-to-all-start.2 = ((f32[8,5,16,128]{3,2,1,0:T(8,128)}), f32[8,5,16,128]{3,2,1,0:T(8,128)S(1)}, u32[]{:S(2)}, u32[]{:S(2)}) async-start(f32[8,5,16,128]{3,2,1,0:T(8,128)} %shard_map.72), calls=%async_computation.2 | async-start | bytes 655360 | tf_op jit(solution)/shard_map/all_to_all | solution.py:195
  65.2 12.4 %collective-permute-start.9 = (f32[4,32,896]{2,1,0:T(8,128)}, f32[4,32,896]{2,1,0:T(8,128)S(1)}, u32[]{:S(2)}, u32[]{:S(2)}) collective-permute-start(f32[4,32,896]{2,1,0:T(8,128)} %get-tuple-element.34), channel_id=1, source_target_pairs={{0,2},{1,3},{2,0},{3,1},{4,6},{5,7},{6,4},{7,5},{8,10},{9,11},{10,... | collective-permute-start | bytes 1376264 | tf_op jit(solution)/shard_map/ppermute | solution.py:172
  67.3 21.1 %collective-permute-start.10 = (f32[4,32,896]{2,1,0:T(8,128)}, f32[4,32,896]{2,1,0:T(8,128)S(1)}, u32[]{:S(2)}, u32[]{:S(2)}) collective-permute-start(f32[4,32,896]{2,1,0:T(8,128)} %get-tuple-element.35), channel_id=1, source_target_pairs={{0,3},{1,0},{2,1},{3,2},{4,7},{5,4},{6,5},{7,6},{8,11},{9,8},{10,9... | collective-permute-start | bytes 1376264 | tf_op jit(solution)/shard_map/ppermute | solution.py:172
  77.6 14.1 %copy-start.4 = (f32[4,32,896]{2,1,0:T(8,128)}, f32[4,32,896]{2,1,0:T(8,128)S(1)}, u32[]{:S(2)}) copy-start(f32[4,32,896]{2,1,0:T(8,128)S(1)} %collective-permute-done.9.refs_0_.refs_2_) | copy-start | bytes 1376260
  91.8 14.8 %copy-start.22 = (f32[4,32,896]{2,1,0:T(8,128)S(1)}, f32[4,32,896]{2,1,0:T(8,128)}, u32[]{:S(2)}) copy-start(f32[4,32,896]{2,1,0:T(8,128)} %get-tuple-element.38) | copy-start | bytes 1376260
  91.8 42.9 %all-to-all-start.3 = ((f32[32,8,16,128]{3,2,1,0:T(8,128)}), f32[32,8,16,128]{3,2,1,0:T(8,128)S(1)}, u32[]{:S(2)}, u32[]{:S(2)}) async-start(f32[32,8,16,128]{3,2,1,0:T(8,128)} %shard_map.75), calls=%async_computation.3 | async-start | bytes 4194304 | tf_op jit(solution)/shard_map/all_to_all | solution.py:195
  100.6 15.3 %collective-permute-start.12 = (f32[4,32,896]{2,1,0:T(8,128)}, f32[4,32,896]{2,1,0:T(8,128)S(1)}, u32[]{:S(2)}, u32[]{:S(2)}) collective-permute-start(f32[4,32,896]{2,1,0:T(8,128)} %get-tuple-element.39), channel_id=1, source_target_pairs={{0,4},{4,8},{8,12},{12,16},{16,20},{20,24},{24,28},{28,0},{1,5},{5... | collective-permute-start | bytes 1376264 | tf_op jit(solution)/shard_map/ppermute | solution.py:176
  102.4 13.4 %collective-permute-start.13 = (f32[4,32,896]{2,1,0:T(8,128)}, f32[4,32,896]{2,1,0:T(8,128)S(1)}, u32[]{:S(2)}, u32[]{:S(2)}) collective-permute-start(f32[4,32,896]{2,1,0:T(8,128)} %get-tuple-element.40), channel_id=1, source_target_pairs={{0,28},{4,0},{8,4},{12,8},{16,12},{20,16},{24,20},{28,24},{1,29},{... | collective-permute-start | bytes 1376264 | tf_op jit(solution)/shard_map/ppermute | solution.py:176
  103.9 21.8 %collective-permute-start.14 = (f32[4,32,896]{2,1,0:T(8,128)}, f32[4,32,896]{2,1,0:T(8,128)S(1)}, u32[]{:S(2)}, u32[]{:S(2)}) collective-permute-start(f32[4,32,896]{2,1,0:T(8,128)} %get-tuple-element.41), channel_id=1, source_target_pairs={{0,24},{4,28},{8,0},{12,4},{16,8},{20,12},{24,16},{28,20},{32,40},... | collective-permute-start | bytes 1376264 | tf_op jit(solution)/shard_map/ppermute | solution.py:183
  106.5 28.1 %collective-permute-start.11 = (f32[4,32,896]{2,1,0:T(8,128)S(1)}, f32[4,32,896]{2,1,0:T(8,128)}, u32[]{:S(2)}, u32[]{:S(2)}) collective-permute-start(f32[4,32,896]{2,1,0:T(8,128)S(1)} %copy-done.22), channel_id=1, source_target_pairs={{0,1},{1,2},{2,3},{3,0},{4,5},{5,6},{6,7},{7,4},{8,9},{9,10},{10,1... | collective-permute-start | bytes 1376264 | tf_op jit(solution)/shard_map/ppermute | solution.py:172
  115.8 18.8 %copy-start.23 = (f32[4,32,896]{2,1,0:T(8,128)}, f32[4,32,896]{2,1,0:T(8,128)S(1)}, u32[]{:S(2)}) copy-start(f32[4,32,896]{2,1,0:T(8,128)S(1)} %collective-permute-done.12.refs_5_) | copy-start | bytes 1376260
  115.8 18.8 %copy-start.24 = (f32[4,32,896]{2,1,0:T(8,128)}, f32[4,32,896]{2,1,0:T(8,128)S(1)}, u32[]{:S(2)}) copy-start(f32[4,32,896]{2,1,0:T(8,128)S(1)} %collective-permute-done.13.refs_6_) | copy-start | bytes 1376260
  144.1 54.2 %all-to-all-start.4 = ((f32[32,16,896]{2,1,0:T(8,128)}), f32[32,16,896]{2,1,0:T(8,128)S(1)}, u32[]{:S(2)}, u32[]{:S(2)}) async-start(f32[32,16,896]{2,1,0:T(8,128)} %shard_map.76), calls=%async_computation.4 | async-start | bytes 3670016 | tf_op jit(solution)/shard_map/all_to_all | solution.py:195
  155.8 42.8 %copy-start.20 = (f32[16,14336]{1,0:T(8,128)S(1)}, f32[16,14336]{1,0:T(8,128)}, u32[]{:S(2)}) copy-start(f32[16,14336]{1,0:T(8,128)} %param.9) | copy-start | bytes 2752516
  (14 other events, 32.3 us)

commit v14 on v13

--- a/solution.py
+++ b/solution.py
@@ -13,6 +13,8 @@
 SPREAD = ("x", "c", "y")
 QUAD = 4
 NEAR = (0, -1, 1, 2, -2)
+SIDES = ((0, 0), (0, 1), (0, 3), (1, 0))
+OTHERS = ((1, 1), (1, 2), (1, 3), (0, 2))
 VMEM = pl.BlockSpec(memory_space=pltpu.VMEM)
 ANY = pl.BlockSpec(memory_space=pl.ANY)
 SMEM = pl.BlockSpec(memory_space=pltpu.SMEM)
@@ -120,40 +122,35 @@
     classes = around(place[0])
     width = by_y[0].shape[2]
     copies = []
-    for r in range(Y):
-        for k in range(QUAD):
+    for k in range(QUAD):
+        targets = [by_class[k].at[i] for i in range(4)] + [by_y[i].at[k] for i in range(4)]
+        for (panel, r), target in zip(SIDES + OTHERS, targets):
             strip = pl.multiple_of((classes[k] * Y + (place[1] + r) % Y) * width, width)
-            copies.append((factor.at[0, :, pl.ds(strip, width)], by_class[k].at[r]))
-            copies.append((factor.at[1, :, pl.ds(strip, width)], by_y[r].at[k]))
+            copies.append((factor.at[panel, :, pl.ds(strip, width)], target))
     copy_all(copies, sems)
 
 
 def turn_kernel(*refs):
     arrived, sent, sems = refs[:4], refs[4:8], refs[8]
-    copy_all([(arrived[k].at[r], sent[r].at[k]) for r in range(Y) for k in range(QUAD)], sems)
-
-
-def merge_kernel(place, *refs):
-    arrived, sent, sems = refs[:4], refs[4:8], refs[8]
-    copy_all([(arrived[r].at[k], sent[k].at[(place[1] + Y - r) % Y]) for r in range(Y) for k in range(QUAD)], sems)
+    copy_all([(arrived[a].at[b], sent[b].at[a]) for b in range(4) for a in range(4)], sems)
 
 
 def update_kernel(place, rows, *refs):
-    by_r, by_k = refs[:Y], refs[Y:Y + QUAD]
-    out, factor, high, low, result, sems = refs[Y + QUAD:]
+    blocks = refs[:8]
+    out, factor, high, low, result, sems = refs[8:]
     start = lambda src, dst, i: pltpu.make_async_copy(src, dst, sems.at[i])
-    slots = [(place[1] + Y - r) % Y for r in range(Y)]
-    arriving = [start(by_r[r], factor.at[0, r], r) for r in range(Y)]
-    arriving += [start(by_k[k], factor.at[1, k], Y + k) for k in range(QUAD)]
+    slot = lambda r: (place[1] + Y - r) % Y
+    arriving = [start(blocks[i], factor.at[i], i) for i in range(8)]
     for copy in arriving:
         copy.start()
     left_high, left_low = split(jnp.concatenate([rows[:, k].reshape(-1, 128) for k in range(2 * QUAD)], axis=1))
-    for r in range(Y):
-        arriving[r].wait()
-        high[0, :, slots[r]], low[0, :, slots[r]] = split(factor[0, r])
+    for i, (panel, r) in enumerate(SIDES):
+        arriving[i].wait()
+        high[panel, :, slot(r)], low[panel, :, slot(r)] = split(factor[i])
     for k in range(QUAD):
-        arriving[Y + k].wait()
-        high[1, k], low[1, k] = split(factor[1, k])
+        arriving[4 + k].wait()
+        for i, (panel, r) in enumerate(OTHERS):
+            high[panel, k, slot(r)], low[panel, k, slot(r)] = split(factor[4 + k, i])
     dot = functools.partial(jnp.dot, preferred_element_type=jnp.float32)
     width = result.shape[2]
     sent = []
@@ -162,7 +159,7 @@
         right_high, right_low = (part[..., at].reshape(2 * QUAD * 128, -1) for part in (high, low))
         product = dot(left_high, right_high) + (dot(left_high, right_low) + dot(left_low, right_high))
         result[..., at] = product.reshape(result.shape[0], 16, -1)
-        sent.append(start(result.at[..., at], out.at[..., at], Y + QUAD + i))
+        sent.append(start(result.at[..., at], out.at[..., at], 8 + i))
         sent[-1].start()
     for copy in sent:
         copy.wait()
@@ -185,10 +182,6 @@
 
 def to_windows(own, up, down, far):
     return own, shift_z(up, 1), shift_z(down, -1), shift_far(far)
-
-
-def to_ys(own, *others):
-    return own, *(shift_y(other, step + 1) for step, other in enumerate(others))
 
 
 def exchange(value, axes):
@@ -214,12 +207,13 @@
         share_kernel, (f32(72, 1024),) * Y, (place, second_rhs, diag_inv, coupling),
         (VMEM,) * Y, (SMEM,) + (VMEM,) * 3,
     )
-    shared = to_ys(*shared)
+    shared = [shared[0]] + [shift_y(shared[r], r) for r in range(1, Y)]
 
     cut = call(
         cut_kernel, (block,) * 8, (place, trail_factor), (ANY,) * 8, (SMEM, VMEM), sems(32), moved=7340032, limit=60,
     )
-    by_class, by_y = to_windows(*cut[:4]), to_ys(*cut[4:])
+    by_class = to_windows(*cut[:4])
+    by_y = [shift_y(piece, r) for piece, (_, r) in zip(cut[4:], OTHERS)]
 
     terms = call(
         couple_kernel, f32(Z, 2, 16, 128), (place, arrived, *shared, cut[0], cut[4]),
@@ -227,23 +221,23 @@
     )
     first = exchange(terms, "z")
     by_r = call(turn_kernel, (block,) * 4, by_class, (ANY,) * 4, (VMEM,) * 4, sems(16), moved=3670016, limit=60)
-    first_factor = to_ys(*by_r)
+    first_factor = [shift_y(piece, r) if r else piece for piece, (_, r) in zip(by_r, SIDES)]
 
     terms = call(
-        latter_kernel, f32(Z, len(NEAR), 16, 128), (place, first, *shared, *by_class[1:], *by_y[1:]),
-        VMEM, (SMEM,) + (VMEM,) * 5 + (ANY,) * 6, matrix, limit=60,
+        latter_kernel, f32(Z, len(NEAR), 16, 128), (place, first, *shared, *by_class[1:], *by_y),
+        VMEM, (SMEM,) + (VMEM,) * 5 + (ANY,) * 7, matrix, limit=60,
     )
     arrived = exchange(terms, "z")
-    by_k = call(merge_kernel, (block,) * 4, (place, *by_y), (ANY,) * 4, (SMEM,) + (VMEM,) * 4, sems(16), moved=3670016, limit=60)
+    by_k = call(turn_kernel, (block,) * 4, by_y, (ANY,) * 4, (VMEM,) * 4, sems(16), moved=3670016, limit=60)
     latter_factor = to_windows(*by_k)
-    copies = call(close_kernel, f32(X * C * Y, 2 * QUAD, 16, 128), (place, first, arrived, first_factor[2], first_factor[3], by_k[0]), VMEM, (SMEM, VMEM, VMEM) + (ANY,) * 3)
+    copies = call(close_kernel, f32(X * C * Y, 2 * QUAD, 16, 128), (place, first, arrived, first_factor[1], first_factor[2]), VMEM, (SMEM, VMEM, VMEM, ANY, ANY))
     rows = exchange(copies, SPREAD)
 
-    factor = lambda dtype: pltpu.VMEM((2, QUAD, *block.shape), dtype)
+    part = pltpu.VMEM((2, QUAD, *block.shape), jnp.bfloat16)
     update = call(
         update_kernel, f32(X * C * Y, 16, width), (place, rows, *first_factor, *latter_factor),
         ANY, (SMEM, VMEM) + (ANY,) * 8,
-        [factor(jnp.float32), factor(jnp.bfloat16), factor(jnp.bfloat16), pltpu.VMEM((X * C * Y, 16, width), jnp.float32)] + sems(12),
+        [pltpu.VMEM((8, *block.shape), jnp.float32), part, part, pltpu.VMEM((X * C * Y, 16, width), jnp.float32)] + sems(12),
         flops=2818572288, moved=7602176, limit=56,
     )
     parts = exchange(update, COLS)

time: 201 us -> 192 us (0.955)
  waiting for transfers between devices: 99.3 us -> 93.2 us
  local copies, waits for them, and re-layouts: 8.14 us -> 4.71 us
    ppermute x2, waiting for transfers between devices: 19.7 us -> 9.84 us  [shift_far(): return lax.ppermute(value, ('c', 'z'), pairs)]
    ppermute x9, waiting for transfers between devices: 24.7 us -> 28.5 us  [shift_y(): return lax.ppermute(value, 'y', [(y, (y + step) % Y) for y in range(Y)])]
    unnamed x54 -> x48, local copies, waits for them, and re-layouts: 7.07 us -> 3.64 us
    all_to_all x5, starting transfers between devices: 38.5 us -> 35.8 us  [exchange(): return lax.all_to_all(value, axes, 0, 0, tiled=True)]
  transfers between devices with their start and end apart: 20 -> 20, of which waited for: 9 -> 12; matrix products, arithmetic and copies ran while one was open for 1% -> 1% of each run, Pallas kernels for 5% -> 5%
where the time goes in v14:
time: 192 us; the launch traced here: 190 us
  waiting for transfers between devices  93.2 us (49%)
  starting transfers between devices  63.3 us (33%)
  Pallas kernels  26.5 us (14%)
  local copies, waits for them, and re-layouts  4.71 us (2%)
    all_to_all x5, waiting for transfers between devices, exchange(): return lax.all_to_all(value, axes, 0, 0, tiled=True)  45.6 us
    all_to_all x5, starting transfers between devices, exchange(): return lax.all_to_all(value, axes, 0, 0, tiled=True)  35.8 us
    ppermute x9, waiting for transfers between devices, shift_y(): return lax.ppermute(value, 'y', [(y, (y + step) % Y) for y in range(Y)])  28.5 us
    pallas_call x9, Pallas kernels, call(): pl.pallas_call(kernel, out_shape=outs, in_specs=in_specs, out_specs=out_s...  26.5 us
    ppermute x9, starting transfers between devices, shift_y(): return lax.ppermute(value, 'y', [(y, (y + step) % Y) for y in range(Y)])  11.7 us
    ppermute x2, waiting for transfers between devices, shift_far(): return lax.ppermute(value, ('c', 'z'), pairs)  9.84 us
    ppermute x4, starting transfers between devices, shift_z(): return lax.ppermute(value, 'z', [(z, (z + step) % Z) for z in range(Z)])  9.52 us
    ppermute x4, waiting for transfers between devices, shift_z(): return lax.ppermute(value, 'z', [(z, (z + step) % Z) for z in range(Z)])  9.31 us
  transfers between devices with their start and end apart: 20, of which 12 were waited for; matrix products, arithmetic and copies ran while one was open for 1% of the time, Pallas kernels for 5%

profile of v14, /device:TPU:20, one launch (start us, length us, event | category | flops | bytes accessed | tf_op | source)
XLA Modules:
  0.0 190.5 jit_solution(15757517680520924477)
XLA Ops:
  1.3 4.2 %shard_map.70 = (f32[4,32,896]{2,1,0:T(8,128)}, f32[4,32,896]{2,1,0:T(8,128)}, f32[4,32,896]{2,1,0:T(8,128)}, f32[4,32,896]{2,1,0:T(8,128)}, f32[4,32,896]{2,1,0...) custom-call(s32[2]{0:T(128)} %pad_add_fusion.place, f32[2,32,14336]{2,1,0:T(8,128)} %factor.1), custom_call_target="tpu_custom_call" | custom-call | bytes 7340032 | tf_op jit(solution)/shard_map/pallas_call | solution.py:28
  5.5 2.0 %collective-permute-start.3 = (f32[4,32,896]{2,1,0:T(8,128)}, f32[4,32,896]{2,1,0:T(8,128)S(1)}, u32[]{:S(2)}, u32[]{:S(2)}) collective-permute-start(f32[4,32,896]{2,1,0:T(8,128)} %get-tuple-element.28), channel_id=1, source_target_pairs={{0,4},{4,8},{8,12},{12,16},{16,20},{20,24},{24,28},{28,0},{1,5},{5... | collective-permute-start | bytes 1376264 | tf_op jit(solution)/shard_map/ppermute | solution.py:173
  7.5 4.0 %collective-permute-start.4 = (f32[4,32,896]{2,1,0:T(8,128)}, f32[4,32,896]{2,1,0:T(8,128)S(1)}, u32[]{:S(2)}, u32[]{:S(2)}) collective-permute-start(f32[4,32,896]{2,1,0:T(8,128)} %get-tuple-element.29), channel_id=1, source_target_pairs={{0,28},{4,0},{8,4},{12,8},{16,12},{20,16},{24,20},{28,24},{1,29},{... | collective-permute-start | bytes 1376264 | tf_op jit(solution)/shard_map/ppermute | solution.py:173
  13.1 1.3 collective-permute-start
  15.1 1.1 collective-permute-start.2
  16.1 1.0 shard_map.68
  17.2 9.3 %all-to-all-start = ((f32[32,16,128]{2,1,0:T(8,128)}), f32[32,16,128]{2,1,0:T(8,128)}, u32[]{:S(2)}, u32[]{:S(2)}) async-start(f32[32,16,128]{2,1,0:T(8,128)} %shard_map.68), calls=%async_computation | async-start | bytes 524288 | tf_op jit(solution)/shard_map/all_to_all | solution.py:188
  26.5 3.6 %collective-permute-start.5 = (f32[4,32,896]{2,1,0:T(8,128)}, f32[4,32,896]{2,1,0:T(8,128)}, u32[]{:S(2)}, u32[]{:S(2)}) collective-permute-start(f32[4,32,896]{2,1,0:T(8,128)} %get-tuple-element.30), channel_id=1, source_target_pairs={{0,24},{4,28},{8,0},{12,4},{16,8},{20,12},{24,16},{28,20},{32,40},... | collective-permute-start | bytes 1376264 | tf_op jit(solution)/shard_map/ppermute | solution.py:180
  32.8 2.1 %collective-permute-start.9 = (f32[4,32,896]{2,1,0:T(8,128)}, f32[4,32,896]{2,1,0:T(8,128)S(1)}, u32[]{:S(2)}, u32[]{:S(2)}) collective-permute-start(f32[4,32,896]{2,1,0:T(8,128)} %get-tuple-element.33), channel_id=1, source_target_pairs={{0,2},{1,3},{2,0},{3,1},{4,6},{5,7},{6,4},{7,5},{8,10},{9,11},{10,... | collective-permute-start | bytes 1376264 | tf_op jit(solution)/shard_map/ppermute | solution.py:169
  34.9 1.5 collective-permute-start.6
  36.4 3.1 %all-to-all-done.arrived = f32[32,16,128]{2,1,0:T(8,128)} async-done(((f32[32,16,128]{2,1,0:T(8,128)}), f32[32,16,128]{2,1,0:T(8,128)}, u32[]{:S(2)}, u32[]{:S(2)}) %all-to-all-start) | async-done | bytes 262176 | tf_op jit(solution)/shard_map/all_to_all | solution.py:188
  39.5 2.4 %shard_map.71 = f32[8,2,16,128]{3,2,1,0:T(8,128)} custom-call(s32[2]{0:T(128)} %pad_add_fusion.place, f32[32,16,128]{2,1,0:T(8,128)} %all-to-all-done.arrived, f32[72,1024]{1,0:T(8,128)} %copy-done, f32[72,1024]{1,0:T(8,128)} %copy-done.15, f32[72,1024]{1,0:T(8,128)} %copy-done.16, f32[72,1024]{1,0:T(8,128)} %copy-done.17, ...), custom_call_target="tpu_custom_call" | custom-call | tf_op jit(solution)/shard_map/pallas_call | solution.py:28
  41.9 3.4 %all-to-all-start.1 = ((f32[8,2,16,128]{3,2,1,0:T(8,128)}), f32[8,2,16,128]{3,2,1,0:T(8,128)S(1)}, u32[]{:S(2)}, u32[]{:S(2)}) async-start(f32[8,2,16,128]{3,2,1,0:T(8,128)} %shard_map.71), calls=%async_computation.1 | async-start | bytes 262144 | tf_op jit(solution)/shard_map/all_to_all | solution.py:188
  45.7 9.0 %collective-permute-done.8.refs_9_.refs_2_ = f32[4,32,896]{2,1,0:T(8,128)S(1)} collective-permute-done((f32[4,32,896]{2,1,0:T(8,128)}, f32[4,32,896]{2,1,0:T(8,128)S(1)}, u32[]{:S(2)}, u32[]{:S(2)}) %collective-permute-start.8) | collective-permute-done | bytes 458784 | tf_op jit(solution)/shard_map/ppermute | solution.py:169
  55.5 6.2 %collective-permute-done.6.refs_7_.refs_0_ = f32[4,32,896]{2,1,0:T(8,128)} collective-permute-done((f32[4,32,896]{2,1,0:T(8,128)}, f32[4,32,896]{2,1,0:T(8,128)}, u32[]{:S(2)}, u32[]{:S(2)}) %collective-permute-start.6) | collective-permute-done | bytes 458784 | tf_op jit(solution)/shard_map/ppermute | solution.py:169
  62.4 2.4 %shard_map.72 = f32[8,5,16,128]{3,2,1,0:T(8,128)} custom-call(s32[2]{0:T(128)} %pad_add_fusion.place, f32[8,2,16,128]{3,2,1,0:T(8,128)} %copy-done.1, f32[72,1024]{1,0:T(8,128)} %copy-done, f32[72,1024]{1,0:T(8,128)} %copy-done.15, f32[72,1024]{1,0:T(8,128)} %copy-done.16, f32[72,1024]{1,0:T(8,128)} %copy-done.17, f32[4,32,896]{2,1,0:T(8,128)} %copy-done.10, ...), custom_call_target="tpu_custom_call" | custom-call | tf_op jit(solution)/shard_map/pallas_call | solution.py:28
  64.8 5.1 %all-to-all-start.2 = ((f32[8,5,16,128]{3,2,1,0:T(8,128)}), f32[8,5,16,128]{3,2,1,0:T(8,128)S(1)}, u32[]{:S(2)}, u32[]{:S(2)}) async-start(f32[8,5,16,128]{3,2,1,0:T(8,128)} %shard_map.72), calls=%async_computation.2 | async-start | bytes 655360 | tf_op jit(solution)/shard_map/all_to_all | solution.py:188
  69.9 2.8 %shard_map.73 = (f32[4,32,896]{2,1,0:T(8,128)}, f32[4,32,896]{2,1,0:T(8,128)}, f32[4,32,896]{2,1,0:T(8,128)}, f32[4,32,896]{2,1,0:T(8,128)}) custom-call(f32[4,32,896]{2,1,0:T(8,128)} %get-tuple-element.26.refs_4_.refs_0_, f32[4,32,896]{2,1,0:T(8,128)} %copy-done.10, f32[4,32,896]{2,1,0:T(8,128)} %copy-done.11, ...), custom_call_target="tpu_custom_call" | custom-call | bytes 3670016 | tf_op jit(solution)/shard_map/pallas_call | solution.py:28
  72.8 2.7 %collective-permute-start.10 = (f32[4,32,896]{2,1,0:T(8,128)}, f32[4,32,896]{2,1,0:T(8,128)S(1)}, u32[]{:S(2)}, u32[]{:S(2)}) collective-permute-start(f32[4,32,896]{2,1,0:T(8,128)} %get-tuple-element.34), channel_id=1, source_target_pairs={{0,1},{1,2},{2,3},{3,0},{4,5},{5,6},{6,7},{7,4},{8,9},{9,10},{10,1... | collective-permute-start | bytes 1376264 | tf_op jit(solution)/shard_map/ppermute | solution.py:169
  76.0 9.3 %collective-permute-done.10.refs_0_.refs_1_ = f32[4,32,896]{2,1,0:T(8,128)S(1)} collective-permute-done((f32[4,32,896]{2,1,0:T(8,128)}, f32[4,32,896]{2,1,0:T(8,128)S(1)}, u32[]{:S(2)}, u32[]{:S(2)}) %collective-permute-start.10) | collective-permute-done | bytes 458784 | tf_op jit(solution)/shard_map/ppermute | solution.py:169
  85.3 2.1 %collective-permute-done.11.refs_1_.refs_2_ = f32[4,32,896]{2,1,0:T(8,128)S(1)} collective-permute-done((f32[4,32,896]{2,1,0:T(8,128)}, f32[4,32,896]{2,1,0:T(8,128)S(1)}, u32[]{:S(2)}, u32[]{:S(2)}) %collective-permute-start.11) | collective-permute-done | bytes 458784 | tf_op jit(solution)/shard_map/ppermute | solution.py:169
  87.4 2.1 %shard_map.74 = f32[32,8,16,128]{3,2,1,0:T(8,128)} custom-call(s32[2]{0:T(128)S(1)} %copy-done.8, f32[8,2,16,128]{3,2,1,0:T(8,128)S(1)} %copy-done.2, f32[8,5,16,128]{3,2,1,0:T(8,128)S(1)} %all-to-all-done.2.arrived, f32[4,32,896]{2,1,0:T(8,128)S(1)} %collective-permute-done.10.refs_0_.refs_1_, f32[4,32,896]{2,1,0:T(8,128)S(1)} %collective-permute-done.11.refs_1_.refs_2_), custom_call_target="tpu_custom_call" | custom-call | tf_op jit(solution)/shard_map/pallas_call | solution.py:28
  89.5 8.9 %all-to-all-start.3 = ((f32[32,8,16,128]{3,2,1,0:T(8,128)}), f32[32,8,16,128]{3,2,1,0:T(8,128)S(1)}, u32[]{:S(2)}, u32[]{:S(2)}) async-start(f32[32,8,16,128]{3,2,1,0:T(8,128)} %shard_map.74), calls=%async_computation.3 | async-start | bytes 4194304 | tf_op jit(solution)/shard_map/all_to_all | solution.py:188
  98.4 2.8 %shard_map.75 = (f32[4,32,896]{2,1,0:T(8,128)}, f32[4,32,896]{2,1,0:T(8,128)}, f32[4,32,896]{2,1,0:T(8,128)}, f32[4,32,896]{2,1,0:T(8,128)}) custom-call(f32[4,32,896]{2,1,0:T(8,128)} %collective-permute-done.6.refs_7_.refs_0_, f32[4,32,896]{2,1,0:T(8,128)} %copy-done.12, f32[4,32,896]{2,1,0:T(8,128)} %copy-done.13, f32[4,32,896]{2,1,0:T(8,128)} %copy-done.14), custom_call_target="tpu_custom_call" | custom-call | bytes 3670016 | tf_op jit(solution)/shard_map/pallas_call | solution.py:28
  101.2 2.0 %collective-permute-start.12 = (f32[4,32,896]{2,1,0:T(8,128)}, f32[4,32,896]{2,1,0:T(8,128)S(1)}, u32[]{:S(2)}, u32[]{:S(2)}) collective-permute-start(f32[4,32,896]{2,1,0:T(8,128)} %get-tuple-element.39), channel_id=1, source_target_pairs={{0,4},{4,8},{8,12},{12,16},{16,20},{20,24},{24,28},{28,0},{1,5},{5... | collective-permute-start | bytes 1376264 | tf_op jit(solution)/shard_map/ppermute | solution.py:173
  103.2 1.5 collective-permute-start.13
  104.7 2.6 %collective-permute-start.14 = (f32[4,32,896]{2,1,0:T(8,128)}, f32[4,32,896]{2,1,0:T(8,128)S(1)}, u32[]{:S(2)}, u32[]{:S(2)}) collective-permute-start(f32[4,32,896]{2,1,0:T(8,128)} %get-tuple-element.41), channel_id=1, source_target_pairs={{0,24},{4,28},{8,0},{12,4},{16,8},{20,12},{24,16},{28,20},{32,40},... | collective-permute-start | bytes 1376264 | tf_op jit(solution)/shard_map/ppermute | solution.py:180
  107.3 9.3 %collective-permute-done.12.refs_5_ = f32[4,32,896]{2,1,0:T(8,128)S(1)} collective-permute-done((f32[4,32,896]{2,1,0:T(8,128)}, f32[4,32,896]{2,1,0:T(8,128)S(1)}, u32[]{:S(2)}, u32[]{:S(2)}) %collective-permute-start.12) | collective-permute-done | bytes 458784 | tf_op jit(solution)/shard_map/ppermute | solution.py:173
  116.6 9.8 %collective-permute-done.14.refs_7_ = f32[4,32,896]{2,1,0:T(8,128)S(1)} collective-permute-done((f32[4,32,896]{2,1,0:T(8,128)}, f32[4,32,896]{2,1,0:T(8,128)S(1)}, u32[]{:S(2)}, u32[]{:S(2)}) %collective-permute-start.14) | collective-permute-done | bytes 458784 | tf_op jit(solution)/shard_map/ppermute | solution.py:180
  128.0 8.1 %shard_map.76 = f32[32,16,896]{2,1,0:T(8,128)} custom-call(s32[2]{0:T(128)} %pad_add_fusion.place, f32[32,8,16,128]{3,2,1,0:T(8,128)} %copy-done.9, f32[4,32,896]{2,1,0:T(8,128)} %get-tuple-element.36.refs_0_, f32[4,32,896]{2,1,0:T(8,128)} %copy-done.4, f32[4,32,896]{2,1,0:T(8,128)} %copy-done.5, f32[4,32,896]{2,1,0:T(8,128)} %get-tuple-element.37.refs_3_, ...), custom_call_target="tpu_custom_call" | custom-call | flops 2818572288 | bytes 7602176 | tf_op jit(solution)/shard_map/pallas_call | solution.py:28
  136.1 9.1 %all-to-all-start.4 = ((f32[32,16,896]{2,1,0:T(8,128)}), f32[32,16,896]{2,1,0:T(8,128)S(1)}, u32[]{:S(2)}, u32[]{:S(2)}) async-start(f32[32,16,896]{2,1,0:T(8,128)} %shard_map.76), calls=%async_computation.4 | async-start | bytes 3670016 | tf_op jit(solution)/shard_map/all_to_all | solution.py:188
  146.8 42.4 %all-to-all-done.4 = f32[32,16,896]{2,1,0:T(8,128)S(1)} async-done(((f32[32,16,896]{2,1,0:T(8,128)}), f32[32,16,896]{2,1,0:T(8,128)S(1)}, u32[]{:S(2)}, u32[]{:S(2)}) %all-to-all-start.4) | async-done | bytes 1835040 | tf_op jit(solution)/shard_map/all_to_all | solution.py:188
  (77 shorter events, 12.3 us)
Async XLA Ops:
  0.6 10.9 %copy-start.19 = (f32[64,2,32]{0,2,1:T(8,128)S(1)}, f32[64,2,32]{0,2,1:T(8,128)}, u32[]{:S(2)}) copy-start(f32[64,2,32]{0,2,1:T(8,128)} %param.5) | copy-start | bytes 49156
  1.3 10.5 %copy-start.3 = (f32[2,32,1024]{2,1,0:T(8,128)S(1)}, f32[2,32,1024]{2,1,0:T(8,128)}, u32[]{:S(2)}) copy-start(f32[2,32,1024]{2,1,0:T(8,128)} %inverse.3) | copy-start | bytes 786436
  1.3 10.5 %copy-start.6 = (f32[32,1024]{1,0:T(8,128)S(1)}, f32[32,1024]{1,0:T(8,128)}, u32[]{:S(2)}) copy-start(f32[32,1024]{1,0:T(8,128)} %couple.1) | copy-start | bytes 393220
  1.3 10.5 %copy-start.7 = (s32[2]{0:T(128)S(1)}, s32[2]{0:T(128)}, u32[]{:S(2)}) copy-start(s32[2]{0:T(128)} %pad_add_fusion.place) | copy-start | bytes 28
  5.5 27.4 %collective-permute-start.3 = (f32[4,32,896]{2,1,0:T(8,128)}, f32[4,32,896]{2,1,0:T(8,128)S(1)}, u32[]{:S(2)}, u32[]{:S(2)}) collective-permute-start(f32[4,32,896]{2,1,0:T(8,128)} %get-tuple-element.28), channel_id=1, source_target_pairs={{0,4},{4,8},{8,12},{12,16},{16,20},{20,24},{24,28},{28,0},{1,5},{5... | collective-permute-start | bytes 1376264 | tf_op jit(solution)/shard_map/ppermute | solution.py:173
  7.5 27.4 %collective-permute-start.4 = (f32[4,32,896]{2,1,0:T(8,128)}, f32[4,32,896]{2,1,0:T(8,128)S(1)}, u32[]{:S(2)}, u32[]{:S(2)}) collective-permute-start(f32[4,32,896]{2,1,0:T(8,128)} %get-tuple-element.29), channel_id=1, source_target_pairs={{0,28},{4,0},{8,4},{12,8},{16,12},{20,16},{24,20},{28,24},{1,29},{... | collective-permute-start | bytes 1376264 | tf_op jit(solution)/shard_map/ppermute | solution.py:173
  13.1 13.4 %collective-permute-start = (f32[72,1024]{1,0:T(8,128)S(1)}, f32[72,1024]{1,0:T(8,128)S(1)}, u32[]{:S(2)}, u32[]{:S(2)}) collective-permute-start(f32[72,1024]{1,0:T(8,128)S(1)} %get-tuple-element.23), channel_id=1, source_target_pairs={{0,1},{1,2},{2,3},{3,0},{4,5},{5,6},{6,7},{7,4},{8,9},{9,10},{10,1... | collective-permute-start | bytes 884744 | tf_op jit(solution)/shard_map/ppermute | solution.py:169
  14.4 15.7 %collective-permute-start.1 = (f32[72,1024]{1,0:T(8,128)S(1)}, f32[72,1024]{1,0:T(8,128)S(1)}, u32[]{:S(2)}, u32[]{:S(2)}) collective-permute-start(f32[72,1024]{1,0:T(8,128)S(1)} %get-tuple-element.24), channel_id=1, source_target_pairs={{0,2},{1,3},{2,0},{3,1},{4,6},{5,7},{6,4},{7,5},{8,10},{9,11},{10,... | collective-permute-start | bytes 884744 | tf_op jit(solution)/shard_map/ppermute | solution.py:169
  15.1 16.7 %collective-permute-start.2 = (f32[72,1024]{1,0:T(8,128)S(1)}, f32[72,1024]{1,0:T(8,128)S(1)}, u32[]{:S(2)}, u32[]{:S(2)}) collective-permute-start(f32[72,1024]{1,0:T(8,128)S(1)} %get-tuple-element.25), channel_id=1, source_target_pairs={{0,3},{1,0},{2,1},{3,2},{4,7},{5,4},{6,5},{7,6},{8,11},{9,8},{10,9... | collective-permute-start | bytes 884744 | tf_op jit(solution)/shard_map/ppermute | solution.py:169
  17.2 22.3 %all-to-all-start = ((f32[32,16,128]{2,1,0:T(8,128)}), f32[32,16,128]{2,1,0:T(8,128)}, u32[]{:S(2)}, u32[]{:S(2)}) async-start(f32[32,16,128]{2,1,0:T(8,128)} %shard_map.68), calls=%async_computation | async-start | bytes 524288 | tf_op jit(solution)/shard_map/all_to_all | solution.py:188
  26.5 13.0 %copy-start.15 = (f32[72,1024]{1,0:T(8,128)}, f32[72,1024]{1,0:T(8,128)S(1)}, u32[]{:S(2)}) copy-start(f32[72,1024]{1,0:T(8,128)S(1)} %collective-permute-done.refs_1_) | copy-start | bytes 884740
  26.5 18.8 %collective-permute-start.5 = (f32[4,32,896]{2,1,0:T(8,128)}, f32[4,32,896]{2,1,0:T(8,128)}, u32[]{:S(2)}, u32[]{:S(2)}) collective-permute-start(f32[4,32,896]{2,1,0:T(8,128)} %get-tuple-element.30), channel_id=1, source_target_pairs={{0,24},{4,28},{8,0},{12,4},{16,8},{20,12},{24,16},{28,20},{32,40},... | collective-permute-start | bytes 1376264 | tf_op jit(solution)/shard_map/ppermute | solution.py:180
  30.2 15.6 %collective-permute-start.7 = (f32[4,32,896]{2,1,0:T(8,128)}, f32[4,32,896]{2,1,0:T(8,128)S(1)}, u32[]{:S(2)}, u32[]{:S(2)}) collective-permute-start(f32[4,32,896]{2,1,0:T(8,128)} %get-tuple-element.31), channel_id=1, source_target_pairs={{0,2},{1,3},{2,0},{3,1},{4,6},{5,7},{6,4},{7,5},{8,10},{9,11},{10,... | collective-permute-start | bytes 1376264 | tf_op jit(solution)/shard_map/ppermute | solution.py:169
  31.8 22.9 %collective-permute-start.8 = (f32[4,32,896]{2,1,0:T(8,128)}, f32[4,32,896]{2,1,0:T(8,128)S(1)}, u32[]{:S(2)}, u32[]{:S(2)}) collective-permute-start(f32[4,32,896]{2,1,0:T(8,128)} %get-tuple-element.32), channel_id=1, source_target_pairs={{0,3},{1,0},{2,1},{3,2},{4,7},{5,4},{6,5},{7,6},{8,11},{9,8},{10,9... | collective-permute-start | bytes 1376264 | tf_op jit(solution)/shard_map/ppermute | solution.py:169
  32.8 28.9 %copy-start.10 = (f32[4,32,896]{2,1,0:T(8,128)}, f32[4,32,896]{2,1,0:T(8,128)S(1)}, u32[]{:S(2)}) copy-start(f32[4,32,896]{2,1,0:T(8,128)S(1)} %collective-permute-done.3.refs_4_.refs_1_) | copy-start | bytes 1376260
  32.8 22.7 %collective-permute-start.9 = (f32[4,32,896]{2,1,0:T(8,128)}, f32[4,32,896]{2,1,0:T(8,128)S(1)}, u32[]{:S(2)}, u32[]{:S(2)}) collective-permute-start(f32[4,32,896]{2,1,0:T(8,128)} %get-tuple-element.33), channel_id=1, source_target_pairs={{0,2},{1,3},{2,0},{3,1},{4,6},{5,7},{6,4},{7,5},{8,10},{9,11},{10,... | collective-permute-start | bytes 1376264 | tf_op jit(solution)/shard_map/ppermute | solution.py:169
  34.9 26.9 %copy-start.11 = (f32[4,32,896]{2,1,0:T(8,128)}, f32[4,32,896]{2,1,0:T(8,128)S(1)}, u32[]{:S(2)}) copy-start(f32[4,32,896]{2,1,0:T(8,128)S(1)} %collective-permute-done.4.refs_5_.refs_2_) | copy-start | bytes 1376260
  34.9 26.8 %collective-permute-start.6 = (f32[4,32,896]{2,1,0:T(8,128)}, f32[4,32,896]{2,1,0:T(8,128)}, u32[]{:S(2)}, u32[]{:S(2)}) collective-permute-start(f32[4,32,896]{2,1,0:T(8,128)} %get-tuple-element.27.refs_5_), channel_id=1, source_target_pairs={{0,1},{1,2},{2,3},{3,0},{4,5},{5,6},{6,7},{7,4},{8,9},{9,10},{10,1... | collective-permute-start | bytes 1376264 | tf_op jit(solution)/shard_map/ppermute | solution.py:169
  41.9 19.9 %all-to-all-start.1 = ((f32[8,2,16,128]{3,2,1,0:T(8,128)}), f32[8,2,16,128]{3,2,1,0:T(8,128)S(1)}, u32[]{:S(2)}, u32[]{:S(2)}) async-start(f32[8,2,16,128]{3,2,1,0:T(8,128)} %shard_map.71), calls=%async_computation.1 | async-start | bytes 262144 | tf_op jit(solution)/shard_map/all_to_all | solution.py:188
  45.7 16.0 %copy-start.12 = (f32[4,32,896]{2,1,0:T(8,128)}, f32[4,32,896]{2,1,0:T(8,128)S(1)}, u32[]{:S(2)}) copy-start(f32[4,32,896]{2,1,0:T(8,128)S(1)} %collective-permute-done.7.refs_8_.refs_1_) | copy-start | bytes 1376260
  64.8 22.6 %copy-start.2 = (f32[8,2,16,128]{3,2,1,0:T(8,128)S(1)}, f32[8,2,16,128]{3,2,1,0:T(8,128)}, u32[]{:S(2)}) copy-start(f32[8,2,16,128]{3,2,1,0:T(8,128)} %copy-done.1) | copy-start | bytes 393220
  64.8 22.6 %copy-start.8 = (s32[2]{0:T(128)S(1)}, s32[2]{0:T(128)}, u32[]{:S(2)}) copy-start(s32[2]{0:T(128)} %pad_add_fusion.place) | copy-start | bytes 28
  64.8 22.6 %all-to-all-start.2 = ((f32[8,5,16,128]{3,2,1,0:T(8,128)}), f32[8,5,16,128]{3,2,1,0:T(8,128)S(1)}, u32[]{:S(2)}, u32[]{:S(2)}) async-start(f32[8,5,16,128]{3,2,1,0:T(8,128)} %shard_map.72), calls=%async_computation.2 | async-start | bytes 655360 | tf_op jit(solution)/shard_map/all_to_all | solution.py:188
  72.8 12.5 %collective-permute-start.10 = (f32[4,32,896]{2,1,0:T(8,128)}, f32[4,32,896]{2,1,0:T(8,128)S(1)}, u32[]{:S(2)}, u32[]{:S(2)}) collective-permute-start(f32[4,32,896]{2,1,0:T(8,128)} %get-tuple-element.34), channel_id=1, source_target_pairs={{0,1},{1,2},{2,3},{3,0},{4,5},{5,6},{6,7},{7,4},{8,9},{9,10},{10,1... | collective-permute-start | bytes 1376264 | tf_op jit(solution)/shard_map/ppermute | solution.py:169
  75.4 11.9 %collective-permute-start.11 = (f32[4,32,896]{2,1,0:T(8,128)}, f32[4,32,896]{2,1,0:T(8,128)S(1)}, u32[]{:S(2)}, u32[]{:S(2)}) collective-permute-start(f32[4,32,896]{2,1,0:T(8,128)} %get-tuple-element.35), channel_id=1, source_target_pairs={{0,3},{1,0},{2,1},{3,2},{4,7},{5,4},{6,5},{7,6},{8,11},{9,8},{10,9... | collective-permute-start | bytes 1376264 | tf_op jit(solution)/shard_map/ppermute | solution.py:169
  89.5 37.0 %all-to-all-start.3 = ((f32[32,8,16,128]{3,2,1,0:T(8,128)}), f32[32,8,16,128]{3,2,1,0:T(8,128)S(1)}, u32[]{:S(2)}, u32[]{:S(2)}) async-start(f32[32,8,16,128]{3,2,1,0:T(8,128)} %shard_map.74), calls=%async_computation.3 | async-start | bytes 4194304 | tf_op jit(solution)/shard_map/all_to_all | solution.py:188
  101.2 15.4 %collective-permute-start.12 = (f32[4,32,896]{2,1,0:T(8,128)}, f32[4,32,896]{2,1,0:T(8,128)S(1)}, u32[]{:S(2)}, u32[]{:S(2)}) collective-permute-start(f32[4,32,896]{2,1,0:T(8,128)} %get-tuple-element.39), channel_id=1, source_target_pairs={{0,4},{4,8},{8,12},{12,16},{16,20},{20,24},{24,28},{28,0},{1,5},{5... | collective-permute-start | bytes 1376264 | tf_op jit(solution)/shard_map/ppermute | solution.py:173
  103.2 13.4 %collective-permute-start.13 = (f32[4,32,896]{2,1,0:T(8,128)}, f32[4,32,896]{2,1,0:T(8,128)S(1)}, u32[]{:S(2)}, u32[]{:S(2)}) collective-permute-start(f32[4,32,896]{2,1,0:T(8,128)} %get-tuple-element.40), channel_id=1, source_target_pairs={{0,28},{4,0},{8,4},{12,8},{16,12},{20,16},{24,20},{28,24},{1,29},{... | collective-permute-start | bytes 1376264 | tf_op jit(solution)/shard_map/ppermute | solution.py:173
  104.7 21.8 %collective-permute-start.14 = (f32[4,32,896]{2,1,0:T(8,128)}, f32[4,32,896]{2,1,0:T(8,128)S(1)}, u32[]{:S(2)}, u32[]{:S(2)}) collective-permute-start(f32[4,32,896]{2,1,0:T(8,128)} %get-tuple-element.41), channel_id=1, source_target_pairs={{0,24},{4,28},{8,0},{12,4},{16,8},{20,12},{24,16},{28,20},{32,40},... | collective-permute-start | bytes 1376264 | tf_op jit(solution)/shard_map/ppermute | solution.py:180
  116.6 9.9 %copy-start.21 = (f32[4,32,896]{2,1,0:T(8,128)}, f32[4,32,896]{2,1,0:T(8,128)S(1)}, u32[]{:S(2)}) copy-start(f32[4,32,896]{2,1,0:T(8,128)S(1)} %collective-permute-done.13.refs_6_) | copy-start | bytes 1376260
  136.1 53.2 %all-to-all-start.4 = ((f32[32,16,896]{2,1,0:T(8,128)}), f32[32,16,896]{2,1,0:T(8,128)S(1)}, u32[]{:S(2)}, u32[]{:S(2)}) async-start(f32[32,16,896]{2,1,0:T(8,128)} %shard_map.76), calls=%async_computation.4 | async-start | bytes 3670016 | tf_op jit(solution)/shard_map/all_to_all | solution.py:188
  146.8 42.6 %copy-start.18 = (f32[16,14336]{1,0:T(8,128)S(1)}, f32[16,14336]{1,0:T(8,128)}, u32[]{:S(2)}) copy-start(f32[16,14336]{1,0:T(8,128)} %param.9) | copy-start | bytes 2752516
  (11 other events, 50.1 us)

commit v15 on v14

--- a/solution.py
+++ b/solution.py
@@ -224,8 +224,8 @@
     first_factor = [shift_y(piece, r) if r else piece for piece, (_, r) in zip(by_r, SIDES)]
 
     terms = call(
-        latter_kernel, f32(Z, len(NEAR), 16, 128), (place, first, *shared, *by_class[1:], *by_y),
-        VMEM, (SMEM,) + (VMEM,) * 5 + (ANY,) * 7, matrix, limit=60,
+        latter_kernel, f32(Z, len(NEAR), 16, 128), (place, first, *shared, *by_class[1:], *by_y[1:]),
+        VMEM, (SMEM,) + (VMEM,) * 5 + (ANY,) * 6, matrix, limit=60,
     )
     arrived = exchange(terms, "z")
     by_k = call(turn_kernel, (block,) * 4, by_y, (ANY,) * 4, (VMEM,) * 4, sems(16), moved=3670016, limit=60)

time: 192 us -> 223 us (1.16)
  waiting for transfers between devices: 93.2 us -> 119 us
  starting transfers between devices: 63.3 us -> 67 us
    ppermute x9, waiting for transfers between devices: 28.5 us -> 44.6 us  [shift_y(): return lax.ppermute(value, 'y', [(y, (y + step) % Y) for y in range(Y)])]
    ppermute x2, waiting for transfers between devices: 9.84 us -> 18.7 us  [shift_far(): return lax.ppermute(value, ('c', 'z'), pairs)]
    ppermute x9, starting transfers between devices: 11.7 us -> 17.8 us  [shift_y(): return lax.ppermute(value, 'y', [(y, (y + step) % Y) for y in range(Y)])]
    unnamed x48 -> x52, local copies, waits for them, and re-layouts: 3.64 us -> 5.38 us
  transfers between devices with their start and end apart: 20 -> 20, of which waited for: 12 -> 9; matrix products, arithmetic and copies ran while one was open for 1% -> 1% of each run, Pallas kernels for 5% -> 4%
where the time goes in v15:
time: 223 us; the launch traced here: 221 us
  waiting for transfers between devices  119 us (53%)
  starting transfers between devices  67 us (30%)
  Pallas kernels  26.6 us (12%)
  local copies, waits for them, and re-layouts  6.45 us (3%)
    all_to_all x5, waiting for transfers between devices, exchange(): return lax.all_to_all(value, axes, 0, 0, tiled=True)  45.5 us
    ppermute x9, waiting for transfers between devices, shift_y(): return lax.ppermute(value, 'y', [(y, (y + step) % Y) for y in range(Y)])  44.6 us
    all_to_all x5, starting transfers between devices, exchange(): return lax.all_to_all(value, axes, 0, 0, tiled=True)  35.9 us
    pallas_call x9, Pallas kernels, call(): pl.pallas_call(kernel, out_shape=outs, in_specs=in_specs, out_specs=out_s...  26.6 us
    ppermute x2, waiting for transfers between devices, shift_far(): return lax.ppermute(value, ('c', 'z'), pairs)  18.7 us
    ppermute x9, starting transfers between devices, shift_y(): return lax.ppermute(value, 'y', [(y, (y + step) % Y) for y in range(Y)])  17.8 us
    ppermute x4, waiting for transfers between devices, shift_z(): return lax.ppermute(value, 'z', [(z, (z + step) % Z) for z in range(Z)])  9.92 us
    ppermute x4, starting transfers between devices, shift_z(): return lax.ppermute(value, 'z', [(z, (z + step) % Z) for z in range(Z)])  8.32 us
  transfers between devices with their start and end apart: 20, of which 9 were waited for; matrix products, arithmetic and copies ran while one was open for 1% of the time, Pallas kernels for 4%

profile of v15, /device:TPU:20, one launch (start us, length us, event | category | flops | bytes accessed | tf_op | source)
XLA Modules:
  0.0 221.5 jit_solution(1525474592802056906)
XLA Ops:
  1.3 4.2 %shard_map.70 = (f32[4,32,896]{2,1,0:T(8,128)}, f32[4,32,896]{2,1,0:T(8,128)}, f32[4,32,896]{2,1,0:T(8,128)}, f32[4,32,896]{2,1,0:T(8,128)}, f32[4,32,896]{2,1,0...) custom-call(s32[2]{0:T(128)} %pad_add_fusion.place, f32[2,32,14336]{2,1,0:T(8,128)} %factor.1), custom_call_target="tpu_custom_call" | custom-call | bytes 7340032 | tf_op jit(solution)/shard_map/pallas_call | solution.py:28
  5.5 2.0 collective-permute-start.3
  9.2 1.3 collective-permute-start
  12.1 1.1 shard_map.68
  13.2 11.1 %all-to-all-start = ((f32[32,16,128]{2,1,0:T(8,128)}), f32[32,16,128]{2,1,0:T(8,128)}, u32[]{:S(2)}, u32[]{:S(2)}) async-start(f32[32,16,128]{2,1,0:T(8,128)} %shard_map.68), calls=%async_computation | async-start | bytes 524288 | tf_op jit(solution)/shard_map/all_to_all | solution.py:188
  24.3 2.8 %collective-permute-start.4 = (f32[4,32,896]{2,1,0:T(8,128)}, f32[4,32,896]{2,1,0:T(8,128)S(1)}, u32[]{:S(2)}, u32[]{:S(2)}) collective-permute-start(f32[4,32,896]{2,1,0:T(8,128)} %get-tuple-element.29), channel_id=1, source_target_pairs={{0,28},{4,0},{8,4},{12,8},{16,12},{20,16},{24,20},{28,24},{1,29},{... | collective-permute-start | bytes 1376264 | tf_op jit(solution)/shard_map/ppermute | solution.py:173
  27.1 2.3 %collective-permute-start.5 = (f32[4,32,896]{2,1,0:T(8,128)}, f32[4,32,896]{2,1,0:T(8,128)}, u32[]{:S(2)}, u32[]{:S(2)}) collective-permute-start(f32[4,32,896]{2,1,0:T(8,128)} %get-tuple-element.30), channel_id=1, source_target_pairs={{0,24},{4,28},{8,0},{12,4},{16,8},{20,12},{24,16},{28,20},{32,40},... | collective-permute-start | bytes 1376264 | tf_op jit(solution)/shard_map/ppermute | solution.py:180
  30.0 2.1 collective-permute-start.7
  32.1 2.1 collective-permute-start.8
  34.1 3.1 %all-to-all-done.arrived = f32[32,16,128]{2,1,0:T(8,128)} async-done(((f32[32,16,128]{2,1,0:T(8,128)}), f32[32,16,128]{2,1,0:T(8,128)}, u32[]{:S(2)}, u32[]{:S(2)}) %all-to-all-start) | async-done | bytes 262176 | tf_op jit(solution)/shard_map/all_to_all | solution.py:188
  37.2 2.4 %shard_map.71 = f32[8,2,16,128]{3,2,1,0:T(8,128)} custom-call(s32[2]{0:T(128)} %pad_add_fusion.place, f32[32,16,128]{2,1,0:T(8,128)} %all-to-all-done.arrived, f32[72,1024]{1,0:T(8,128)} %copy-done, f32[72,1024]{1,0:T(8,128)} %copy-done.15, f32[72,1024]{1,0:T(8,128)} %copy-done.16, f32[72,1024]{1,0:T(8,128)} %copy-done.17, ...), custom_call_target="tpu_custom_call" | custom-call | tf_op jit(solution)/shard_map/pallas_call | solution.py:28
  39.6 3.4 %all-to-all-start.1 = ((f32[8,2,16,128]{3,2,1,0:T(8,128)}), f32[8,2,16,128]{3,2,1,0:T(8,128)S(1)}, u32[]{:S(2)}, u32[]{:S(2)}) async-start(f32[8,2,16,128]{3,2,1,0:T(8,128)} %shard_map.71), calls=%async_computation.1 | async-start | bytes 262144 | tf_op jit(solution)/shard_map/all_to_all | solution.py:188
  43.0 10.0 %collective-permute-done.5.refs_6_.refs_3_ = f32[4,32,896]{2,1,0:T(8,128)} collective-permute-done((f32[4,32,896]{2,1,0:T(8,128)}, f32[4,32,896]{2,1,0:T(8,128)}, u32[]{:S(2)}, u32[]{:S(2)}) %collective-permute-start.5) | collective-permute-done | bytes 458784 | tf_op jit(solution)/shard_map/ppermute | solution.py:180
  55.3 2.4 %shard_map.72 = f32[8,5,16,128]{3,2,1,0:T(8,128)} custom-call(s32[2]{0:T(128)} %pad_add_fusion.place, f32[8,2,16,128]{3,2,1,0:T(8,128)} %copy-done.1, f32[72,1024]{1,0:T(8,128)} %copy-done, f32[72,1024]{1,0:T(8,128)} %copy-done.15, f32[72,1024]{1,0:T(8,128)} %copy-done.16, f32[72,1024]{1,0:T(8,128)} %copy-done.17, f32[4,32,896]{2,1,0:T(8,128)} %copy-done.10, ...), custom_call_target="tpu_custom_call" | custom-call | tf_op jit(solution)/shard_map/pallas_call | solution.py:28
  57.7 4.6 %all-to-all-start.2 = ((f32[8,5,16,128]{3,2,1,0:T(8,128)}), f32[8,5,16,128]{3,2,1,0:T(8,128)S(1)}, u32[]{:S(2)}, u32[]{:S(2)}) async-start(f32[8,5,16,128]{3,2,1,0:T(8,128)} %shard_map.72), calls=%async_computation.2 | async-start | bytes 655360 | tf_op jit(solution)/shard_map/all_to_all | solution.py:188
  62.4 2.9 %shard_map.73 = (f32[4,32,896]{2,1,0:T(8,128)}, f32[4,32,896]{2,1,0:T(8,128)}, f32[4,32,896]{2,1,0:T(8,128)}, f32[4,32,896]{2,1,0:T(8,128)}) custom-call(f32[4,32,896]{2,1,0:T(8,128)} %get-tuple-element.26.refs_4_.refs_0_, f32[4,32,896]{2,1,0:T(8,128)} %copy-done.10, f32[4,32,896]{2,1,0:T(8,128)} %copy-done.14, ...), custom_call_target="tpu_custom_call" | custom-call | bytes 3670016 | tf_op jit(solution)/shard_map/pallas_call | solution.py:28
  65.2 8.3 %collective-permute-start.9 = (f32[4,32,896]{2,1,0:T(8,128)}, f32[4,32,896]{2,1,0:T(8,128)S(1)}, u32[]{:S(2)}, u32[]{:S(2)}) collective-permute-start(f32[4,32,896]{2,1,0:T(8,128)} %get-tuple-element.34), channel_id=1, source_target_pairs={{0,1},{1,2},{2,3},{3,0},{4,5},{5,6},{6,7},{7,4},{8,9},{9,10},{10,1... | collective-permute-start | bytes 1376264 | tf_op jit(solution)/shard_map/ppermute | solution.py:169
  74.1 9.7 %collective-permute-done.9.refs_0_.refs_1_ = f32[4,32,896]{2,1,0:T(8,128)S(1)} collective-permute-done((f32[4,32,896]{2,1,0:T(8,128)}, f32[4,32,896]{2,1,0:T(8,128)S(1)}, u32[]{:S(2)}, u32[]{:S(2)}) %collective-permute-start.9) | collective-permute-done | bytes 458784 | tf_op jit(solution)/shard_map/ppermute | solution.py:169
  83.8 1.5 collective-permute-done.10.refs_1_.refs_2_
  85.3 2.1 shard_map.74
  87.5 7.6 %all-to-all-start.3 = ((f32[32,8,16,128]{3,2,1,0:T(8,128)}), f32[32,8,16,128]{3,2,1,0:T(8,128)S(1)}, u32[]{:S(2)}, u32[]{:S(2)}) async-start(f32[32,8,16,128]{3,2,1,0:T(8,128)} %shard_map.74), calls=%async_computation.3 | async-start | bytes 4194304 | tf_op jit(solution)/shard_map/all_to_all | solution.py:188
  95.1 1.2 collective-permute-start.11
  96.4 32.7 %collective-permute-done.11.refs_0_ = f32[4,32,896]{2,1,0:T(8,128)S(1)} collective-permute-done((f32[4,32,896]{2,1,0:T(8,128)S(1)}, f32[4,32,896]{2,1,0:T(8,128)S(1)}, u32[]{:S(2)}, u32[]{:S(2)}) %collective-permute-start.11) | collective-permute-done | bytes 458784 | tf_op jit(solution)/shard_map/ppermute | solution.py:169
  129.8 2.8 %shard_map.75 = (f32[4,32,896]{2,1,0:T(8,128)}, f32[4,32,896]{2,1,0:T(8,128)}, f32[4,32,896]{2,1,0:T(8,128)}, f32[4,32,896]{2,1,0:T(8,128)}) custom-call(f32[4,32,896]{2,1,0:T(8,128)} %copy-done.19, f32[4,32,896]{2,1,0:T(8,128)} %copy-done.11, f32[4,32,896]{2,1,0:T(8,128)} %copy-done.12, f32[4,32,896]{2,1,0:T(8,128)} %copy-done.13), custom_call_target="tpu_custom_call" | custom-call | bytes 3670016 | tf_op jit(solution)/shard_map/pallas_call | solution.py:28
  132.6 2.0 collective-permute-start.12
  134.6 1.5 collective-permute-start.13
  136.1 2.6 %collective-permute-start.14 = (f32[4,32,896]{2,1,0:T(8,128)}, f32[4,32,896]{2,1,0:T(8,128)S(1)}, u32[]{:S(2)}, u32[]{:S(2)}) collective-permute-start(f32[4,32,896]{2,1,0:T(8,128)} %get-tuple-element.41), channel_id=1, source_target_pairs={{0,24},{4,28},{8,0},{12,4},{16,8},{20,12},{24,16},{28,20},{32,40},... | collective-permute-start | bytes 1376264 | tf_op jit(solution)/shard_map/ppermute | solution.py:180
  138.7 9.9 %collective-permute-done.12.refs_5_ = f32[4,32,896]{2,1,0:T(8,128)S(1)} collective-permute-done((f32[4,32,896]{2,1,0:T(8,128)}, f32[4,32,896]{2,1,0:T(8,128)S(1)}, u32[]{:S(2)}, u32[]{:S(2)}) %collective-permute-start.12) | collective-permute-done | bytes 458784 | tf_op jit(solution)/shard_map/ppermute | solution.py:173
  148.7 8.7 %collective-permute-done.14.refs_7_ = f32[4,32,896]{2,1,0:T(8,128)S(1)} collective-permute-done((f32[4,32,896]{2,1,0:T(8,128)}, f32[4,32,896]{2,1,0:T(8,128)S(1)}, u32[]{:S(2)}, u32[]{:S(2)}) %collective-permute-start.14) | collective-permute-done | bytes 458784 | tf_op jit(solution)/shard_map/ppermute | solution.py:180
  158.9 8.2 %shard_map.76 = f32[32,16,896]{2,1,0:T(8,128)} custom-call(s32[2]{0:T(128)} %pad_add_fusion.place, f32[32,8,16,128]{3,2,1,0:T(8,128)} %copy-done.9, f32[4,32,896]{2,1,0:T(8,128)} %get-tuple-element.36.refs_0_, f32[4,32,896]{2,1,0:T(8,128)} %copy-done.4, f32[4,32,896]{2,1,0:T(8,128)} %copy-done.5, f32[4,32,896]{2,1,0:T(8,128)} %get-tuple-element.37.refs_3_, ...), custom_call_target="tpu_custom_call" | custom-call | flops 2818572288 | bytes 7602176 | tf_op jit(solution)/shard_map/pallas_call | solution.py:28
  167.1 9.2 %all-to-all-start.4 = ((f32[32,16,896]{2,1,0:T(8,128)}), f32[32,16,896]{2,1,0:T(8,128)S(1)}, u32[]{:S(2)}, u32[]{:S(2)}) async-start(f32[32,16,896]{2,1,0:T(8,128)} %shard_map.76), calls=%async_computation.4 | async-start | bytes 3670016 | tf_op jit(solution)/shard_map/all_to_all | solution.py:188
  177.8 42.4 %all-to-all-done.4 = f32[32,16,896]{2,1,0:T(8,128)S(1)} async-done(((f32[32,16,896]{2,1,0:T(8,128)}), f32[32,16,896]{2,1,0:T(8,128)S(1)}, u32[]{:S(2)}, u32[]{:S(2)}) %all-to-all-start.4) | async-done | bytes 1835040 | tf_op jit(solution)/shard_map/all_to_all | solution.py:188
  (81 shorter events, 12.4 us)
Async XLA Ops:
  0.6 6.9 %copy-start.21 = (f32[64,2,32]{0,2,1:T(8,128)S(1)}, f32[64,2,32]{0,2,1:T(8,128)}, u32[]{:S(2)}) copy-start(f32[64,2,32]{0,2,1:T(8,128)} %param.5) | copy-start | bytes 49156
  5.5 26.6 %collective-permute-start.3 = (f32[4,32,896]{2,1,0:T(8,128)}, f32[4,32,896]{2,1,0:T(8,128)S(1)}, u32[]{:S(2)}, u32[]{:S(2)}) collective-permute-start(f32[4,32,896]{2,1,0:T(8,128)} %get-tuple-element.28), channel_id=1, source_target_pairs={{0,4},{4,8},{8,12},{12,16},{16,20},{20,24},{24,28},{28,0},{1,5},{5... | collective-permute-start | bytes 1376264 | tf_op jit(solution)/shard_map/ppermute | solution.py:173
  9.2 18.0 %collective-permute-start = (f32[72,1024]{1,0:T(8,128)S(1)}, f32[72,1024]{1,0:T(8,128)S(1)}, u32[]{:S(2)}, u32[]{:S(2)}) collective-permute-start(f32[72,1024]{1,0:T(8,128)S(1)} %get-tuple-element.23), channel_id=1, source_target_pairs={{0,1},{1,2},{2,3},{3,0},{4,5},{5,6},{6,7},{7,4},{8,9},{9,10},{10,1... | collective-permute-start | bytes 884744 | tf_op jit(solution)/shard_map/ppermute | solution.py:169
  10.4 19.0 %collective-permute-start.1 = (f32[72,1024]{1,0:T(8,128)S(1)}, f32[72,1024]{1,0:T(8,128)S(1)}, u32[]{:S(2)}, u32[]{:S(2)}) collective-permute-start(f32[72,1024]{1,0:T(8,128)S(1)} %get-tuple-element.24), channel_id=1, source_target_pairs={{0,2},{1,3},{2,0},{3,1},{4,6},{5,7},{6,4},{7,5},{8,10},{9,11},{10,... | collective-permute-start | bytes 884744 | tf_op jit(solution)/shard_map/ppermute | solution.py:169
  11.1 18.9 %collective-permute-start.2 = (f32[72,1024]{1,0:T(8,128)S(1)}, f32[72,1024]{1,0:T(8,128)S(1)}, u32[]{:S(2)}, u32[]{:S(2)}) collective-permute-start(f32[72,1024]{1,0:T(8,128)S(1)} %get-tuple-element.25), channel_id=1, source_target_pairs={{0,3},{1,0},{2,1},{3,2},{4,7},{5,4},{6,5},{7,6},{8,11},{9,8},{10,9... | collective-permute-start | bytes 884744 | tf_op jit(solution)/shard_map/ppermute | solution.py:169
  13.2 24.0 %all-to-all-start = ((f32[32,16,128]{2,1,0:T(8,128)}), f32[32,16,128]{2,1,0:T(8,128)}, u32[]{:S(2)}, u32[]{:S(2)}) async-start(f32[32,16,128]{2,1,0:T(8,128)} %shard_map.68), calls=%async_computation | async-start | bytes 524288 | tf_op jit(solution)/shard_map/all_to_all | solution.py:188
  24.3 18.7 %collective-permute-start.4 = (f32[4,32,896]{2,1,0:T(8,128)}, f32[4,32,896]{2,1,0:T(8,128)S(1)}, u32[]{:S(2)}, u32[]{:S(2)}) collective-permute-start(f32[4,32,896]{2,1,0:T(8,128)} %get-tuple-element.29), channel_id=1, source_target_pairs={{0,28},{4,0},{8,4},{12,8},{16,12},{20,16},{24,20},{28,24},{1,29},{... | collective-permute-start | bytes 1376264 | tf_op jit(solution)/shard_map/ppermute | solution.py:173
  27.1 10.1 %copy-start.15 = (f32[72,1024]{1,0:T(8,128)}, f32[72,1024]{1,0:T(8,128)S(1)}, u32[]{:S(2)}) copy-start(f32[72,1024]{1,0:T(8,128)S(1)} %collective-permute-done.refs_1_) | copy-start | bytes 884740
  27.1 25.9 %collective-permute-start.5 = (f32[4,32,896]{2,1,0:T(8,128)}, f32[4,32,896]{2,1,0:T(8,128)}, u32[]{:S(2)}, u32[]{:S(2)}) collective-permute-start(f32[4,32,896]{2,1,0:T(8,128)} %get-tuple-element.30), channel_id=1, source_target_pairs={{0,24},{4,28},{8,0},{12,4},{16,8},{20,12},{24,16},{28,20},{32,40},... | collective-permute-start | bytes 1376264 | tf_op jit(solution)/shard_map/ppermute | solution.py:180
  29.4 7.8 %copy-start.16 = (f32[72,1024]{1,0:T(8,128)}, f32[72,1024]{1,0:T(8,128)S(1)}, u32[]{:S(2)}) copy-start(f32[72,1024]{1,0:T(8,128)S(1)} %collective-permute-done.1.refs_2_) | copy-start | bytes 884740
  29.4 23.6 %collective-permute-start.6 = (f32[4,32,896]{2,1,0:T(8,128)}, f32[4,32,896]{2,1,0:T(8,128)S(1)}, u32[]{:S(2)}, u32[]{:S(2)}) collective-permute-start(f32[4,32,896]{2,1,0:T(8,128)} %get-tuple-element.31), channel_id=1, source_target_pairs={{0,2},{1,3},{2,0},{3,1},{4,6},{5,7},{6,4},{7,5},{8,10},{9,11},{10,... | collective-permute-start | bytes 1376264 | tf_op jit(solution)/shard_map/ppermute | solution.py:169
  30.0 7.2 %copy-start.17 = (f32[72,1024]{1,0:T(8,128)}, f32[72,1024]{1,0:T(8,128)S(1)}, u32[]{:S(2)}) copy-start(f32[72,1024]{1,0:T(8,128)S(1)} %collective-permute-done.2.refs_3_) | copy-start | bytes 884740
  30.0 23.7 %collective-permute-start.7 = (f32[4,32,896]{2,1,0:T(8,128)}, f32[4,32,896]{2,1,0:T(8,128)S(1)}, u32[]{:S(2)}, u32[]{:S(2)}) collective-permute-start(f32[4,32,896]{2,1,0:T(8,128)} %get-tuple-element.32), channel_id=1, source_target_pairs={{0,3},{1,0},{2,1},{3,2},{4,7},{5,4},{6,5},{7,6},{8,11},{9,8},{10,9... | collective-permute-start | bytes 1376264 | tf_op jit(solution)/shard_map/ppermute | solution.py:169
  32.1 21.6 %copy-start.10 = (f32[4,32,896]{2,1,0:T(8,128)}, f32[4,32,896]{2,1,0:T(8,128)S(1)}, u32[]{:S(2)}) copy-start(f32[4,32,896]{2,1,0:T(8,128)S(1)} %collective-permute-done.3.refs_4_.refs_1_) | copy-start | bytes 1376260
  32.1 21.6 %collective-permute-start.8 = (f32[4,32,896]{2,1,0:T(8,128)}, f32[4,32,896]{2,1,0:T(8,128)S(1)}, u32[]{:S(2)}, u32[]{:S(2)}) collective-permute-start(f32[4,32,896]{2,1,0:T(8,128)} %get-tuple-element.33), channel_id=1, source_target_pairs={{0,2},{1,3},{2,0},{3,1},{4,6},{5,7},{6,4},{7,5},{8,10},{9,11},{10,... | collective-permute-start | bytes 1376264 | tf_op jit(solution)/shard_map/ppermute | solution.py:169
  39.6 14.1 %all-to-all-start.1 = ((f32[8,2,16,128]{3,2,1,0:T(8,128)}), f32[8,2,16,128]{3,2,1,0:T(8,128)S(1)}, u32[]{:S(2)}, u32[]{:S(2)}) async-start(f32[8,2,16,128]{3,2,1,0:T(8,128)} %shard_map.71), calls=%async_computation.1 | async-start | bytes 262144 | tf_op jit(solution)/shard_map/all_to_all | solution.py:188
  43.0 10.7 %copy-start.14 = (f32[4,32,896]{2,1,0:T(8,128)}, f32[4,32,896]{2,1,0:T(8,128)S(1)}, u32[]{:S(2)}) copy-start(f32[4,32,896]{2,1,0:T(8,128)S(1)} %collective-permute-done.4.refs_5_.refs_2_) | copy-start | bytes 1376260
  57.7 27.6 %copy-start.2 = (f32[8,2,16,128]{3,2,1,0:T(8,128)S(1)}, f32[8,2,16,128]{3,2,1,0:T(8,128)}, u32[]{:S(2)}) copy-start(f32[8,2,16,128]{3,2,1,0:T(8,128)} %copy-done.1) | copy-start | bytes 393220
  57.7 27.6 %copy-start.8 = (s32[2]{0:T(128)S(1)}, s32[2]{0:T(128)}, u32[]{:S(2)}) copy-start(s32[2]{0:T(128)} %pad_add_fusion.place) | copy-start | bytes 28
  57.7 27.6 %all-to-all-start.2 = ((f32[8,5,16,128]{3,2,1,0:T(8,128)}), f32[8,5,16,128]{3,2,1,0:T(8,128)S(1)}, u32[]{:S(2)}, u32[]{:S(2)}) async-start(f32[8,5,16,128]{3,2,1,0:T(8,128)} %shard_map.72), calls=%async_computation.2 | async-start | bytes 655360 | tf_op jit(solution)/shard_map/all_to_all | solution.py:188
  65.2 18.6 %collective-permute-start.9 = (f32[4,32,896]{2,1,0:T(8,128)}, f32[4,32,896]{2,1,0:T(8,128)S(1)}, u32[]{:S(2)}, u32[]{:S(2)}) collective-permute-start(f32[4,32,896]{2,1,0:T(8,128)} %get-tuple-element.34), channel_id=1, source_target_pairs={{0,1},{1,2},{2,3},{3,0},{4,5},{5,6},{6,7},{7,4},{8,9},{9,10},{10,1... | collective-permute-start | bytes 1376264 | tf_op jit(solution)/shard_map/ppermute | solution.py:169
  73.6 11.7 %collective-permute-start.10 = (f32[4,32,896]{2,1,0:T(8,128)}, f32[4,32,896]{2,1,0:T(8,128)S(1)}, u32[]{:S(2)}, u32[]{:S(2)}) collective-permute-start(f32[4,32,896]{2,1,0:T(8,128)} %get-tuple-element.35), channel_id=1, source_target_pairs={{0,3},{1,0},{2,1},{3,2},{4,7},{5,4},{6,5},{7,6},{8,11},{9,8},{10,9... | collective-permute-start | bytes 1376264 | tf_op jit(solution)/shard_map/ppermute | solution.py:169
  87.5 7.6 %copy-start.20 = (f32[4,32,896]{2,1,0:T(8,128)S(1)}, f32[4,32,896]{2,1,0:T(8,128)}, u32[]{:S(2)}) copy-start(f32[4,32,896]{2,1,0:T(8,128)} %get-tuple-element.27.refs_5_) | copy-start | bytes 1376260
  87.5 69.9 %all-to-all-start.3 = ((f32[32,8,16,128]{3,2,1,0:T(8,128)}), f32[32,8,16,128]{3,2,1,0:T(8,128)S(1)}, u32[]{:S(2)}, u32[]{:S(2)}) async-start(f32[32,8,16,128]{3,2,1,0:T(8,128)} %shard_map.74), calls=%async_computation.3 | async-start | bytes 4194304 | tf_op jit(solution)/shard_map/all_to_all | solution.py:188
  95.1 33.9 %collective-permute-start.11 = (f32[4,32,896]{2,1,0:T(8,128)S(1)}, f32[4,32,896]{2,1,0:T(8,128)S(1)}, u32[]{:S(2)}, u32[]{:S(2)}) collective-permute-start(f32[4,32,896]{2,1,0:T(8,128)S(1)} %copy-done.20), channel_id=1, source_target_pairs={{0,1},{1,2},{2,3},{3,0},{4,5},{5,6},{6,7},{7,4},{8,9},{9,10},{10,1... | collective-permute-start | bytes 1376264 | tf_op jit(solution)/shard_map/ppermute | solution.py:169
  132.6 16.1 %collective-permute-start.12 = (f32[4,32,896]{2,1,0:T(8,128)}, f32[4,32,896]{2,1,0:T(8,128)S(1)}, u32[]{:S(2)}, u32[]{:S(2)}) collective-permute-start(f32[4,32,896]{2,1,0:T(8,128)} %get-tuple-element.39), channel_id=1, source_target_pairs={{0,4},{4,8},{8,12},{12,16},{16,20},{20,24},{24,28},{28,0},{1,5},{5... | collective-permute-start | bytes 1376264 | tf_op jit(solution)/shard_map/ppermute | solution.py:173
  134.6 14.1 %collective-permute-start.13 = (f32[4,32,896]{2,1,0:T(8,128)}, f32[4,32,896]{2,1,0:T(8,128)S(1)}, u32[]{:S(2)}, u32[]{:S(2)}) collective-permute-start(f32[4,32,896]{2,1,0:T(8,128)} %get-tuple-element.40), channel_id=1, source_target_pairs={{0,28},{4,0},{8,4},{12,8},{16,12},{20,16},{24,20},{28,24},{1,29},{... | collective-permute-start | bytes 1376264 | tf_op jit(solution)/shard_map/ppermute | solution.py:173
  136.1 21.3 %collective-permute-start.14 = (f32[4,32,896]{2,1,0:T(8,128)}, f32[4,32,896]{2,1,0:T(8,128)S(1)}, u32[]{:S(2)}, u32[]{:S(2)}) collective-permute-start(f32[4,32,896]{2,1,0:T(8,128)} %get-tuple-element.41), channel_id=1, source_target_pairs={{0,24},{4,28},{8,0},{12,4},{16,8},{20,12},{24,16},{28,20},{32,40},... | collective-permute-start | bytes 1376264 | tf_op jit(solution)/shard_map/ppermute | solution.py:180
  148.7 8.7 %copy-start.22 = (f32[4,32,896]{2,1,0:T(8,128)}, f32[4,32,896]{2,1,0:T(8,128)S(1)}, u32[]{:S(2)}) copy-start(f32[4,32,896]{2,1,0:T(8,128)S(1)} %collective-permute-done.12.refs_5_) | copy-start | bytes 1376260
  148.7 8.7 %copy-start.23 = (f32[4,32,896]{2,1,0:T(8,128)}, f32[4,32,896]{2,1,0:T(8,128)S(1)}, u32[]{:S(2)}) copy-start(f32[4,32,896]{2,1,0:T(8,128)S(1)} %collective-permute-done.13.refs_6_) | copy-start | bytes 1376260
  167.1 53.2 %all-to-all-start.4 = ((f32[32,16,896]{2,1,0:T(8,128)}), f32[32,16,896]{2,1,0:T(8,128)S(1)}, u32[]{:S(2)}, u32[]{:S(2)}) async-start(f32[32,16,896]{2,1,0:T(8,128)} %shard_map.76), calls=%async_computation.4 | async-start | bytes 3670016 | tf_op jit(solution)/shard_map/all_to_all | solution.py:188
  177.8 42.6 %copy-start.18 = (f32[16,14336]{1,0:T(8,128)S(1)}, f32[16,14336]{1,0:T(8,128)}, u32[]{:S(2)}) copy-start(f32[16,14336]{1,0:T(8,128)} %param.9) | copy-start | bytes 2752516
  (13 other events, 32.2 us)

commit v16 on v13

--- a/solution.py
+++ b/solution.py
@@ -236,7 +236,7 @@
     arrived = exchange(terms, "z")
     by_k = call(merge_kernel, (block,) * 4, (place, *by_y), (ANY,) * 4, (SMEM,) + (VMEM,) * 4, sems(16), moved=3670016, limit=60)
     latter_factor = to_windows(*by_k)
-    copies = call(close_kernel, f32(X * C * Y, 2 * QUAD, 16, 128), (place, first, arrived, first_factor[2], first_factor[3], by_k[0]), VMEM, (SMEM, VMEM, VMEM) + (ANY,) * 3)
+    copies = call(close_kernel, f32(X * C * Y, 2 * QUAD, 16, 128), (place, first, arrived, first_factor[1], first_factor[3], by_k[0]), VMEM, (SMEM, VMEM, VMEM) + (ANY,) * 3)
     rows = exchange(copies, SPREAD)
 
     factor = lambda dtype: pltpu.VMEM((2, QUAD, *block.shape), dtype)

time: 201 us -> 192 us (0.955)
  waiting for transfers between devices: 99.3 us -> 93.5 us
  starting transfers between devices: 62.8 us -> 60.4 us
    ppermute x9, waiting for transfers between devices: 24.7 us -> 17.3 us  [shift_y(): return lax.ppermute(value, 'y', [(y, (y + step) % Y) for y in range(Y)])]
    ppermute x9, starting transfers between devices: 11.2 us -> 9.15 us  [shift_y(): return lax.ppermute(value, 'y', [(y, (y + step) % Y) for y in range(Y)])]
where the time goes in v16:
time: 192 us; the launch traced here: 191 us
  waiting for transfers between devices  93.5 us (49%)
  starting transfers between devices  60.4 us (31%)
  Pallas kernels  26.5 us (14%)
  local copies, waits for them, and re-layouts  8.14 us (4%)
    all_to_all x5, waiting for transfers between devices, exchange(): return lax.all_to_all(value, axes, 0, 0, tiled=True)  47.7 us
    all_to_all x5, starting transfers between devices, exchange(): return lax.all_to_all(value, axes, 0, 0, tiled=True)  38.2 us
    pallas_call x9, Pallas kernels, call(): pl.pallas_call(kernel, out_shape=outs, in_specs=in_specs, out_specs=out_s...  26.5 us
    ppermute x2, waiting for transfers between devices, shift_far(): return lax.ppermute(value, ('c', 'z'), pairs)  19.7 us
    ppermute x9, waiting for transfers between devices, shift_y(): return lax.ppermute(value, 'y', [(y, (y + step) % Y) for y in range(Y)])  17.3 us
    ppermute x9, starting transfers between devices, shift_y(): return lax.ppermute(value, 'y', [(y, (y + step) % Y) for y in range(Y)])  9.15 us
    ppermute x4, waiting for transfers between devices, shift_z(): return lax.ppermute(value, 'z', [(z, (z + step) % Z) for z in range(Z)])  8.74 us
    ppermute x4, starting transfers between devices, shift_z(): return lax.ppermute(value, 'z', [(z, (z + step) % Z) for z in range(Z)])  8.14 us
  transfers between devices with their start and end apart: 20, of which 9 were waited for; matrix products, arithmetic and copies ran while one was open for 1% of the time, Pallas kernels for 5%

profile of v16, /device:TPU:20, one launch (start us, length us, event | category | flops | bytes accessed | tf_op | source)
XLA Modules:
  0.0 191.2 jit_solution(636147110999458835)
XLA Ops:
  1.3 4.2 %shard_map.70 = (f32[4,32,896]{2,1,0:T(8,128)}, f32[4,32,896]{2,1,0:T(8,128)}, f32[4,32,896]{2,1,0:T(8,128)}, f32[4,32,896]{2,1,0:T(8,128)}, f32[4,32,896]{2,1,0...) custom-call(s32[2]{0:T(128)} %pad_add_fusion.place, f32[2,32,14336]{2,1,0:T(8,128)} %factor.1), custom_call_target="tpu_custom_call" | custom-call | bytes 7340032 | tf_op jit(solution)/shard_map/pallas_call | solution.py:26
  5.5 2.0 %collective-permute-start.3 = (f32[4,32,896]{2,1,0:T(8,128)}, f32[4,32,896]{2,1,0:T(8,128)S(1)}, u32[]{:S(2)}, u32[]{:S(2)}) collective-permute-start(f32[4,32,896]{2,1,0:T(8,128)} %get-tuple-element.28), channel_id=1, source_target_pairs={{0,4},{4,8},{8,12},{12,16},{16,20},{20,24},{24,28},{28,0},{1,5},{5... | collective-permute-start | bytes 1376264 | tf_op jit(solution)/shard_map/ppermute | solution.py:176
  9.2 1.3 collective-permute-start
  13.2 11.1 %all-to-all-start = ((f32[32,16,128]{2,1,0:T(8,128)}), f32[32,16,128]{2,1,0:T(8,128)}, u32[]{:S(2)}, u32[]{:S(2)}) async-start(f32[32,16,128]{2,1,0:T(8,128)} %shard_map.68), calls=%async_computation | async-start | bytes 524288 | tf_op jit(solution)/shard_map/all_to_all | solution.py:195
  24.3 2.8 %collective-permute-start.4 = (f32[4,32,896]{2,1,0:T(8,128)}, f32[4,32,896]{2,1,0:T(8,128)S(1)}, u32[]{:S(2)}, u32[]{:S(2)}) collective-permute-start(f32[4,32,896]{2,1,0:T(8,128)} %get-tuple-element.29), channel_id=1, source_target_pairs={{0,28},{4,0},{8,4},{12,8},{16,12},{20,16},{24,20},{28,24},{1,29},{... | collective-permute-start | bytes 1376264 | tf_op jit(solution)/shard_map/ppermute | solution.py:176
  27.1 2.3 %collective-permute-start.5 = (f32[4,32,896]{2,1,0:T(8,128)}, f32[4,32,896]{2,1,0:T(8,128)S(1)}, u32[]{:S(2)}, u32[]{:S(2)}) collective-permute-start(f32[4,32,896]{2,1,0:T(8,128)} %get-tuple-element.30), channel_id=1, source_target_pairs={{0,24},{4,28},{8,0},{12,4},{16,8},{20,12},{24,16},{28,20},{32,40},... | collective-permute-start | bytes 1376264 | tf_op jit(solution)/shard_map/ppermute | solution.py:183
  29.4 1.2 collective-permute-start.6
  32.2 1.2 collective-permute-start.8
  33.4 3.9 %all-to-all-done.arrived = f32[32,16,128]{2,1,0:T(8,128)} async-done(((f32[32,16,128]{2,1,0:T(8,128)}), f32[32,16,128]{2,1,0:T(8,128)}, u32[]{:S(2)}, u32[]{:S(2)}) %all-to-all-start) | async-done | bytes 262176 | tf_op jit(solution)/shard_map/all_to_all | solution.py:195
  37.2 2.4 %shard_map.71 = f32[8,2,16,128]{3,2,1,0:T(8,128)} custom-call(s32[2]{0:T(128)} %pad_add_fusion.place, f32[32,16,128]{2,1,0:T(8,128)} %all-to-all-done.arrived, f32[72,1024]{1,0:T(8,128)} %copy-done, f32[72,1024]{1,0:T(8,128)} %copy-done.17, f32[72,1024]{1,0:T(8,128)} %copy-done.18, f32[72,1024]{1,0:T(8,128)} %copy-done.19, ...), custom_call_target="tpu_custom_call" | custom-call | tf_op jit(solution)/shard_map/pallas_call | solution.py:26
  39.6 3.4 %all-to-all-start.1 = ((f32[8,2,16,128]{3,2,1,0:T(8,128)}), f32[8,2,16,128]{3,2,1,0:T(8,128)S(1)}, u32[]{:S(2)}, u32[]{:S(2)}) async-start(f32[8,2,16,128]{3,2,1,0:T(8,128)} %shard_map.71), calls=%async_computation.1 | async-start | bytes 262144 | tf_op jit(solution)/shard_map/all_to_all | solution.py:195
  43.0 9.9 %collective-permute-done.5.refs_6_.refs_3_ = f32[4,32,896]{2,1,0:T(8,128)S(1)} collective-permute-done((f32[4,32,896]{2,1,0:T(8,128)}, f32[4,32,896]{2,1,0:T(8,128)S(1)}, u32[]{:S(2)}, u32[]{:S(2)}) %collective-permute-start.5) | collective-permute-done | bytes 458784 | tf_op jit(solution)/shard_map/ppermute | solution.py:183
  54.8 2.4 %shard_map.72 = f32[8,5,16,128]{3,2,1,0:T(8,128)} custom-call(s32[2]{0:T(128)} %pad_add_fusion.place, f32[8,2,16,128]{3,2,1,0:T(8,128)} %copy-done.1, f32[72,1024]{1,0:T(8,128)} %copy-done, f32[72,1024]{1,0:T(8,128)} %copy-done.17, f32[72,1024]{1,0:T(8,128)} %copy-done.18, f32[72,1024]{1,0:T(8,128)} %copy-done.19, f32[4,32,896]{2,1,0:T(8,128)} %copy-done.11, ...), custom_call_target="tpu_custom_call" | custom-call | tf_op jit(solution)/shard_map/pallas_call | solution.py:26
  57.2 5.2 %all-to-all-start.2 = ((f32[8,5,16,128]{3,2,1,0:T(8,128)}), f32[8,5,16,128]{3,2,1,0:T(8,128)S(1)}, u32[]{:S(2)}, u32[]{:S(2)}) async-start(f32[8,5,16,128]{3,2,1,0:T(8,128)} %shard_map.72), calls=%async_computation.2 | async-start | bytes 655360 | tf_op jit(solution)/shard_map/all_to_all | solution.py:195
  62.4 2.8 %shard_map.73 = (f32[4,32,896]{2,1,0:T(8,128)}, f32[4,32,896]{2,1,0:T(8,128)}, f32[4,32,896]{2,1,0:T(8,128)}, f32[4,32,896]{2,1,0:T(8,128)}) custom-call(f32[4,32,896]{2,1,0:T(8,128)} %get-tuple-element.26.refs_4_.refs_0_, f32[4,32,896]{2,1,0:T(8,128)} %copy-done.11, f32[4,32,896]{2,1,0:T(8,128)} %copy-done.12, f32[4,32,896]{2,1,0:T(8,128)} %copy-done.13), custom_call_target="tpu_custom_call" | custom-call | bytes 3670016 | tf_op jit(solution)/shard_map/pallas_call | solution.py:26
  65.2 2.4 %collective-permute-start.9 = (f32[4,32,896]{2,1,0:T(8,128)}, f32[4,32,896]{2,1,0:T(8,128)S(1)}, u32[]{:S(2)}, u32[]{:S(2)}) collective-permute-start(f32[4,32,896]{2,1,0:T(8,128)} %get-tuple-element.34), channel_id=1, source_target_pairs={{0,1},{1,2},{2,3},{3,0},{4,5},{5,6},{6,7},{7,4},{8,9},{9,10},{10,1... | collective-permute-start | bytes 1376264 | tf_op jit(solution)/shard_map/ppermute | solution.py:172
  67.6 2.8 %shard_map.74 = (f32[4,32,896]{2,1,0:T(8,128)}, f32[4,32,896]{2,1,0:T(8,128)}, f32[4,32,896]{2,1,0:T(8,128)}, f32[4,32,896]{2,1,0:T(8,128)}) custom-call(s32[2]{0:T(128)} %pad_add_fusion.place, f32[4,32,896]{2,1,0:T(8,128)} %get-tuple-element.27.refs_5_.refs_0_, f32[4,32,896]{2,1,0:T(8,128)} %copy-done.14, f32[4,32,896]{2,1,0:T(8,128)} %copy-done.15, ...), custom_call_target="tpu_custom_call" | custom-call | bytes 3670016 | tf_op jit(solution)/shard_map/pallas_call | solution.py:26
  70.4 7.0 %collective-permute-done.9.refs_0_.refs_1_ = f32[4,32,896]{2,1,0:T(8,128)S(1)} collective-permute-done((f32[4,32,896]{2,1,0:T(8,128)}, f32[4,32,896]{2,1,0:T(8,128)S(1)}, u32[]{:S(2)}, u32[]{:S(2)}) %collective-permute-start.9) | collective-permute-done | bytes 458784 | tf_op jit(solution)/shard_map/ppermute | solution.py:172
  77.4 2.1 %collective-permute-done.10.refs_1_.refs_3_ = f32[4,32,896]{2,1,0:T(8,128)S(1)} collective-permute-done((f32[4,32,896]{2,1,0:T(8,128)}, f32[4,32,896]{2,1,0:T(8,128)S(1)}, u32[]{:S(2)}, u32[]{:S(2)}) %collective-permute-start.10) | collective-permute-done | bytes 458784 | tf_op jit(solution)/shard_map/ppermute | solution.py:172
  79.6 1.2 copy-done.6
  80.7 2.1 %shard_map.75 = f32[32,8,16,128]{3,2,1,0:T(8,128)} custom-call(s32[2]{0:T(128)S(1)} %copy-done.9, f32[8,2,16,128]{3,2,1,0:T(8,128)S(1)} %copy-done.2, f32[8,5,16,128]{3,2,1,0:T(8,128)S(1)} %all-to-all-done.2.arrived, f32[4,32,896]{2,1,0:T(8,128)S(1)} %collective-permute-done.9.refs_0_.refs_1_, f32[4,32,896]{2,1,0:T(8,128)S(1)} %collective-permute-done.10.refs_1_.refs_3_, ...), custom_call_target="tpu_custom_call" | custom-call | tf_op jit(solution)/shard_map/pallas_call | solution.py:26
  82.9 7.6 %all-to-all-start.3 = ((f32[32,8,16,128]{3,2,1,0:T(8,128)}), f32[32,8,16,128]{3,2,1,0:T(8,128)S(1)}, u32[]{:S(2)}, u32[]{:S(2)}) async-start(f32[32,8,16,128]{3,2,1,0:T(8,128)} %shard_map.75), calls=%async_computation.3 | async-start | bytes 4194304 | tf_op jit(solution)/shard_map/all_to_all | solution.py:195
  90.5 1.8 collective-permute-start.12
  92.3 1.5 collective-permute-start.13
  93.8 2.6 %collective-permute-start.14 = (f32[4,32,896]{2,1,0:T(8,128)}, f32[4,32,896]{2,1,0:T(8,128)S(1)}, u32[]{:S(2)}, u32[]{:S(2)}) collective-permute-start(f32[4,32,896]{2,1,0:T(8,128)} %get-tuple-element.41), channel_id=1, source_target_pairs={{0,24},{4,28},{8,0},{12,4},{16,8},{20,12},{24,16},{28,20},{32,40},... | collective-permute-start | bytes 1376264 | tf_op jit(solution)/shard_map/ppermute | solution.py:183
  97.0 8.7 %collective-permute-done.12.refs_5_ = f32[4,32,896]{2,1,0:T(8,128)S(1)} collective-permute-done((f32[4,32,896]{2,1,0:T(8,128)}, f32[4,32,896]{2,1,0:T(8,128)S(1)}, u32[]{:S(2)}, u32[]{:S(2)}) %collective-permute-start.12) | collective-permute-done | bytes 458784 | tf_op jit(solution)/shard_map/ppermute | solution.py:176
  105.8 9.8 %collective-permute-done.14.refs_7_ = f32[4,32,896]{2,1,0:T(8,128)S(1)} collective-permute-done((f32[4,32,896]{2,1,0:T(8,128)}, f32[4,32,896]{2,1,0:T(8,128)S(1)}, u32[]{:S(2)}, u32[]{:S(2)}) %collective-permute-start.14) | collective-permute-done | bytes 458784 | tf_op jit(solution)/shard_map/ppermute | solution.py:183
  116.4 8.2 %collective-permute-done.11.refs_2_ = f32[4,32,896]{2,1,0:T(8,128)} collective-permute-done((f32[4,32,896]{2,1,0:T(8,128)S(1)}, f32[4,32,896]{2,1,0:T(8,128)}, u32[]{:S(2)}, u32[]{:S(2)}) %collective-permute-start.11) | collective-permute-done | bytes 458784 | tf_op jit(solution)/shard_map/ppermute | solution.py:172
  124.6 1.3 copy-done.10
  125.9 8.1 %shard_map.76 = f32[32,16,896]{2,1,0:T(8,128)} custom-call(s32[2]{0:T(128)} %pad_add_fusion.place, f32[32,8,16,128]{3,2,1,0:T(8,128)} %copy-done.10, f32[4,32,896]{2,1,0:T(8,128)} %get-tuple-element.37.refs_0_, f32[4,32,896]{2,1,0:T(8,128)} %copy-done.4, f32[4,32,896]{2,1,0:T(8,128)} %collective-permute-done.11.refs_2_, f32[4,32,896]{2,1,0:T(8,128)} %copy-done.5, ...), custom_call_target="tpu_custom_call" | custom-call | flops 2818572288 | bytes 7602176 | tf_op jit(solution)/shard_map/pallas_call | solution.py:26
  134.0 10.9 %all-to-all-start.4 = ((f32[32,16,896]{2,1,0:T(8,128)}), f32[32,16,896]{2,1,0:T(8,128)S(1)}, u32[]{:S(2)}, u32[]{:S(2)}) async-start(f32[32,16,896]{2,1,0:T(8,128)} %shard_map.76), calls=%async_computation.4 | async-start | bytes 3670016 | tf_op jit(solution)/shard_map/all_to_all | solution.py:195
  146.5 43.6 %all-to-all-done.4 = f32[32,16,896]{2,1,0:T(8,128)S(1)} async-done(((f32[32,16,896]{2,1,0:T(8,128)}), f32[32,16,896]{2,1,0:T(8,128)S(1)}, u32[]{:S(2)}, u32[]{:S(2)}) %all-to-all-start.4) | async-done | bytes 1835040 | tf_op jit(solution)/shard_map/all_to_all | solution.py:195
  (83 shorter events, 12.6 us)
Async XLA Ops:
  0.6 6.9 %copy-start.21 = (f32[64,2,32]{0,2,1:T(8,128)S(1)}, f32[64,2,32]{0,2,1:T(8,128)}, u32[]{:S(2)}) copy-start(f32[64,2,32]{0,2,1:T(8,128)} %param.5) | copy-start | bytes 49156
  1.3 6.5 %copy-start.8 = (s32[2]{0:T(128)S(1)}, s32[2]{0:T(128)}, u32[]{:S(2)}) copy-start(s32[2]{0:T(128)} %pad_add_fusion.place) | copy-start | bytes 28
  5.5 26.7 %collective-permute-start.3 = (f32[4,32,896]{2,1,0:T(8,128)}, f32[4,32,896]{2,1,0:T(8,128)S(1)}, u32[]{:S(2)}, u32[]{:S(2)}) collective-permute-start(f32[4,32,896]{2,1,0:T(8,128)} %get-tuple-element.28), channel_id=1, source_target_pairs={{0,4},{4,8},{8,12},{12,16},{16,20},{20,24},{24,28},{28,0},{1,5},{5... | collective-permute-start | bytes 1376264 | tf_op jit(solution)/shard_map/ppermute | solution.py:176
  9.2 18.0 %collective-permute-start = (f32[72,1024]{1,0:T(8,128)S(1)}, f32[72,1024]{1,0:T(8,128)S(1)}, u32[]{:S(2)}, u32[]{:S(2)}) collective-permute-start(f32[72,1024]{1,0:T(8,128)S(1)} %get-tuple-element.23), channel_id=1, source_target_pairs={{0,1},{1,2},{2,3},{3,0},{4,5},{5,6},{6,7},{7,4},{8,9},{9,10},{10,1... | collective-permute-start | bytes 884744 | tf_op jit(solution)/shard_map/ppermute | solution.py:172
  10.5 19.0 %collective-permute-start.1 = (f32[72,1024]{1,0:T(8,128)S(1)}, f32[72,1024]{1,0:T(8,128)S(1)}, u32[]{:S(2)}, u32[]{:S(2)}) collective-permute-start(f32[72,1024]{1,0:T(8,128)S(1)} %get-tuple-element.24), channel_id=1, source_target_pairs={{0,2},{1,3},{2,0},{3,1},{4,6},{5,7},{6,4},{7,5},{8,10},{9,11},{10,... | collective-permute-start | bytes 884744 | tf_op jit(solution)/shard_map/ppermute | solution.py:172
  11.1 19.5 %collective-permute-start.2 = (f32[72,1024]{1,0:T(8,128)S(1)}, f32[72,1024]{1,0:T(8,128)S(1)}, u32[]{:S(2)}, u32[]{:S(2)}) collective-permute-start(f32[72,1024]{1,0:T(8,128)S(1)} %get-tuple-element.25), channel_id=1, source_target_pairs={{0,3},{1,0},{2,1},{3,2},{4,7},{5,4},{6,5},{7,6},{8,11},{9,8},{10,9... | collective-permute-start | bytes 884744 | tf_op jit(solution)/shard_map/ppermute | solution.py:172
  13.2 24.0 %all-to-all-start = ((f32[32,16,128]{2,1,0:T(8,128)}), f32[32,16,128]{2,1,0:T(8,128)}, u32[]{:S(2)}, u32[]{:S(2)}) async-start(f32[32,16,128]{2,1,0:T(8,128)} %shard_map.68), calls=%async_computation | async-start | bytes 524288 | tf_op jit(solution)/shard_map/all_to_all | solution.py:195
  24.3 18.7 %collective-permute-start.4 = (f32[4,32,896]{2,1,0:T(8,128)}, f32[4,32,896]{2,1,0:T(8,128)S(1)}, u32[]{:S(2)}, u32[]{:S(2)}) collective-permute-start(f32[4,32,896]{2,1,0:T(8,128)} %get-tuple-element.29), channel_id=1, source_target_pairs={{0,28},{4,0},{8,4},{12,8},{16,12},{20,16},{24,20},{28,24},{1,29},{... | collective-permute-start | bytes 1376264 | tf_op jit(solution)/shard_map/ppermute | solution.py:176
  27.1 10.1 %copy-start.17 = (f32[72,1024]{1,0:T(8,128)}, f32[72,1024]{1,0:T(8,128)S(1)}, u32[]{:S(2)}) copy-start(f32[72,1024]{1,0:T(8,128)S(1)} %collective-permute-done.refs_1_) | copy-start | bytes 884740
  27.1 25.8 %collective-permute-start.5 = (f32[4,32,896]{2,1,0:T(8,128)}, f32[4,32,896]{2,1,0:T(8,128)S(1)}, u32[]{:S(2)}, u32[]{:S(2)}) collective-permute-start(f32[4,32,896]{2,1,0:T(8,128)} %get-tuple-element.30), channel_id=1, source_target_pairs={{0,24},{4,28},{8,0},{12,4},{16,8},{20,12},{24,16},{28,20},{32,40},... | collective-permute-start | bytes 1376264 | tf_op jit(solution)/shard_map/ppermute | solution.py:183
  29.4 7.8 %copy-start.18 = (f32[72,1024]{1,0:T(8,128)}, f32[72,1024]{1,0:T(8,128)S(1)}, u32[]{:S(2)}) copy-start(f32[72,1024]{1,0:T(8,128)S(1)} %collective-permute-done.1.refs_2_) | copy-start | bytes 884740
  29.4 23.5 %collective-permute-start.6 = (f32[4,32,896]{2,1,0:T(8,128)}, f32[4,32,896]{2,1,0:T(8,128)S(1)}, u32[]{:S(2)}, u32[]{:S(2)}) collective-permute-start(f32[4,32,896]{2,1,0:T(8,128)} %get-tuple-element.31), channel_id=1, source_target_pairs={{0,1},{1,2},{2,3},{3,0},{4,5},{5,6},{6,7},{7,4},{8,9},{9,10},{10,1... | collective-permute-start | bytes 1376264 | tf_op jit(solution)/shard_map/ppermute | solution.py:172
  31.4 21.6 %collective-permute-start.7 = (f32[4,32,896]{2,1,0:T(8,128)}, f32[4,32,896]{2,1,0:T(8,128)S(1)}, u32[]{:S(2)}, u32[]{:S(2)}) collective-permute-start(f32[4,32,896]{2,1,0:T(8,128)} %get-tuple-element.32), channel_id=1, source_target_pairs={{0,2},{1,3},{2,0},{3,1},{4,6},{5,7},{6,4},{7,5},{8,10},{9,11},{10,... | collective-permute-start | bytes 1376264 | tf_op jit(solution)/shard_map/ppermute | solution.py:172
  32.2 21.0 %copy-start.11 = (f32[4,32,896]{2,1,0:T(8,128)}, f32[4,32,896]{2,1,0:T(8,128)S(1)}, u32[]{:S(2)}) copy-start(f32[4,32,896]{2,1,0:T(8,128)S(1)} %collective-permute-done.3.refs_4_.refs_1_) | copy-start | bytes 1376260
  32.2 20.7 %collective-permute-start.8 = (f32[4,32,896]{2,1,0:T(8,128)}, f32[4,32,896]{2,1,0:T(8,128)S(1)}, u32[]{:S(2)}, u32[]{:S(2)}) collective-permute-start(f32[4,32,896]{2,1,0:T(8,128)} %get-tuple-element.33), channel_id=1, source_target_pairs={{0,3},{1,0},{2,1},{3,2},{4,7},{5,4},{6,5},{7,6},{8,11},{9,8},{10,9... | collective-permute-start | bytes 1376264 | tf_op jit(solution)/shard_map/ppermute | solution.py:172
  39.6 13.6 %all-to-all-start.1 = ((f32[8,2,16,128]{3,2,1,0:T(8,128)}), f32[8,2,16,128]{3,2,1,0:T(8,128)S(1)}, u32[]{:S(2)}, u32[]{:S(2)}) async-start(f32[8,2,16,128]{3,2,1,0:T(8,128)} %shard_map.71), calls=%async_computation.1 | async-start | bytes 262144 | tf_op jit(solution)/shard_map/all_to_all | solution.py:195
  43.0 10.2 %copy-start.12 = (f32[4,32,896]{2,1,0:T(8,128)}, f32[4,32,896]{2,1,0:T(8,128)S(1)}, u32[]{:S(2)}) copy-start(f32[4,32,896]{2,1,0:T(8,128)S(1)} %collective-permute-done.4.refs_5_.refs_2_) | copy-start | bytes 1376260
  57.2 22.4 %copy-start.2 = (f32[8,2,16,128]{3,2,1,0:T(8,128)S(1)}, f32[8,2,16,128]{3,2,1,0:T(8,128)}, u32[]{:S(2)}) copy-start(f32[8,2,16,128]{3,2,1,0:T(8,128)} %copy-done.1) | copy-start | bytes 393220
  57.2 22.4 %copy-start.9 = (s32[2]{0:T(128)S(1)}, s32[2]{0:T(128)}, u32[]{:S(2)}) copy-start(s32[2]{0:T(128)} %pad_add_fusion.place) | copy-start | bytes 28
  57.2 22.3 %all-to-all-start.2 = ((f32[8,5,16,128]{3,2,1,0:T(8,128)}), f32[8,5,16,128]{3,2,1,0:T(8,128)S(1)}, u32[]{:S(2)}, u32[]{:S(2)}) async-start(f32[8,5,16,128]{3,2,1,0:T(8,128)} %shard_map.72), calls=%async_computation.2 | async-start | bytes 655360 | tf_op jit(solution)/shard_map/all_to_all | solution.py:195
  65.2 12.2 %collective-permute-start.9 = (f32[4,32,896]{2,1,0:T(8,128)}, f32[4,32,896]{2,1,0:T(8,128)S(1)}, u32[]{:S(2)}, u32[]{:S(2)}) collective-permute-start(f32[4,32,896]{2,1,0:T(8,128)} %get-tuple-element.34), channel_id=1, source_target_pairs={{0,1},{1,2},{2,3},{3,0},{4,5},{5,6},{6,7},{7,4},{8,9},{9,10},{10,1... | collective-permute-start | bytes 1376264 | tf_op jit(solution)/shard_map/ppermute | solution.py:172
  67.6 11.9 %collective-permute-start.10 = (f32[4,32,896]{2,1,0:T(8,128)}, f32[4,32,896]{2,1,0:T(8,128)S(1)}, u32[]{:S(2)}, u32[]{:S(2)}) collective-permute-start(f32[4,32,896]{2,1,0:T(8,128)} %get-tuple-element.35), channel_id=1, source_target_pairs={{0,3},{1,0},{2,1},{3,2},{4,7},{5,4},{6,5},{7,6},{8,11},{9,8},{10,9... | collective-permute-start | bytes 1376264 | tf_op jit(solution)/shard_map/ppermute | solution.py:172
  82.9 13.6 %copy-start.22 = (f32[4,32,896]{2,1,0:T(8,128)S(1)}, f32[4,32,896]{2,1,0:T(8,128)}, u32[]{:S(2)}) copy-start(f32[4,32,896]{2,1,0:T(8,128)} %get-tuple-element.38) | copy-start | bytes 1376260
  82.9 41.7 %all-to-all-start.3 = ((f32[32,8,16,128]{3,2,1,0:T(8,128)}), f32[32,8,16,128]{3,2,1,0:T(8,128)S(1)}, u32[]{:S(2)}, u32[]{:S(2)}) async-start(f32[32,8,16,128]{3,2,1,0:T(8,128)} %shard_map.75), calls=%async_computation.3 | async-start | bytes 4194304 | tf_op jit(solution)/shard_map/all_to_all | solution.py:195
  90.5 15.3 %collective-permute-start.12 = (f32[4,32,896]{2,1,0:T(8,128)}, f32[4,32,896]{2,1,0:T(8,128)S(1)}, u32[]{:S(2)}, u32[]{:S(2)}) collective-permute-start(f32[4,32,896]{2,1,0:T(8,128)} %get-tuple-element.39), channel_id=1, source_target_pairs={{0,4},{4,8},{8,12},{12,16},{16,20},{20,24},{24,28},{28,0},{1,5},{5... | collective-permute-start | bytes 1376264 | tf_op jit(solution)/shard_map/ppermute | solution.py:176
  92.3 13.4 %collective-permute-start.13 = (f32[4,32,896]{2,1,0:T(8,128)}, f32[4,32,896]{2,1,0:T(8,128)S(1)}, u32[]{:S(2)}, u32[]{:S(2)}) collective-permute-start(f32[4,32,896]{2,1,0:T(8,128)} %get-tuple-element.40), channel_id=1, source_target_pairs={{0,28},{4,0},{8,4},{12,8},{16,12},{20,16},{24,20},{28,24},{1,29},{... | collective-permute-start | bytes 1376264 | tf_op jit(solution)/shard_map/ppermute | solution.py:176
  93.8 21.8 %collective-permute-start.14 = (f32[4,32,896]{2,1,0:T(8,128)}, f32[4,32,896]{2,1,0:T(8,128)S(1)}, u32[]{:S(2)}, u32[]{:S(2)}) collective-permute-start(f32[4,32,896]{2,1,0:T(8,128)} %get-tuple-element.41), channel_id=1, source_target_pairs={{0,24},{4,28},{8,0},{12,4},{16,8},{20,12},{24,16},{28,20},{32,40},... | collective-permute-start | bytes 1376264 | tf_op jit(solution)/shard_map/ppermute | solution.py:183
  96.5 28.1 %collective-permute-start.11 = (f32[4,32,896]{2,1,0:T(8,128)S(1)}, f32[4,32,896]{2,1,0:T(8,128)}, u32[]{:S(2)}, u32[]{:S(2)}) collective-permute-start(f32[4,32,896]{2,1,0:T(8,128)S(1)} %copy-done.22), channel_id=1, source_target_pairs={{0,2},{1,3},{2,0},{3,1},{4,6},{5,7},{6,4},{7,5},{8,10},{9,11},{10,... | collective-permute-start | bytes 1376264 | tf_op jit(solution)/shard_map/ppermute | solution.py:172
  105.8 18.8 %copy-start.23 = (f32[4,32,896]{2,1,0:T(8,128)}, f32[4,32,896]{2,1,0:T(8,128)S(1)}, u32[]{:S(2)}) copy-start(f32[4,32,896]{2,1,0:T(8,128)S(1)} %collective-permute-done.12.refs_5_) | copy-start | bytes 1376260
  105.8 18.8 %copy-start.24 = (f32[4,32,896]{2,1,0:T(8,128)}, f32[4,32,896]{2,1,0:T(8,128)S(1)}, u32[]{:S(2)}) copy-start(f32[4,32,896]{2,1,0:T(8,128)S(1)} %collective-permute-done.13.refs_6_) | copy-start | bytes 1376260
  134.0 56.0 %all-to-all-start.4 = ((f32[32,16,896]{2,1,0:T(8,128)}), f32[32,16,896]{2,1,0:T(8,128)S(1)}, u32[]{:S(2)}, u32[]{:S(2)}) async-start(f32[32,16,896]{2,1,0:T(8,128)} %shard_map.76), calls=%async_computation.4 | async-start | bytes 3670016 | tf_op jit(solution)/shard_map/all_to_all | solution.py:195
  146.5 43.7 %copy-start.20 = (f32[16,14336]{1,0:T(8,128)S(1)}, f32[16,14336]{1,0:T(8,128)}, u32[]{:S(2)}) copy-start(f32[16,14336]{1,0:T(8,128)} %param.9) | copy-start | bytes 2752516
  (14 other events, 31.2 us)

commit v17 on v11

--- a/solution.py
+++ b/solution.py
@@ -73,27 +73,36 @@
         shared[r][64:72, 128:256] = piece[8:16]
 
 
-def in_order(place, shared, rows, matrix):
-    for r in range(Y):
-        matrix[(place[1] + Y - r) % Y] = shared[r][rows]
-    return matrix[...].reshape(Y * 32, -1)
+def fetch(place, shared, rows, matrix, sems):
+    copies = [
+        pltpu.make_async_copy(shared[r].at[rows], matrix.at[(place[1] + Y - r) % Y], sems.at[r]) for r in range(Y)
+    ]
+    for copy in copies:
+        copy.start()
+    return copies
 
 
 def couple_kernel(place, arrived, *refs):
-    shared, (terms, matrix) = refs[:Y], refs[-2:]
+    shared, (terms, matrix, sems) = refs[:Y], refs[-3:]
+    copies = fetch(place, shared, pl.ds(0, 32), matrix, sems)
     total = jnp.sum(arrived[...], axis=0)
-    product = exact_dot(total, in_order(place, shared, slice(0, 32), matrix))
+    for copy in copies:
+        copy.wait()
+    product = exact_dot(total, matrix[...].reshape(Y * 32, -1))
     for z in range(Z):
         terms[z, 0] = product[:, z * 128:(z + 1) * 128]
         terms[z, 1] = total
 
 
 def latter_kernel(place, arrived, *refs):
-    shared, (terms, matrix) = refs[:Y], refs[-2:]
-    rhs = sum(piece[64:72] for piece in shared)
+    shared, (terms, matrix, sems) = refs[:Y], refs[-3:]
+    copies = fetch(place, shared, pl.ds(32, 40), matrix, sems)
+    for copy in copies:
+        copy.wait()
+    rhs = jnp.sum(matrix[:, 32:40], axis=0)
     rhs = jnp.concatenate([rhs[:, 0:128], rhs[:, 128:256]], axis=0)
     second = rhs - jnp.sum(arrived[:, 0], axis=0)
-    product = exact_dot(second, in_order(place, shared, slice(32, 64), matrix))
+    product = exact_dot(second, matrix[:, 0:32].reshape(Y * 32, -1))
     part = lambda z: product[:, (z % Z) * 128:(z % Z + 1) * 128]
     for z in range(Z):
         for k, step in enumerate(NEAR):
@@ -203,7 +212,7 @@
     width = trail_rhs.shape[1] // (QUAD * Y)
     block = f32(QUAD, 32, width)
     sems = lambda n: [pltpu.SemaphoreType.DMA((n,))]
-    matrix = [pltpu.VMEM((Y, 32, 1024), jnp.float32)]
+    matrix = lambda rows: [pltpu.VMEM((Y, rows, 1024), jnp.float32)] + sems(Y)
 
     rhs = panel_rhs.transpose(1, 0, 2)
     lanes = lax.broadcasted_iota(jnp.int32, (1, 128), 1) // narrow
@@ -223,7 +232,7 @@
 
     terms = call(
         couple_kernel, f32(Z, 2, 16, 128), (place, arrived, *shared, cut[0], cut[4]),
-        VMEM, (SMEM,) + (VMEM,) * 5 + (ANY,) * 2, matrix, limit=60,
+        VMEM, (SMEM, VMEM) + (ANY,) * 6, matrix(32), limit=60,
     )
     first = exchange(terms, "z")
     by_r = call(turn_kernel, (block,) * 4, by_class, (ANY,) * 4, (VMEM,) * 4, sems(16), moved=3670016, limit=60)
@@ -231,7 +240,7 @@
 
     terms = call(
         latter_kernel, f32(Z, len(NEAR), 16, 128), (place, first, *shared, *by_class[1:], *by_y[1:]),
-        VMEM, (SMEM,) + (VMEM,) * 5 + (ANY,) * 6, matrix, limit=60,
+        VMEM, (SMEM, VMEM) + (ANY,) * 10, matrix(40), limit=60,
     )
     arrived = exchange(terms, "z")
     by_k = call(merge_kernel, (block,) * 4, (place, *by_y), (ANY,) * 4, (SMEM,) + (VMEM,) * 4, sems(16), moved=3670016, limit=60)

time: 189 us -> 190 us (level)
  transfers between devices with their start and end apart: 20 -> 20, of which waited for: 9 -> 9; matrix products, arithmetic and copies ran while one was open for 1% -> 1% of each run, Pallas kernels for 5% -> 6%
where the time goes in v17:
time: 190 us
  waiting for transfers between devices  92.6 us (49%)
  starting transfers between devices  60 us (32%)
  Pallas kernels  28.1 us (15%)
  local copies, waits for them, and re-layouts  6.11 us (3%)
    all_to_all x5, waiting for transfers between devices, exchange(): return lax.all_to_all(value, axes, 0, 0, tiled=True)  48.5 us
    all_to_all x5, starting transfers between devices, exchange(): return lax.all_to_all(value, axes, 0, 0, tiled=True)  38.1 us
    pallas_call x9, Pallas kernels, call(): pl.pallas_call(kernel, out_shape=outs, in_specs=in_specs, out_specs=out_s...  28.1 us
    ppermute x2, waiting for transfers between devices, shift_far(): return lax.ppermute(value, ('c', 'z'), pairs)  19 us
    ppermute x9, waiting for transfers between devices, shift_y(): return lax.ppermute(value, 'y', [(y, (y + step) % Y) for y in range(Y)])  16.4 us
    ppermute x9, starting transfers between devices, shift_y(): return lax.ppermute(value, 'y', [(y, (y + step) % Y) for y in range(Y)])  8.79 us
    ppermute x4, waiting for transfers between devices, shift_z(): return lax.ppermute(value, 'z', [(z, (z + step) % Z) for z in range(Z)])  8.77 us
    ppermute x4, starting transfers between devices, shift_z(): return lax.ppermute(value, 'z', [(z, (z + step) % Z) for z in range(Z)])  8.14 us
  transfers between devices with their start and end apart: 20, of which 9 were waited for; matrix products, arithmetic and copies ran while one was open for 1% of the time, Pallas kernels for 6%

profile of v17, /device:TPU:20, one launch (start us, length us, event | category | flops | bytes accessed | tf_op | source)
XLA Modules:
  0.0 189.6 jit_solution(15872265207794776397)
XLA Ops:
  1.3 4.2 %shard_map.70 = (f32[4,32,896]{2,1,0:T(8,128)}, f32[4,32,896]{2,1,0:T(8,128)}, f32[4,32,896]{2,1,0:T(8,128)}, f32[4,32,896]{2,1,0:T(8,128)}, f32[4,32,896]{2,1,0...) custom-call(s32[2]{0:T(128)} %pad_add_fusion.place, f32[2,32,14336]{2,1,0:T(8,128)} %factor.1), custom_call_target="tpu_custom_call" | custom-call | bytes 7340032 | tf_op jit(solution)/shard_map/pallas_call | solution.py:26
  5.5 2.0 %collective-permute-start.3 = (f32[4,32,896]{2,1,0:T(8,128)}, f32[4,32,896]{2,1,0:T(8,128)S(1)}, u32[]{:S(2)}, u32[]{:S(2)}) collective-permute-start(f32[4,32,896]{2,1,0:T(8,128)} %get-tuple-element.28), channel_id=1, source_target_pairs={{0,4},{4,8},{8,12},{12,16},{16,20},{20,24},{24,28},{28,0},{1,5},{5... | collective-permute-start | bytes 1376264 | tf_op jit(solution)/shard_map/ppermute | solution.py:185
  9.2 1.3 collective-permute-start
  11.1 1.1 collective-permute-start.2
  13.2 11.1 %all-to-all-start = ((f32[32,16,128]{2,1,0:T(8,128)}), f32[32,16,128]{2,1,0:T(8,128)}, u32[]{:S(2)}, u32[]{:S(2)}) async-start(f32[32,16,128]{2,1,0:T(8,128)} %shard_map.68), calls=%async_computation | async-start | bytes 524288 | tf_op jit(solution)/shard_map/all_to_all | solution.py:204
  24.3 2.8 %collective-permute-start.4 = (f32[4,32,896]{2,1,0:T(8,128)}, f32[4,32,896]{2,1,0:T(8,128)S(1)}, u32[]{:S(2)}, u32[]{:S(2)}) collective-permute-start(f32[4,32,896]{2,1,0:T(8,128)} %get-tuple-element.29), channel_id=1, source_target_pairs={{0,28},{4,0},{8,4},{12,8},{16,12},{20,16},{24,20},{28,24},{1,29},{... | collective-permute-start | bytes 1376264 | tf_op jit(solution)/shard_map/ppermute | solution.py:185
  27.1 2.3 %collective-permute-start.5 = (f32[4,32,896]{2,1,0:T(8,128)}, f32[4,32,896]{2,1,0:T(8,128)S(1)}, u32[]{:S(2)}, u32[]{:S(2)}) collective-permute-start(f32[4,32,896]{2,1,0:T(8,128)} %get-tuple-element.30), channel_id=1, source_target_pairs={{0,24},{4,28},{8,0},{12,4},{16,8},{20,12},{24,16},{28,20},{32,40},... | collective-permute-start | bytes 1376264 | tf_op jit(solution)/shard_map/ppermute | solution.py:192
  29.4 1.2 collective-permute-start.6
  31.5 1.2 collective-permute-start.8
  32.6 4.6 %all-to-all-done.arrived = f32[32,16,128]{2,1,0:T(8,128)} async-done(((f32[32,16,128]{2,1,0:T(8,128)}), f32[32,16,128]{2,1,0:T(8,128)}, u32[]{:S(2)}, u32[]{:S(2)}) %all-to-all-start) | async-done | bytes 262176 | tf_op jit(solution)/shard_map/all_to_all | solution.py:204
  37.2 3.1 %shard_map.71 = f32[8,2,16,128]{3,2,1,0:T(8,128)} custom-call(s32[2]{0:T(128)} %pad_add_fusion.place, f32[32,16,128]{2,1,0:T(8,128)} %all-to-all-done.arrived, f32[72,1024]{1,0:T(8,128)} %copy-done, f32[72,1024]{1,0:T(8,128)} %copy-done.15, f32[72,1024]{1,0:T(8,128)} %copy-done.16, f32[72,1024]{1,0:T(8,128)} %copy-done.17, ...), custom_call_target="tpu_custom_call" | custom-call | tf_op jit(solution)/shard_map/pallas_call | solution.py:26
  40.4 3.4 %all-to-all-start.1 = ((f32[8,2,16,128]{3,2,1,0:T(8,128)}), f32[8,2,16,128]{3,2,1,0:T(8,128)S(1)}, u32[]{:S(2)}, u32[]{:S(2)}) async-start(f32[8,2,16,128]{3,2,1,0:T(8,128)} %shard_map.71), calls=%async_computation.1 | async-start | bytes 262144 | tf_op jit(solution)/shard_map/all_to_all | solution.py:204
  43.8 9.1 %collective-permute-done.5.refs_6_.refs_3_ = f32[4,32,896]{2,1,0:T(8,128)S(1)} collective-permute-done((f32[4,32,896]{2,1,0:T(8,128)}, f32[4,32,896]{2,1,0:T(8,128)S(1)}, u32[]{:S(2)}, u32[]{:S(2)}) %collective-permute-start.5) | collective-permute-done | bytes 458784 | tf_op jit(solution)/shard_map/ppermute | solution.py:192
  54.6 3.2 %shard_map.72 = f32[8,5,16,128]{3,2,1,0:T(8,128)} custom-call(s32[2]{0:T(128)} %pad_add_fusion.place, f32[8,2,16,128]{3,2,1,0:T(8,128)} %copy-done.1, f32[72,1024]{1,0:T(8,128)} %copy-done, f32[72,1024]{1,0:T(8,128)} %copy-done.15, f32[72,1024]{1,0:T(8,128)} %copy-done.16, f32[72,1024]{1,0:T(8,128)} %copy-done.17, f32[4,32,896]{2,1,0:T(8,128)} %copy-done.10, ...), custom_call_target="tpu_custom_call" | custom-call | tf_op jit(solution)/shard_map/pallas_call | solution.py:26
  57.9 5.2 %all-to-all-start.2 = ((f32[8,5,16,128]{3,2,1,0:T(8,128)}), f32[8,5,16,128]{3,2,1,0:T(8,128)S(1)}, u32[]{:S(2)}, u32[]{:S(2)}) async-start(f32[8,5,16,128]{3,2,1,0:T(8,128)} %shard_map.72), calls=%async_computation.2 | async-start | bytes 655360 | tf_op jit(solution)/shard_map/all_to_all | solution.py:204
  63.1 2.8 %shard_map.73 = (f32[4,32,896]{2,1,0:T(8,128)}, f32[4,32,896]{2,1,0:T(8,128)}, f32[4,32,896]{2,1,0:T(8,128)}, f32[4,32,896]{2,1,0:T(8,128)}) custom-call(f32[4,32,896]{2,1,0:T(8,128)} %get-tuple-element.26.refs_4_.refs_0_, f32[4,32,896]{2,1,0:T(8,128)} %copy-done.10, f32[4,32,896]{2,1,0:T(8,128)} %copy-done.11, f32[4,32,896]{2,1,0:T(8,128)} %copy-done.12), custom_call_target="tpu_custom_call" | custom-call | bytes 3670016 | tf_op jit(solution)/shard_map/pallas_call | solution.py:26
  65.9 1.3 collective-permute-start.9
  68.0 9.0 %collective-permute-done.9.refs_0_.refs_1_ = f32[4,32,896]{2,1,0:T(8,128)S(1)} collective-permute-done((f32[4,32,896]{2,1,0:T(8,128)}, f32[4,32,896]{2,1,0:T(8,128)S(1)}, u32[]{:S(2)}, u32[]{:S(2)}) %collective-permute-start.9) | collective-permute-done | bytes 458784 | tf_op jit(solution)/shard_map/ppermute | solution.py:181
  77.0 2.1 %collective-permute-done.10.refs_1_.refs_3_ = f32[4,32,896]{2,1,0:T(8,128)S(1)} collective-permute-done((f32[4,32,896]{2,1,0:T(8,128)}, f32[4,32,896]{2,1,0:T(8,128)S(1)}, u32[]{:S(2)}, u32[]{:S(2)}) %collective-permute-start.10) | collective-permute-done | bytes 458784 | tf_op jit(solution)/shard_map/ppermute | solution.py:181
  79.1 2.1 %shard_map.74 = f32[32,8,16,128]{3,2,1,0:T(8,128)} custom-call(s32[2]{0:T(128)S(1)} %copy-done.8, f32[8,2,16,128]{3,2,1,0:T(8,128)S(1)} %copy-done.2, f32[8,5,16,128]{3,2,1,0:T(8,128)S(1)} %all-to-all-done.2.arrived, f32[4,32,896]{2,1,0:T(8,128)S(1)} %collective-permute-done.9.refs_0_.refs_1_, f32[4,32,896]{2,1,0:T(8,128)S(1)} %collective-permute-done.10.refs_1_.refs_3_), custom_call_target="tpu_custom_call" | custom-call | tf_op jit(solution)/shard_map/pallas_call | solution.py:26
  81.2 7.6 %all-to-all-start.3 = ((f32[32,8,16,128]{3,2,1,0:T(8,128)}), f32[32,8,16,128]{3,2,1,0:T(8,128)S(1)}, u32[]{:S(2)}, u32[]{:S(2)}) async-start(f32[32,8,16,128]{3,2,1,0:T(8,128)} %shard_map.74), calls=%async_computation.3 | async-start | bytes 4194304 | tf_op jit(solution)/shard_map/all_to_all | solution.py:204
  88.9 2.9 %shard_map.75 = (f32[4,32,896]{2,1,0:T(8,128)}, f32[4,32,896]{2,1,0:T(8,128)}, f32[4,32,896]{2,1,0:T(8,128)}, f32[4,32,896]{2,1,0:T(8,128)}) custom-call(s32[2]{0:T(128)} %pad_add_fusion.place, f32[4,32,896]{2,1,0:T(8,128)} %get-tuple-element.27.refs_5_.refs_0_, f32[4,32,896]{2,1,0:T(8,128)} %copy-done.13, f32[4,32,896]{2,1,0:T(8,128)} %copy-done.14, ...), custom_call_target="tpu_custom_call" | custom-call | bytes 3670016 | tf_op jit(solution)/shard_map/pallas_call | solution.py:26
  91.8 1.8 collective-permute-start.12
  93.6 1.5 collective-permute-start.13
  95.1 2.6 %collective-permute-start.14 = (f32[4,32,896]{2,1,0:T(8,128)}, f32[4,32,896]{2,1,0:T(8,128)S(1)}, u32[]{:S(2)}, u32[]{:S(2)}) collective-permute-start(f32[4,32,896]{2,1,0:T(8,128)} %get-tuple-element.41), channel_id=1, source_target_pairs={{0,24},{4,28},{8,0},{12,4},{16,8},{20,12},{24,16},{28,20},{32,40},... | collective-permute-start | bytes 1376264 | tf_op jit(solution)/shard_map/ppermute | solution.py:192
  98.2 8.8 %collective-permute-done.12.refs_5_ = f32[4,32,896]{2,1,0:T(8,128)S(1)} collective-permute-done((f32[4,32,896]{2,1,0:T(8,128)}, f32[4,32,896]{2,1,0:T(8,128)S(1)}, u32[]{:S(2)}, u32[]{:S(2)}) %collective-permute-start.12) | collective-permute-done | bytes 458784 | tf_op jit(solution)/shard_map/ppermute | solution.py:185
  107.0 9.8 %collective-permute-done.14.refs_7_ = f32[4,32,896]{2,1,0:T(8,128)S(1)} collective-permute-done((f32[4,32,896]{2,1,0:T(8,128)}, f32[4,32,896]{2,1,0:T(8,128)S(1)}, u32[]{:S(2)}, u32[]{:S(2)}) %collective-permute-start.14) | collective-permute-done | bytes 458784 | tf_op jit(solution)/shard_map/ppermute | solution.py:192
  117.6 5.3 %collective-permute-done.11.refs_2_ = f32[4,32,896]{2,1,0:T(8,128)} collective-permute-done((f32[4,32,896]{2,1,0:T(8,128)S(1)}, f32[4,32,896]{2,1,0:T(8,128)}, u32[]{:S(2)}, u32[]{:S(2)}) %collective-permute-start.11) | collective-permute-done | bytes 458784 | tf_op jit(solution)/shard_map/ppermute | solution.py:181
  123.0 1.3 copy-done.9
  124.3 8.1 %shard_map.76 = f32[32,16,896]{2,1,0:T(8,128)} custom-call(s32[2]{0:T(128)} %pad_add_fusion.place, f32[32,8,16,128]{3,2,1,0:T(8,128)} %copy-done.9, f32[4,32,896]{2,1,0:T(8,128)} %get-tuple-element.36.refs_0_, f32[4,32,896]{2,1,0:T(8,128)} %copy-done.4, f32[4,32,896]{2,1,0:T(8,128)} %collective-permute-done.11.refs_2_, f32[4,32,896]{2,1,0:T(8,128)} %copy-done.5, ...), custom_call_target="tpu_custom_call" | custom-call | flops 2818572288 | bytes 7602176 | tf_op jit(solution)/shard_map/pallas_call | solution.py:26
  132.4 10.8 %all-to-all-start.4 = ((f32[32,16,896]{2,1,0:T(8,128)}), f32[32,16,896]{2,1,0:T(8,128)S(1)}, u32[]{:S(2)}, u32[]{:S(2)}) async-start(f32[32,16,896]{2,1,0:T(8,128)} %shard_map.76), calls=%async_computation.4 | async-start | bytes 3670016 | tf_op jit(solution)/shard_map/all_to_all | solution.py:204
  144.8 43.6 %all-to-all-done.4 = f32[32,16,896]{2,1,0:T(8,128)S(1)} async-done(((f32[32,16,896]{2,1,0:T(8,128)}), f32[32,16,896]{2,1,0:T(8,128)S(1)}, u32[]{:S(2)}, u32[]{:S(2)}) %all-to-all-start.4) | async-done | bytes 1835040 | tf_op jit(solution)/shard_map/all_to_all | solution.py:204
  (79 shorter events, 11.5 us)
Async XLA Ops:
  0.6 6.9 %copy-start.19 = (f32[64,2,32]{0,2,1:T(8,128)S(1)}, f32[64,2,32]{0,2,1:T(8,128)}, u32[]{:S(2)}) copy-start(f32[64,2,32]{0,2,1:T(8,128)} %param.5) | copy-start | bytes 49156
  5.5 26.0 %collective-permute-start.3 = (f32[4,32,896]{2,1,0:T(8,128)}, f32[4,32,896]{2,1,0:T(8,128)S(1)}, u32[]{:S(2)}, u32[]{:S(2)}) collective-permute-start(f32[4,32,896]{2,1,0:T(8,128)} %get-tuple-element.28), channel_id=1, source_target_pairs={{0,4},{4,8},{8,12},{12,16},{16,20},{20,24},{24,28},{28,0},{1,5},{5... | collective-permute-start | bytes 1376264 | tf_op jit(solution)/shard_map/ppermute | solution.py:185
  9.2 17.9 %collective-permute-start = (f32[72,1024]{1,0:T(8,128)S(1)}, f32[72,1024]{1,0:T(8,128)S(1)}, u32[]{:S(2)}, u32[]{:S(2)}) collective-permute-start(f32[72,1024]{1,0:T(8,128)S(1)} %get-tuple-element.23), channel_id=1, source_target_pairs={{0,1},{1,2},{2,3},{3,0},{4,5},{5,6},{6,7},{7,4},{8,9},{9,10},{10,1... | collective-permute-start | bytes 884744 | tf_op jit(solution)/shard_map/ppermute | solution.py:181
  10.5 19.0 %collective-permute-start.1 = (f32[72,1024]{1,0:T(8,128)S(1)}, f32[72,1024]{1,0:T(8,128)S(1)}, u32[]{:S(2)}, u32[]{:S(2)}) collective-permute-start(f32[72,1024]{1,0:T(8,128)S(1)} %get-tuple-element.24), channel_id=1, source_target_pairs={{0,2},{1,3},{2,0},{3,1},{4,6},{5,7},{6,4},{7,5},{8,10},{9,11},{10,... | collective-permute-start | bytes 884744 | tf_op jit(solution)/shard_map/ppermute | solution.py:181
  11.1 19.5 %collective-permute-start.2 = (f32[72,1024]{1,0:T(8,128)S(1)}, f32[72,1024]{1,0:T(8,128)S(1)}, u32[]{:S(2)}, u32[]{:S(2)}) collective-permute-start(f32[72,1024]{1,0:T(8,128)S(1)} %get-tuple-element.25), channel_id=1, source_target_pairs={{0,3},{1,0},{2,1},{3,2},{4,7},{5,4},{6,5},{7,6},{8,11},{9,8},{10,9... | collective-permute-start | bytes 884744 | tf_op jit(solution)/shard_map/ppermute | solution.py:181
  13.2 24.0 %all-to-all-start = ((f32[32,16,128]{2,1,0:T(8,128)}), f32[32,16,128]{2,1,0:T(8,128)}, u32[]{:S(2)}, u32[]{:S(2)}) async-start(f32[32,16,128]{2,1,0:T(8,128)} %shard_map.68), calls=%async_computation | async-start | bytes 524288 | tf_op jit(solution)/shard_map/all_to_all | solution.py:204
  24.3 19.5 %collective-permute-start.4 = (f32[4,32,896]{2,1,0:T(8,128)}, f32[4,32,896]{2,1,0:T(8,128)S(1)}, u32[]{:S(2)}, u32[]{:S(2)}) collective-permute-start(f32[4,32,896]{2,1,0:T(8,128)} %get-tuple-element.29), channel_id=1, source_target_pairs={{0,28},{4,0},{8,4},{12,8},{16,12},{20,16},{24,20},{28,24},{1,29},{... | collective-permute-start | bytes 1376264 | tf_op jit(solution)/shard_map/ppermute | solution.py:185
  27.1 10.1 %copy-start.15 = (f32[72,1024]{1,0:T(8,128)}, f32[72,1024]{1,0:T(8,128)S(1)}, u32[]{:S(2)}) copy-start(f32[72,1024]{1,0:T(8,128)S(1)} %collective-permute-done.refs_1_) | copy-start | bytes 884740
  27.1 25.8 %collective-permute-start.5 = (f32[4,32,896]{2,1,0:T(8,128)}, f32[4,32,896]{2,1,0:T(8,128)S(1)}, u32[]{:S(2)}, u32[]{:S(2)}) collective-permute-start(f32[4,32,896]{2,1,0:T(8,128)} %get-tuple-element.30), channel_id=1, source_target_pairs={{0,24},{4,28},{8,0},{12,4},{16,8},{20,12},{24,16},{28,20},{32,40},... | collective-permute-start | bytes 1376264 | tf_op jit(solution)/shard_map/ppermute | solution.py:192
  29.4 7.8 %copy-start.16 = (f32[72,1024]{1,0:T(8,128)}, f32[72,1024]{1,0:T(8,128)S(1)}, u32[]{:S(2)}) copy-start(f32[72,1024]{1,0:T(8,128)S(1)} %collective-permute-done.1.refs_2_) | copy-start | bytes 884740
  29.4 23.5 %collective-permute-start.6 = (f32[4,32,896]{2,1,0:T(8,128)}, f32[4,32,896]{2,1,0:T(8,128)S(1)}, u32[]{:S(2)}, u32[]{:S(2)}) collective-permute-start(f32[4,32,896]{2,1,0:T(8,128)} %get-tuple-element.31), channel_id=1, source_target_pairs={{0,1},{1,2},{2,3},{3,0},{4,5},{5,6},{6,7},{7,4},{8,9},{9,10},{10,1... | collective-permute-start | bytes 1376264 | tf_op jit(solution)/shard_map/ppermute | solution.py:181
  30.6 6.6 %copy-start.17 = (f32[72,1024]{1,0:T(8,128)}, f32[72,1024]{1,0:T(8,128)S(1)}, u32[]{:S(2)}) copy-start(f32[72,1024]{1,0:T(8,128)S(1)} %collective-permute-done.2.refs_3_) | copy-start | bytes 884740
  30.6 22.3 %collective-permute-start.7 = (f32[4,32,896]{2,1,0:T(8,128)}, f32[4,32,896]{2,1,0:T(8,128)S(1)}, u32[]{:S(2)}, u32[]{:S(2)}) collective-permute-start(f32[4,32,896]{2,1,0:T(8,128)} %get-tuple-element.32), channel_id=1, source_target_pairs={{0,2},{1,3},{2,0},{3,1},{4,6},{5,7},{6,4},{7,5},{8,10},{9,11},{10,... | collective-permute-start | bytes 1376264 | tf_op jit(solution)/shard_map/ppermute | solution.py:181
  31.5 21.8 %copy-start.10 = (f32[4,32,896]{2,1,0:T(8,128)}, f32[4,32,896]{2,1,0:T(8,128)S(1)}, u32[]{:S(2)}) copy-start(f32[4,32,896]{2,1,0:T(8,128)S(1)} %collective-permute-done.3.refs_4_.refs_1_) | copy-start | bytes 1376260
  31.5 21.5 %collective-permute-start.8 = (f32[4,32,896]{2,1,0:T(8,128)}, f32[4,32,896]{2,1,0:T(8,128)}, u32[]{:S(2)}, u32[]{:S(2)}) collective-permute-start(f32[4,32,896]{2,1,0:T(8,128)} %get-tuple-element.33), channel_id=1, source_target_pairs={{0,3},{1,0},{2,1},{3,2},{4,7},{5,4},{6,5},{7,6},{8,11},{9,8},{10,9... | collective-permute-start | bytes 1376264 | tf_op jit(solution)/shard_map/ppermute | solution.py:181
  40.4 12.9 %all-to-all-start.1 = ((f32[8,2,16,128]{3,2,1,0:T(8,128)}), f32[8,2,16,128]{3,2,1,0:T(8,128)S(1)}, u32[]{:S(2)}, u32[]{:S(2)}) async-start(f32[8,2,16,128]{3,2,1,0:T(8,128)} %shard_map.71), calls=%async_computation.1 | async-start | bytes 262144 | tf_op jit(solution)/shard_map/all_to_all | solution.py:204
  43.8 9.5 %copy-start.11 = (f32[4,32,896]{2,1,0:T(8,128)}, f32[4,32,896]{2,1,0:T(8,128)S(1)}, u32[]{:S(2)}) copy-start(f32[4,32,896]{2,1,0:T(8,128)S(1)} %collective-permute-done.4.refs_5_.refs_2_) | copy-start | bytes 1376260
  57.9 21.3 %copy-start.2 = (f32[8,2,16,128]{3,2,1,0:T(8,128)S(1)}, f32[8,2,16,128]{3,2,1,0:T(8,128)}, u32[]{:S(2)}) copy-start(f32[8,2,16,128]{3,2,1,0:T(8,128)} %copy-done.1) | copy-start | bytes 393220
  57.9 21.2 %copy-start.8 = (s32[2]{0:T(128)S(1)}, s32[2]{0:T(128)}, u32[]{:S(2)}) copy-start(s32[2]{0:T(128)} %pad_add_fusion.place) | copy-start | bytes 28
  57.9 21.2 %all-to-all-start.2 = ((f32[8,5,16,128]{3,2,1,0:T(8,128)}), f32[8,5,16,128]{3,2,1,0:T(8,128)S(1)}, u32[]{:S(2)}, u32[]{:S(2)}) async-start(f32[8,5,16,128]{3,2,1,0:T(8,128)} %shard_map.72), calls=%async_computation.2 | async-start | bytes 655360 | tf_op jit(solution)/shard_map/all_to_all | solution.py:204
  65.9 11.1 %collective-permute-start.9 = (f32[4,32,896]{2,1,0:T(8,128)}, f32[4,32,896]{2,1,0:T(8,128)S(1)}, u32[]{:S(2)}, u32[]{:S(2)}) collective-permute-start(f32[4,32,896]{2,1,0:T(8,128)} %get-tuple-element.34), channel_id=1, source_target_pairs={{0,1},{1,2},{2,3},{3,0},{4,5},{5,6},{6,7},{7,4},{8,9},{9,10},{10,1... | collective-permute-start | bytes 1376264 | tf_op jit(solution)/shard_map/ppermute | solution.py:181
  67.2 11.9 %collective-permute-start.10 = (f32[4,32,896]{2,1,0:T(8,128)}, f32[4,32,896]{2,1,0:T(8,128)S(1)}, u32[]{:S(2)}, u32[]{:S(2)}) collective-permute-start(f32[4,32,896]{2,1,0:T(8,128)} %get-tuple-element.35), channel_id=1, source_target_pairs={{0,3},{1,0},{2,1},{3,2},{4,7},{5,4},{6,5},{7,6},{8,11},{9,8},{10,9... | collective-permute-start | bytes 1376264 | tf_op jit(solution)/shard_map/ppermute | solution.py:181
  81.2 16.5 %copy-start.20 = (f32[4,32,896]{2,1,0:T(8,128)S(1)}, f32[4,32,896]{2,1,0:T(8,128)}, u32[]{:S(2)}) copy-start(f32[4,32,896]{2,1,0:T(8,128)} %get-tuple-element.37) | copy-start | bytes 1376260
  81.2 41.7 %all-to-all-start.3 = ((f32[32,8,16,128]{3,2,1,0:T(8,128)}), f32[32,8,16,128]{3,2,1,0:T(8,128)S(1)}, u32[]{:S(2)}, u32[]{:S(2)}) async-start(f32[32,8,16,128]{3,2,1,0:T(8,128)} %shard_map.74), calls=%async_computation.3 | async-start | bytes 4194304 | tf_op jit(solution)/shard_map/all_to_all | solution.py:204
  91.8 15.3 %collective-permute-start.12 = (f32[4,32,896]{2,1,0:T(8,128)}, f32[4,32,896]{2,1,0:T(8,128)S(1)}, u32[]{:S(2)}, u32[]{:S(2)}) collective-permute-start(f32[4,32,896]{2,1,0:T(8,128)} %get-tuple-element.39), channel_id=1, source_target_pairs={{0,4},{4,8},{8,12},{12,16},{16,20},{20,24},{24,28},{28,0},{1,5},{5... | collective-permute-start | bytes 1376264 | tf_op jit(solution)/shard_map/ppermute | solution.py:185
  93.6 13.4 %collective-permute-start.13 = (f32[4,32,896]{2,1,0:T(8,128)}, f32[4,32,896]{2,1,0:T(8,128)S(1)}, u32[]{:S(2)}, u32[]{:S(2)}) collective-permute-start(f32[4,32,896]{2,1,0:T(8,128)} %get-tuple-element.40), channel_id=1, source_target_pairs={{0,28},{4,0},{8,4},{12,8},{16,12},{20,16},{24,20},{28,24},{1,29},{... | collective-permute-start | bytes 1376264 | tf_op jit(solution)/shard_map/ppermute | solution.py:185
  95.1 21.8 %collective-permute-start.14 = (f32[4,32,896]{2,1,0:T(8,128)}, f32[4,32,896]{2,1,0:T(8,128)S(1)}, u32[]{:S(2)}, u32[]{:S(2)}) collective-permute-start(f32[4,32,896]{2,1,0:T(8,128)} %get-tuple-element.41), channel_id=1, source_target_pairs={{0,24},{4,28},{8,0},{12,4},{16,8},{20,12},{24,16},{28,20},{32,40},... | collective-permute-start | bytes 1376264 | tf_op jit(solution)/shard_map/ppermute | solution.py:192
  97.7 25.2 %collective-permute-start.11 = (f32[4,32,896]{2,1,0:T(8,128)S(1)}, f32[4,32,896]{2,1,0:T(8,128)}, u32[]{:S(2)}, u32[]{:S(2)}) collective-permute-start(f32[4,32,896]{2,1,0:T(8,128)S(1)} %copy-done.20), channel_id=1, source_target_pairs={{0,2},{1,3},{2,0},{3,1},{4,6},{5,7},{6,4},{7,5},{8,10},{9,11},{10,... | collective-permute-start | bytes 1376264 | tf_op jit(solution)/shard_map/ppermute | solution.py:181
  107.0 15.9 %copy-start.21 = (f32[4,32,896]{2,1,0:T(8,128)}, f32[4,32,896]{2,1,0:T(8,128)S(1)}, u32[]{:S(2)}) copy-start(f32[4,32,896]{2,1,0:T(8,128)S(1)} %collective-permute-done.12.refs_5_) | copy-start | bytes 1376260
  107.0 15.9 %copy-start.22 = (f32[4,32,896]{2,1,0:T(8,128)}, f32[4,32,896]{2,1,0:T(8,128)S(1)}, u32[]{:S(2)}) copy-start(f32[4,32,896]{2,1,0:T(8,128)S(1)} %collective-permute-done.13.refs_6_) | copy-start | bytes 1376260
  132.4 56.0 %all-to-all-start.4 = ((f32[32,16,896]{2,1,0:T(8,128)}), f32[32,16,896]{2,1,0:T(8,128)S(1)}, u32[]{:S(2)}, u32[]{:S(2)}) async-start(f32[32,16,896]{2,1,0:T(8,128)} %shard_map.76), calls=%async_computation.4 | async-start | bytes 3670016 | tf_op jit(solution)/shard_map/all_to_all | solution.py:204
  144.8 43.7 %copy-start.18 = (f32[16,14336]{1,0:T(8,128)S(1)}, f32[16,14336]{1,0:T(8,128)}, u32[]{:S(2)}) copy-start(f32[16,14336]{1,0:T(8,128)} %param.9) | copy-start | bytes 2752516
  (12 other events, 32.2 us)
